TPU v7x, 32 devices: a whole 2x2x4 slice. The times are simulated.
32 devices in a mesh: dp: 8 (over z, x), mp: 4 (over y, core).
Axes of the slice: x: 2, y: 2, z: 4, core: 2. Of those that a mesh axis runs over, the one named last changes fastest.
Arguments:
- out_grads: bfloat16 [2048, 8192], P('dp'), may hold values from -6 to 6
- hidden_acts: bfloat16 [2048, 28672], P('dp', 'mp'), may hold values from -6 to 6
- out_basis: bfloat16 [16, 512, 512], P('mp'), may hold values from -0.25 to 0.25
- in_basis: bfloat16 [112, 256, 256], P('mp'), may hold values from -0.375 to 0.375
- left_store: bfloat16 [8, 512, 8192], P('dp', None, 'mp'), may hold values from -0.0625 to 0.0625
- right_store: bfloat16 [8, 512, 28672], P('dp', None, 'mp'), may hold values from -0.03125 to 0.03125
- owners: int32 [16], replicated, may hold values from 0 to 7, as said below
Outputs:
- scores: float32 [16, 16], P('dp')
Inputs may be any that keep to these rules, and one draw needn't show every extreme that they name: `owners`: every group index is the owner of exactly 16 // 8 queries.
All inputs are finite; a program needn't handle non-finite values.
Results may differ from a plain program's by a relative error of at most 0.0003.
Values may be sent and summed in bfloat16 or wider, within the bound.
No kernel may reach another device: no remote copies, remote signals or barrier semaphores. Data moves between devices by JAX's collectives and lax.ppermute only.
A program may use at most 128 MiB of HBM per device.

v0:
```python
import jax
import jax.numpy as jnp
from jax import lax
from jax.sharding import PartitionSpec as P

NQ = 16
R = 32
LEN = 128


def spread(array, axis, root):
    mine = lax.axis_index(axis) == root
    return lax.psum(jnp.where(mine, array, jnp.zeros_like(array)), axis)


def block_rotate(matrix_rows, eigenbasis):
    block_width = eigenbasis.shape[1]
    blocks = matrix_rows.reshape(matrix_rows.shape[0], -1, block_width)
    turned = jnp.einsum("tbi,bij->tbj", blocks, eigenbasis, preferred_element_type=jnp.float32)
    return turned.reshape(matrix_rows.shape[0], -1)


def contract_rows(first, second):
    return lax.dot_general(first, second, (((1,), (1,)), ((), ())), precision=lax.Precision.HIGHEST)


def on_device(out_grads, hidden_acts, out_basis, in_basis, left_store, right_store, owners):
    left_local = left_store[0]
    right_local = right_store[0]
    width_left = left_local.shape[1]
    row_count = out_grads.shape[0]
    joined = jnp.concatenate([left_local, right_local], axis=1)

    def take_query(query_index, collected):
        offset = query_index * R
        portion = lax.dynamic_slice_in_dim(joined, offset, R, 0)
        arrived = spread(portion, "dp", owners[query_index])
        return lax.dynamic_update_slice_in_dim(collected, arrived, offset, 0)

    gathered = lax.fori_loop(0, NQ, take_query, jnp.zeros_like(joined))
    left_fac = gathered[:, :width_left].astype(jnp.float32)
    right_fac = gathered[:, width_left:].astype(jnp.float32)
    projected_part = contract_rows(block_rotate(hidden_acts, in_basis), right_fac)
    block_width = out_basis.shape[1]
    left_full = lax.all_gather(left_fac.astype(jnp.bfloat16), "mp", axis=1, tiled=True)
    left_wide = left_full.astype(jnp.float32)
    portion = lax.all_gather(out_basis, "mp", axis=0, tiled=True)
    count = portion.shape[0]
    turned = jnp.einsum(
        "tbi,bij->tbj",
        out_grads.reshape(row_count, count, block_width),
        portion,
        preferred_element_type=jnp.float32,
    )
    coefficient = contract_rows(turned.reshape(row_count, count * block_width), left_wide)
    per_sequence = jnp.sum(
        (coefficient * projected_part).reshape(-1, LEN, NQ, R), axis=(1, 3)
    ) / jnp.float32(LEN)
    return lax.psum(per_sequence, "mp")


def solution(mesh):
    in_specs = (
        P("dp", None),
        P("dp", "mp"),
        P("mp", None, None),
        P("mp", None, None),
        P("dp", None, "mp"),
        P("dp", None, "mp"),
        P(),
    )
    out_specs = P("dp", None)
    return jax.shard_map(
        on_device, mesh=mesh, in_specs=in_specs, out_specs=out_specs, check_vma=False
    )
```

profile of v0, /device:TPU:0, one launch (start us, length us, event | category | flops | bytes accessed | tf_op | source)
XLA Modules:
  0.0 1418.9 jit_solution(18201298602513244871)
XLA Ops:
  7.4 8.0 pad_maximum_fusion
  15.4 4.8 broadcast_in_dim.3
  20.2 1248.6 %while.13 = (s32[]{:T(128)}, bf16[512,9216]{1,0:T(8,128)(2,1)}, s32[16]{0:T(128)S(1)}, bf16[512,9216]{1,0:T(8,128)(2,1)}, s32[]{:T(128)}, /*index=5*/s32[]{:T(128)}, s32[]{:T(128)}, s32[]{:T(128)}, u32[]{:T(128)}, u32[]{:T(128)}) while((s32[]{:T(128)}, bf16[512,9216]{1,0:T(8,128)(2,1)}, s32[16]{0:T(128)S(1)}, bf16[512,9216]{1,0:T(8,128)(2,1)}, ...), condition=%wide.region_2.3_spmd, body=%wide.region_0.2_spmd.sunk | while | flops 589834 | bytes 5898489 | solution.py:40
  20.2 0.6 dynamic_slice.18
  21.4 2.0 dynamic-slice_select_fusion.2
  23.4 76.7 %all-reduce.2.cloned.1.call-done = bf16[32,9216]{1,0:T(8,128)(2,1)} async-done(((bf16[32,9216]{1,0:T(8,128)(2,1)}), bf16[32,9216]{1,0:T(8,128)(2,1)}) %all-reduce.2.cloned.1.call-update) | async-done | bytes 589840 | tf_op jit(solution)/shard_map/while/body/eval_jaxpr/psum | solution.py:13
  100.1 1.9 constant_dynamic-update-slice_fusion.2
  103.2 2.0 dynamic-slice_select_fusion.2
  105.3 72.8 %all-reduce.2.cloned.1.call-done = bf16[32,9216]{1,0:T(8,128)(2,1)} async-done(((bf16[32,9216]{1,0:T(8,128)(2,1)}), bf16[32,9216]{1,0:T(8,128)(2,1)}) %all-reduce.2.cloned.1.call-update) | async-done | bytes 589840 | tf_op jit(solution)/shard_map/while/body/eval_jaxpr/psum | solution.py:13
  178.0 1.9 constant_dynamic-update-slice_fusion.2
  181.2 2.0 dynamic-slice_select_fusion.2
  183.2 72.8 %all-reduce.2.cloned.1.call-done = bf16[32,9216]{1,0:T(8,128)(2,1)} async-done(((bf16[32,9216]{1,0:T(8,128)(2,1)}), bf16[32,9216]{1,0:T(8,128)(2,1)}) %all-reduce.2.cloned.1.call-update) | async-done | bytes 589840 | tf_op jit(solution)/shard_map/while/body/eval_jaxpr/psum | solution.py:13
  256.0 2.0 constant_dynamic-update-slice_fusion.2
  257.9 0.6 dynamic_slice.18
  259.2 2.0 dynamic-slice_select_fusion.2
  261.2 72.5 %all-reduce.2.cloned.1.call-done = bf16[32,9216]{1,0:T(8,128)(2,1)} async-done(((bf16[32,9216]{1,0:T(8,128)(2,1)}), bf16[32,9216]{1,0:T(8,128)(2,1)}) %all-reduce.2.cloned.1.call-update) | async-done | bytes 589840 | tf_op jit(solution)/shard_map/while/body/eval_jaxpr/psum | solution.py:13
  333.6 1.9 constant_dynamic-update-slice_fusion.2
  335.6 0.6 dynamic_slice.18
  336.8 2.0 dynamic-slice_select_fusion.2
  338.8 72.5 %all-reduce.2.cloned.1.call-done = bf16[32,9216]{1,0:T(8,128)(2,1)} async-done(((bf16[32,9216]{1,0:T(8,128)(2,1)}), bf16[32,9216]{1,0:T(8,128)(2,1)}) %all-reduce.2.cloned.1.call-update) | async-done | bytes 589840 | tf_op jit(solution)/shard_map/while/body/eval_jaxpr/psum | solution.py:13
  411.3 1.9 constant_dynamic-update-slice_fusion.2
  414.4 2.0 dynamic-slice_select_fusion.2
  416.4 72.5 %all-reduce.2.cloned.1.call-done = bf16[32,9216]{1,0:T(8,128)(2,1)} async-done(((bf16[32,9216]{1,0:T(8,128)(2,1)}), bf16[32,9216]{1,0:T(8,128)(2,1)}) %all-reduce.2.cloned.1.call-update) | async-done | bytes 589840 | tf_op jit(solution)/shard_map/while/body/eval_jaxpr/psum | solution.py:13
  488.9 1.9 constant_dynamic-update-slice_fusion.2
  492.0 2.0 dynamic-slice_select_fusion.2
  494.0 72.8 %all-reduce.2.cloned.1.call-done = bf16[32,9216]{1,0:T(8,128)(2,1)} async-done(((bf16[32,9216]{1,0:T(8,128)(2,1)}), bf16[32,9216]{1,0:T(8,128)(2,1)}) %all-reduce.2.cloned.1.call-update) | async-done | bytes 589840 | tf_op jit(solution)/shard_map/while/body/eval_jaxpr/psum | solution.py:13
  566.8 1.9 constant_dynamic-update-slice_fusion.2
  570.0 2.0 dynamic-slice_select_fusion.2
  572.0 72.8 %all-reduce.2.cloned.1.call-done = bf16[32,9216]{1,0:T(8,128)(2,1)} async-done(((bf16[32,9216]{1,0:T(8,128)(2,1)}), bf16[32,9216]{1,0:T(8,128)(2,1)}) %all-reduce.2.cloned.1.call-update) | async-done | bytes 589840 | tf_op jit(solution)/shard_map/while/body/eval_jaxpr/psum | solution.py:13
  644.8 1.9 constant_dynamic-update-slice_fusion.2
  647.9 2.0 dynamic-slice_select_fusion.2
  649.9 72.8 %all-reduce.2.cloned.1.call-done = bf16[32,9216]{1,0:T(8,128)(2,1)} async-done(((bf16[32,9216]{1,0:T(8,128)(2,1)}), bf16[32,9216]{1,0:T(8,128)(2,1)}) %all-reduce.2.cloned.1.call-update) | async-done | bytes 589840 | tf_op jit(solution)/shard_map/while/body/eval_jaxpr/psum | solution.py:13
  722.7 1.9 constant_dynamic-update-slice_fusion.2
  725.8 2.0 dynamic-slice_select_fusion.2
  727.8 72.5 %all-reduce.2.cloned.1.call-done = bf16[32,9216]{1,0:T(8,128)(2,1)} async-done(((bf16[32,9216]{1,0:T(8,128)(2,1)}), bf16[32,9216]{1,0:T(8,128)(2,1)}) %all-reduce.2.cloned.1.call-update) | async-done | bytes 589840 | tf_op jit(solution)/shard_map/while/body/eval_jaxpr/psum | solution.py:13
  800.3 2.0 constant_dynamic-update-slice_fusion.2
  803.5 2.0 dynamic-slice_select_fusion.2
  805.5 72.8 %all-reduce.2.cloned.1.call-done = bf16[32,9216]{1,0:T(8,128)(2,1)} async-done(((bf16[32,9216]{1,0:T(8,128)(2,1)}), bf16[32,9216]{1,0:T(8,128)(2,1)}) %all-reduce.2.cloned.1.call-update) | async-done | bytes 589840 | tf_op jit(solution)/shard_map/while/body/eval_jaxpr/psum | solution.py:13
  878.3 1.9 constant_dynamic-update-slice_fusion.2
  881.4 2.0 dynamic-slice_select_fusion.2
  883.4 72.5 %all-reduce.2.cloned.1.call-done = bf16[32,9216]{1,0:T(8,128)(2,1)} async-done(((bf16[32,9216]{1,0:T(8,128)(2,1)}), bf16[32,9216]{1,0:T(8,128)(2,1)}) %all-reduce.2.cloned.1.call-update) | async-done | bytes 589840 | tf_op jit(solution)/shard_map/while/body/eval_jaxpr/psum | solution.py:13
  955.9 1.9 constant_dynamic-update-slice_fusion.2
  959.0 2.0 dynamic-slice_select_fusion.2
  961.0 72.8 %all-reduce.2.cloned.1.call-done = bf16[32,9216]{1,0:T(8,128)(2,1)} async-done(((bf16[32,9216]{1,0:T(8,128)(2,1)}), bf16[32,9216]{1,0:T(8,128)(2,1)}) %all-reduce.2.cloned.1.call-update) | async-done | bytes 589840 | tf_op jit(solution)/shard_map/while/body/eval_jaxpr/psum | solution.py:13
  1033.8 1.9 constant_dynamic-update-slice_fusion.2
  1037.0 2.0 dynamic-slice_select_fusion.2
  1039.0 72.5 %all-reduce.2.cloned.1.call-done = bf16[32,9216]{1,0:T(8,128)(2,1)} async-done(((bf16[32,9216]{1,0:T(8,128)(2,1)}), bf16[32,9216]{1,0:T(8,128)(2,1)}) %all-reduce.2.cloned.1.call-update) | async-done | bytes 589840 | tf_op jit(solution)/shard_map/while/body/eval_jaxpr/psum | solution.py:13
  1111.5 1.9 constant_dynamic-update-slice_fusion.2
  1114.6 2.0 dynamic-slice_select_fusion.2
  1116.6 72.5 %all-reduce.2.cloned.1.call-done = bf16[32,9216]{1,0:T(8,128)(2,1)} async-done(((bf16[32,9216]{1,0:T(8,128)(2,1)}), bf16[32,9216]{1,0:T(8,128)(2,1)}) %all-reduce.2.cloned.1.call-update) | async-done | bytes 589840 | tf_op jit(solution)/shard_map/while/body/eval_jaxpr/psum | solution.py:13
  1189.1 2.0 constant_dynamic-update-slice_fusion.2
  1192.3 2.0 dynamic-slice_select_fusion.2
  1194.3 72.5 %all-reduce.2.cloned.1.call-done = bf16[32,9216]{1,0:T(8,128)(2,1)} async-done(((bf16[32,9216]{1,0:T(8,128)(2,1)}), bf16[32,9216]{1,0:T(8,128)(2,1)}) %all-reduce.2.cloned.1.call-update) | async-done | bytes 589840 | tf_op jit(solution)/shard_map/while/body/eval_jaxpr/psum | solution.py:13
  1266.8 2.0 constant_dynamic-update-slice_fusion.2
  1269.4 3.2 slice.6
  1272.6 5.9 copy.20
  1278.5 5.8 fusion.5
  1284.3 13.9 fusion
  1298.2 29.6 %all-gather.3.cloned.1.call-done = bf16[16,512,512]{2,1,0:T(8,128)(2,1)} async-done(((bf16[4,512,512]{2,1,0:T(8,128)(2,1)}), bf16[16,512,512]{2,1,0:T(8,128)(2,1)}) %all-gather.3.cloned.1.call-update) | async-done | bytes 8388624 | tf_op jit(solution)/shard_map/all_gather | solution.py:47
  1327.9 11.2 fusion.2
  1339.0 48.4 %all-gather.5.cloned.1.call-done = bf16[512,8192]{1,0:T(8,128)(2,1)} async-done(((bf16[512,2048]{1,0:T(8,128)(2,1)}), bf16[512,8192]{1,0:T(8,128)(2,1)}) %all-gather.5.cloned.1.call-update) | async-done | bytes 8388624 | tf_op jit(solution)/shard_map/all_gather | solution.py:45
  1387.4 17.0 %convolution_multiply_fusion = f32[256,512]{1,0:T(8,128)S(1)} fusion(f32[256,512]{1,0:T(8,128)S(1)} %fusion, f32[256,8192]{0,1:T(8,128)} %bitcast.24, bf16[512,8192]{1,0:T(8,128)(2,1)} %all-gather.5.cloned.1.call-done), kind=kOutput, calls=%fused_computation.8 | convolution fusion | flops 12885032960 | bytes 17825792 | tf_op jit(solution)/shard_map/dot_general | solution.py:24
  1405.1 6.0 psum.18
  1411.1 0.6 copy.24
  (55 shorter events, 9.3 us)
Async XLA Ops:
  15.4 4.8 copy-start
  20.2 79.9 %all-reduce.2.cloned.1.call-start = ((), (), s32[]{:S(2)}) async-start(), calls=%async_computation.2 | async-start | bytes 1179648 | tf_op jit(solution)/shard_map/while/body/eval_jaxpr/psum | solution.py:13
  102.0 76.0 %all-reduce.2.cloned.1.call-start = ((), (), s32[]{:S(2)}) async-start(), calls=%async_computation.2 | async-start | bytes 1179648 | tf_op jit(solution)/shard_map/while/body/eval_jaxpr/psum | solution.py:13
  180.0 76.0 %all-reduce.2.cloned.1.call-start = ((), (), s32[]{:S(2)}) async-start(), calls=%async_computation.2 | async-start | bytes 1179648 | tf_op jit(solution)/shard_map/while/body/eval_jaxpr/psum | solution.py:13
  257.9 75.7 %all-reduce.2.cloned.1.call-start = ((), (), s32[]{:S(2)}) async-start(), calls=%async_computation.2 | async-start | bytes 1179648 | tf_op jit(solution)/shard_map/while/body/eval_jaxpr/psum | solution.py:13
  335.6 75.7 %all-reduce.2.cloned.1.call-start = ((), (), s32[]{:S(2)}) async-start(), calls=%async_computation.2 | async-start | bytes 1179648 | tf_op jit(solution)/shard_map/while/body/eval_jaxpr/psum | solution.py:13
  413.2 75.7 %all-reduce.2.cloned.1.call-start = ((), (), s32[]{:S(2)}) async-start(), calls=%async_computation.2 | async-start | bytes 1179648 | tf_op jit(solution)/shard_map/while/body/eval_jaxpr/psum | solution.py:13
  490.8 76.0 %all-reduce.2.cloned.1.call-start = ((), (), s32[]{:S(2)}) async-start(), calls=%async_computation.2 | async-start | bytes 1179648 | tf_op jit(solution)/shard_map/while/body/eval_jaxpr/psum | solution.py:13
  568.8 76.0 %all-reduce.2.cloned.1.call-start = ((), (), s32[]{:S(2)}) async-start(), calls=%async_computation.2 | async-start | bytes 1179648 | tf_op jit(solution)/shard_map/while/body/eval_jaxpr/psum | solution.py:13
  646.7 76.0 %all-reduce.2.cloned.1.call-start = ((), (), s32[]{:S(2)}) async-start(), calls=%async_computation.2 | async-start | bytes 1179648 | tf_op jit(solution)/shard_map/while/body/eval_jaxpr/psum | solution.py:13
  724.6 75.7 %all-reduce.2.cloned.1.call-start = ((), (), s32[]{:S(2)}) async-start(), calls=%async_computation.2 | async-start | bytes 1179648 | tf_op jit(solution)/shard_map/while/body/eval_jaxpr/psum | solution.py:13
  802.3 76.0 %all-reduce.2.cloned.1.call-start = ((), (), s32[]{:S(2)}) async-start(), calls=%async_computation.2 | async-start | bytes 1179648 | tf_op jit(solution)/shard_map/while/body/eval_jaxpr/psum | solution.py:13
  880.2 75.7 %all-reduce.2.cloned.1.call-start = ((), (), s32[]{:S(2)}) async-start(), calls=%async_computation.2 | async-start | bytes 1179648 | tf_op jit(solution)/shard_map/while/body/eval_jaxpr/psum | solution.py:13
  957.8 76.0 %all-reduce.2.cloned.1.call-start = ((), (), s32[]{:S(2)}) async-start(), calls=%async_computation.2 | async-start | bytes 1179648 | tf_op jit(solution)/shard_map/while/body/eval_jaxpr/psum | solution.py:13
  1035.8 75.7 %all-reduce.2.cloned.1.call-start = ((), (), s32[]{:S(2)}) async-start(), calls=%async_computation.2 | async-start | bytes 1179648 | tf_op jit(solution)/shard_map/while/body/eval_jaxpr/psum | solution.py:13
  1113.4 75.7 %all-reduce.2.cloned.1.call-start = ((), (), s32[]{:S(2)}) async-start(), calls=%async_computation.2 | async-start | bytes 1179648 | tf_op jit(solution)/shard_map/while/body/eval_jaxpr/psum | solution.py:13
  1191.1 75.7 %all-reduce.2.cloned.1.call-start = ((), (), s32[]{:S(2)}) async-start(), calls=%async_computation.2 | async-start | bytes 1179648 | tf_op jit(solution)/shard_map/while/body/eval_jaxpr/psum | solution.py:13
  1268.8 59.1 %all-gather.3.cloned.1.call-start = ((), (), s32[]{:S(2)}) async-start(), calls=%async_computation | async-start | bytes 10485760 | tf_op jit(solution)/shard_map/all_gather | solution.py:47
  1269.3 118.1 %all-gather.5.cloned.1.call-start = ((), (), s32[]{:S(2)}) async-start(), calls=%async_computation.1 | async-start | bytes 10485760 | tf_op jit(solution)/shard_map/all_gather | solution.py:45
Sparse Core Ops, SparseCore 0:
  24.4 75.6 all-reduce.1
  106.2 71.7 all-reduce.1
  184.2 71.7 all-reduce.1
  261.8 71.7 all-reduce.1
  339.5 71.7 all-reduce.1
  417.1 71.7 all-reduce.1
  495.0 71.7 all-reduce.1
  573.0 71.7 all-reduce.1
  650.9 71.7 all-reduce.1
  728.5 71.7 all-reduce.1
  806.5 71.7 all-reduce.1
  884.1 71.7 all-reduce.1
  962.0 71.7 all-reduce.1
  1039.6 71.7 all-reduce.1
  1117.3 71.7 all-reduce.1
  1195.0 71.7 all-reduce.1
Sparse Core Ops, SparseCore 1:
  1270.8 57.0 all-gather.2
  1329.3 58.1 all-gather.4
where the time goes:
time: 1420 us
  waiting for transfers between devices  1240 us (87%)
  local copies, waits for them, and re-layouts  55.3 us (4%)
  matrix products  47.9 us (3%)
  other arithmetic  40 us (3%)
  between operations  14.6 us (1%)
    psum x16, waiting for transfers between devices, spread(): return lax.psum(jnp.where(mine, array, jnp.zeros_like(array)), axis)  1170 us
    all_gather x1, waiting for transfers between devices, on_device(): lax.all_gather(left_fac.astype(jnp.bfloat16), 'mp', axis=1, tiled=True)  48.4 us
    select_n x16, other arithmetic, spread(): return lax.psum(jnp.where(mine, array, jnp.zeros_like(array)), axis)  31.8 us
    dynamic_update_slice x16, local copies, waits for them, and re-layouts, take_query(): return lax.dynamic_update_slice_in_dim(collected, arrived, offset, 0)  31 us
    dot_general x2, matrix products, contract_rows(): lax.dot_general(first, second, (((1,), (1,)), ((), ())), precision=lax.Pr...  30.9 us
    all_gather x1, waiting for transfers between devices, on_device(): portion = lax.all_gather(out_basis, 'mp', axis=0, tiled=True)  29.6 us
  transfers between devices with their start and end apart: 18, of which 18 were waited for; matrix products, arithmetic and copies ran while one was open for 3% of the time, Pallas kernels for 0%

commit v1 on v0

v1 whole, which is shorter than its diff:
```python
import jax
import jax.numpy as jnp
from jax import lax
from jax.sharding import PartitionSpec as P

NQ = 16
R = 32
LEN = 128


def block_rotate(matrix_rows, eigenbasis):
    block_width = eigenbasis.shape[1]
    blocks = matrix_rows.reshape(matrix_rows.shape[0], -1, block_width)
    turned = jnp.einsum("tbi,bij->tbj", blocks, eigenbasis, preferred_element_type=jnp.float32)
    return turned.reshape(matrix_rows.shape[0], -1)


def contract_rows(first, second):
    high = lax.reduce_precision(first, 8, 7)
    low = (first - high).astype(jnp.bfloat16)
    rows = first.shape[0]
    both = jnp.concatenate([high.astype(jnp.bfloat16), low], axis=0)
    out = lax.dot_general(
        both, second, (((1,), (1,)), ((), ())), preferred_element_type=jnp.float32
    )
    return out[:rows] + out[rows:]


def ranks(owners):
    at = jnp.arange(NQ, dtype=jnp.int32)
    before = (owners[None, :] < owners[:, None]) | (
        (owners[None, :] == owners[:, None]) & (at[None, :] < at[:, None])
    )
    place = jnp.sum(before.astype(jnp.int32), axis=1)
    order = jnp.sum(jnp.where(place[None, :] == at[:, None], at[None, :], 0), axis=1)
    return place, order


def on_device(groups, out_grads, hidden_acts, out_basis, in_basis, left_store, right_store, owners):
    per = NQ // groups
    group = lax.axis_index("dp")
    shard = lax.axis_index("mp")
    place, order = ranks(owners)

    def own_rows(store):
        return jnp.concatenate(
            [
                lax.dynamic_slice_in_dim(store[0], order[group * per + i] * R, R, 0)
                for i in range(per)
            ],
            axis=0,
        )

    left_fac = lax.all_gather(own_rows(left_store), "dp", axis=0, tiled=True)
    right_fac = lax.all_gather(own_rows(right_store), "dp", axis=0, tiled=True)

    width_left = left_store.shape[2]
    grads = lax.dynamic_slice_in_dim(out_grads, shard * width_left, width_left, 1)
    coefficient = lax.psum(contract_rows(block_rotate(grads, out_basis), left_fac), "mp")
    projected = contract_rows(block_rotate(hidden_acts, in_basis), right_fac)
    per_sequence = jnp.sum(
        (coefficient * projected).reshape(-1, LEN, NQ, R), axis=(1, 3)
    ) / jnp.float32(LEN)
    scores = lax.psum(per_sequence, "mp")
    at = jnp.arange(NQ, dtype=jnp.int32)
    return jnp.sum(jnp.where(place[None, None, :] == at[None, :, None], scores[:, :, None], 0.0), axis=1)


def solution(mesh):
    in_specs = (
        P("dp", None),
        P("dp", "mp"),
        P("mp", None, None),
        P("mp", None, None),
        P("dp", None, "mp"),
        P("dp", None, "mp"),
        P(),
    )
    out_specs = P("dp", None)
    groups = mesh.shape["dp"]

    def whole(*arrays):
        return on_device(groups, *arrays)

    return jax.shard_map(whole, mesh=mesh, in_specs=in_specs, out_specs=out_specs, check_vma=False)
```

time: 1420 us -> 226 us (0.16)
  waiting for transfers between devices: 1240 us -> 156 us
  local copies, waits for them, and re-layouts: 55.3 us -> 16 us
  matrix products: 47.9 us -> 18.8 us
  other arithmetic: 40 us -> 13.8 us
    psum x16 -> x1, waiting for transfers between devices: 1170 us -> 23.6 us  [on_device(): lax.psum(contract_rows(block_rotate(grads, out_basis), left_fac), 'mp')]
    all_gather x2, waiting for transfers between devices: 78 us -> 133 us  [the longest x1 109 us: on_device(): right_fac = lax.all_gather(own_rows(right_store), 'dp', axis=0, tiled=True)]
    select_n x16 -> x0, other arithmetic: 31.8 us -> none  [spread(): return lax.psum(jnp.where(mine, array, jnp.zeros_like(array)), axis)]
    dynamic_update_slice x16 -> x0, local copies, waits for them, and re-layouts: 31 us -> none  [take_query(): return lax.dynamic_update_slice_in_dim(collected, arrived, offset, 0)]
    dot_general x3 -> x2, matrix products: 42.1 us -> 13.4 us  [contract_rows(): lax.dot_general(both, second, (((1,), (1,)), ((), ())), preferred_element...]
  transfers between devices with their start and end apart: 18 -> 3, of which waited for: 18 -> 3; matrix products, arithmetic and copies ran while one was open for 3% -> 19% of each run, Pallas kernels for 0% -> 0%
where the time goes in v1:
time: 226 us; the launch traced here: 225 us
  waiting for transfers between devices  156 us (69%)
  matrix products  18.8 us (8%)
  local copies, waits for them, and re-layouts  16 us (7%)
  between operations  14.5 us (6%)
  other arithmetic  13.8 us (6%)
  blocking collectives  5.85 us (3%)
    all_gather x1, waiting for transfers between devices, on_device(): right_fac = lax.all_gather(own_rows(right_store), 'dp', axis=0, tiled=True)  109 us
    all_gather x1, waiting for transfers between devices, on_device(): left_fac = lax.all_gather(own_rows(left_store), 'dp', axis=0, tiled=True)  24.1 us
    psum x1, waiting for transfers between devices, on_device(): lax.psum(contract_rows(block_rotate(grads, out_basis), left_fac), 'mp')  23.6 us
    dot_general x2, matrix products, contract_rows(): lax.dot_general(both, second, (((1,), (1,)), ((), ())), preferred_element...  13.4 us
    convert_element_type x2, other arithmetic, contract_rows(): both = jnp.concatenate([high.astype(jnp.bfloat16), low], axis=0)  7.67 us
    unnamed x6, local copies, waits for them, and re-layouts  7.4 us
    psum x1, blocking collectives, on_device(): scores = lax.psum(per_sequence, 'mp')  5.85 us
    dot_general x2, matrix products, block_rotate(): jnp.einsum('tbi,bij->tbj', blocks, eigenbasis, preferred_element_type=jnp...  5.37 us
  transfers between devices with their start and end apart: 3, of which 3 were waited for; matrix products, arithmetic and copies ran while one was open for 19% of the time, Pallas kernels for 0%

profile of v1, /device:TPU:0, one launch (start us, length us, event | category | flops | bytes accessed | tf_op | source)
XLA Modules:
  0.0 225.4 jit_solution(8910269270584718246)
XLA Ops:
  6.5 0.0 copy-start
  6.5 0.0 all-gather.3.cloned.1.call-start
  6.5 1.0 convert_reduce_fusion
  7.5 0.1 select_reduce_fusion.1
  7.7 0.7 fusion.15
  9.7 1.0 dynamic-slice_bitcast_fusion.3
  10.7 0.7 pad_maximum_fusion.1
  11.4 0.0 all-gather.3.cloned.1.call-update
  11.4 0.0 all-gather.5.cloned.1.call-start
  11.5 1.2 dynamic-slice_bitcast_fusion.1
  12.7 1.0 pad_maximum_fusion
  13.7 0.0 all-gather.5.cloned.1.call-update
  13.7 0.0 all-reduce.2.cloned.1.call-start
  13.8 5.9 %copy.28 = bf16[256,7168]{0,1:T(8,128)(2,1)} copy(bf16[256,7168]{1,0:T(8,128)(2,1)} %param.8) | data formatting | bytes 7340032 | tf_op args[1]
  19.7 2.3 %constant_dynamic-slice_fusion = bf16[256,2048]{1,0:T(8,128)(2,1)} fusion(bf16[256,8192]{1,0:T(8,128)(2,1)} %param.7, s32[]{:T(128)S(6)} %select_n.27), kind=kLoop, calls=%fused_computation.32 | loop fusion | bytes 2097156 | tf_op jit(solution)/shard_map/dynamic_slice | solution.py:58
  22.0 1.5 copy.36
  23.5 0.0 copy-done
  23.5 2.1 convolution_bitcast_fusion
  25.6 2.9 %copy.27 = f32[256,4,512]{0,2,1:T(8,128)} copy(f32[256,4,512]{2,0,1:T(8,128)} %convolution_bitcast_fusion) | data formatting | bytes 4194304 | tf_op jit(solution)/shard_map/tbi,bij->tbj/transpose | solution.py:14
  28.5 0.0 copy-start.1
  28.5 3.1 %reduce-precision_convert_fusion.1 = (bf16[256,2048]{0,1:T(8,128)(2,1)S(1)}, bf16[256,2048]{0,1:T(8,128)(2,1)}) fusion(f32[256,4,512]{0,2,1:T(8,128)} %copy.27), kind=kLoop, calls=%fused_computation.8 | loop fusion | flops 2097152 | bytes 4194304 | tf_op jit(solution)/shard_map/convert_element_type | solution.py:22
  31.6 0.0 copy-done.1
  31.6 3.3 %fusion.16 = f32[28,256,256]{2,1,0:T(8,128)S(1)} fusion(bf16[28,256,256]{2,1,0:T(8,128)(2,1)} %param.10, bf16[256,28,256]{0,2,1:T(8,128)(2,1)S(1)} %bitcast.30), kind=kOutput, calls=%fused_computation.36 | convolution fusion | flops 939524096 | bytes 14680064 | tf_op jit(solution)/shard_map/tbi,bij->tbj/dot_general | solution.py:14
  34.9 4.6 %reduce-precision_convert_fusion = (bf16[256,7168]{0,1:T(8,128)(2,1)}, bf16[256,7168]{0,1:T(8,128)(2,1)}) fusion(f32[28,256,256]{2,1,0:T(8,128)S(1)} %fusion.16), kind=kLoop, calls=%fused_computation.1 | loop fusion | flops 7340032 | bytes 14680064 | tf_op jit(solution)/shard_map/convert_element_type | solution.py:22
  39.4 24.1 %all-gather.3.cloned.1.call-done = bf16[512,2048]{1,0:T(8,128)(2,1)} async-done(((bf16[64,2048]{1,0:T(8,128)(2,1)}), bf16[512,2048]{1,0:T(8,128)(2,1)}) %all-gather.3.cloned.1.call-update) | async-done | bytes 2097168 | tf_op jit(solution)/shard_map/all_gather | solution.py:54
  63.6 3.2 %fusion.6 = f32[512,512]{1,0:T(8,128)S(1)} fusion(bf16[512,2048]{1,0:T(8,128)(2,1)} %all-gather.3.cloned.1.call-done, bf16[256,2048]{0,1:T(8,128)(2,1)} %get-tuple-element.10, bf16[256,2048]{0,1:T(8,128)(2,1)S(1)} %get-tuple-element.9), kind=kOutput, calls=%fused_computation.10 | convolution fusion | flops 1077936128 | bytes 5242880 | tf_op jit(solution)/shard_map/dot_general | solution.py:23
  66.8 0.9 slice_add_fusion.1
  67.7 0.0 all-reduce.2.cloned.1.call-update
  67.7 108.5 %all-gather.5.cloned.1.call-done = bf16[512,7168]{1,0:T(8,128)(2,1)} async-done(((bf16[64,7168]{1,0:T(8,128)(2,1)}), bf16[512,7168]{1,0:T(8,128)(2,1)}) %all-gather.5.cloned.1.call-update) | async-done | bytes 7340048 | tf_op jit(solution)/shard_map/all_gather | solution.py:55
  176.3 10.2 %fusion.1 = f32[512,512]{1,0:T(8,128)} fusion(bf16[512,7168]{1,0:T(8,128)(2,1)} %all-gather.5.cloned.1.call-done, bf16[256,7168]{0,1:T(8,128)(2,1)} %get-tuple-element.6, bf16[256,7168]{0,1:T(8,128)(2,1)} %get-tuple-element.5), kind=kOutput, calls=%fused_computation.3 | convolution fusion | flops 3772776448 | bytes 15728640 | tf_op jit(solution)/shard_map/dot_general | solution.py:23
  186.5 23.6 %all-reduce.2.cloned.1.call-done = f32[256,512]{1,0:T(8,128)} async-done(((f32[256,512]{1,0:T(8,128)}), f32[256,512]{1,0:T(8,128)}) %all-reduce.2.cloned.1.call-update) | async-done | bytes 524304 | tf_op jit(solution)/shard_map/psum | solution.py:59
  210.0 1.5 fusion.10
  211.5 0.2 copy.31
  211.7 0.3 reshape.56
  212.0 0.2 reduce_sum.38
  212.3 5.8 %psum.15 = f32[2,16]{0,1:T(8,128)S(1)} all-reduce(f32[2,16]{0,1:T(8,128)S(1)} %broadcast_multiply_fusion), channel_id=1, replica_groups=mesh['dp'=8,'mp'=4] {'mp'}, use_global_device_ids=true, to_apply=%region_4.5 | all-reduce | flops 32 | bytes 256 | tf_op jit(solution)/shard_map/psum | solution.py:64
  218.1 0.1 copy.32
  218.2 0.7 select_reduce_fusion
  (2 shorter events, 0.0 us)
Async XLA Ops:
  6.5 17.0 %copy-start = (bf16[4,512,512]{2,1,0:T(8,128)(2,1)S(1)}, bf16[4,512,512]{2,1,0:T(8,128)(2,1)}, u32[]{:S(2)}) copy-start(bf16[4,512,512]{2,1,0:T(8,128)(2,1)} %param.9) | copy-start | bytes 6291460
  6.5 57.0 %all-gather.3.cloned.1.call-start = ((), (), s32[]{:S(2)}) async-start(), calls=%async_computation | async-start | bytes 2359296 | tf_op jit(solution)/shard_map/all_gather | solution.py:54
  11.4 164.8 %all-gather.5.cloned.1.call-start = ((), (), s32[]{:S(2)}) async-start(), calls=%async_computation.2 | async-start | bytes 8257536 | tf_op jit(solution)/shard_map/all_gather | solution.py:55
  13.7 196.3 %all-reduce.2.cloned.1.call-start = ((), (), s32[]{:S(2)}) async-start(), calls=%async_computation.1 | async-start | bytes 1048576 | tf_op jit(solution)/shard_map/psum | solution.py:59
  28.5 3.1 %copy-start.1 = (bf16[256,7168]{0,1:T(8,128)(2,1)S(1)}, bf16[256,7168]{0,1:T(8,128)(2,1)}, u32[]{:S(2)}) copy-start(bf16[256,7168]{0,1:T(8,128)(2,1)} %copy.28) | copy-start | bytes 11010052
Sparse Core Ops, SparseCore 0:
  11.5 51.9 all-gather.2
  65.8 110.4 all-gather.4
  178.6 31.3 all-reduce.1

commit v2 on v1

v2 whole, which is shorter than its diff:
```python
import jax
import jax.numpy as jnp
from jax import lax
from jax.sharding import Mesh, PartitionSpec as P

NQ = 16
R = 32
LEN = 128


def block_rotate(matrix_rows, eigenbasis):
    block_width = eigenbasis.shape[1]
    blocks = matrix_rows.reshape(matrix_rows.shape[0], -1, block_width)
    turned = jnp.einsum("tbi,bij->tbj", blocks, eigenbasis, preferred_element_type=jnp.float32)
    return turned.reshape(matrix_rows.shape[0], -1)


def two_terms(first):
    high = lax.reduce_precision(first, 8, 7)
    low = (first - high).astype(jnp.bfloat16)
    return jnp.concatenate([high.astype(jnp.bfloat16), low], axis=0)


def contract_rows(both, second):
    rows = both.shape[0] // 2
    out = lax.dot_general(
        both, second, (((1,), (1,)), ((), ())), preferred_element_type=jnp.float32
    )
    return out[:rows] + out[rows:]


def ranks(owners):
    at = jnp.arange(NQ, dtype=jnp.int32)
    before = (owners[None, :] < owners[:, None]) | (
        (owners[None, :] == owners[:, None]) & (at[None, :] < at[:, None])
    )
    place = jnp.sum(before.astype(jnp.int32), axis=1)
    order = jnp.sum(jnp.where(place[None, :] == at[:, None], at[None, :], 0), axis=1)
    return place, order


def by_query(scores, column_of):
    at = jnp.arange(NQ, dtype=jnp.int32)
    return jnp.sum(
        jnp.where(column_of[None, None, :] == at[None, :, None], scores[:, :, None], 0.0), axis=1
    )


def whole_width(groups, out_grads, hidden_acts, out_basis, in_basis, left_store, right_store, owners):
    per = NQ // groups
    group = lax.axis_index("dp")
    shard = lax.axis_index("mp")
    place, order = ranks(owners)

    def own_rows(store):
        return jnp.concatenate(
            [
                lax.dynamic_slice_in_dim(store[0], order[group * per + i] * R, R, 0)
                for i in range(per)
            ],
            axis=0,
        )

    left_fac = lax.all_gather(own_rows(left_store), "dp", axis=0, tiled=True)
    right_fac = lax.all_gather(own_rows(right_store), "dp", axis=0, tiled=True)
    width_left = left_store.shape[2]
    grads = lax.dynamic_slice_in_dim(out_grads, shard * width_left, width_left, 1)
    coefficient = lax.psum(
        contract_rows(two_terms(block_rotate(grads, out_basis)), left_fac), "mp"
    )
    projected = contract_rows(two_terms(block_rotate(hidden_acts, in_basis)), right_fac)
    per_sequence = jnp.sum(
        (coefficient * projected).reshape(-1, LEN, NQ, R), axis=(1, 3)
    ) / jnp.float32(LEN)
    return by_query(lax.psum(per_sequence, "mp"), place)


def arrivals(count):
    table = []
    for z in range(count):
        got = []
        for hops in range(1, count):
            if z - hops >= 0:
                got.append((0, hops))
            if z + hops < count:
                got.append((1, hops))
        table.append(got)
    return table


def half_width(count, out_grads, hidden_acts, out_basis, in_basis, left_store, right_store, owners):
    per = NQ // (2 * count)
    line = lax.axis_index("hi")
    side = lax.axis_index("lo")
    shard = lax.axis_index("mp")
    place, order = ranks(owners)
    group = line * 2 + side
    tokens = out_grads.shape[0]
    half_left = left_store.shape[2] // 2
    half_right = right_store.shape[2] // 2
    swap = [(0, 1), (1, 0)]

    def own_rows(store, half, which):
        return jnp.concatenate(
            [
                lax.dynamic_slice(
                    store[0], (order[group * per + i] * R, which * half), (R, half)
                )
                for i in range(per)
            ],
            axis=0,
        )

    def along_line(own):
        ups, downs = [own], [own]
        for hops in range(1, count):
            ups.append(lax.ppermute(ups[-1], "hi", [(i, i + 1) for i in range(hops - 1, count - 1)]))
            downs.append(lax.ppermute(downs[-1], "hi", [(i, i - 1) for i in range(1, count - hops + 1)]))
        return ups, downs

    table = arrivals(count)

    def slot(pieces, i):
        if i == 0:
            return pieces[0][0]
        chosen = None
        for z in range(count):
            direction, hops = table[z][i - 1]
            piece = pieces[direction][hops]
            chosen = piece if chosen is None else jnp.where(line == z, piece, chosen)
        return chosen

    def halves(matrix, half, base):
        keep = lax.dynamic_slice_in_dim(matrix, base + side * half, half, 1)
        give = lax.dynamic_slice_in_dim(matrix, base + (1 - side) * half, half, 1)
        return keep, give

    left_own = own_rows(left_store, half_left, side)
    right_own = own_rows(right_store, half_right, side)
    left_other = lax.ppermute(own_rows(left_store, half_left, 1 - side), "lo", swap)
    right_other = lax.ppermute(own_rows(right_store, half_right, 1 - side), "lo", swap)
    grads_keep, grads_give = halves(out_grads, half_left, shard * left_store.shape[2])
    acts_keep, acts_give = halves(hidden_acts, half_right, 0)
    grads_other = lax.ppermute(grads_give, "lo", swap)
    acts_other = lax.ppermute(acts_give, "lo", swap)

    left_line = along_line(left_own)
    left_line_other = along_line(left_other)
    right_line = along_line(right_own)
    right_line_other = along_line(right_other)

    def own_basis(basis):
        blocks = basis.shape[0] // 2
        return lax.dynamic_slice_in_dim(basis, side * blocks, blocks, 0)

    out_half = own_basis(out_basis)
    in_half = own_basis(in_basis)
    grads = two_terms(block_rotate(jnp.concatenate([grads_keep, grads_other], axis=0), out_half))
    acts = two_terms(block_rotate(jnp.concatenate([acts_keep, acts_other], axis=0), in_half))

    left_fac = jnp.concatenate(
        [piece for i in range(count) for piece in (slot(left_line, i), slot(left_line_other, i))], axis=0
    )
    chunk = per * R

    def other_way(matrix):
        turned = matrix.reshape(2, tokens, count, 2, chunk)[::-1, :, :, ::-1]
        return jnp.where(side == 0, matrix, turned.reshape(matrix.shape))

    coefficient = contract_rows(grads, left_fac)
    coefficient = other_way(lax.psum(other_way(coefficient), ("lo", "mp")))

    parts = []
    for i in range(count):
        right_fac = jnp.concatenate([slot(right_line, i), slot(right_line_other, i)], axis=0)
        projected = contract_rows(acts, right_fac)
        terms = coefficient[:, 2 * i * chunk : 2 * (i + 1) * chunk] * projected
        parts.append(jnp.sum(terms.reshape(-1, LEN, 2 * per, R), axis=(1, 3)))
    partial = jnp.concatenate(parts, axis=1) / jnp.float32(LEN)
    sequences = tokens // LEN
    turned = partial.reshape(2, sequences, count, 2, per)[::-1, :, :, ::-1].reshape(partial.shape)
    partial = jnp.where(side == 0, partial, turned)
    scores = lax.psum(partial, ("lo", "mp"))
    scores = lax.dynamic_slice_in_dim(scores, side * sequences, sequences, 0)

    owner_group = place // per
    owner_line = owner_group // 2
    slot_of = []
    for z in range(count):
        places = [0] * count
        for i, (direction, hops) in enumerate(table[z]):
            places[z - hops if direction == 0 else z + hops] = i + 1
        slot_of.append(places)
    slots = jnp.zeros_like(owner_line)
    for z in range(count):
        for source in range(count):
            slots = jnp.where((line == z) & (owner_line == source), slot_of[z][source], slots)
    column_of = (slots * 2 + owner_group % 2) * per + place % per
    return by_query(scores, column_of)


def solution(mesh):
    groups = mesh.shape["dp"]
    shards = mesh.shape["mp"]
    paired = Mesh(mesh.devices.reshape(groups // 2, 2, shards), ("hi", "lo", "mp"))

    def whole(*arrays):
        blocks = [basis.shape[0] // shards for basis in arrays[2:4]]
        if any(count % 2 for count in blocks):
            dp, used = "dp", mesh
            body = lambda *local: whole_width(groups, *local)
        else:
            dp, used = ("hi", "lo"), paired
            body = lambda *local: half_width(groups // 2, *local)
        in_specs = (
            P(dp, None),
            P(dp, "mp"),
            P("mp", None, None),
            P("mp", None, None),
            P(dp, None, "mp"),
            P(dp, None, "mp"),
            P(),
        )
        return jax.shard_map(
            body, mesh=used, in_specs=in_specs, out_specs=P(dp, None), check_vma=False
        )(*arrays)

    return whole
```

time: 226 us -> 238 us (1.053)
  waiting for transfers between devices: 156 us -> 81.1 us
  starting transfers between devices: 0.09 us -> 46.6 us
  local copies, waits for them, and re-layouts: 16 us -> 46.8 us
  other arithmetic: 13.8 us -> 21.9 us
  matrix products: 18.8 us -> 12.6 us
  blocking collectives: 5.85 us -> 11.9 us
    all_gather x2 -> x0, waiting for transfers between devices: 133 us -> none  [the longest x1 109 us: on_device(): right_fac = lax.all_gather(own_rows(right_store), 'dp', axis=0, tiled=True)]
    ppermute x0 -> x28, starting transfers between devices: none -> 46.6 us  [the longest x12 26 us: along_line(): lax.ppermute(ups[-1], 'hi', [(i, i + 1) for i in range(hops - 1, count -...]
    ppermute x0 -> x28, waiting for transfers between devices: none -> 31.1 us  [the longest x12 21.5 us: along_line(): lax.ppermute(downs[-1], 'hi', [(i, i - 1) for i in range(1, count - hops...]
    psum x1, waiting for transfers between devices: 23.6 us -> 50 us  [half_width(): coefficient = other_way(lax.psum(other_way(coefficient), ('lo', 'mp')))]
    rev x0 -> x2, local copies, waits for them, and re-layouts: none -> 10.3 us  [other_way(): turned = matrix.reshape(2, tokens, count, 2, chunk)[::-1, :, :, ::-1]]
    unnamed x6 -> x25, local copies, waits for them, and re-layouts: 7.4 us -> 16.1 us
    reshape x1 -> x9, local copies, waits for them, and re-layouts: 0.27 us -> 8.06 us  [the longest x2 4.1 us: other_way(): return jnp.where(side == 0, matrix, turned.reshape(matrix.shape))]
    psum x1, blocking collectives: 5.85 us -> 11.9 us  [half_width(): scores = lax.psum(partial, ('lo', 'mp'))]
  transfers between devices with their start and end apart: 3 -> 29, of which waited for: 3 -> 8; matrix products, arithmetic and copies ran while one was open for 19% -> 26% of each run, Pallas kernels for 0% -> 0%
where the time goes in v2:
time: 238 us; the launch traced here: 236 us
  waiting for transfers between devices  81.1 us (34%)
  local copies, waits for them, and re-layouts  46.8 us (20%)
  starting transfers between devices  46.6 us (20%)
  other arithmetic  21.9 us (9%)
  between operations  15.3 us (6%)
  matrix products  12.6 us (5%)
  blocking collectives  11.9 us (5%)
    psum x1, waiting for transfers between devices, half_width(): coefficient = other_way(lax.psum(other_way(coefficient), ('lo', 'mp')))  50 us
    ppermute x12, starting transfers between devices, along_line(): lax.ppermute(ups[-1], 'hi', [(i, i + 1) for i in range(hops - 1, count -...  26 us
    ppermute x12, waiting for transfers between devices, along_line(): lax.ppermute(downs[-1], 'hi', [(i, i - 1) for i in range(1, count - hops...  21.5 us
    unnamed x25, local copies, waits for them, and re-layouts  16.1 us
    ppermute x12, starting transfers between devices, along_line(): lax.ppermute(downs[-1], 'hi', [(i, i - 1) for i in range(1, count - hops...  15.6 us
    psum x1, blocking collectives, half_width(): scores = lax.psum(partial, ('lo', 'mp'))  11.9 us
    dot_general x5, matrix products, contract_rows(): lax.dot_general(both, second, (((1,), (1,)), ((), ())), preferred_element...  10.7 us
    rev x2, local copies, waits for them, and re-layouts, other_way(): turned = matrix.reshape(2, tokens, count, 2, chunk)[::-1, :, :, ::-1]  10.3 us
  transfers between devices with their start and end apart: 29, of which 8 were waited for; matrix products, arithmetic and copies ran while one was open for 26% of the time, Pallas kernels for 0%

profile of v2, /device:TPU:0, one launch (start us, length us, event | category | flops | bytes accessed | tf_op | source)
XLA Modules:
  0.0 236.3 jit_solution(11217343215190368953)
XLA Ops:
  9.6 1.5 constant_dynamic-update-slice_fusion.2
  11.0 1.5 constant_dynamic-update-slice_fusion.1
  13.2 5.6 %collective-permute-start.2 = (bf16[64,1024]{1,0:T(8,128)(2,1)}, bf16[64,1024]{1,0:T(8,128)(2,1)}, u32[]{:S(2)}, u32[]{:S(2)}) collective-permute-start(bf16[64,1024]{1,0:T(8,128)(2,1)} %pad_maximum_fusion.6), channel_id=1, source_target_pairs={{0,8},{8,16},{16,24},{1,9},{9,17},{17,25},{2,10},{10,18},{18,26},{... | collective-permute-start | bytes 393224 | tf_op jit(solution)/shard_map/ppermute | solution.py:117
  18.7 1.3 collective-permute-start.3
  20.0 2.1 dynamic-slice_bitcast_fusion.3
  23.0 1.5 collective-permute-start.15
  26.5 1.3 constant_dynamic-slice_fusion.4
  27.8 1.0 copy.89
  28.8 1.5 collective-permute-start
  30.3 1.7 pad_maximum_fusion.4
  32.2 7.3 %collective-permute-done.1 = bf16[64,1024]{1,0:T(8,128)(2,1)} collective-permute-done((bf16[64,1024]{1,0:T(8,128)(2,1)}, bf16[64,1024]{1,0:T(8,128)(2,1)}, u32[]{:S(2)}, u32[]{:S(2)}) %collective-permute-start.1) | collective-permute-done | bytes 131104 | tf_op jit(solution)/shard_map/ppermute | solution.py:140
  39.5 5.4 %collective-permute-start.16 = (bf16[64,3584]{1,0:T(8,128)(2,1)}, bf16[64,3584]{1,0:T(8,128)(2,1)}, u32[]{:S(2)}, u32[]{:S(2)}) collective-permute-start(bf16[64,3584]{1,0:T(8,128)(2,1)} %pad_maximum_fusion.4), channel_id=1, source_target_pairs={{0,8},{8,16},{16,24},{1,9},{9,17},{17,25},{2,10},{10,18},{18,26},{... | collective-permute-start | bytes 1376264 | tf_op jit(solution)/shard_map/ppermute | solution.py:117
  44.9 1.6 constant_dynamic-update-slice_fusion
  46.5 2.0 collective-permute-start.4
  48.5 1.3 collective-permute-start.5
  49.8 1.6 fusion.34
  51.4 2.3 collective-permute-done.4
  54.4 1.2 collective-permute-done.5
  55.6 1.3 collective-permute-start.7
  58.3 6.1 %collective-permute-done.7 = bf16[64,1024]{1,0:T(8,128)(2,1)S(1)} collective-permute-done((bf16[64,1024]{1,0:T(8,128)(2,1)S(1)}, bf16[64,1024]{1,0:T(8,128)(2,1)S(1)}, u32[]{:S(2)}, u32[]{:S(2)}) %collective-permute-start.7) | collective-permute-done | bytes 131104 | tf_op jit(solution)/shard_map/ppermute | solution.py:118
  64.4 1.3 collective-permute-start.9
  67.1 5.2 %collective-permute-done.9 = bf16[64,1024]{1,0:T(8,128)(2,1)S(1)} collective-permute-done((bf16[64,1024]{1,0:T(8,128)(2,1)S(1)}, bf16[64,1024]{1,0:T(8,128)(2,1)S(1)}, u32[]{:S(2)}, u32[]{:S(2)}) %collective-permute-start.9) | collective-permute-done | bytes 131104 | tf_op jit(solution)/shard_map/ppermute | solution.py:118
  72.3 1.3 collective-permute-start.11
  74.3 1.3 collective-permute-start.17
  75.6 4.7 %collective-permute-done.11 = bf16[64,1024]{1,0:T(8,128)(2,1)S(1)} collective-permute-done((bf16[64,1024]{1,0:T(8,128)(2,1)S(1)}, bf16[64,1024]{1,0:T(8,128)(2,1)S(1)}, u32[]{:S(2)}, u32[]{:S(2)}) %collective-permute-start.11) | collective-permute-done | bytes 131104 | tf_op jit(solution)/shard_map/ppermute | solution.py:118
  81.8 1.3 collective-permute-start.13
  83.1 5.4 %collective-permute-start.18 = (bf16[64,3584]{1,0:T(8,128)(2,1)}, bf16[64,3584]{1,0:T(8,128)(2,1)}, u32[]{:S(2)}, u32[]{:S(2)}) collective-permute-start(bf16[64,3584]{1,0:T(8,128)(2,1)} %collective-permute-done.15), channel_id=1, source_target_pairs={{0,8},{8,16},{16,24},{1,9},{9,17},{17,25},{2,10},{10,18},{18,26},{... | collective-permute-start | bytes 1376264 | tf_op jit(solution)/shard_map/ppermute | solution.py:117
  88.4 1.1 pad_maximum_fusion.2
  90.7 1.3 collective-permute-start.19
  92.0 1.5 collective-permute-start.20
  93.5 1.3 collective-permute-start.21
  94.9 1.3 fusion.2
  96.4 1.3 copy.69
  97.7 1.9 reshape.175
  99.6 4.2 %rev.9 = f32[2,256,4,2,64]{1,0,4,3,2:T(2,128)} reverse(f32[2,256,4,2,64]{1,0,4,3,2:T(2,128)S(1)} %reshape.175), dimensions={0,3} | reverse | bytes 2097152 | tf_op jit(solution)/shard_map/rev | solution.py:167
  103.8 2.3 copy.93
  106.1 1.6 copy.70
  107.6 1.3 broadcast_select_fusion.1
  109.0 3.5 %constant_dynamic-slice_fusion.1 = (bf16[256,3584]{1,0:T(8,128)(2,1)}, bf16[256,3584]{1,0:T(8,128)(2,1)S(1)}) fusion(bf16[256,7168]{1,0:T(8,128)(2,1)} %param.8, s32[]{:T(128)S(6)} %select_n.440, s32[]{:T(128)S(6)} %select_n.441), kind=kLoop, calls=%fused_computation.91 | loop fusion | bytes 7340040 | tf_op jit(solution)/shard_map/dynamic_slice | solution.py:134
  112.5 2.3 copy.92
  114.8 1.5 collective-permute-start.14
  116.3 2.9 %copy.91 = bf16[256,3584]{0,1:T(8,128)(2,1)S(1)} copy(bf16[256,3584]{1,0:T(8,128)(2,1)} %get-tuple-element.17) | data formatting | bytes 3670016
  119.3 1.4 collective-permute-start.22
  120.7 1.3 collective-permute-start.23
  122.0 1.4 collective-permute-start.24
  123.4 1.3 collective-permute-start.25
  124.7 50.0 %all-reduce.2.cloned.1.call-done = f32[512,512]{1,0:T(8,128)} async-done(((f32[512,512]{1,0:T(8,128)}), f32[512,512]{1,0:T(8,128)}) %all-reduce.2.cloned.1.call-update) | async-done | bytes 1048592 | tf_op jit(solution)/shard_map/psum | solution.py:171
  174.7 1.6 copy.71
  176.3 1.6 reshape.177
  177.9 6.1 %rev.10 = f32[2,256,4,2,64]{1,0,4,3,2:T(2,128)} reverse(f32[2,256,4,2,64]{1,0,4,3,2:T(2,128)} %reshape.177), dimensions={0,3} | reverse | bytes 2097152 | tf_op jit(solution)/shard_map/rev | solution.py:167
  184.1 2.3 copy.94
  186.3 2.5 %copy.72 = f32[512,512]{1,0:T(8,128)} copy(f32[512,512]{0,1:T(8,128)} %bitcast.62) | data formatting | bytes 2097152 | tf_op jit(solution)/shard_map/reshape | solution.py:168
  189.8 1.5 collective-permute-start.27
  191.3 2.7 %fusion.28 = (bf16[64,3584]{1,0:T(8,128)(2,1)}, bf16[64,3584]{1,0:T(8,128)(2,1)}, bf16[64,3584]{1,0:T(8,128)(2,1)S(1)}) fusion(bf16[64,3584]{1,0:T(8,128)(2,1)} %collective-permute-done.20, bf16[64,3584]{1,0:T(8,128)(2,1)} %collective-permute-done.17, bf16[64,3584]{1,0:T(8,128)(2,1)} %collective-permute-done.21, pred[]{:T(512)S(6)} %eq.60, pred[]{:T(512)S(6)} %eq.59, ...), kind=kLoop, calls=%fused_computation.42 | loop fusion | flops 2064384 | bytes 4128771 | tf_op jit(solution)/shard_map/jit(_where)/select_n | solution.py:130
  194.0 1.9 pad_maximum_fusion.1
  196.6 1.2 fusion.6
  197.7 1.3 reduce-precision_convert_fusion
  199.1 4.2 %collective-permute-done.27 = bf16[64,3584]{1,0:T(8,128)(2,1)} collective-permute-done((bf16[64,3584]{1,0:T(8,128)(2,1)}, bf16[64,3584]{1,0:T(8,128)(2,1)}, u32[]{:S(2)}, u32[]{:S(2)}) %collective-permute-start.27) | collective-permute-done | bytes 458784 | tf_op jit(solution)/shard_map/ppermute | solution.py:118
  203.2 1.7 fusion.29
  205.0 2.1 fusion.24
  207.1 2.1 fusion.20
  209.2 2.1 fusion.16
  211.3 3.1 %fusion.10 = f32[1024,128]{1,0:T(8,128)S(1)} fusion(bf16[64,3584]{1,0:T(8,128)(2,1)} %collective-permute-done.15, bf16[32,3584]{1,0:T(8,128)(2,1)S(1)} %copy-done.4, bf16[32,3584]{1,0:T(8,128)(2,1)S(1)} %get-tuple-element.11, bf16[512,3584]{0,1:T(8,128)(2,1)S(1)} %get-tuple-element.10, bf16[512,3584]{0,1:T(8,128)(2,1)S(1)} %get-tuple-element.9), kind=kOutput, calls=%fused_computation.18 | convolution fusion | flops 956956672 | bytes 8781824 | tf_op jit(solution)/shard_map/dot_general | solution.py:26
  216.8 11.9 %psum.15 = f32[4,16]{1,0:T(4,128)S(1)} all-reduce(f32[4,16]{1,0:T(4,128)S(1)} %multiply_select_fusion), channel_id=1, replica_groups=mesh['hi'=4,'lo'=2,'mp'=4] {'lo','mp'}, use_global_device_ids=true, to_apply=%region_7.8 | all-reduce | flops 64 | bytes 512 | tf_op jit(solution)/shard_map/psum | solution.py:183
  (89 shorter events, 17.1 us)
Async XLA Ops:
  6.5 83.0 %copy-start = (bf16[4,512,512]{2,1,0:T(8,128)(2,1)S(1)}, bf16[4,512,512]{2,1,0:T(8,128)(2,1)}, u32[]{:S(2)}) copy-start(bf16[4,512,512]{2,1,0:T(8,128)(2,1)} %param.9) | copy-start | bytes 6291460
  6.5 168.2 %all-reduce.2.cloned.1.call-start = ((), (), s32[]{:S(2)}) async-start(), calls=%async_computation | async-start | bytes 2097152 | tf_op jit(solution)/shard_map/psum | solution.py:171
  13.2 33.3 %collective-permute-start.2 = (bf16[64,1024]{1,0:T(8,128)(2,1)}, bf16[64,1024]{1,0:T(8,128)(2,1)}, u32[]{:S(2)}, u32[]{:S(2)}) collective-permute-start(bf16[64,1024]{1,0:T(8,128)(2,1)} %pad_maximum_fusion.6), channel_id=1, source_target_pairs={{0,8},{8,16},{16,24},{1,9},{9,17},{17,25},{2,10},{10,18},{18,26},{... | collective-permute-start | bytes 393224 | tf_op jit(solution)/shard_map/ppermute | solution.py:117
  18.7 29.8 %collective-permute-start.3 = (bf16[64,1024]{1,0:T(8,128)(2,1)}, bf16[64,1024]{1,0:T(8,128)(2,1)S(1)}, u32[]{:S(2)}, u32[]{:S(2)}) collective-permute-start(bf16[64,1024]{1,0:T(8,128)(2,1)} %pad_maximum_fusion.6), channel_id=1, source_target_pairs={{8,0},{16,8},{24,16},{9,1},{17,9},{25,17},{10,2},{18,10},{26,18},{... | collective-permute-start | bytes 393224 | tf_op jit(solution)/shard_map/ppermute | solution.py:118
  23.0 58.8 %collective-permute-start.15 = (bf16[64,3584]{1,0:T(8,128)(2,1)}, bf16[64,3584]{1,0:T(8,128)(2,1)}, u32[]{:S(2)}, u32[]{:S(2)}) collective-permute-start(bf16[64,3584]{1,0:T(8,128)(2,1)} %pad_maximum_fusion.3), channel_id=1, source_target_pairs={{0,4},{4,0},{1,5},{5,1},{2,6},{6,2},{3,7},{7,3},{8,12},{12,8},{9,1... | collective-permute-start | bytes 1376264 | tf_op jit(solution)/shard_map/ppermute | solution.py:141
  26.0 13.5 %collective-permute-start.1 = (bf16[64,1024]{1,0:T(8,128)(2,1)}, bf16[64,1024]{1,0:T(8,128)(2,1)}, u32[]{:S(2)}, u32[]{:S(2)}) collective-permute-start(bf16[64,1024]{1,0:T(8,128)(2,1)} %pad_maximum_fusion.5), channel_id=1, source_target_pairs={{0,4},{4,0},{1,5},{5,1},{2,6},{6,2},{3,7},{7,3},{8,12},{12,8},{9,1... | collective-permute-start | bytes 393224 | tf_op jit(solution)/shard_map/ppermute | solution.py:140
  28.8 54.2 %collective-permute-start = (bf16[256,1024]{0,1:T(8,128)(2,1)}, bf16[256,1024]{0,1:T(8,128)(2,1)}, u32[]{:S(2)}, u32[]{:S(2)}) collective-permute-start(bf16[256,1024]{0,1:T(8,128)(2,1)} %copy.89), channel_id=1, source_target_pairs={{0,4},{4,0},{1,5},{5,1},{2,6},{6,2},{3,7},{7,3},{8,12},{12,8},{9,1... | collective-permute-start | bytes 1572872 | tf_op jit(solution)/shard_map/ppermute | solution.py:144
  39.5 51.2 %collective-permute-start.16 = (bf16[64,3584]{1,0:T(8,128)(2,1)}, bf16[64,3584]{1,0:T(8,128)(2,1)}, u32[]{:S(2)}, u32[]{:S(2)}) collective-permute-start(bf16[64,3584]{1,0:T(8,128)(2,1)} %pad_maximum_fusion.4), channel_id=1, source_target_pairs={{0,8},{8,16},{16,24},{1,9},{9,17},{17,25},{2,10},{10,18},{18,26},{... | collective-permute-start | bytes 1376264 | tf_op jit(solution)/shard_map/ppermute | solution.py:117
  46.5 7.3 %collective-permute-start.4 = (bf16[64,1024]{1,0:T(8,128)(2,1)}, bf16[64,1024]{1,0:T(8,128)(2,1)S(1)}, u32[]{:S(2)}, u32[]{:S(2)}) collective-permute-start(bf16[64,1024]{1,0:T(8,128)(2,1)} %collective-permute-done.1), channel_id=1, source_target_pairs={{0,8},{8,16},{16,24},{1,9},{9,17},{17,25},{2,10},{10,18},{18,26},{... | collective-permute-start | bytes 393224 | tf_op jit(solution)/shard_map/ppermute | solution.py:117
  48.5 7.1 %collective-permute-start.5 = (bf16[64,1024]{1,0:T(8,128)(2,1)}, bf16[64,1024]{1,0:T(8,128)(2,1)S(1)}, u32[]{:S(2)}, u32[]{:S(2)}) collective-permute-start(bf16[64,1024]{1,0:T(8,128)(2,1)} %collective-permute-done.1), channel_id=1, source_target_pairs={{8,0},{16,8},{24,16},{9,1},{17,9},{25,17},{10,2},{18,10},{26,18},{... | collective-permute-start | bytes 393224 | tf_op jit(solution)/shard_map/ppermute | solution.py:118
  53.7 3.9 %collective-permute-start.6 = (bf16[64,1024]{1,0:T(8,128)(2,1)}, bf16[64,1024]{1,0:T(8,128)(2,1)S(1)}, u32[]{:S(2)}, u32[]{:S(2)}) collective-permute-start(bf16[64,1024]{1,0:T(8,128)(2,1)} %collective-permute-done.2), channel_id=1, source_target_pairs={{8,16},{16,24},{9,17},{17,25},{10,18},{18,26},{11,19},{19,27},{12,... | collective-permute-start | bytes 393224 | tf_op jit(solution)/shard_map/ppermute | solution.py:117
  55.6 8.8 %collective-permute-start.7 = (bf16[64,1024]{1,0:T(8,128)(2,1)S(1)}, bf16[64,1024]{1,0:T(8,128)(2,1)S(1)}, u32[]{:S(2)}, u32[]{:S(2)}) collective-permute-start(bf16[64,1024]{1,0:T(8,128)(2,1)S(1)} %collective-permute-done.3), channel_id=1, source_target_pairs={{8,0},{16,8},{9,1},{17,9},{10,2},{18,10},{11,3},{19,11},{12,4},{20... | collective-permute-start | bytes 393224 | tf_op jit(solution)/shard_map/ppermute | solution.py:118
  57.6 8.8 %collective-permute-start.8 = (bf16[64,1024]{1,0:T(8,128)(2,1)S(1)}, bf16[64,1024]{1,0:T(8,128)(2,1)S(1)}, u32[]{:S(2)}, u32[]{:S(2)}) collective-permute-start(bf16[64,1024]{1,0:T(8,128)(2,1)S(1)} %collective-permute-done.4), channel_id=1, source_target_pairs={{8,16},{16,24},{9,17},{17,25},{10,18},{18,26},{11,19},{19,27},{12,... | collective-permute-start | bytes 393224 | tf_op jit(solution)/shard_map/ppermute | solution.py:117
  64.4 7.9 %collective-permute-start.9 = (bf16[64,1024]{1,0:T(8,128)(2,1)S(1)}, bf16[64,1024]{1,0:T(8,128)(2,1)S(1)}, u32[]{:S(2)}, u32[]{:S(2)}) collective-permute-start(bf16[64,1024]{1,0:T(8,128)(2,1)S(1)} %collective-permute-done.5), channel_id=1, source_target_pairs={{8,0},{16,8},{9,1},{17,9},{10,2},{18,10},{11,3},{19,11},{12,4},{20... | collective-permute-start | bytes 393224 | tf_op jit(solution)/shard_map/ppermute | solution.py:118
  66.4 7.9 %collective-permute-start.10 = (bf16[64,1024]{1,0:T(8,128)(2,1)S(1)}, bf16[64,1024]{1,0:T(8,128)(2,1)S(1)}, u32[]{:S(2)}, u32[]{:S(2)}) collective-permute-start(bf16[64,1024]{1,0:T(8,128)(2,1)S(1)} %collective-permute-done.6), channel_id=1, source_target_pairs={{16,24},{17,25},{18,26},{19,27},{20,28},{21,29},{22,30},{23,31}} | collective-permute-start | bytes 393224 | tf_op jit(solution)/shard_map/ppermute | solution.py:117
  72.3 8.0 %collective-permute-start.11 = (bf16[64,1024]{1,0:T(8,128)(2,1)S(1)}, bf16[64,1024]{1,0:T(8,128)(2,1)S(1)}, u32[]{:S(2)}, u32[]{:S(2)}) collective-permute-start(bf16[64,1024]{1,0:T(8,128)(2,1)S(1)} %collective-permute-done.7), channel_id=1, source_target_pairs={{8,0},{9,1},{10,2},{11,3},{12,4},{13,5},{14,6},{15,7}} | collective-permute-start | bytes 393224 | tf_op jit(solution)/shard_map/ppermute | solution.py:118
  74.3 17.7 %collective-permute-start.17 = (bf16[64,3584]{1,0:T(8,128)(2,1)}, bf16[64,3584]{1,0:T(8,128)(2,1)}, u32[]{:S(2)}, u32[]{:S(2)}) collective-permute-start(bf16[64,3584]{1,0:T(8,128)(2,1)} %pad_maximum_fusion.4), channel_id=1, source_target_pairs={{8,0},{16,8},{24,16},{9,1},{17,9},{25,17},{10,2},{18,10},{26,18},{... | collective-permute-start | bytes 1376264 | tf_op jit(solution)/shard_map/ppermute | solution.py:118
  80.4 13.2 %collective-permute-start.12 = (bf16[64,1024]{1,0:T(8,128)(2,1)S(1)}, bf16[64,1024]{1,0:T(8,128)(2,1)S(1)}, u32[]{:S(2)}, u32[]{:S(2)}) collective-permute-start(bf16[64,1024]{1,0:T(8,128)(2,1)S(1)} %collective-permute-done.8), channel_id=1, source_target_pairs={{16,24},{17,25},{18,26},{19,27},{20,28},{21,29},{22,30},{23,31}} | collective-permute-start | bytes 393224 | tf_op jit(solution)/shard_map/ppermute | solution.py:117
  81.8 13.0 %collective-permute-start.13 = (bf16[64,1024]{1,0:T(8,128)(2,1)S(1)}, bf16[64,1024]{1,0:T(8,128)(2,1)S(1)}, u32[]{:S(2)}, u32[]{:S(2)}) collective-permute-start(bf16[64,1024]{1,0:T(8,128)(2,1)S(1)} %collective-permute-done.9), channel_id=1, source_target_pairs={{8,0},{9,1},{10,2},{11,3},{12,4},{13,5},{14,6},{15,7}} | collective-permute-start | bytes 393224 | tf_op jit(solution)/shard_map/ppermute | solution.py:118
  83.1 36.2 %collective-permute-start.18 = (bf16[64,3584]{1,0:T(8,128)(2,1)}, bf16[64,3584]{1,0:T(8,128)(2,1)}, u32[]{:S(2)}, u32[]{:S(2)}) collective-permute-start(bf16[64,3584]{1,0:T(8,128)(2,1)} %collective-permute-done.15), channel_id=1, source_target_pairs={{0,8},{8,16},{16,24},{1,9},{9,17},{17,25},{2,10},{10,18},{18,26},{... | collective-permute-start | bytes 1376264 | tf_op jit(solution)/shard_map/ppermute | solution.py:117
  89.6 5.2 %copy-start.7 = (bf16[512,1024]{1,0:T(8,128)(2,1)S(1)}, bf16[512,1024]{1,0:T(8,128)(2,1)}, u32[]{:S(2)}) copy-start(bf16[512,1024]{1,0:T(8,128)(2,1)} %select_dynamic-update-slice_fusion.1) | copy-start | bytes 3145732
  90.7 30.0 %collective-permute-start.19 = (bf16[64,3584]{1,0:T(8,128)(2,1)}, bf16[64,3584]{1,0:T(8,128)(2,1)}, u32[]{:S(2)}, u32[]{:S(2)}) collective-permute-start(bf16[64,3584]{1,0:T(8,128)(2,1)} %collective-permute-done.15), channel_id=1, source_target_pairs={{8,0},{16,8},{24,16},{9,1},{17,9},{25,17},{10,2},{18,10},{26,18},{... | collective-permute-start | bytes 1376264 | tf_op jit(solution)/shard_map/ppermute | solution.py:118
  92.0 30.0 %collective-permute-start.20 = (bf16[64,3584]{1,0:T(8,128)(2,1)}, bf16[64,3584]{1,0:T(8,128)(2,1)}, u32[]{:S(2)}, u32[]{:S(2)}) collective-permute-start(bf16[64,3584]{1,0:T(8,128)(2,1)} %collective-permute-done.16), channel_id=1, source_target_pairs={{8,16},{16,24},{9,17},{17,25},{10,18},{18,26},{11,19},{19,27},{12,... | collective-permute-start | bytes 1376264 | tf_op jit(solution)/shard_map/ppermute | solution.py:117
  93.5 29.9 %collective-permute-start.21 = (bf16[64,3584]{1,0:T(8,128)(2,1)}, bf16[64,3584]{1,0:T(8,128)(2,1)}, u32[]{:S(2)}, u32[]{:S(2)}) collective-permute-start(bf16[64,3584]{1,0:T(8,128)(2,1)} %collective-permute-done.17), channel_id=1, source_target_pairs={{8,0},{16,8},{9,1},{17,9},{10,2},{18,10},{11,3},{19,11},{12,4},{20... | collective-permute-start | bytes 1376264 | tf_op jit(solution)/shard_map/ppermute | solution.py:118
  114.8 79.1 %collective-permute-start.14 = (bf16[256,3584]{0,1:T(8,128)(2,1)}, bf16[256,3584]{0,1:T(8,128)(2,1)}, u32[]{:S(2)}, u32[]{:S(2)}) collective-permute-start(bf16[256,3584]{0,1:T(8,128)(2,1)} %copy.92), channel_id=1, source_target_pairs={{0,4},{4,0},{1,5},{5,1},{2,6},{6,2},{3,7},{7,3},{8,12},{12,8},{9,1... | collective-permute-start | bytes 5505032 | tf_op jit(solution)/shard_map/ppermute | solution.py:145
  119.3 69.8 %collective-permute-start.22 = (bf16[64,3584]{1,0:T(8,128)(2,1)}, bf16[64,3584]{1,0:T(8,128)(2,1)}, u32[]{:S(2)}, u32[]{:S(2)}) collective-permute-start(bf16[64,3584]{1,0:T(8,128)(2,1)} %collective-permute-done.18), channel_id=1, source_target_pairs={{8,16},{16,24},{9,17},{17,25},{10,18},{18,26},{11,19},{19,27},{12,... | collective-permute-start | bytes 1376264 | tf_op jit(solution)/shard_map/ppermute | solution.py:117
  120.7 69.1 %collective-permute-start.23 = (bf16[64,3584]{1,0:T(8,128)(2,1)}, bf16[64,3584]{1,0:T(8,128)(2,1)}, u32[]{:S(2)}, u32[]{:S(2)}) collective-permute-start(bf16[64,3584]{1,0:T(8,128)(2,1)} %collective-permute-done.19), channel_id=1, source_target_pairs={{8,0},{16,8},{9,1},{17,9},{10,2},{18,10},{11,3},{19,11},{12,4},{20... | collective-permute-start | bytes 1376264 | tf_op jit(solution)/shard_map/ppermute | solution.py:118
  122.0 69.3 %collective-permute-start.24 = (bf16[64,3584]{1,0:T(8,128)(2,1)}, bf16[64,3584]{1,0:T(8,128)(2,1)}, u32[]{:S(2)}, u32[]{:S(2)}) collective-permute-start(bf16[64,3584]{1,0:T(8,128)(2,1)} %collective-permute-done.20), channel_id=1, source_target_pairs={{16,24},{17,25},{18,26},{19,27},{20,28},{21,29},{22,30},{23,31}} | collective-permute-start | bytes 1376264 | tf_op jit(solution)/shard_map/ppermute | solution.py:117
  123.4 67.9 %collective-permute-start.25 = (bf16[64,3584]{1,0:T(8,128)(2,1)}, bf16[64,3584]{1,0:T(8,128)(2,1)}, u32[]{:S(2)}, u32[]{:S(2)}) collective-permute-start(bf16[64,3584]{1,0:T(8,128)(2,1)} %collective-permute-done.21), channel_id=1, source_target_pairs={{8,0},{9,1},{10,2},{11,3},{12,4},{13,5},{14,6},{15,7}} | collective-permute-start | bytes 1376264 | tf_op jit(solution)/shard_map/ppermute | solution.py:118
  177.9 10.9 %copy-start.2 = (f32[512,512]{1,0:T(8,128)S(1)}, f32[512,512]{1,0:T(8,128)}, u32[]{:S(2)}) copy-start(f32[512,512]{1,0:T(8,128)} %all-reduce.2.cloned.1.call-done) | copy-start | bytes 3145732
  189.1 10.0 %collective-permute-start.26 = (bf16[64,3584]{1,0:T(8,128)(2,1)}, bf16[64,3584]{1,0:T(8,128)(2,1)S(1)}, u32[]{:S(2)}, u32[]{:S(2)}) collective-permute-start(bf16[64,3584]{1,0:T(8,128)(2,1)} %collective-permute-done.22), channel_id=1, source_target_pairs={{16,24},{17,25},{18,26},{19,27},{20,28},{21,29},{22,30},{23,31}} | collective-permute-start | bytes 1376264 | tf_op jit(solution)/shard_map/ppermute | solution.py:117
  189.8 13.4 %collective-permute-start.27 = (bf16[64,3584]{1,0:T(8,128)(2,1)}, bf16[64,3584]{1,0:T(8,128)(2,1)}, u32[]{:S(2)}, u32[]{:S(2)}) collective-permute-start(bf16[64,3584]{1,0:T(8,128)(2,1)} %collective-permute-done.23), channel_id=1, source_target_pairs={{8,0},{9,1},{10,2},{11,3},{12,4},{13,5},{14,6},{15,7}} | collective-permute-start | bytes 1376264 | tf_op jit(solution)/shard_map/ppermute | solution.py:118
  194.0 2.6 %copy-start.3 = (bf16[28,256,256]{2,1,0:T(8,128)(2,1)S(1)}, bf16[28,256,256]{2,1,0:T(8,128)(2,1)}, u32[]{:S(2)}) copy-start(bf16[28,256,256]{2,1,0:T(8,128)(2,1)} %param.10) | copy-start | bytes 11010052
  199.0 5.9 %copy-start.6 = (bf16[64,3584]{1,0:T(8,128)(2,1)S(1)}, bf16[64,3584]{1,0:T(8,128)(2,1)}, u32[]{:S(2)}) copy-start(bf16[64,3584]{1,0:T(8,128)(2,1)} %get-tuple-element.28) | copy-start | bytes 1376260
  205.0 2.1 copy-start.5
  209.2 2.1 copy-start.4
  214.4 15.0 %copy-start.1 = (bf16[4,512,512]{2,1,0:T(8,128)(2,1)S(1)}, bf16[4,512,512]{2,1,0:T(8,128)(2,1)}, u32[]{:S(2)}) copy-start(bf16[4,512,512]{2,1,0:T(8,128)(2,1)} %param.9) | copy-start | bytes 6291460
Sparse Core Ops, SparseCore 0:
  109.1 65.5 all-reduce.1

commit v3 on v1

v3 whole, which is shorter than its diff:
```python
import jax
import jax.numpy as jnp
from jax import lax
from jax.experimental import pallas as pl
from jax.experimental.pallas import tpu as pltpu
from jax.sharding import PartitionSpec as P

NQ = 16
R = 32
LEN = 128


def params():
    return pltpu.CompilerParams(vmem_limit_bytes=48 * 2**20)


def pick_rows(groups, owners, left_store, right_store):
    per = NQ // groups
    width_left = left_store.shape[2]
    half = right_store.shape[2] // 2

    def kernel(owners_ref, left_ref, right_ref, left_out, first_out, second_out, sems):
        group = lax.axis_index("dp")
        found = jnp.int32(0)
        queries = [jnp.int32(0)] * per
        for q in range(NQ):
            own = owners_ref[q] == group
            queries = [jnp.where(own & (found == i), q, at) for i, at in enumerate(queries)]
            found = found + own.astype(jnp.int32)
        copies = []
        for i in range(per):
            rows = pl.ds(pl.multiple_of(queries[i] * R, R), R)
            here = pl.ds(i * R, R)
            pairs = [
                (left_ref.at[0, rows, :], left_out.at[here, :]),
                (right_ref.at[0, rows, pl.ds(0, half)], first_out.at[here, :]),
                (right_ref.at[0, rows, pl.ds(half, half)], second_out.at[here, :]),
            ]
            for j, (source, target) in enumerate(pairs):
                copies.append(pltpu.make_async_copy(source, target, sems.at[i, j]))
        for copy in copies:
            copy.start()
        for copy in copies:
            copy.wait()

    shape = lambda width: jax.ShapeDtypeStruct((per * R, width), jnp.bfloat16)
    anywhere = pl.BlockSpec(memory_space=pl.ANY)
    return pl.pallas_call(
        kernel,
        out_shape=(shape(width_left), shape(half), shape(half)),
        in_specs=[pl.BlockSpec(memory_space=pltpu.SMEM), anywhere, anywhere],
        out_specs=(anywhere, anywhere, anywhere),
        scratch_shapes=[pltpu.SemaphoreType.DMA((per, 3))],
        compiler_params=params(),
        name="pick_rows",
    )(owners, left_store, right_store)


def rotate(matrix, basis, shard):
    rows = matrix.shape[0]
    blocks, width = basis.shape[0], basis.shape[1]
    each = max(n for n in range(1, 5) if blocks % n == 0 and n * width <= 1024)
    steps = blocks // each

    def kernel(shard_ref, matrix_ref, basis_ref, out_ref):
        for k in range(each):
            columns = slice(k * width, (k + 1) * width)
            turned = jnp.dot(
                matrix_ref[:, columns], basis_ref[k], preferred_element_type=jnp.float32
            )
            high = turned.astype(jnp.bfloat16)
            out_ref[:rows, columns] = high
            out_ref[rows:, columns] = (turned - high.astype(jnp.float32)).astype(jnp.bfloat16)

    total = blocks * width
    return pl.pallas_call(
        kernel,
        out_shape=jax.ShapeDtypeStruct((2 * rows, total), jnp.bfloat16),
        grid_spec=pltpu.PrefetchScalarGridSpec(
            num_scalar_prefetch=1,
            grid=(steps,),
            in_specs=[
                pl.BlockSpec((rows, each * width), lambda k, at: (0, at[0] * steps + k)),
                pl.BlockSpec((each, width, width), lambda k, at: (k, 0, 0)),
            ],
            out_specs=pl.BlockSpec((2 * rows, each * width), lambda k, at: (0, k)),
        ),
        compiler_params=params(),
        cost_estimate=pl.CostEstimate(
            flops=2 * rows * total * width,
            bytes_accessed=2 * (3 * rows * total + total * width),
            transcendentals=0,
        ),
        name="rotate",
    )(jnp.reshape(shard, (1,)).astype(jnp.int32), matrix, basis)


def contract_rows(both, second):
    rows = both.shape[0] // 2
    out = lax.dot_general(
        both, second, (((1,), (1,)), ((), ())), preferred_element_type=jnp.float32
    )
    return out[:rows] + out[rows:]


def places(owners):
    at = jnp.arange(NQ, dtype=jnp.int32)
    before = (owners[None, :] < owners[:, None]) | (
        (owners[None, :] == owners[:, None]) & (at[None, :] < at[:, None])
    )
    return jnp.sum(before.astype(jnp.int32), axis=1)


def swapped(piece, distance, shards):
    return lax.ppermute(piece, "mp", [(i, i ^ distance) for i in range(shards)])


def small_sum(array, shards):
    distance = 1
    while distance < shards:
        reach = min(4, shards // distance)
        array = sum([swapped(array, distance * k, shards) for k in range(1, reach)], array)
        distance *= reach
    return array


def after(value, others):
    return lax.optimization_barrier((value, others))[0] if others else value


def sum_over_shards(matrix, shards, others):
    others = iter(others)
    shard = lax.axis_index("mp")
    bit = shard % 2
    half = matrix.shape[0] // 2

    mine = lax.dynamic_slice_in_dim(matrix, bit * half, half, 0)
    got = swapped(lax.dynamic_slice_in_dim(matrix, (1 - bit) * half, half, 0), 1, shards)
    mine = mine + after(got, next(others, None))
    distance = 2
    while distance < shards:
        mine = mine + after(swapped(mine, distance, shards), next(others, None))
        distance *= 2
    other = swapped(mine, 1, shards)
    return jnp.where(
        bit == 0, jnp.concatenate([mine, other], axis=0), jnp.concatenate([other, mine], axis=0)
    )


def on_device(groups, shards, out_grads, hidden_acts, out_basis, in_basis, left_store, right_store, owners):
    per = NQ // groups
    group = lax.axis_index("dp")
    shard = lax.axis_index("mp")
    place = places(owners)
    chunk = per * R
    ring = list(range(0, groups, 2)) + list(range(groups - 1, 0, -2))
    forward = [(ring[i], ring[(i + 1) % groups]) for i in range(groups)]
    backward = [(b, a) for a, b in forward]
    reach = groups // 2

    own = pick_rows(groups, owners, left_store, right_store)
    half = own[1].shape[1]

    order = [(0, 1), (1, 1)]
    for hops in range(2, reach + 1):
        order += [(0, hops), (2, hops // 2) if hops % 2 == 0 else (1, hops // 2 + 1)]
    for hops in range(1, reach + 1):
        order += [(piece, hops) for piece in (1, 2) if (piece, hops) not in order]
    steps = [[], [], []]
    came = []
    for piece, hops in order:
        ahead, behind = steps[piece][-1] if hops > 1 else (own[piece], own[piece])
        if hops == reach:
            ahead, behind = ahead[: chunk // 2], behind[chunk // 2 :]
        ahead, behind = after((ahead, behind), came[-3:-1])
        got = (lax.ppermute(ahead, "dp", forward), lax.ppermute(behind, "dp", backward))
        steps[piece].append(got)
        came.append(got)

    grads = rotate(out_grads, out_basis, shard)
    acts = rotate(hidden_acts, in_basis, 0)

    left_fac = jnp.concatenate([own[0]] + [piece for step in steps[0] for piece in step], axis=0)
    coefficient = sum_over_shards(
        contract_rows(grads, left_fac), shards, came[order.index((0, reach)) + 1 :]
    )

    parts = []
    at = 0
    for step in range(reach + 1):
        projected = 0.0
        if step == 0:
            factors = own[1:]
        else:
            factors = lax.optimization_barrier((steps[1][step - 1], steps[2][step - 1]))
            factors = [jnp.concatenate(pair, axis=0) for pair in factors]
        for part, factor in enumerate(factors):
            projected += contract_rows(acts[:, part * half : (part + 1) * half], factor)
        width = projected.shape[1]
        terms = coefficient[:, at : at + width] * projected
        parts.append(jnp.sum(terms.reshape(-1, LEN, width), axis=1))
        at += width
    partial = jnp.concatenate(parts, axis=1) / jnp.float32(LEN)

    def position(index):
        return jnp.where(index % 2 == 0, index // 2, groups - 1 - index // 2)

    here = position(group)
    row = jnp.arange(chunk, dtype=jnp.int32) // R
    sources = [(here + 0 * row, row)]
    for hops in range(1, reach + 1):
        ahead, behind = here - hops + 0 * row, here + hops + 0 * row
        if hops < reach:
            sources += [(ahead, row), (behind, row)]
        else:
            cut = chunk // 2
            sources += [(ahead[:cut], row[:cut]), (behind[cut:], row[cut:])]
    source = jnp.concatenate([s for s, _ in sources]) % groups
    row = jnp.concatenate([r for _, r in sources])
    owner = place // per
    hit = (source[:, None] == position(owner)[None, :]) & (row[:, None] == (place % per)[None, :])
    scores = jnp.sum(jnp.where(hit[None], partial[:, :, None], 0.0), axis=1)
    return small_sum(scores, shards)


def solution(mesh):
    groups = mesh.shape["dp"]
    shards = mesh.shape["mp"]
    in_specs = (
        P("dp", None),
        P("dp", "mp"),
        P("mp", None, None),
        P("mp", None, None),
        P("dp", None, "mp"),
        P("dp", None, "mp"),
        P(),
    )

    def whole(*arrays):
        return on_device(groups, shards, *arrays)

    return jax.shard_map(
        whole, mesh=mesh, in_specs=in_specs, out_specs=P("dp", None), check_vma=False
    )
```

time: 226 us -> 119 us (0.53)
  waiting for transfers between devices: 156 us -> 49.1 us
  starting transfers between devices: 0.09 us -> 29.3 us
  between operations: 14.5 us -> 0.46 us
  Pallas kernels: 0 us -> 12 us
  other arithmetic: 13.8 us -> 2.82 us
  local copies, waits for them, and re-layouts: 16 us -> 7.68 us
  blocking collectives: 5.85 us -> 0 us
    all_gather x2 -> x0, waiting for transfers between devices: 133 us -> none  [the longest x1 109 us: on_device(): right_fac = lax.all_gather(own_rows(right_store), 'dp', axis=0, tiled=True)]
    ppermute x0 -> x30, waiting for transfers between devices: none -> 49.1 us  [the longest x12 34.6 us: on_device(): lax.ppermute(ahead, 'dp', forward)]
    ppermute x0 -> x30, starting transfers between devices: none -> 29.3 us  [the longest x12 17.6 us: on_device(): lax.ppermute(ahead, 'dp', forward)]
    psum x1 -> x0, waiting for transfers between devices: 23.6 us -> none  [on_device(): lax.psum(contract_rows(block_rotate(grads, out_basis), left_fac), 'mp')]
    pallas_call x0 -> x3, Pallas kernels: none -> 12 us  [the longest x2 9.85 us: rotate(): pl.pallas_call(kernel, out_shape=jax.ShapeDtypeStruct((2 * rows, total),...]
    convert_element_type x2 -> x0, other arithmetic: 7.67 us -> none  [contract_rows(): both = jnp.concatenate([high.astype(jnp.bfloat16), low], axis=0)]
    psum x1 -> x0, blocking collectives: 5.85 us -> none  [on_device(): scores = lax.psum(per_sequence, 'mp')]
    dot_general x2 -> x0, matrix products: 5.37 us -> none  [block_rotate(): jnp.einsum('tbi,bij->tbj', blocks, eigenbasis, preferred_element_type=jnp...]
  transfers between devices with their start and end apart: 3 -> 30, of which waited for: 3 -> 16; matrix products, arithmetic and copies ran while one was open for 19% -> 17% of each run, Pallas kernels for 0% -> 8%
where the time goes in v3:
time: 119 us
  waiting for transfers between devices  49.1 us (41%)
  starting transfers between devices  29.3 us (25%)
  matrix products  17.4 us (15%)
  Pallas kernels  12 us (10%)
  local copies, waits for them, and re-layouts  7.68 us (6%)
  other arithmetic  2.82 us (2%)
    ppermute x12, waiting for transfers between devices, on_device(): lax.ppermute(ahead, 'dp', forward)  34.6 us
    ppermute x12, starting transfers between devices, on_device(): lax.ppermute(ahead, 'dp', forward)  17.6 us
    dot_general x11, matrix products, contract_rows(): lax.dot_general(both, second, (((1,), (1,)), ((), ())), preferred_element...  17.4 us
    pallas_call x2, Pallas kernels, rotate(): pl.pallas_call(kernel, out_shape=jax.ShapeDtypeStruct((2 * rows, total),...  9.85 us
    ppermute x12, waiting for transfers between devices, on_device(): lax.ppermute(behind, 'dp', backward)  9.59 us
    ppermute x12, starting transfers between devices, on_device(): lax.ppermute(behind, 'dp', backward)  8.08 us
    unnamed x26, local copies, waits for them, and re-layouts  7.26 us
    ppermute x6, waiting for transfers between devices, swapped(): return lax.ppermute(piece, 'mp', [(i, i ^ distance) for i in range(shards)])  4.85 us
  transfers between devices with their start and end apart: 30, of which 16 were waited for; matrix products, arithmetic and copies ran while one was open for 17% of the time, Pallas kernels for 8%

profile of v3, /device:TPU:0, one launch (start us, length us, event | category | flops | bytes accessed | tf_op | source)
XLA Modules:
  0.0 118.7 jit_solution(5807830891024952000)
XLA Ops:
  0.0 1.6 %copy-done.1 = bf16[1,512,2048]{2,1,0:T(8,128)(2,1)S(1)} copy-done((bf16[1,512,2048]{2,1,0:T(8,128)(2,1)S(1)}, bf16[1,512,2048]{2,1,0:T(8,128)(2,1)}, u32[]{:S(2)}) %copy-start.1) | copy-done | bytes 2097176
  1.6 0.7 copy-done.3
  2.2 2.1 %pick_rows.1 = (bf16[64,2048]{1,0:T(8,128)(2,1)S(1)}, bf16[64,3584]{1,0:T(8,128)(2,1)S(1)}, bf16[64,3584]{1,0:T(8,128)(2,1)S(1)}) custom-call(s32[16]{0:T(128)S(1)} %copy-done.3, bf16[1,512,2048]{2,1,0:T(8,128)(2,1)S(1)} %copy-done.1, bf16[1,512,7168]{2,1,0:T(8,128)(2,1)} %right_ref.1), custom_call_target="tpu_custom_call" | custom-call | tf_op jit(solution)/shard_map/pick_rows/pallas_call | solution.py:48
  4.4 3.0 %collective-permute-start.1 = (bf16[64,2048]{1,0:T(8,128)(2,1)S(1)}, bf16[64,2048]{1,0:T(8,128)(2,1)}, u32[]{:S(2)}, u32[]{:S(2)}) collective-permute-start(bf16[64,2048]{1,0:T(8,128)(2,1)S(1)} %get-tuple-element.46), channel_id=1, source_target_pairs={{8,0},{16,8},{24,16},{28,24},{20,28},{12,20},{4,12},{0,4},{9,1},{1... | collective-permute-start | bytes 786440 | tf_op jit(solution)/shard_map/ppermute | solution.py:176
  7.5 1.9 %collective-permute-start.5 = (bf16[64,3584]{1,0:T(8,128)(2,1)S(1)}, bf16[64,3584]{1,0:T(8,128)(2,1)}, u32[]{:S(2)}, u32[]{:S(2)}) collective-permute-start(bf16[64,3584]{1,0:T(8,128)(2,1)S(1)} %get-tuple-element.49), channel_id=1, source_target_pairs={{8,0},{16,8},{24,16},{28,24},{20,28},{12,20},{4,12},{0,4},{9,1},{1... | collective-permute-start | bytes 1376264 | tf_op jit(solution)/shard_map/ppermute | solution.py:176
  10.0 0.6 compare_select_fusion
  10.7 2.0 %copy-done = bf16[256,7168]{1,0:T(8,128)(2,1)S(1)} copy-done((bf16[256,7168]{1,0:T(8,128)(2,1)S(1)}, bf16[256,7168]{1,0:T(8,128)(2,1)}, u32[]{:S(2)}) %copy-start) | copy-done | bytes 3670040
  12.7 7.7 %rotate.3 = bf16[512,7168]{1,0:T(8,128)(2,1)} custom-call(s32[1]{0:T(128)} %constant.123.clone.1.shard_ref, bf16[256,7168]{1,0:T(8,128)(2,1)S(1)} %copy-done, bf16[28,256,256]{2,1,0:T(8,128)(2,1)} %basis_ref.3), custom_call_target="tpu_custom_call" | custom-call | flops 939524096 | bytes 14680064 | tf_op jit(solution)/shard_map/rotate/pallas_call | solution.py:76
  20.4 3.3 %fusion.18 = f32[512,64]{1,0:T(8,128)S(1)} fusion(bf16[64,3584]{1,0:T(8,128)(2,1)S(1)} %get-tuple-element.49, bf16[512,7168]{1,0:T(8,128)(2,1)} %rotate.3), kind=kOutput, calls=%fused_computation.18 | convolution fusion | flops 234881024 | bytes 4259840 | tf_op jit(solution)/shard_map/dot_general | solution.py:100
  23.7 0.9 copy-done.5
  24.6 1.8 %fusion.8 = f32[512,64]{1,0:T(8,128)} fusion(bf16[64,3584]{1,0:T(8,128)(2,1)S(1)} %get-tuple-element.54, bf16[512,7168]{1,0:T(8,128)(2,1)S(1)} %copy-done.5), kind=kOutput, calls=%fused_computation.8 | convolution fusion | flops 234881024 | bytes 4259840 | tf_op jit(solution)/shard_map/dot_general | solution.py:100
  26.4 0.8 compare_and_fusion
  27.2 2.1 %rotate.2 = bf16[512,2048]{1,0:T(8,128)(2,1)S(1)} custom-call(s32[1]{0:T(128)} %bitcast.shard_ref, bf16[256,8192]{1,0:T(8,128)(2,1)} %matrix_ref.2, bf16[4,512,512]{2,1,0:T(8,128)(2,1)S(1)} %copy-done.2), custom_call_target="tpu_custom_call" | custom-call | flops 536870912 | bytes 5242880 | tf_op jit(solution)/shard_map/rotate/pallas_call | solution.py:76
  29.4 2.0 %collective-permute-start.2 = (bf16[64,2048]{1,0:T(8,128)(2,1)}, bf16[64,2048]{1,0:T(8,128)(2,1)S(1)}, u32[]{:S(2)}, u32[]{:S(2)}) collective-permute-start(bf16[64,2048]{1,0:T(8,128)(2,1)} %collective-permute-done), channel_id=1, source_target_pairs={{0,8},{8,16},{16,24},{24,28},{28,20},{20,12},{12,4},{4,0},{1,9},{9... | collective-permute-start | bytes 786440 | tf_op jit(solution)/shard_map/ppermute | solution.py:176
  31.4 1.0 constant_dynamic-update-slice_fusion.7
  32.4 1.0 constant_dynamic-update-slice_fusion.6
  33.4 2.0 %collective-permute-start.8 = (bf16[64,3584]{1,0:T(8,128)(2,1)S(1)}, bf16[64,3584]{1,0:T(8,128)(2,1)S(1)}, u32[]{:S(2)}, u32[]{:S(2)}) collective-permute-start(bf16[64,3584]{1,0:T(8,128)(2,1)S(1)} %get-tuple-element.54), channel_id=1, source_target_pairs={{0,8},{8,16},{16,24},{24,28},{28,20},{20,12},{12,4},{4,0},{1,9},{9... | collective-permute-start | bytes 1376264 | tf_op jit(solution)/shard_map/ppermute | solution.py:176
  35.5 3.4 %collective-permute-done.2 = bf16[64,2048]{1,0:T(8,128)(2,1)S(1)} collective-permute-done((bf16[64,2048]{1,0:T(8,128)(2,1)}, bf16[64,2048]{1,0:T(8,128)(2,1)S(1)}, u32[]{:S(2)}, u32[]{:S(2)}) %collective-permute-start.2) | collective-permute-done | bytes 262176 | tf_op jit(solution)/shard_map/ppermute | solution.py:176
  38.9 1.7 %collective-permute-done.3 = bf16[64,2048]{1,0:T(8,128)(2,1)S(1)} collective-permute-done((bf16[64,2048]{1,0:T(8,128)(2,1)}, bf16[64,2048]{1,0:T(8,128)(2,1)S(1)}, u32[]{:S(2)}, u32[]{:S(2)}) %collective-permute-start.3) | collective-permute-done | bytes 262176 | tf_op jit(solution)/shard_map/ppermute | solution.py:176
  40.6 1.6 %collective-permute-start.6 = (bf16[64,2048]{1,0:T(8,128)(2,1)S(1)}, bf16[64,2048]{1,0:T(8,128)(2,1)S(1)}, u32[]{:S(2)}, u32[]{:S(2)}) collective-permute-start(bf16[64,2048]{1,0:T(8,128)(2,1)S(1)} %collective-permute-done.2), channel_id=1, source_target_pairs={{0,8},{8,16},{16,24},{24,28},{28,20},{20,12},{12,4},{4,0},{1,9},{9... | collective-permute-start | bytes 786440 | tf_op jit(solution)/shard_map/ppermute | solution.py:176
  42.2 0.4 collective-permute-start.7
  42.7 9.6 %collective-permute-done.6 = bf16[64,2048]{1,0:T(8,128)(2,1)S(1)} collective-permute-done((bf16[64,2048]{1,0:T(8,128)(2,1)S(1)}, bf16[64,2048]{1,0:T(8,128)(2,1)S(1)}, u32[]{:S(2)}, u32[]{:S(2)}) %collective-permute-start.6) | collective-permute-done | bytes 262176 | tf_op jit(solution)/shard_map/ppermute | solution.py:176
  52.3 1.4 %collective-permute-done.7 = bf16[64,2048]{1,0:T(8,128)(2,1)S(1)} collective-permute-done((bf16[64,2048]{1,0:T(8,128)(2,1)S(1)}, bf16[64,2048]{1,0:T(8,128)(2,1)S(1)}, u32[]{:S(2)}, u32[]{:S(2)}) %collective-permute-start.7) | collective-permute-done | bytes 262176 | tf_op jit(solution)/shard_map/ppermute | solution.py:176
  53.8 1.6 %collective-permute-start.10 = (bf16[32,2048]{1,0:T(8,128)(2,1)S(1)}, bf16[32,2048]{1,0:T(8,128)(2,1)S(1)}, u32[]{:S(2)}, u32[]{:S(2)}) collective-permute-start(bf16[32,2048]{1,0:T(8,128)(2,1)S(1)} %slice.159), channel_id=1, source_target_pairs={{0,8},{8,16},{16,24},{24,28},{28,20},{20,12},{12,4},{4,0},{1,9},{9... | collective-permute-start | bytes 393224 | tf_op jit(solution)/shard_map/ppermute | solution.py:176
  55.4 0.4 collective-permute-start.11
  55.9 1.6 %collective-permute-start.13 = (bf16[64,3584]{1,0:T(8,128)(2,1)}, bf16[64,3584]{1,0:T(8,128)(2,1)S(1)}, u32[]{:S(2)}, u32[]{:S(2)}) collective-permute-start(bf16[64,3584]{1,0:T(8,128)(2,1)} %collective-permute-done.4), channel_id=1, source_target_pairs={{0,8},{8,16},{16,24},{24,28},{28,20},{20,12},{12,4},{4,0},{1,9},{9... | collective-permute-start | bytes 1376264 | tf_op jit(solution)/shard_map/ppermute | solution.py:176
  57.4 0.4 collective-permute-start.14
  57.9 3.4 %fusion.16 = f32[512,128]{1,0:T(8,128)S(1)} fusion(bf16[512,7168]{1,0:T(8,128)(2,1)} %rotate.3, bf16[64,3584]{1,0:T(8,128)(2,1)} %collective-permute-done.5, bf16[64,3584]{1,0:T(8,128)(2,1)} %collective-permute-done.4), kind=kOutput, calls=%fused_computation.16 | convolution fusion | flops 471597056 | bytes 4849664 | tf_op jit(solution)/shard_map/dot_general | solution.py:100
  61.3 0.6 collective-permute-done.11
  61.9 1.3 %fusion.65 = f32[512,512]{1,0:T(8,128)S(1)} fusion(bf16[512,2048]{1,0:T(8,128)(2,1)S(1)} %rotate.2, bf16[512,2048]{1,0:T(8,128)(2,1)S(1)} %constant_dynamic-update-slice_fusion), kind=kOutput, calls=%fused_computation.117 | convolution fusion | flops 1073741824 | bytes 5242880 | tf_op jit(solution)/shard_map/dot_general | solution.py:100
  63.2 3.8 %collective-permute-done.13 = bf16[64,3584]{1,0:T(8,128)(2,1)S(1)} collective-permute-done((bf16[64,3584]{1,0:T(8,128)(2,1)}, bf16[64,3584]{1,0:T(8,128)(2,1)S(1)}, u32[]{:S(2)}, u32[]{:S(2)}) %collective-permute-start.13) | collective-permute-done | bytes 458784 | tf_op jit(solution)/shard_map/ppermute | solution.py:176
  67.1 1.3 %collective-permute-done.14 = bf16[64,3584]{1,0:T(8,128)(2,1)S(1)} collective-permute-done((bf16[64,3584]{1,0:T(8,128)(2,1)}, bf16[64,3584]{1,0:T(8,128)(2,1)S(1)}, u32[]{:S(2)}, u32[]{:S(2)}) %collective-permute-start.14) | collective-permute-done | bytes 458784 | tf_op jit(solution)/shard_map/ppermute | solution.py:176
  68.4 1.6 %collective-permute-start.15 = (bf16[64,3584]{1,0:T(8,128)(2,1)S(1)}, bf16[64,3584]{1,0:T(8,128)(2,1)S(1)}, u32[]{:S(2)}, u32[]{:S(2)}) collective-permute-start(bf16[64,3584]{1,0:T(8,128)(2,1)S(1)} %collective-permute-done.8), channel_id=1, source_target_pairs={{0,8},{8,16},{16,24},{24,28},{28,20},{20,12},{12,4},{4,0},{1,9},{9... | collective-permute-start | bytes 1376264 | tf_op jit(solution)/shard_map/ppermute | solution.py:176
  69.9 0.4 collective-permute-start.16
  70.4 1.6 %collective-permute-start.18 = (bf16[64,3584]{1,0:T(8,128)(2,1)S(1)}, bf16[64,3584]{1,0:T(8,128)(2,1)S(1)}, u32[]{:S(2)}, u32[]{:S(2)}) collective-permute-start(bf16[64,3584]{1,0:T(8,128)(2,1)S(1)} %collective-permute-done.13), channel_id=1, source_target_pairs={{0,8},{8,16},{16,24},{24,28},{28,20},{20,12},{12,4},{4,0},{1,9},{9... | collective-permute-start | bytes 1376264 | tf_op jit(solution)/shard_map/ppermute | solution.py:176
  72.0 0.4 collective-permute-start.19
  72.5 1.1 fusion.6
  73.7 8.2 %collective-permute-done.15 = bf16[64,3584]{1,0:T(8,128)(2,1)S(1)} collective-permute-done((bf16[64,3584]{1,0:T(8,128)(2,1)S(1)}, bf16[64,3584]{1,0:T(8,128)(2,1)S(1)}, u32[]{:S(2)}, u32[]{:S(2)}) %collective-permute-start.15) | collective-permute-done | bytes 458784 | tf_op jit(solution)/shard_map/ppermute | solution.py:176
  81.8 1.6 %collective-permute-done.16 = bf16[64,3584]{1,0:T(8,128)(2,1)S(1)} collective-permute-done((bf16[64,3584]{1,0:T(8,128)(2,1)S(1)}, bf16[64,3584]{1,0:T(8,128)(2,1)S(1)}, u32[]{:S(2)}, u32[]{:S(2)}) %collective-permute-start.16) | collective-permute-done | bytes 458784 | tf_op jit(solution)/shard_map/ppermute | solution.py:176
  83.4 1.7 %collective-permute-start.21 = (bf16[64,3584]{1,0:T(8,128)(2,1)S(1)}, bf16[64,3584]{1,0:T(8,128)(2,1)S(1)}, u32[]{:S(2)}, u32[]{:S(2)}) collective-permute-start(bf16[64,3584]{1,0:T(8,128)(2,1)S(1)} %collective-permute-done.15), channel_id=1, source_target_pairs={{0,8},{8,16},{16,24},{24,28},{28,20},{20,12},{12,4},{4,0},{1,9},{9... | collective-permute-start | bytes 1376264 | tf_op jit(solution)/shard_map/ppermute | solution.py:176
  85.1 0.3 collective-permute-start.22
  85.4 6.2 %collective-permute-done.18 = bf16[64,3584]{1,0:T(8,128)(2,1)S(1)} collective-permute-done((bf16[64,3584]{1,0:T(8,128)(2,1)S(1)}, bf16[64,3584]{1,0:T(8,128)(2,1)S(1)}, u32[]{:S(2)}, u32[]{:S(2)}) %collective-permute-start.18) | collective-permute-done | bytes 458784 | tf_op jit(solution)/shard_map/ppermute | solution.py:176
  91.7 1.6 %collective-permute-done.19 = bf16[64,3584]{1,0:T(8,128)(2,1)S(1)} collective-permute-done((bf16[64,3584]{1,0:T(8,128)(2,1)S(1)}, bf16[64,3584]{1,0:T(8,128)(2,1)S(1)}, u32[]{:S(2)}, u32[]{:S(2)}) %collective-permute-start.19) | collective-permute-done | bytes 458784 | tf_op jit(solution)/shard_map/ppermute | solution.py:176
  93.2 1.8 %collective-permute-start.23 = (bf16[32,3584]{1,0:T(8,128)(2,1)S(1)}, bf16[32,3584]{1,0:T(8,128)(2,1)S(1)}, u32[]{:S(2)}, u32[]{:S(2)}) collective-permute-start(bf16[32,3584]{1,0:T(8,128)(2,1)S(1)} %slice.186), channel_id=1, source_target_pairs={{0,8},{8,16},{16,24},{24,28},{28,20},{20,12},{12,4},{4,0},{1,9},{9... | collective-permute-start | bytes 688136 | tf_op jit(solution)/shard_map/ppermute | solution.py:176
  95.0 0.3 collective-permute-start.24
  95.4 1.6 %collective-permute-start.17 = (f32[128,512]{1,0:T(8,128)S(1)}, f32[128,512]{1,0:T(8,128)S(1)}, u32[]{:S(2)}, u32[]{:S(2)}) collective-permute-start(f32[128,512]{1,0:T(8,128)S(1)} %dynamic-slice_add_fusion), channel_id=1, source_target_pairs={{0,2},{1,3},{2,0},{3,1},{4,6},{5,7},{6,4},{7,5},{8,10},{9,11},{10,... | collective-permute-start | bytes 786440 | tf_op jit(solution)/shard_map/ppermute | solution.py:115
  97.0 1.1 fusion.14
  98.1 1.1 fusion.4
  99.2 2.6 %collective-permute-done.17 = f32[128,512]{1,0:T(8,128)S(1)} collective-permute-done((f32[128,512]{1,0:T(8,128)S(1)}, f32[128,512]{1,0:T(8,128)S(1)}, u32[]{:S(2)}, u32[]{:S(2)}) %collective-permute-start.17) | collective-permute-done | bytes 262176 | tf_op jit(solution)/shard_map/ppermute | solution.py:115
  102.0 1.8 %collective-permute-start.25 = (bf16[32,3584]{1,0:T(8,128)(2,1)S(1)}, bf16[32,3584]{1,0:T(8,128)(2,1)S(1)}, u32[]{:S(2)}, u32[]{:S(2)}) collective-permute-start(bf16[32,3584]{1,0:T(8,128)(2,1)S(1)} %slice.188), channel_id=1, source_target_pairs={{0,8},{8,16},{16,24},{24,28},{28,20},{20,12},{12,4},{4,0},{1,9},{9... | collective-permute-start | bytes 688136 | tf_op jit(solution)/shard_map/ppermute | solution.py:176
  103.8 0.3 collective-permute-start.26
  104.1 1.1 fusion.12
  105.2 1.1 fusion.2
  106.4 0.3 bitcast_reduce_fusion.1
  106.6 3.4 %collective-permute-done.25 = bf16[32,3584]{1,0:T(8,128)(2,1)S(1)} collective-permute-done((bf16[32,3584]{1,0:T(8,128)(2,1)S(1)}, bf16[32,3584]{1,0:T(8,128)(2,1)S(1)}, u32[]{:S(2)}, u32[]{:S(2)}) %collective-permute-start.25) | collective-permute-done | bytes 229408 | tf_op jit(solution)/shard_map/ppermute | solution.py:176
  110.0 1.5 %collective-permute-done.26 = bf16[32,3584]{1,0:T(8,128)(2,1)S(1)} collective-permute-done((bf16[32,3584]{1,0:T(8,128)(2,1)S(1)}, bf16[32,3584]{1,0:T(8,128)(2,1)S(1)}, u32[]{:S(2)}, u32[]{:S(2)}) %collective-permute-start.26) | collective-permute-done | bytes 229408 | tf_op jit(solution)/shard_map/ppermute | solution.py:176
  111.5 1.1 fusion.10
  112.6 1.1 fusion
  114.1 0.5 collective-permute-start.29
  114.6 1.1 collective-permute-start.28
  115.6 0.3 collective-permute-start.27
  115.9 1.1 collective-permute-done.29
  117.1 1.1 collective-permute-done.28
  118.1 0.6 add_add_fusion
  (71 shorter events, 1.8 us)
Async XLA Ops:
  0.0 1.6 %copy-start.1 = (bf16[1,512,2048]{2,1,0:T(8,128)(2,1)S(1)}, bf16[1,512,2048]{2,1,0:T(8,128)(2,1)}, u32[]{:S(2)}) copy-start(bf16[1,512,2048]{2,1,0:T(8,128)(2,1)} %left_ref.1) | copy-start | bytes 6291460
  1.6 0.7 copy-start.3
  2.2 7.3 %copy-start.4 = (s32[16]{0:T(128)S(1)}, s32[16]{0:T(128)}, u32[]{:S(2)}) copy-start(s32[16]{0:T(128)} %owners_ref.1) | copy-start | bytes 196
  4.4 25.0 %collective-permute-start.1 = (bf16[64,2048]{1,0:T(8,128)(2,1)S(1)}, bf16[64,2048]{1,0:T(8,128)(2,1)}, u32[]{:S(2)}, u32[]{:S(2)}) collective-permute-start(bf16[64,2048]{1,0:T(8,128)(2,1)S(1)} %get-tuple-element.46), channel_id=1, source_target_pairs={{8,0},{16,8},{24,16},{28,24},{20,28},{12,20},{4,12},{0,4},{9,1},{1... | collective-permute-start | bytes 786440 | tf_op jit(solution)/shard_map/ppermute | solution.py:176
  7.4 22.0 %collective-permute-start = (bf16[64,2048]{1,0:T(8,128)(2,1)S(1)}, bf16[64,2048]{1,0:T(8,128)(2,1)}, u32[]{:S(2)}, u32[]{:S(2)}) collective-permute-start(bf16[64,2048]{1,0:T(8,128)(2,1)S(1)} %get-tuple-element.46), channel_id=1, source_target_pairs={{0,8},{8,16},{16,24},{24,28},{28,20},{20,12},{12,4},{4,0},{1,9},{9... | collective-permute-start | bytes 786440 | tf_op jit(solution)/shard_map/ppermute | solution.py:176
  7.5 25.9 %collective-permute-start.5 = (bf16[64,3584]{1,0:T(8,128)(2,1)S(1)}, bf16[64,3584]{1,0:T(8,128)(2,1)}, u32[]{:S(2)}, u32[]{:S(2)}) collective-permute-start(bf16[64,3584]{1,0:T(8,128)(2,1)S(1)} %get-tuple-element.49), channel_id=1, source_target_pairs={{8,0},{16,8},{24,16},{28,24},{20,28},{12,20},{4,12},{0,4},{9,1},{1... | collective-permute-start | bytes 1376264 | tf_op jit(solution)/shard_map/ppermute | solution.py:176
  9.4 24.0 %collective-permute-start.4 = (bf16[64,3584]{1,0:T(8,128)(2,1)S(1)}, bf16[64,3584]{1,0:T(8,128)(2,1)}, u32[]{:S(2)}, u32[]{:S(2)}) collective-permute-start(bf16[64,3584]{1,0:T(8,128)(2,1)S(1)} %get-tuple-element.49), channel_id=1, source_target_pairs={{0,8},{8,16},{16,24},{24,28},{28,20},{20,12},{12,4},{4,0},{1,9},{9... | collective-permute-start | bytes 1376264 | tf_op jit(solution)/shard_map/ppermute | solution.py:176
  10.6 2.0 %copy-start = (bf16[256,7168]{1,0:T(8,128)(2,1)S(1)}, bf16[256,7168]{1,0:T(8,128)(2,1)}, u32[]{:S(2)}) copy-start(bf16[256,7168]{1,0:T(8,128)(2,1)} %matrix_ref.3) | copy-start | bytes 11010052
  20.4 4.2 %copy-start.5 = (bf16[512,7168]{1,0:T(8,128)(2,1)S(1)}, bf16[512,7168]{1,0:T(8,128)(2,1)}, u32[]{:S(2)}) copy-start(bf16[512,7168]{1,0:T(8,128)(2,1)} %rotate.3) | copy-start | bytes 22020100
  24.6 2.6 %copy-start.2 = (bf16[4,512,512]{2,1,0:T(8,128)(2,1)S(1)}, bf16[4,512,512]{2,1,0:T(8,128)(2,1)}, u32[]{:S(2)}) copy-start(bf16[4,512,512]{2,1,0:T(8,128)(2,1)} %basis_ref.2) | copy-start | bytes 6291460
  29.4 9.5 %collective-permute-start.2 = (bf16[64,2048]{1,0:T(8,128)(2,1)}, bf16[64,2048]{1,0:T(8,128)(2,1)S(1)}, u32[]{:S(2)}, u32[]{:S(2)}) collective-permute-start(bf16[64,2048]{1,0:T(8,128)(2,1)} %collective-permute-done), channel_id=1, source_target_pairs={{0,8},{8,16},{16,24},{24,28},{28,20},{20,12},{12,4},{4,0},{1,9},{9... | collective-permute-start | bytes 786440 | tf_op jit(solution)/shard_map/ppermute | solution.py:176
  31.4 9.2 %collective-permute-start.3 = (bf16[64,2048]{1,0:T(8,128)(2,1)}, bf16[64,2048]{1,0:T(8,128)(2,1)S(1)}, u32[]{:S(2)}, u32[]{:S(2)}) collective-permute-start(bf16[64,2048]{1,0:T(8,128)(2,1)} %collective-permute-done.1), channel_id=1, source_target_pairs={{8,0},{16,8},{24,16},{28,24},{20,28},{12,20},{4,12},{0,4},{9,1},{1... | collective-permute-start | bytes 786440 | tf_op jit(solution)/shard_map/ppermute | solution.py:176
  33.4 20.3 %collective-permute-start.8 = (bf16[64,3584]{1,0:T(8,128)(2,1)S(1)}, bf16[64,3584]{1,0:T(8,128)(2,1)S(1)}, u32[]{:S(2)}, u32[]{:S(2)}) collective-permute-start(bf16[64,3584]{1,0:T(8,128)(2,1)S(1)} %get-tuple-element.54), channel_id=1, source_target_pairs={{0,8},{8,16},{16,24},{24,28},{28,20},{20,12},{12,4},{4,0},{1,9},{9... | collective-permute-start | bytes 1376264 | tf_op jit(solution)/shard_map/ppermute | solution.py:176
  35.4 18.3 %collective-permute-start.9 = (bf16[64,3584]{1,0:T(8,128)(2,1)S(1)}, bf16[64,3584]{1,0:T(8,128)(2,1)S(1)}, u32[]{:S(2)}, u32[]{:S(2)}) collective-permute-start(bf16[64,3584]{1,0:T(8,128)(2,1)S(1)} %get-tuple-element.54), channel_id=1, source_target_pairs={{8,0},{16,8},{24,16},{28,24},{20,28},{12,20},{4,12},{0,4},{9,1},{1... | collective-permute-start | bytes 1376264 | tf_op jit(solution)/shard_map/ppermute | solution.py:176
  40.6 11.7 %collective-permute-start.6 = (bf16[64,2048]{1,0:T(8,128)(2,1)S(1)}, bf16[64,2048]{1,0:T(8,128)(2,1)S(1)}, u32[]{:S(2)}, u32[]{:S(2)}) collective-permute-start(bf16[64,2048]{1,0:T(8,128)(2,1)S(1)} %collective-permute-done.2), channel_id=1, source_target_pairs={{0,8},{8,16},{16,24},{24,28},{28,20},{20,12},{12,4},{4,0},{1,9},{9... | collective-permute-start | bytes 786440 | tf_op jit(solution)/shard_map/ppermute | solution.py:176
  42.2 11.5 %collective-permute-start.7 = (bf16[64,2048]{1,0:T(8,128)(2,1)S(1)}, bf16[64,2048]{1,0:T(8,128)(2,1)S(1)}, u32[]{:S(2)}, u32[]{:S(2)}) collective-permute-start(bf16[64,2048]{1,0:T(8,128)(2,1)S(1)} %collective-permute-done.3), channel_id=1, source_target_pairs={{8,0},{16,8},{24,16},{28,24},{20,28},{12,20},{4,12},{0,4},{9,1},{1... | collective-permute-start | bytes 786440 | tf_op jit(solution)/shard_map/ppermute | solution.py:176
  53.8 7.5 %collective-permute-start.10 = (bf16[32,2048]{1,0:T(8,128)(2,1)S(1)}, bf16[32,2048]{1,0:T(8,128)(2,1)S(1)}, u32[]{:S(2)}, u32[]{:S(2)}) collective-permute-start(bf16[32,2048]{1,0:T(8,128)(2,1)S(1)} %slice.159), channel_id=1, source_target_pairs={{0,8},{8,16},{16,24},{24,28},{28,20},{20,12},{12,4},{4,0},{1,9},{9... | collective-permute-start | bytes 393224 | tf_op jit(solution)/shard_map/ppermute | solution.py:176
  55.4 6.4 %collective-permute-start.11 = (bf16[32,2048]{1,0:T(8,128)(2,1)S(1)}, bf16[32,2048]{1,0:T(8,128)(2,1)S(1)}, u32[]{:S(2)}, u32[]{:S(2)}) collective-permute-start(bf16[32,2048]{1,0:T(8,128)(2,1)S(1)} %slice.160), channel_id=1, source_target_pairs={{8,0},{16,8},{24,16},{28,24},{20,28},{12,20},{4,12},{0,4},{9,1},{1... | collective-permute-start | bytes 393224 | tf_op jit(solution)/shard_map/ppermute | solution.py:176
  55.9 11.2 %collective-permute-start.13 = (bf16[64,3584]{1,0:T(8,128)(2,1)}, bf16[64,3584]{1,0:T(8,128)(2,1)S(1)}, u32[]{:S(2)}, u32[]{:S(2)}) collective-permute-start(bf16[64,3584]{1,0:T(8,128)(2,1)} %collective-permute-done.4), channel_id=1, source_target_pairs={{0,8},{8,16},{16,24},{24,28},{28,20},{20,12},{12,4},{4,0},{1,9},{9... | collective-permute-start | bytes 1376264 | tf_op jit(solution)/shard_map/ppermute | solution.py:176
  57.4 10.9 %collective-permute-start.14 = (bf16[64,3584]{1,0:T(8,128)(2,1)}, bf16[64,3584]{1,0:T(8,128)(2,1)S(1)}, u32[]{:S(2)}, u32[]{:S(2)}) collective-permute-start(bf16[64,3584]{1,0:T(8,128)(2,1)} %collective-permute-done.5), channel_id=1, source_target_pairs={{8,0},{16,8},{24,16},{28,24},{20,28},{12,20},{4,12},{0,4},{9,1},{1... | collective-permute-start | bytes 1376264 | tf_op jit(solution)/shard_map/ppermute | solution.py:176
  61.3 11.3 %slice-start = ((s8[7340032]{0:T(1024)(128)(4,1)}), s8[4194304]{0:T(1024)(128)(4,1)S(1)}, s32[]{:S(2)}) async-start(s8[7340032]{0:T(1024)(128)(4,1)} %bitcast.15), calls=%async_computation | async-start | bytes 8388608
  61.9 10.7 %slice-start.1 = ((s8[7340032]{0:T(1024)(128)(4,1)}), s8[3145728]{0:T(1024)(128)(4,1)S(1)}, s32[]{:S(2)}) async-start(s8[7340032]{0:T(1024)(128)(4,1)} %bitcast.15), calls=%async_computation.1 | async-start | bytes 6291456
  68.4 13.5 %collective-permute-start.15 = (bf16[64,3584]{1,0:T(8,128)(2,1)S(1)}, bf16[64,3584]{1,0:T(8,128)(2,1)S(1)}, u32[]{:S(2)}, u32[]{:S(2)}) collective-permute-start(bf16[64,3584]{1,0:T(8,128)(2,1)S(1)} %collective-permute-done.8), channel_id=1, source_target_pairs={{0,8},{8,16},{16,24},{24,28},{28,20},{20,12},{12,4},{4,0},{1,9},{9... | collective-permute-start | bytes 1376264 | tf_op jit(solution)/shard_map/ppermute | solution.py:176
  69.9 13.5 %collective-permute-start.16 = (bf16[64,3584]{1,0:T(8,128)(2,1)S(1)}, bf16[64,3584]{1,0:T(8,128)(2,1)S(1)}, u32[]{:S(2)}, u32[]{:S(2)}) collective-permute-start(bf16[64,3584]{1,0:T(8,128)(2,1)S(1)} %collective-permute-done.9), channel_id=1, source_target_pairs={{8,0},{16,8},{24,16},{28,24},{20,28},{12,20},{4,12},{0,4},{9,1},{1... | collective-permute-start | bytes 1376264 | tf_op jit(solution)/shard_map/ppermute | solution.py:176
  70.4 21.3 %collective-permute-start.18 = (bf16[64,3584]{1,0:T(8,128)(2,1)S(1)}, bf16[64,3584]{1,0:T(8,128)(2,1)S(1)}, u32[]{:S(2)}, u32[]{:S(2)}) collective-permute-start(bf16[64,3584]{1,0:T(8,128)(2,1)S(1)} %collective-permute-done.13), channel_id=1, source_target_pairs={{0,8},{8,16},{16,24},{24,28},{28,20},{20,12},{12,4},{4,0},{1,9},{9... | collective-permute-start | bytes 1376264 | tf_op jit(solution)/shard_map/ppermute | solution.py:176
  72.0 21.3 %collective-permute-start.19 = (bf16[64,3584]{1,0:T(8,128)(2,1)S(1)}, bf16[64,3584]{1,0:T(8,128)(2,1)S(1)}, u32[]{:S(2)}, u32[]{:S(2)}) collective-permute-start(bf16[64,3584]{1,0:T(8,128)(2,1)S(1)} %collective-permute-done.14), channel_id=1, source_target_pairs={{8,0},{16,8},{24,16},{28,24},{20,28},{12,20},{4,12},{0,4},{9,1},{1... | collective-permute-start | bytes 1376264 | tf_op jit(solution)/shard_map/ppermute | solution.py:176
  72.4 22.9 %collective-permute-start.12 = (f32[128,512]{1,0:T(8,128)S(1)}, f32[128,512]{1,0:T(8,128)S(1)}, u32[]{:S(2)}, u32[]{:S(2)}) collective-permute-start(f32[128,512]{1,0:T(8,128)S(1)} %constant_dynamic-slice_fusion), channel_id=1, source_target_pairs={{0,1},{1,0},{2,3},{3,2},{4,5},{5,4},{6,7},{7,6},{8,9},{9,8},{10,11... | collective-permute-start | bytes 786440 | tf_op jit(solution)/shard_map/ppermute | solution.py:115
  83.4 18.5 %collective-permute-start.21 = (bf16[64,3584]{1,0:T(8,128)(2,1)S(1)}, bf16[64,3584]{1,0:T(8,128)(2,1)S(1)}, u32[]{:S(2)}, u32[]{:S(2)}) collective-permute-start(bf16[64,3584]{1,0:T(8,128)(2,1)S(1)} %collective-permute-done.15), channel_id=1, source_target_pairs={{0,8},{8,16},{16,24},{24,28},{28,20},{20,12},{12,4},{4,0},{1,9},{9... | collective-permute-start | bytes 1376264 | tf_op jit(solution)/shard_map/ppermute | solution.py:176
  85.1 16.8 %collective-permute-start.22 = (bf16[64,3584]{1,0:T(8,128)(2,1)S(1)}, bf16[64,3584]{1,0:T(8,128)(2,1)S(1)}, u32[]{:S(2)}, u32[]{:S(2)}) collective-permute-start(bf16[64,3584]{1,0:T(8,128)(2,1)S(1)} %collective-permute-done.16), channel_id=1, source_target_pairs={{8,0},{16,8},{24,16},{28,24},{20,28},{12,20},{4,12},{0,4},{9,1},{1... | collective-permute-start | bytes 1376264 | tf_op jit(solution)/shard_map/ppermute | solution.py:176
  93.2 13.4 %collective-permute-start.23 = (bf16[32,3584]{1,0:T(8,128)(2,1)S(1)}, bf16[32,3584]{1,0:T(8,128)(2,1)S(1)}, u32[]{:S(2)}, u32[]{:S(2)}) collective-permute-start(bf16[32,3584]{1,0:T(8,128)(2,1)S(1)} %slice.186), channel_id=1, source_target_pairs={{0,8},{8,16},{16,24},{24,28},{28,20},{20,12},{12,4},{4,0},{1,9},{9... | collective-permute-start | bytes 688136 | tf_op jit(solution)/shard_map/ppermute | solution.py:176
  95.0 11.6 %collective-permute-start.24 = (bf16[32,3584]{1,0:T(8,128)(2,1)S(1)}, bf16[32,3584]{1,0:T(8,128)(2,1)S(1)}, u32[]{:S(2)}, u32[]{:S(2)}) collective-permute-start(bf16[32,3584]{1,0:T(8,128)(2,1)S(1)} %slice.187), channel_id=1, source_target_pairs={{8,0},{16,8},{24,16},{28,24},{20,28},{12,20},{4,12},{0,4},{9,1},{1... | collective-permute-start | bytes 688136 | tf_op jit(solution)/shard_map/ppermute | solution.py:176
  95.4 6.4 %collective-permute-start.17 = (f32[128,512]{1,0:T(8,128)S(1)}, f32[128,512]{1,0:T(8,128)S(1)}, u32[]{:S(2)}, u32[]{:S(2)}) collective-permute-start(f32[128,512]{1,0:T(8,128)S(1)} %dynamic-slice_add_fusion), channel_id=1, source_target_pairs={{0,2},{1,3},{2,0},{3,1},{4,6},{5,7},{6,4},{7,5},{8,10},{9,11},{10,... | collective-permute-start | bytes 786440 | tf_op jit(solution)/shard_map/ppermute | solution.py:115
  101.8 4.4 %collective-permute-start.20 = (f32[128,512]{1,0:T(8,128)S(1)}, f32[128,512]{1,0:T(8,128)S(1)}, u32[]{:S(2)}, u32[]{:S(2)}) collective-permute-start(f32[128,512]{1,0:T(8,128)S(1)} %add.175), channel_id=1, source_target_pairs={{0,1},{1,0},{2,3},{3,2},{4,5},{5,4},{6,7},{7,6},{8,9},{9,8},{10,11... | collective-permute-start | bytes 786440 | tf_op jit(solution)/shard_map/ppermute | solution.py:115
  102.0 8.0 %collective-permute-start.25 = (bf16[32,3584]{1,0:T(8,128)(2,1)S(1)}, bf16[32,3584]{1,0:T(8,128)(2,1)S(1)}, u32[]{:S(2)}, u32[]{:S(2)}) collective-permute-start(bf16[32,3584]{1,0:T(8,128)(2,1)S(1)} %slice.188), channel_id=1, source_target_pairs={{0,8},{8,16},{16,24},{24,28},{28,20},{20,12},{12,4},{4,0},{1,9},{9... | collective-permute-start | bytes 688136 | tf_op jit(solution)/shard_map/ppermute | solution.py:176
  103.8 7.7 %collective-permute-start.26 = (bf16[32,3584]{1,0:T(8,128)(2,1)S(1)}, bf16[32,3584]{1,0:T(8,128)(2,1)S(1)}, u32[]{:S(2)}, u32[]{:S(2)}) collective-permute-start(bf16[32,3584]{1,0:T(8,128)(2,1)S(1)} %slice.189), channel_id=1, source_target_pairs={{8,0},{16,8},{24,16},{28,24},{20,28},{12,20},{4,12},{0,4},{9,1},{1... | collective-permute-start | bytes 688136 | tf_op jit(solution)/shard_map/ppermute | solution.py:176
  112.6 1.1 copy-start.6
  114.1 3.0 %collective-permute-start.29 = (f32[2,16]{1,0:T(2,128)S(1)}, f32[2,16]{1,0:T(2,128)S(1)}, u32[]{:S(2)}, u32[]{:S(2)}) collective-permute-start(f32[2,16]{1,0:T(2,128)S(1)} %select_reduce_fusion), channel_id=1, source_target_pairs={{0,3},{1,2},{2,1},{3,0},{4,7},{5,6},{6,5},{7,4},{8,11},{9,10},{10,... | collective-permute-start | bytes 392 | tf_op jit(solution)/shard_map/ppermute | solution.py:115
  114.6 3.6 %collective-permute-start.28 = (f32[2,16]{1,0:T(2,128)S(1)}, f32[2,16]{1,0:T(2,128)S(1)}, u32[]{:S(2)}, u32[]{:S(2)}) collective-permute-start(f32[2,16]{1,0:T(2,128)S(1)} %select_reduce_fusion), channel_id=1, source_target_pairs={{0,2},{1,3},{2,0},{3,1},{4,6},{5,7},{6,4},{7,5},{8,10},{9,11},{10,... | collective-permute-start | bytes 392 | tf_op jit(solution)/shard_map/ppermute | solution.py:115
  115.6 2.5 %collective-permute-start.27 = (f32[2,16]{1,0:T(2,128)S(1)}, f32[2,16]{1,0:T(2,128)S(1)}, u32[]{:S(2)}, u32[]{:S(2)}) collective-permute-start(f32[2,16]{1,0:T(2,128)S(1)} %select_reduce_fusion), channel_id=1, source_target_pairs={{0,1},{1,0},{2,3},{3,2},{4,5},{5,4},{6,7},{7,6},{8,9},{9,8},{10,11... | collective-permute-start | bytes 392 | tf_op jit(solution)/shard_map/ppermute | solution.py:115

commit v4 on v3

--- a/solution.py
+++ b/solution.py
@@ -17,9 +17,10 @@
 def pick_rows(groups, owners, left_store, right_store):
     per = NQ // groups
     width_left = left_store.shape[2]
-    half = right_store.shape[2] // 2
-
-    def kernel(owners_ref, left_ref, right_ref, left_out, first_out, second_out, sems):
+    width_right = right_store.shape[2]
+    cut = max(width_right // 4 // 256 * 256, 128)
+
+    def kernel(owners_ref, left_ref, right_ref, first_out, second_out, sems):
         group = lax.axis_index("dp")
         found = jnp.int32(0)
         queries = [jnp.int32(0)] * per
@@ -32,9 +33,9 @@
             rows = pl.ds(pl.multiple_of(queries[i] * R, R), R)
             here = pl.ds(i * R, R)
             pairs = [
-                (left_ref.at[0, rows, :], left_out.at[here, :]),
-                (right_ref.at[0, rows, pl.ds(0, half)], first_out.at[here, :]),
-                (right_ref.at[0, rows, pl.ds(half, half)], second_out.at[here, :]),
+                (left_ref.at[0, rows, :], first_out.at[here, pl.ds(0, width_left)]),
+                (right_ref.at[0, rows, pl.ds(0, cut)], first_out.at[here, pl.ds(width_left, cut)]),
+                (right_ref.at[0, rows, pl.ds(cut, width_right - cut)], second_out.at[here, :]),
             ]
             for j, (source, target) in enumerate(pairs):
                 copies.append(pltpu.make_async_copy(source, target, sems.at[i, j]))
@@ -44,12 +45,12 @@
             copy.wait()
 
     shape = lambda width: jax.ShapeDtypeStruct((per * R, width), jnp.bfloat16)
-    anywhere = pl.BlockSpec(memory_space=pl.ANY)
+    in_hbm = pl.BlockSpec(memory_space=pltpu.HBM)
     return pl.pallas_call(
         kernel,
-        out_shape=(shape(width_left), shape(half), shape(half)),
-        in_specs=[pl.BlockSpec(memory_space=pltpu.SMEM), anywhere, anywhere],
-        out_specs=(anywhere, anywhere, anywhere),
+        out_shape=(shape(width_left + cut), shape(width_right - cut)),
+        in_specs=[pl.BlockSpec(memory_space=pltpu.SMEM), in_hbm, in_hbm],
+        out_specs=(in_hbm, in_hbm),
         scratch_shapes=[pltpu.SemaphoreType.DMA((per, 3))],
         compiler_params=params(),
         name="pick_rows",
@@ -159,43 +160,41 @@
     reach = groups // 2
 
     own = pick_rows(groups, owners, left_store, right_store)
-    half = own[1].shape[1]
-
-    order = [(0, 1), (1, 1)]
-    for hops in range(2, reach + 1):
-        order += [(0, hops), (2, hops // 2) if hops % 2 == 0 else (1, hops // 2 + 1)]
+    width_left = left_store.shape[2]
+    cut = own[0].shape[1] - width_left
+
+    across = lax.ppermute(
+        own[0][:, :width_left], "dp", [(ring[i], ring[i - reach]) for i in range(groups)]
+    )
+    steps = [[], []]
+    came = []
     for hops in range(1, reach + 1):
-        order += [(piece, hops) for piece in (1, 2) if (piece, hops) not in order]
-    steps = [[], [], []]
-    came = []
-    for piece, hops in order:
-        ahead, behind = steps[piece][-1] if hops > 1 else (own[piece], own[piece])
-        if hops == reach:
-            ahead, behind = ahead[: chunk // 2], behind[chunk // 2 :]
-        ahead, behind = after((ahead, behind), came[-3:-1])
-        got = (lax.ppermute(ahead, "dp", forward), lax.ppermute(behind, "dp", backward))
-        steps[piece].append(got)
-        came.append(got)
+        for piece in range(2):
+            ahead, behind = steps[piece][-1] if hops > 1 else (own[piece], own[piece])
+            if hops == reach:
+                base = width_left if piece == 0 else 0
+                ahead, behind = ahead[: chunk // 2, base:], behind[chunk // 2 :, base:]
+            ahead, behind = after((ahead, behind), came[-3:-1])
+            got = (lax.ppermute(ahead, "dp", forward), lax.ppermute(behind, "dp", backward))
+            steps[piece].append(got)
+            came.append(got)
 
     grads = rotate(out_grads, out_basis, shard)
     acts = rotate(hidden_acts, in_basis, 0)
 
-    left_fac = jnp.concatenate([own[0]] + [piece for step in steps[0] for piece in step], axis=0)
+    steps[0][-1], steps[1][-1] = lax.optimization_barrier((steps[0][-1], steps[1][-1]))
+    first = [own[0]] + [jnp.concatenate(pair, axis=0) for pair in steps[0]]
+    second = [own[1]] + [jnp.concatenate(pair, axis=0) for pair in steps[1]]
+    left_fac = [piece[:, :width_left] for piece in first[:-1]] + [across]
     coefficient = sum_over_shards(
-        contract_rows(grads, left_fac), shards, came[order.index((0, reach)) + 1 :]
+        contract_rows(grads, jnp.concatenate(left_fac, axis=0)), shards, [came[-3]]
     )
 
     parts = []
     at = 0
     for step in range(reach + 1):
-        projected = 0.0
-        if step == 0:
-            factors = own[1:]
-        else:
-            factors = lax.optimization_barrier((steps[1][step - 1], steps[2][step - 1]))
-            factors = [jnp.concatenate(pair, axis=0) for pair in factors]
-        for part, factor in enumerate(factors):
-            projected += contract_rows(acts[:, part * half : (part + 1) * half], factor)
+        projected = contract_rows(acts[:, :cut], first[step][:, -cut:])
+        projected += contract_rows(acts[:, cut:], second[step])
         width = projected.shape[1]
         terms = coefficient[:, at : at + width] * projected
         parts.append(jnp.sum(terms.reshape(-1, LEN, width), axis=1))

time: 119 us -> 114 us (0.958)
  waiting for transfers between devices: 49.1 us -> 33.8 us
  starting transfers between devices: 29.3 us -> 39.6 us
  local copies, waits for them, and re-layouts: 7.68 us -> 10.3 us
  matrix products: 17.4 us -> 16 us
  other arithmetic: 2.82 us -> 1.54 us
    ppermute x12 -> x8, waiting for transfers between devices: 9.59 us -> 0.88 us  [on_device(): lax.ppermute(behind, 'dp', backward)]
    ppermute x12 -> x8, waiting for transfers between devices: 34.6 us -> 27.2 us  [on_device(): lax.ppermute(ahead, 'dp', forward)]
    ppermute x12 -> x8, starting transfers between devices: 17.6 us -> 24.2 us  [on_device(): lax.ppermute(ahead, 'dp', forward)]
    ppermute x0 -> x1, starting transfers between devices: none -> 4.91 us  [on_device(): lax.ppermute(own[0][:, :width_left], 'dp', [(ring[i], ring[i - reach]) fo...]
    concatenate x1 -> x4, local copies, waits for them, and re-layouts: 0.01 us -> 2.25 us  [the longest x3 1.28 us: on_device(): first = [own[0]] + [jnp.concatenate(pair, axis=0) for pair in steps[0]]]
    dot_general x11, matrix products: 17.4 us -> 16 us  [contract_rows(): lax.dot_general(both, second, (((1,), (1,)), ((), ())), preferred_element...]
    ppermute x12 -> x8, starting transfers between devices: 8.08 us -> 6.89 us  [on_device(): lax.ppermute(behind, 'dp', backward)]
    unnamed x26 -> x22, local copies, waits for them, and re-layouts: 7.26 us -> 6.89 us
  transfers between devices with their start and end apart: 30 -> 23, of which waited for: 16 -> 8; matrix products, arithmetic and copies ran while one was open for 17% -> 18% of each run, Pallas kernels for 8% -> 9%
where the time goes in v4:
time: 114 us; the launch traced here: 113 us
  starting transfers between devices  39.6 us (35%)
  waiting for transfers between devices  33.8 us (30%)
  matrix products  16 us (14%)
  Pallas kernels  11.9 us (10%)
  local copies, waits for them, and re-layouts  10.3 us (9%)
  other arithmetic  1.54 us (1%)
    ppermute x8, waiting for transfers between devices, on_device(): lax.ppermute(ahead, 'dp', forward)  27.2 us
    ppermute x8, starting transfers between devices, on_device(): lax.ppermute(ahead, 'dp', forward)  24.2 us
    dot_general x11, matrix products, contract_rows(): lax.dot_general(both, second, (((1,), (1,)), ((), ())), preferred_element...  16 us
    pallas_call x2, Pallas kernels, rotate(): pl.pallas_call(kernel, out_shape=jax.ShapeDtypeStruct((2 * rows, total),...  10 us
    ppermute x8, starting transfers between devices, on_device(): lax.ppermute(behind, 'dp', backward)  6.89 us
    unnamed x22, local copies, waits for them, and re-layouts  6.89 us
    ppermute x6, waiting for transfers between devices, swapped(): return lax.ppermute(piece, 'mp', [(i, i ^ distance) for i in range(shards)])  5.73 us
    ppermute x1, starting transfers between devices, on_device(): lax.ppermute(own[0][:, :width_left], 'dp', [(ring[i], ring[i - reach]) fo...  4.91 us
  transfers between devices with their start and end apart: 23, of which 8 were waited for; matrix products, arithmetic and copies ran while one was open for 18% of the time, Pallas kernels for 9%

profile of v4, /device:TPU:0, one launch (start us, length us, event | category | flops | bytes accessed | tf_op | source)
XLA Modules:
  0.0 113.5 jit_solution(13575366273826706770)
XLA Ops:
  0.0 1.6 %copy-done.1 = bf16[1,512,2048]{2,1,0:T(8,128)(2,1)S(1)} copy-done((bf16[1,512,2048]{2,1,0:T(8,128)(2,1)S(1)}, bf16[1,512,2048]{2,1,0:T(8,128)(2,1)}, u32[]{:S(2)}) %copy-start.1) | copy-done | bytes 2097176
  1.6 0.7 copy-done.3
  2.2 1.9 %pick_rows.1 = (bf16[64,3840]{1,0:T(8,128)(2,1)S(1)}, bf16[64,5376]{1,0:T(8,128)(2,1)S(1)}) custom-call(s32[16]{0:T(128)S(1)} %copy-done.3, bf16[1,512,2048]{2,1,0:T(8,128)(2,1)S(1)} %copy-done.1, bf16[1,512,7168]{2,1,0:T(8,128)(2,1)} %right_ref.1), custom_call_target="tpu_custom_call" | custom-call | tf_op jit(solution)/shard_map/pick_rows/pallas_call | solution.py:49
  4.2 3.0 %collective-permute-start.1 = (bf16[64,3840]{1,0:T(8,128)(2,1)S(1)}, bf16[64,3840]{1,0:T(8,128)(2,1)}, u32[]{:S(2)}, u32[]{:S(2)}) collective-permute-start(bf16[64,3840]{1,0:T(8,128)(2,1)S(1)} %get-tuple-element.24), channel_id=1, source_target_pairs={{8,0},{16,8},{24,16},{28,24},{20,28},{12,20},{4,12},{0,4},{9,1},{1... | collective-permute-start | bytes 1474568 | tf_op jit(solution)/shard_map/ppermute | solution.py:178
  7.1 0.2 collective-permute-start
  7.3 1.9 %collective-permute-start.5 = (bf16[64,5376]{1,0:T(8,128)(2,1)S(1)}, bf16[64,5376]{1,0:T(8,128)(2,1)}, u32[]{:S(2)}, u32[]{:S(2)}) collective-permute-start(bf16[64,5376]{1,0:T(8,128)(2,1)S(1)} %get-tuple-element.27), channel_id=1, source_target_pairs={{8,0},{16,8},{24,16},{28,24},{20,28},{12,20},{4,12},{0,4},{9,1},{1... | collective-permute-start | bytes 2064392 | tf_op jit(solution)/shard_map/ppermute | solution.py:178
  9.2 0.2 collective-permute-start.4
  9.3 0.7 fusion.57
  10.1 4.9 %collective-permute-start.8 = (bf16[64,2048]{1,0:T(8,128)(2,1)S(1)}, bf16[64,2048]{1,0:T(8,128)(2,1)}, u32[]{:S(2)}, u32[]{:S(2)}) collective-permute-start(bf16[64,2048]{1,0:T(8,128)(2,1)S(1)} %get-tuple-element.48), channel_id=1, source_target_pairs={{0,28},{8,20},{16,12},{24,4},{28,0},{20,8},{12,16},{4,24},{1,29},{... | collective-permute-start | bytes 786440 | tf_op jit(solution)/shard_map/ppermute | solution.py:166
  15.0 0.2 convert_reduce_fusion
  15.3 0.1 concatenate.57
  15.4 0.1 concatenate.58
  15.5 2.0 %copy-done = bf16[256,7168]{1,0:T(8,128)(2,1)S(1)} copy-done((bf16[256,7168]{1,0:T(8,128)(2,1)S(1)}, bf16[256,7168]{1,0:T(8,128)(2,1)}, u32[]{:S(2)}) %copy-start) | copy-done | bytes 3670040
  17.5 7.7 %rotate.3 = bf16[512,7168]{1,0:T(8,128)(2,1)} custom-call(s32[1]{0:T(128)} %constant.123.clone.1.shard_ref, bf16[256,7168]{1,0:T(8,128)(2,1)S(1)} %copy-done, bf16[28,256,256]{2,1,0:T(8,128)(2,1)} %basis_ref.3), custom_call_target="tpu_custom_call" | custom-call | flops 939524096 | bytes 14680064 | tf_op jit(solution)/shard_map/rotate/pallas_call | solution.py:77
  25.3 3.0 %fusion.27 = f32[512,64]{1,0:T(8,128)} fusion(bf16[512,7168]{1,0:T(8,128)(2,1)} %rotate.3, bf16[64,3840]{1,0:T(8,128)(2,1)S(1)} %get-tuple-element.24), kind=kOutput, calls=%fused_computation.27 | convolution fusion | flops 117440512 | bytes 2195456 | tf_op jit(solution)/shard_map/dot_general | solution.py:101
  28.3 2.2 %rotate.2 = bf16[512,2048]{1,0:T(8,128)(2,1)S(1)} custom-call(s32[1]{0:T(128)} %bitcast.shard_ref, bf16[256,8192]{1,0:T(8,128)(2,1)} %matrix_ref.2, bf16[4,512,512]{2,1,0:T(8,128)(2,1)S(1)} %copy-done.2), custom_call_target="tpu_custom_call" | custom-call | flops 536870912 | bytes 5242880 | tf_op jit(solution)/shard_map/rotate/pallas_call | solution.py:77
  30.5 0.1 compare_and_fusion
  30.6 1.1 copy-done.5
  31.7 1.6 %fusion.8 = f32[512,64]{1,0:T(8,128)S(1)} fusion(bf16[64,5376]{1,0:T(8,128)(2,1)S(1)} %get-tuple-element.27, bf16[512,7168]{1,0:T(8,128)(2,1)S(1)} %copy-done.5), kind=kOutput, calls=%fused_computation.8 | convolution fusion | flops 352321536 | bytes 6324224 | tf_op jit(solution)/shard_map/dot_general | solution.py:101
  33.2 0.0 collective-permute-done
  33.2 0.1 collective-permute-start.2
  33.3 2.0 %collective-permute-start.3 = (bf16[64,3840]{1,0:T(8,128)(2,1)}, bf16[64,3840]{1,0:T(8,128)(2,1)S(1)}, u32[]{:S(2)}, u32[]{:S(2)}) collective-permute-start(bf16[64,3840]{1,0:T(8,128)(2,1)} %collective-permute-done.1), channel_id=1, source_target_pairs={{8,0},{16,8},{24,16},{28,24},{20,28},{12,20},{4,12},{0,4},{9,1},{1... | collective-permute-start | bytes 1474568 | tf_op jit(solution)/shard_map/ppermute | solution.py:178
  35.3 1.1 constant_dynamic-update-slice_fusion.1
  36.4 1.2 %constant_dynamic-update-slice_fusion = bf16[128,3840]{1,0:T(8,128)(2,1)S(1)} fusion(bf16[128,3840]{1,0:T(8,128)(2,1)S(1)} %constant_dynamic-update-slice_fusion.1, bf16[64,3840]{1,0:T(8,128)(2,1)} %collective-permute-done.1), kind=kLoop, calls=%fused_computation.72 | loop fusion | bytes 983040 | tf_op jit(solution)/shard_map/concatenate | solution.py:186
  37.6 0.6 fusion.25
  38.3 0.0 collective-permute-done.4
  38.3 2.8 %collective-permute-start.10 = (bf16[64,5376]{1,0:T(8,128)(2,1)}, bf16[64,5376]{1,0:T(8,128)(2,1)S(1)}, u32[]{:S(2)}, u32[]{:S(2)}) collective-permute-start(bf16[64,5376]{1,0:T(8,128)(2,1)} %collective-permute-done.4), channel_id=1, source_target_pairs={{0,8},{8,16},{16,24},{24,28},{28,20},{20,12},{12,4},{4,0},{1,9},{9... | collective-permute-start | bytes 2064392 | tf_op jit(solution)/shard_map/ppermute | solution.py:178
  41.1 0.0 collective-permute-start.11
  41.1 2.9 %fusion.6 = f32[512,128]{1,0:T(8,128)S(1)} fusion(bf16[512,7168]{1,0:T(8,128)(2,1)S(1)} %copy-done.5, bf16[64,5376]{1,0:T(8,128)(2,1)} %collective-permute-done.5, bf16[64,5376]{1,0:T(8,128)(2,1)} %collective-permute-done.4), kind=kOutput, calls=%fused_computation.6 | convolution fusion | flops 707395584 | bytes 7143424 | tf_op jit(solution)/shard_map/dot_general | solution.py:101
  44.0 8.8 %collective-permute-done.2 = bf16[64,3840]{1,0:T(8,128)(2,1)S(1)} collective-permute-done((bf16[64,3840]{1,0:T(8,128)(2,1)}, bf16[64,3840]{1,0:T(8,128)(2,1)S(1)}, u32[]{:S(2)}, u32[]{:S(2)}) %collective-permute-start.2) | collective-permute-done | bytes 491552 | tf_op jit(solution)/shard_map/ppermute | solution.py:178
  52.8 5.0 %collective-permute-start.6 = (bf16[64,3840]{1,0:T(8,128)(2,1)S(1)}, bf16[64,3840]{1,0:T(8,128)(2,1)S(1)}, u32[]{:S(2)}, u32[]{:S(2)}) collective-permute-start(bf16[64,3840]{1,0:T(8,128)(2,1)S(1)} %collective-permute-done.2), channel_id=1, source_target_pairs={{0,8},{8,16},{16,24},{24,28},{28,20},{20,12},{12,4},{4,0},{1,9},{9... | collective-permute-start | bytes 1474568 | tf_op jit(solution)/shard_map/ppermute | solution.py:178
  57.9 0.6 fusion.23
  58.6 8.9 %collective-permute-done.10 = bf16[64,5376]{1,0:T(8,128)(2,1)S(1)} collective-permute-done((bf16[64,5376]{1,0:T(8,128)(2,1)}, bf16[64,5376]{1,0:T(8,128)(2,1)S(1)}, u32[]{:S(2)}, u32[]{:S(2)}) %collective-permute-start.10) | collective-permute-done | bytes 688160 | tf_op jit(solution)/shard_map/ppermute | solution.py:178
  67.6 0.0 collective-permute-done.11
  67.6 5.0 %collective-permute-start.12 = (bf16[64,5376]{1,0:T(8,128)(2,1)S(1)}, bf16[64,5376]{1,0:T(8,128)(2,1)S(1)}, u32[]{:S(2)}, u32[]{:S(2)}) collective-permute-start(bf16[64,5376]{1,0:T(8,128)(2,1)S(1)} %collective-permute-done.10), channel_id=1, source_target_pairs={{0,8},{8,16},{16,24},{24,28},{28,20},{20,12},{12,4},{4,0},{1,9},{9... | collective-permute-start | bytes 2064392 | tf_op jit(solution)/shard_map/ppermute | solution.py:178
  72.6 1.6 %fusion.4 = f32[512,128]{1,0:T(8,128)S(1)} fusion(bf16[512,7168]{1,0:T(8,128)(2,1)S(1)} %copy-done.5, bf16[64,5376]{1,0:T(8,128)(2,1)S(1)} %collective-permute-done.11, bf16[64,5376]{1,0:T(8,128)(2,1)S(1)} %collective-permute-done.10), kind=kOutput, calls=%fused_computation.4 | convolution fusion | flops 707395584 | bytes 7143424 | tf_op jit(solution)/shard_map/dot_general | solution.py:101
  74.2 3.9 %collective-permute-done.6 = bf16[64,3840]{1,0:T(8,128)(2,1)S(1)} collective-permute-done((bf16[64,3840]{1,0:T(8,128)(2,1)S(1)}, bf16[64,3840]{1,0:T(8,128)(2,1)S(1)}, u32[]{:S(2)}, u32[]{:S(2)}) %collective-permute-start.6) | collective-permute-done | bytes 491552 | tf_op jit(solution)/shard_map/ppermute | solution.py:178
  78.1 5.1 %collective-permute-start.16 = (bf16[32,1792]{1,0:T(8,128)(2,1)S(1)}, bf16[32,1792]{1,0:T(8,128)(2,1)S(1)}, u32[]{:S(2)}, u32[]{:S(2)}) collective-permute-start(bf16[32,1792]{1,0:T(8,128)(2,1)S(1)} %slice.215), channel_id=1, source_target_pairs={{0,8},{8,16},{16,24},{24,28},{28,20},{20,12},{12,4},{4,0},{1,9},{9... | collective-permute-start | bytes 344072 | tf_op jit(solution)/shard_map/ppermute | solution.py:178
  83.3 1.0 constant_dynamic-update-slice_fusion.6
  84.3 1.3 %fusion.58 = f32[512,512]{1,0:T(8,128)S(1)} fusion(bf16[512,2048]{1,0:T(8,128)(2,1)S(1)} %rotate.2, bf16[512,2048]{1,0:T(8,128)(2,1)S(1)} %constant_dynamic-update-slice_fusion.6), kind=kOutput, calls=%fused_computation.112 | convolution fusion | flops 1073741824 | bytes 5242880 | tf_op jit(solution)/shard_map/dot_general | solution.py:101
  85.6 0.1 slice_add_fusion
  85.7 0.1 collective-permute-start.9
  85.8 0.6 fusion.21
  86.4 5.5 %collective-permute-done.12 = bf16[64,5376]{1,0:T(8,128)(2,1)S(1)} collective-permute-done((bf16[64,5376]{1,0:T(8,128)(2,1)S(1)}, bf16[64,5376]{1,0:T(8,128)(2,1)S(1)}, u32[]{:S(2)}, u32[]{:S(2)}) %collective-permute-start.12) | collective-permute-done | bytes 688160 | tf_op jit(solution)/shard_map/ppermute | solution.py:178
  92.0 5.9 %collective-permute-start.18 = (bf16[32,5376]{1,0:T(8,128)(2,1)S(1)}, bf16[32,5376]{1,0:T(8,128)(2,1)S(1)}, u32[]{:S(2)}, u32[]{:S(2)}) collective-permute-start(bf16[32,5376]{1,0:T(8,128)(2,1)S(1)} %slice.217), channel_id=1, source_target_pairs={{0,8},{8,16},{16,24},{24,28},{28,20},{20,12},{12,4},{4,0},{1,9},{9... | collective-permute-start | bytes 1032200 | tf_op jit(solution)/shard_map/ppermute | solution.py:178
  98.0 0.0 collective-permute-start.19
  98.0 1.6 %collective-permute-start.14 = (f32[128,512]{1,0:T(8,128)S(1)}, f32[128,512]{1,0:T(8,128)S(1)}, u32[]{:S(2)}, u32[]{:S(2)}) collective-permute-start(f32[128,512]{1,0:T(8,128)S(1)} %dynamic-slice_add_fusion), channel_id=1, source_target_pairs={{0,2},{1,3},{2,0},{3,1},{4,6},{5,7},{6,4},{7,5},{8,10},{9,11},{10,... | collective-permute-start | bytes 786440 | tf_op jit(solution)/shard_map/ppermute | solution.py:116
  99.6 1.6 %fusion.2 = f32[512,128]{1,0:T(8,128)S(1)} fusion(bf16[512,7168]{1,0:T(8,128)(2,1)S(1)} %copy-done.5, bf16[64,5376]{1,0:T(8,128)(2,1)S(1)} %collective-permute-done.13, bf16[64,5376]{1,0:T(8,128)(2,1)S(1)} %collective-permute-done.12), kind=kOutput, calls=%fused_computation.2 | convolution fusion | flops 707395584 | bytes 7143424 | tf_op jit(solution)/shard_map/dot_general | solution.py:101
  101.2 3.3 %collective-permute-done.14 = f32[128,512]{1,0:T(8,128)S(1)} collective-permute-done((f32[128,512]{1,0:T(8,128)S(1)}, f32[128,512]{1,0:T(8,128)S(1)}, u32[]{:S(2)}, u32[]{:S(2)}) %collective-permute-start.14) | collective-permute-done | bytes 262176 | tf_op jit(solution)/shard_map/ppermute | solution.py:116
  104.5 0.1 collective-permute-start.15
  104.6 0.9 collective-permute-done.19
  105.5 1.6 %fusion = f32[512,64]{1,0:T(8,128)S(1)} fusion(bf16[512,7168]{1,0:T(8,128)(2,1)S(1)} %copy-done.5, bf16[32,5376]{1,0:T(8,128)(2,1)S(1)} %collective-permute-done.19, bf16[32,5376]{1,0:T(8,128)(2,1)S(1)} %collective-permute-done.18), kind=kOutput, calls=%fused_computation | convolution fusion | flops 353697792 | bytes 6324224 | tf_op jit(solution)/shard_map/dot_general | solution.py:101
  107.0 0.6 fusion.19
  107.7 0.3 copy-done.6
  108.0 0.1 bitcast_reduce_fusion
  108.1 0.2 bitcast_reduce_fusion.1
  108.4 0.1 concatenate.70
  108.5 0.1 select_reduce_fusion
  108.6 0.7 collective-permute-start.22
  109.3 0.8 collective-permute-start.21
  110.2 0.3 collective-permute-start.20
  110.4 1.1 collective-permute-done.22
  111.6 1.3 %collective-permute-done.21 = f32[2,16]{1,0:T(2,128)S(1)} collective-permute-done((f32[2,16]{1,0:T(2,128)S(1)}, f32[2,16]{1,0:T(2,128)S(1)}, u32[]{:S(2)}, u32[]{:S(2)}) %collective-permute-start.21) | collective-permute-done | bytes 160 | tf_op jit(solution)/shard_map/ppermute | solution.py:116
  112.9 0.6 add_add_fusion
  (54 shorter events, 0.6 us)
Async XLA Ops:
  0.0 1.6 %copy-start.1 = (bf16[1,512,2048]{2,1,0:T(8,128)(2,1)S(1)}, bf16[1,512,2048]{2,1,0:T(8,128)(2,1)}, u32[]{:S(2)}) copy-start(bf16[1,512,2048]{2,1,0:T(8,128)(2,1)} %left_ref.1) | copy-start | bytes 6291460
  1.6 0.7 copy-start.3
  2.2 12.7 %copy-start.4 = (s32[16]{0:T(128)S(1)}, s32[16]{0:T(128)}, u32[]{:S(2)}) copy-start(s32[16]{0:T(128)} %owners_ref.1) | copy-start | bytes 196
  4.2 29.1 %collective-permute-start.1 = (bf16[64,3840]{1,0:T(8,128)(2,1)S(1)}, bf16[64,3840]{1,0:T(8,128)(2,1)}, u32[]{:S(2)}, u32[]{:S(2)}) collective-permute-start(bf16[64,3840]{1,0:T(8,128)(2,1)S(1)} %get-tuple-element.24), channel_id=1, source_target_pairs={{8,0},{16,8},{24,16},{28,24},{20,28},{12,20},{4,12},{0,4},{9,1},{1... | collective-permute-start | bytes 1474568 | tf_op jit(solution)/shard_map/ppermute | solution.py:178
  7.1 26.1 %collective-permute-start = (bf16[64,3840]{1,0:T(8,128)(2,1)S(1)}, bf16[64,3840]{1,0:T(8,128)(2,1)}, u32[]{:S(2)}, u32[]{:S(2)}) collective-permute-start(bf16[64,3840]{1,0:T(8,128)(2,1)S(1)} %get-tuple-element.24), channel_id=1, source_target_pairs={{0,8},{8,16},{16,24},{24,28},{28,20},{20,12},{12,4},{4,0},{1,9},{9... | collective-permute-start | bytes 1474568 | tf_op jit(solution)/shard_map/ppermute | solution.py:178
  7.3 31.0 %collective-permute-start.5 = (bf16[64,5376]{1,0:T(8,128)(2,1)S(1)}, bf16[64,5376]{1,0:T(8,128)(2,1)}, u32[]{:S(2)}, u32[]{:S(2)}) collective-permute-start(bf16[64,5376]{1,0:T(8,128)(2,1)S(1)} %get-tuple-element.27), channel_id=1, source_target_pairs={{8,0},{16,8},{24,16},{28,24},{20,28},{12,20},{4,12},{0,4},{9,1},{1... | collective-permute-start | bytes 2064392 | tf_op jit(solution)/shard_map/ppermute | solution.py:178
  9.2 29.2 %collective-permute-start.4 = (bf16[64,5376]{1,0:T(8,128)(2,1)S(1)}, bf16[64,5376]{1,0:T(8,128)(2,1)}, u32[]{:S(2)}, u32[]{:S(2)}) collective-permute-start(bf16[64,5376]{1,0:T(8,128)(2,1)S(1)} %get-tuple-element.27), channel_id=1, source_target_pairs={{0,8},{8,16},{16,24},{24,28},{28,20},{20,12},{12,4},{4,0},{1,9},{9... | collective-permute-start | bytes 2064392 | tf_op jit(solution)/shard_map/ppermute | solution.py:178
  10.1 73.3 %collective-permute-start.8 = (bf16[64,2048]{1,0:T(8,128)(2,1)S(1)}, bf16[64,2048]{1,0:T(8,128)(2,1)}, u32[]{:S(2)}, u32[]{:S(2)}) collective-permute-start(bf16[64,2048]{1,0:T(8,128)(2,1)S(1)} %get-tuple-element.48), channel_id=1, source_target_pairs={{0,28},{8,20},{16,12},{24,4},{28,0},{20,8},{12,16},{4,24},{1,29},{... | collective-permute-start | bytes 786440 | tf_op jit(solution)/shard_map/ppermute | solution.py:166
  15.5 2.0 %copy-start = (bf16[256,7168]{1,0:T(8,128)(2,1)S(1)}, bf16[256,7168]{1,0:T(8,128)(2,1)}, u32[]{:S(2)}) copy-start(bf16[256,7168]{1,0:T(8,128)(2,1)} %matrix_ref.3) | copy-start | bytes 11010052
  25.3 3.0 %copy-start.2 = (bf16[4,512,512]{2,1,0:T(8,128)(2,1)S(1)}, bf16[4,512,512]{2,1,0:T(8,128)(2,1)}, u32[]{:S(2)}) copy-start(bf16[4,512,512]{2,1,0:T(8,128)(2,1)} %basis_ref.2) | copy-start | bytes 6291460
  28.3 3.4 %copy-start.5 = (bf16[512,7168]{1,0:T(8,128)(2,1)S(1)}, bf16[512,7168]{1,0:T(8,128)(2,1)}, u32[]{:S(2)}) copy-start(bf16[512,7168]{1,0:T(8,128)(2,1)} %rotate.3) | copy-start | bytes 22020100
  33.2 19.6 %collective-permute-start.2 = (bf16[64,3840]{1,0:T(8,128)(2,1)}, bf16[64,3840]{1,0:T(8,128)(2,1)S(1)}, u32[]{:S(2)}, u32[]{:S(2)}) collective-permute-start(bf16[64,3840]{1,0:T(8,128)(2,1)} %collective-permute-done), channel_id=1, source_target_pairs={{0,8},{8,16},{16,24},{24,28},{28,20},{20,12},{12,4},{4,0},{1,9},{9... | collective-permute-start | bytes 1474568 | tf_op jit(solution)/shard_map/ppermute | solution.py:178
  33.3 19.5 %collective-permute-start.3 = (bf16[64,3840]{1,0:T(8,128)(2,1)}, bf16[64,3840]{1,0:T(8,128)(2,1)S(1)}, u32[]{:S(2)}, u32[]{:S(2)}) collective-permute-start(bf16[64,3840]{1,0:T(8,128)(2,1)} %collective-permute-done.1), channel_id=1, source_target_pairs={{8,0},{16,8},{24,16},{28,24},{20,28},{12,20},{4,12},{0,4},{9,1},{1... | collective-permute-start | bytes 1474568 | tf_op jit(solution)/shard_map/ppermute | solution.py:178
  36.4 1.9 %copy-start.7 = (bf16[512,2048]{1,0:T(8,128)(2,1)S(1)}, bf16[512,2048]{1,0:T(8,128)(2,1)}, u32[]{:S(2)}) copy-start(bf16[512,2048]{1,0:T(8,128)(2,1)} %get-tuple-element.49) | copy-start | bytes 6291460
  38.3 29.2 %collective-permute-start.10 = (bf16[64,5376]{1,0:T(8,128)(2,1)}, bf16[64,5376]{1,0:T(8,128)(2,1)S(1)}, u32[]{:S(2)}, u32[]{:S(2)}) collective-permute-start(bf16[64,5376]{1,0:T(8,128)(2,1)} %collective-permute-done.4), channel_id=1, source_target_pairs={{0,8},{8,16},{16,24},{24,28},{28,20},{20,12},{12,4},{4,0},{1,9},{9... | collective-permute-start | bytes 2064392 | tf_op jit(solution)/shard_map/ppermute | solution.py:178
  41.1 26.4 %collective-permute-start.11 = (bf16[64,5376]{1,0:T(8,128)(2,1)}, bf16[64,5376]{1,0:T(8,128)(2,1)S(1)}, u32[]{:S(2)}, u32[]{:S(2)}) collective-permute-start(bf16[64,5376]{1,0:T(8,128)(2,1)} %collective-permute-done.5), channel_id=1, source_target_pairs={{8,0},{16,8},{24,16},{28,24},{20,28},{12,20},{4,12},{0,4},{9,1},{1... | collective-permute-start | bytes 2064392 | tf_op jit(solution)/shard_map/ppermute | solution.py:178
  52.8 25.3 %collective-permute-start.6 = (bf16[64,3840]{1,0:T(8,128)(2,1)S(1)}, bf16[64,3840]{1,0:T(8,128)(2,1)S(1)}, u32[]{:S(2)}, u32[]{:S(2)}) collective-permute-start(bf16[64,3840]{1,0:T(8,128)(2,1)S(1)} %collective-permute-done.2), channel_id=1, source_target_pairs={{0,8},{8,16},{16,24},{24,28},{28,20},{20,12},{12,4},{4,0},{1,9},{9... | collective-permute-start | bytes 1474568 | tf_op jit(solution)/shard_map/ppermute | solution.py:178
  57.9 20.3 %collective-permute-start.7 = (bf16[64,3840]{1,0:T(8,128)(2,1)S(1)}, bf16[64,3840]{1,0:T(8,128)(2,1)S(1)}, u32[]{:S(2)}, u32[]{:S(2)}) collective-permute-start(bf16[64,3840]{1,0:T(8,128)(2,1)S(1)} %collective-permute-done.3), channel_id=1, source_target_pairs={{8,0},{16,8},{24,16},{28,24},{20,28},{12,20},{4,12},{0,4},{9,1},{1... | collective-permute-start | bytes 1474568 | tf_op jit(solution)/shard_map/ppermute | solution.py:178
  67.6 24.4 %collective-permute-start.12 = (bf16[64,5376]{1,0:T(8,128)(2,1)S(1)}, bf16[64,5376]{1,0:T(8,128)(2,1)S(1)}, u32[]{:S(2)}, u32[]{:S(2)}) collective-permute-start(bf16[64,5376]{1,0:T(8,128)(2,1)S(1)} %collective-permute-done.10), channel_id=1, source_target_pairs={{0,8},{8,16},{16,24},{24,28},{28,20},{20,12},{12,4},{4,0},{1,9},{9... | collective-permute-start | bytes 2064392 | tf_op jit(solution)/shard_map/ppermute | solution.py:178
  72.6 19.4 %collective-permute-start.13 = (bf16[64,5376]{1,0:T(8,128)(2,1)S(1)}, bf16[64,5376]{1,0:T(8,128)(2,1)S(1)}, u32[]{:S(2)}, u32[]{:S(2)}) collective-permute-start(bf16[64,5376]{1,0:T(8,128)(2,1)S(1)} %collective-permute-done.11), channel_id=1, source_target_pairs={{8,0},{16,8},{24,16},{28,24},{20,28},{12,20},{4,12},{0,4},{9,1},{1... | collective-permute-start | bytes 2064392 | tf_op jit(solution)/shard_map/ppermute | solution.py:178
  78.1 26.4 %collective-permute-start.16 = (bf16[32,1792]{1,0:T(8,128)(2,1)S(1)}, bf16[32,1792]{1,0:T(8,128)(2,1)S(1)}, u32[]{:S(2)}, u32[]{:S(2)}) collective-permute-start(bf16[32,1792]{1,0:T(8,128)(2,1)S(1)} %slice.215), channel_id=1, source_target_pairs={{0,8},{8,16},{16,24},{24,28},{28,20},{20,12},{12,4},{4,0},{1,9},{9... | collective-permute-start | bytes 344072 | tf_op jit(solution)/shard_map/ppermute | solution.py:178
  83.2 21.4 %collective-permute-start.17 = (bf16[32,1792]{1,0:T(8,128)(2,1)S(1)}, bf16[32,1792]{1,0:T(8,128)(2,1)S(1)}, u32[]{:S(2)}, u32[]{:S(2)}) collective-permute-start(bf16[32,1792]{1,0:T(8,128)(2,1)S(1)} %slice.216), channel_id=1, source_target_pairs={{8,0},{16,8},{24,16},{28,24},{20,28},{12,20},{4,12},{0,4},{9,1},{1... | collective-permute-start | bytes 344072 | tf_op jit(solution)/shard_map/ppermute | solution.py:178
  85.7 12.2 %collective-permute-start.9 = (f32[128,512]{1,0:T(8,128)S(1)}, f32[128,512]{1,0:T(8,128)S(1)}, u32[]{:S(2)}, u32[]{:S(2)}) collective-permute-start(f32[128,512]{1,0:T(8,128)S(1)} %constant_dynamic-slice_fusion), channel_id=1, source_target_pairs={{0,1},{1,0},{2,3},{3,2},{4,5},{5,4},{6,7},{7,6},{8,9},{9,8},{10,11... | collective-permute-start | bytes 786440 | tf_op jit(solution)/shard_map/ppermute | solution.py:116
  92.0 12.5 %collective-permute-start.18 = (bf16[32,5376]{1,0:T(8,128)(2,1)S(1)}, bf16[32,5376]{1,0:T(8,128)(2,1)S(1)}, u32[]{:S(2)}, u32[]{:S(2)}) collective-permute-start(bf16[32,5376]{1,0:T(8,128)(2,1)S(1)} %slice.217), channel_id=1, source_target_pairs={{0,8},{8,16},{16,24},{24,28},{28,20},{20,12},{12,4},{4,0},{1,9},{9... | collective-permute-start | bytes 1032200 | tf_op jit(solution)/shard_map/ppermute | solution.py:178
  98.0 7.5 %collective-permute-start.19 = (bf16[32,5376]{1,0:T(8,128)(2,1)S(1)}, bf16[32,5376]{1,0:T(8,128)(2,1)S(1)}, u32[]{:S(2)}, u32[]{:S(2)}) collective-permute-start(bf16[32,5376]{1,0:T(8,128)(2,1)S(1)} %slice.218), channel_id=1, source_target_pairs={{8,0},{16,8},{24,16},{28,24},{20,28},{12,20},{4,12},{0,4},{9,1},{1... | collective-permute-start | bytes 1032200 | tf_op jit(solution)/shard_map/ppermute | solution.py:178
  98.0 6.4 %collective-permute-start.14 = (f32[128,512]{1,0:T(8,128)S(1)}, f32[128,512]{1,0:T(8,128)S(1)}, u32[]{:S(2)}, u32[]{:S(2)}) collective-permute-start(f32[128,512]{1,0:T(8,128)S(1)} %dynamic-slice_add_fusion), channel_id=1, source_target_pairs={{0,2},{1,3},{2,0},{3,1},{4,6},{5,7},{6,4},{7,5},{8,10},{9,11},{10,... | collective-permute-start | bytes 786440 | tf_op jit(solution)/shard_map/ppermute | solution.py:116
  104.5 3.2 %collective-permute-start.15 = (f32[128,512]{1,0:T(8,128)S(1)}, f32[128,512]{1,0:T(8,128)S(1)}, u32[]{:S(2)}, u32[]{:S(2)}) collective-permute-start(f32[128,512]{1,0:T(8,128)S(1)} %add.175), channel_id=1, source_target_pairs={{0,1},{1,0},{2,3},{3,2},{4,5},{5,4},{6,7},{7,6},{8,9},{9,8},{10,11... | collective-permute-start | bytes 786440 | tf_op jit(solution)/shard_map/ppermute | solution.py:116
  107.0 1.0 copy-start.6
  108.6 3.0 %collective-permute-start.22 = (f32[2,16]{1,0:T(2,128)S(1)}, f32[2,16]{1,0:T(2,128)S(1)}, u32[]{:S(2)}, u32[]{:S(2)}) collective-permute-start(f32[2,16]{1,0:T(2,128)S(1)} %select_reduce_fusion), channel_id=1, source_target_pairs={{0,3},{1,2},{2,1},{3,0},{4,7},{5,6},{6,5},{7,4},{8,11},{9,10},{10,... | collective-permute-start | bytes 392 | tf_op jit(solution)/shard_map/ppermute | solution.py:116
  109.3 3.6 %collective-permute-start.21 = (f32[2,16]{1,0:T(2,128)S(1)}, f32[2,16]{1,0:T(2,128)S(1)}, u32[]{:S(2)}, u32[]{:S(2)}) collective-permute-start(f32[2,16]{1,0:T(2,128)S(1)} %select_reduce_fusion), channel_id=1, source_target_pairs={{0,2},{1,3},{2,0},{3,1},{4,6},{5,7},{6,4},{7,5},{8,10},{9,11},{10,... | collective-permute-start | bytes 392 | tf_op jit(solution)/shard_map/ppermute | solution.py:116
  110.2 2.7 %collective-permute-start.20 = (f32[2,16]{1,0:T(2,128)S(1)}, f32[2,16]{1,0:T(2,128)S(1)}, u32[]{:S(2)}, u32[]{:S(2)}) collective-permute-start(f32[2,16]{1,0:T(2,128)S(1)} %select_reduce_fusion), channel_id=1, source_target_pairs={{0,1},{1,0},{2,3},{3,2},{4,5},{5,4},{6,7},{7,6},{8,9},{9,8},{10,11... | collective-permute-start | bytes 392 | tf_op jit(solution)/shard_map/ppermute | solution.py:116

commit v5 on v4

--- a/solution.py
+++ b/solution.py
@@ -10,17 +10,17 @@
 LEN = 128
 
 
-def params():
-    return pltpu.CompilerParams(vmem_limit_bytes=48 * 2**20)
+def params(mebibytes):
+    return pltpu.CompilerParams(vmem_limit_bytes=mebibytes * 2**20)
 
 
 def pick_rows(groups, owners, left_store, right_store):
     per = NQ // groups
     width_left = left_store.shape[2]
     width_right = right_store.shape[2]
-    cut = max(width_right // 4 // 256 * 256, 128)
-
-    def kernel(owners_ref, left_ref, right_ref, first_out, second_out, sems):
+    cut = max(width_right * 5 // 14 // 128 * 128, 128)
+
+    def kernel(owners_ref, left_ref, right_ref, left_out, first_out, second_out, sems):
         group = lax.axis_index("dp")
         found = jnp.int32(0)
         queries = [jnp.int32(0)] * per
@@ -33,8 +33,8 @@
             rows = pl.ds(pl.multiple_of(queries[i] * R, R), R)
             here = pl.ds(i * R, R)
             pairs = [
-                (left_ref.at[0, rows, :], first_out.at[here, pl.ds(0, width_left)]),
-                (right_ref.at[0, rows, pl.ds(0, cut)], first_out.at[here, pl.ds(width_left, cut)]),
+                (left_ref.at[0, rows, :], left_out.at[here, :]),
+                (right_ref.at[0, rows, pl.ds(0, cut)], first_out.at[here, :]),
                 (right_ref.at[0, rows, pl.ds(cut, width_right - cut)], second_out.at[here, :]),
             ]
             for j, (source, target) in enumerate(pairs):
@@ -48,11 +48,11 @@
     in_hbm = pl.BlockSpec(memory_space=pltpu.HBM)
     return pl.pallas_call(
         kernel,
-        out_shape=(shape(width_left + cut), shape(width_right - cut)),
+        out_shape=(shape(width_left), shape(cut), shape(width_right - cut)),
         in_specs=[pl.BlockSpec(memory_space=pltpu.SMEM), in_hbm, in_hbm],
-        out_specs=(in_hbm, in_hbm),
+        out_specs=(in_hbm, in_hbm, in_hbm),
         scratch_shapes=[pltpu.SemaphoreType.DMA((per, 3))],
-        compiler_params=params(),
+        compiler_params=params(62),
         name="pick_rows",
     )(owners, left_store, right_store)
 
@@ -86,7 +86,7 @@
             ],
             out_specs=pl.BlockSpec((2 * rows, each * width), lambda k, at: (0, k)),
         ),
-        compiler_params=params(),
+        compiler_params=params(56),
         cost_estimate=pl.CostEstimate(
             flops=2 * rows * total * width,
             bytes_accessed=2 * (3 * rows * total + total * width),
@@ -160,40 +160,38 @@
     reach = groups // 2
 
     own = pick_rows(groups, owners, left_store, right_store)
-    width_left = left_store.shape[2]
-    cut = own[0].shape[1] - width_left
-
-    across = lax.ppermute(
-        own[0][:, :width_left], "dp", [(ring[i], ring[i - reach]) for i in range(groups)]
-    )
-    steps = [[], []]
-    came = []
-    for hops in range(1, reach + 1):
-        for piece in range(2):
-            ahead, behind = steps[piece][-1] if hops > 1 else (own[piece], own[piece])
+    cut = own[1].shape[1]
+
+    def around(piece, before):
+        steps = []
+        ahead, behind = after((piece, piece), before)
+        for hops in range(1, reach + 1):
             if hops == reach:
-                base = width_left if piece == 0 else 0
-                ahead, behind = ahead[: chunk // 2, base:], behind[chunk // 2 :, base:]
-            ahead, behind = after((ahead, behind), came[-3:-1])
-            got = (lax.ppermute(ahead, "dp", forward), lax.ppermute(behind, "dp", backward))
-            steps[piece].append(got)
-            came.append(got)
+                ahead, behind = ahead[: chunk // 2], behind[chunk // 2 :]
+            ahead = lax.ppermute(ahead, "dp", forward)
+            behind = lax.ppermute(behind, "dp", backward)
+            steps.append((ahead, behind))
+        return steps
+
+    left_steps = around(own[0], None)
+    second_steps = around(own[2], None)
+    first_steps = around(own[1], left_steps[-1])
 
     grads = rotate(out_grads, out_basis, shard)
     acts = rotate(hidden_acts, in_basis, 0)
 
-    steps[0][-1], steps[1][-1] = lax.optimization_barrier((steps[0][-1], steps[1][-1]))
-    first = [own[0]] + [jnp.concatenate(pair, axis=0) for pair in steps[0]]
-    second = [own[1]] + [jnp.concatenate(pair, axis=0) for pair in steps[1]]
-    left_fac = [piece[:, :width_left] for piece in first[:-1]] + [across]
+    left_fac = [own[0]] + [piece for pair in left_steps for piece in pair]
     coefficient = sum_over_shards(
-        contract_rows(grads, jnp.concatenate(left_fac, axis=0)), shards, [came[-3]]
-    )
+        contract_rows(grads, jnp.concatenate(left_fac, axis=0)), shards, []
+    )
+    first_own, second_own = after(own[1:], left_steps[1])
+    first = [first_own] + [jnp.concatenate(pair, axis=0) for pair in first_steps]
+    second = [second_own] + [jnp.concatenate(pair, axis=0) for pair in second_steps]
 
     parts = []
     at = 0
     for step in range(reach + 1):
-        projected = contract_rows(acts[:, :cut], first[step][:, -cut:])
+        projected = contract_rows(acts[:, :cut], first[step])
         projected += contract_rows(acts[:, cut:], second[step])
         width = projected.shape[1]
         terms = coefficient[:, at : at + width] * projected

time: 114 us -> 154 us (1.35)
  Pallas kernels: 11.9 us -> 50.6 us
  waiting for transfers between devices: 33.8 us -> 56 us
  starting transfers between devices: 39.6 us -> 29.7 us
  local copies, waits for them, and re-layouts: 10.3 us -> 0.59 us
    pallas_call x1, Pallas kernels: 1.89 us -> 37.7 us  [pick_rows(): pl.pallas_call(kernel, out_shape=(shape(width_left), shape(cut), shape(wi...]
    ppermute x17 -> x24, waiting for transfers between devices: 28.1 us -> 53.3 us  [the longest x12 49.1 us: around(): ahead = lax.ppermute(ahead, 'dp', forward)]
    ppermute x17 -> x24, starting transfers between devices: 36 us -> 26.1 us  [the longest x12 21.7 us: around(): ahead = lax.ppermute(ahead, 'dp', forward)]
    unnamed x22 -> x18, local copies, waits for them, and re-layouts: 6.89 us -> 0.16 us
    ppermute x6, waiting for transfers between devices: 5.73 us -> 2.73 us  [swapped(): return lax.ppermute(piece, 'mp', [(i, i ^ distance) for i in range(shards)])]
    pallas_call x2, Pallas kernels: 10 us -> 12.9 us  [rotate(): pl.pallas_call(kernel, out_shape=jax.ShapeDtypeStruct((2 * rows, total),...]
  transfers between devices with their start and end apart: 23 -> 30, of which waited for: 8 -> 12; matrix products, arithmetic and copies ran while one was open for 18% -> 10% of each run, Pallas kernels for 9% -> 8%
where the time goes in v5:
time: 154 us
  waiting for transfers between devices  56 us (36%)
  Pallas kernels  50.6 us (33%)
  starting transfers between devices  29.7 us (19%)
  matrix products  14.7 us (10%)
  other arithmetic  1.54 us (1%)
    ppermute x12, waiting for transfers between devices, around(): ahead = lax.ppermute(ahead, 'dp', forward)  49.1 us
    pallas_call x1, Pallas kernels, pick_rows(): pl.pallas_call(kernel, out_shape=(shape(width_left), shape(cut), shape(wi...  37.7 us
    ppermute x12, starting transfers between devices, around(): ahead = lax.ppermute(ahead, 'dp', forward)  21.7 us
    dot_general x11, matrix products, contract_rows(): lax.dot_general(both, second, (((1,), (1,)), ((), ())), preferred_element...  14.7 us
    pallas_call x2, Pallas kernels, rotate(): pl.pallas_call(kernel, out_shape=jax.ShapeDtypeStruct((2 * rows, total),...  12.9 us
    ppermute x12, starting transfers between devices, around(): behind = lax.ppermute(behind, 'dp', backward)  4.34 us
    ppermute x12, waiting for transfers between devices, around(): behind = lax.ppermute(behind, 'dp', backward)  4.2 us
    ppermute x6, starting transfers between devices, swapped(): return lax.ppermute(piece, 'mp', [(i, i ^ distance) for i in range(shards)])  3.59 us
  transfers between devices with their start and end apart: 30, of which 12 were waited for; matrix products, arithmetic and copies ran while one was open for 10% of the time, Pallas kernels for 8%

profile of v5, /device:TPU:0, one launch (start us, length us, event | category | flops | bytes accessed | tf_op | source)
XLA Modules:
  0.0 153.5 jit_solution(5468505197301880907)
XLA Ops:
  0.0 37.7 %pick_rows.1 = (bf16[64,2048]{1,0:T(8,128)(2,1)}, bf16[64,2560]{1,0:T(8,128)(2,1)}, bf16[64,4608]{1,0:T(8,128)(2,1)}) custom-call(s32[16]{0:T(128)} %owners_ref.1, bf16[1,512,2048]{2,1,0:T(8,128)(2,1)} %left_ref.1, bf16[1,512,7168]{2,1,0:T(8,128)(2,1)} %right_ref.1), custom_call_target="tpu_custom_call" | custom-call | tf_op jit(solution)/shard_map/pick_rows/pallas_call | solution.py:49
  37.7 3.1 %collective-permute-start = (bf16[64,2048]{1,0:T(8,128)(2,1)}, bf16[64,2048]{1,0:T(8,128)(2,1)S(1)}, u32[]{:S(2)}, u32[]{:S(2)}) collective-permute-start(bf16[64,2048]{1,0:T(8,128)(2,1)} %get-tuple-element.12), channel_id=1, source_target_pairs={{0,8},{8,16},{16,24},{24,28},{28,20},{20,12},{12,4},{4,0},{1,9},{9... | collective-permute-start | bytes 786440 | tf_op jit(solution)/shard_map/ppermute | solution.py:171
  40.8 2.0 %collective-permute-start.13 = (bf16[64,4608]{1,0:T(8,128)(2,1)}, bf16[64,4608]{1,0:T(8,128)(2,1)}, u32[]{:S(2)}, u32[]{:S(2)}) collective-permute-start(bf16[64,4608]{1,0:T(8,128)(2,1)} %get-tuple-element.16), channel_id=1, source_target_pairs={{0,8},{8,16},{16,24},{24,28},{28,20},{20,12},{12,4},{4,0},{1,9},{9... | collective-permute-start | bytes 1769480 | tf_op jit(solution)/shard_map/ppermute | solution.py:171
  42.8 0.2 convert_reduce_fusion
  43.1 0.1 concatenate.57
  43.3 0.1 concatenate.58
  43.3 9.4 %rotate.3 = bf16[512,7168]{1,0:T(8,128)(2,1)} custom-call(s32[1]{0:T(128)} %constant.123.clone.1.shard_ref, bf16[256,7168]{1,0:T(8,128)(2,1)} %matrix_ref.3, bf16[28,256,256]{2,1,0:T(8,128)(2,1)} %basis_ref.3), custom_call_target="tpu_custom_call" | custom-call | flops 939524096 | bytes 14680064 | tf_op jit(solution)/shard_map/rotate/pallas_call | solution.py:77
  52.7 0.1 compare_and_fusion
  52.8 3.5 %rotate.2 = bf16[512,2048]{1,0:T(8,128)(2,1)} custom-call(s32[1]{0:T(128)} %bitcast.shard_ref, bf16[256,8192]{1,0:T(8,128)(2,1)} %matrix_ref.2, bf16[4,512,512]{2,1,0:T(8,128)(2,1)} %basis_ref.2), custom_call_target="tpu_custom_call" | custom-call | flops 536870912 | bytes 5242880 | tf_op jit(solution)/shard_map/rotate/pallas_call | solution.py:77
  56.4 2.1 %collective-permute-start.2 = (bf16[64,2048]{1,0:T(8,128)(2,1)S(1)}, bf16[64,2048]{1,0:T(8,128)(2,1)S(1)}, u32[]{:S(2)}, u32[]{:S(2)}) collective-permute-start(bf16[64,2048]{1,0:T(8,128)(2,1)S(1)} %collective-permute-done), channel_id=1, source_target_pairs={{0,8},{8,16},{16,24},{24,28},{28,20},{20,12},{12,4},{4,0},{1,9},{9... | collective-permute-start | bytes 786440 | tf_op jit(solution)/shard_map/ppermute | solution.py:171
  58.4 0.0 collective-permute-start.3
  58.5 7.0 %collective-permute-done.2 = bf16[64,2048]{1,0:T(8,128)(2,1)S(1)} collective-permute-done((bf16[64,2048]{1,0:T(8,128)(2,1)S(1)}, bf16[64,2048]{1,0:T(8,128)(2,1)S(1)}, u32[]{:S(2)}, u32[]{:S(2)}) %collective-permute-start.2) | collective-permute-done | bytes 262176 | tf_op jit(solution)/shard_map/ppermute | solution.py:171
  65.5 1.5 %collective-permute-done.3 = bf16[64,2048]{1,0:T(8,128)(2,1)S(1)} collective-permute-done((bf16[64,2048]{1,0:T(8,128)(2,1)S(1)}, bf16[64,2048]{1,0:T(8,128)(2,1)S(1)}, u32[]{:S(2)}, u32[]{:S(2)}) %collective-permute-start.3) | collective-permute-done | bytes 262176 | tf_op jit(solution)/shard_map/ppermute | solution.py:172
  67.1 2.5 %fusion.8 = f32[512,64]{1,0:T(8,128)S(1)} fusion(bf16[64,4608]{1,0:T(8,128)(2,1)} %get-tuple-element.16, bf16[512,7168]{1,0:T(8,128)(2,1)S(1)} %copy-done), kind=kOutput, calls=%fused_computation.8 | convolution fusion | flops 301989888 | bytes 5439488 | tf_op jit(solution)/shard_map/dot_general | solution.py:101
  69.5 0.8 fusion.18
  70.4 1.6 %collective-permute-start.4 = (bf16[64,2048]{1,0:T(8,128)(2,1)S(1)}, bf16[64,2048]{1,0:T(8,128)(2,1)S(1)}, u32[]{:S(2)}, u32[]{:S(2)}) collective-permute-start(bf16[64,2048]{1,0:T(8,128)(2,1)S(1)} %collective-permute-done.2), channel_id=1, source_target_pairs={{0,8},{8,16},{16,24},{24,28},{28,20},{20,12},{12,4},{4,0},{1,9},{9... | collective-permute-start | bytes 786440 | tf_op jit(solution)/shard_map/ppermute | solution.py:171
  72.0 0.4 collective-permute-start.5
  72.5 1.6 %collective-permute-start.17 = (bf16[64,4608]{1,0:T(8,128)(2,1)}, bf16[64,4608]{1,0:T(8,128)(2,1)S(1)}, u32[]{:S(2)}, u32[]{:S(2)}) collective-permute-start(bf16[64,4608]{1,0:T(8,128)(2,1)} %collective-permute-done.13), channel_id=1, source_target_pairs={{0,8},{8,16},{16,24},{24,28},{28,20},{20,12},{12,4},{4,0},{1,9},{9... | collective-permute-start | bytes 1769480 | tf_op jit(solution)/shard_map/ppermute | solution.py:171
  74.2 0.4 collective-permute-start.18
  74.6 5.1 %collective-permute-done.4 = bf16[64,2048]{1,0:T(8,128)(2,1)S(1)} collective-permute-done((bf16[64,2048]{1,0:T(8,128)(2,1)S(1)}, bf16[64,2048]{1,0:T(8,128)(2,1)S(1)}, u32[]{:S(2)}, u32[]{:S(2)}) %collective-permute-start.4) | collective-permute-done | bytes 262176 | tf_op jit(solution)/shard_map/ppermute | solution.py:171
  79.7 1.6 %collective-permute-start.6 = (bf16[32,2048]{1,0:T(8,128)(2,1)S(1)}, bf16[32,2048]{1,0:T(8,128)(2,1)S(1)}, u32[]{:S(2)}, u32[]{:S(2)}) collective-permute-start(bf16[32,2048]{1,0:T(8,128)(2,1)S(1)} %slice.159), channel_id=1, source_target_pairs={{0,8},{8,16},{16,24},{24,28},{28,20},{20,12},{12,4},{4,0},{1,9},{9... | collective-permute-start | bytes 393224 | tf_op jit(solution)/shard_map/ppermute | solution.py:171
  81.3 0.5 collective-permute-start.7
  81.9 10.8 %collective-permute-done.6 = bf16[32,2048]{1,0:T(8,128)(2,1)S(1)} collective-permute-done((bf16[32,2048]{1,0:T(8,128)(2,1)S(1)}, bf16[32,2048]{1,0:T(8,128)(2,1)S(1)}, u32[]{:S(2)}, u32[]{:S(2)}) %collective-permute-start.6) | collective-permute-done | bytes 131104 | tf_op jit(solution)/shard_map/ppermute | solution.py:171
  92.7 1.3 collective-permute-done.7
  94.0 1.4 fusion.65
  95.4 0.1 slice_add_fusion
  95.5 0.1 collective-permute-start.8
  95.6 1.6 %collective-permute-start.11 = (bf16[64,2560]{1,0:T(8,128)(2,1)S(1)}, bf16[64,2560]{1,0:T(8,128)(2,1)S(1)}, u32[]{:S(2)}, u32[]{:S(2)}) collective-permute-start(bf16[64,2560]{1,0:T(8,128)(2,1)S(1)} %copy-done.4), channel_id=1, source_target_pairs={{0,8},{8,16},{16,24},{24,28},{28,20},{20,12},{12,4},{4,0},{1,9},{9... | collective-permute-start | bytes 983048 | tf_op jit(solution)/shard_map/ppermute | solution.py:171
  97.3 0.4 collective-permute-start.12
  97.7 2.6 %fusion.6 = f32[512,128]{1,0:T(8,128)S(1)} fusion(bf16[512,7168]{1,0:T(8,128)(2,1)S(1)} %copy-done, bf16[64,4608]{1,0:T(8,128)(2,1)} %collective-permute-done.14, bf16[64,4608]{1,0:T(8,128)(2,1)} %collective-permute-done.13), kind=kOutput, calls=%fused_computation.6 | convolution fusion | flops 606339072 | bytes 6160384 | tf_op jit(solution)/shard_map/dot_general | solution.py:101
  100.4 1.6 %collective-permute-start.9 = (f32[128,512]{1,0:T(8,128)S(1)}, f32[128,512]{1,0:T(8,128)S(1)}, u32[]{:S(2)}, u32[]{:S(2)}) collective-permute-start(f32[128,512]{1,0:T(8,128)S(1)} %dynamic-slice_add_fusion), channel_id=1, source_target_pairs={{0,2},{1,3},{2,0},{3,1},{4,6},{5,7},{6,4},{7,5},{8,10},{9,11},{10,... | collective-permute-start | bytes 786440 | tf_op jit(solution)/shard_map/ppermute | solution.py:116
  102.0 1.6 %collective-permute-start.21 = (bf16[64,4608]{1,0:T(8,128)(2,1)S(1)}, bf16[64,4608]{1,0:T(8,128)(2,1)S(1)}, u32[]{:S(2)}, u32[]{:S(2)}) collective-permute-start(bf16[64,4608]{1,0:T(8,128)(2,1)S(1)} %collective-permute-done.17), channel_id=1, source_target_pairs={{0,8},{8,16},{16,24},{24,28},{28,20},{20,12},{12,4},{4,0},{1,9},{9... | collective-permute-start | bytes 1769480 | tf_op jit(solution)/shard_map/ppermute | solution.py:171
  103.6 0.4 collective-permute-start.22
  104.0 2.2 %collective-permute-done.11 = bf16[64,2560]{1,0:T(8,128)(2,1)S(1)} collective-permute-done((bf16[64,2560]{1,0:T(8,128)(2,1)S(1)}, bf16[64,2560]{1,0:T(8,128)(2,1)S(1)}, u32[]{:S(2)}, u32[]{:S(2)}) %collective-permute-start.11) | collective-permute-done | bytes 327712 | tf_op jit(solution)/shard_map/ppermute | solution.py:171
  106.2 1.6 %collective-permute-start.15 = (bf16[64,2560]{1,0:T(8,128)(2,1)S(1)}, bf16[64,2560]{1,0:T(8,128)(2,1)S(1)}, u32[]{:S(2)}, u32[]{:S(2)}) collective-permute-start(bf16[64,2560]{1,0:T(8,128)(2,1)S(1)} %collective-permute-done.11), channel_id=1, source_target_pairs={{0,8},{8,16},{16,24},{24,28},{28,20},{20,12},{12,4},{4,0},{1,9},{9... | collective-permute-start | bytes 983048 | tf_op jit(solution)/shard_map/ppermute | solution.py:171
  107.8 0.0 collective-permute-done.12
  107.8 0.4 collective-permute-start.16
  108.3 1.4 fusion.4
  109.6 0.8 fusion.16
  110.5 0.1 collective-permute-start.10
  110.6 14.8 %collective-permute-done.15 = bf16[64,2560]{1,0:T(8,128)(2,1)S(1)} collective-permute-done((bf16[64,2560]{1,0:T(8,128)(2,1)S(1)}, bf16[64,2560]{1,0:T(8,128)(2,1)S(1)}, u32[]{:S(2)}, u32[]{:S(2)}) %collective-permute-start.15) | collective-permute-done | bytes 327712 | tf_op jit(solution)/shard_map/ppermute | solution.py:171
  125.4 1.6 %collective-permute-start.19 = (bf16[64,2560]{1,0:T(8,128)(2,1)S(1)}, bf16[64,2560]{1,0:T(8,128)(2,1)S(1)}, u32[]{:S(2)}, u32[]{:S(2)}) collective-permute-start(bf16[64,2560]{1,0:T(8,128)(2,1)S(1)} %collective-permute-done.15), channel_id=1, source_target_pairs={{0,8},{8,16},{16,24},{24,28},{28,20},{20,12},{12,4},{4,0},{1,9},{9... | collective-permute-start | bytes 983048 | tf_op jit(solution)/shard_map/ppermute | solution.py:171
  127.0 0.4 collective-permute-start.20
  127.4 0.8 fusion.14
  128.4 1.6 %collective-permute-start.25 = (bf16[32,4608]{1,0:T(8,128)(2,1)S(1)}, bf16[32,4608]{1,0:T(8,128)(2,1)S(1)}, u32[]{:S(2)}, u32[]{:S(2)}) collective-permute-start(bf16[32,4608]{1,0:T(8,128)(2,1)S(1)} %slice.190), channel_id=1, source_target_pairs={{0,8},{8,16},{16,24},{24,28},{28,20},{20,12},{12,4},{4,0},{1,9},{9... | collective-permute-start | bytes 884744 | tf_op jit(solution)/shard_map/ppermute | solution.py:171
  130.0 0.5 collective-permute-start.26
  130.5 1.4 fusion.2
  131.9 4.1 %collective-permute-done.19 = bf16[64,2560]{1,0:T(8,128)(2,1)S(1)} collective-permute-done((bf16[64,2560]{1,0:T(8,128)(2,1)S(1)}, bf16[64,2560]{1,0:T(8,128)(2,1)S(1)}, u32[]{:S(2)}, u32[]{:S(2)}) %collective-permute-start.19) | collective-permute-done | bytes 327712 | tf_op jit(solution)/shard_map/ppermute | solution.py:171
  136.0 1.6 %collective-permute-start.23 = (bf16[32,2560]{1,0:T(8,128)(2,1)S(1)}, bf16[32,2560]{1,0:T(8,128)(2,1)S(1)}, u32[]{:S(2)}, u32[]{:S(2)}) collective-permute-start(bf16[32,2560]{1,0:T(8,128)(2,1)S(1)} %slice.186), channel_id=1, source_target_pairs={{0,8},{8,16},{16,24},{24,28},{28,20},{20,12},{12,4},{4,0},{1,9},{9... | collective-permute-start | bytes 491528 | tf_op jit(solution)/shard_map/ppermute | solution.py:171
  137.7 0.7 collective-permute-start.24
  138.4 0.8 fusion.12
  139.2 0.2 bitcast_reduce_fusion.1
  139.5 5.1 %collective-permute-done.23 = bf16[32,2560]{1,0:T(8,128)(2,1)S(1)} collective-permute-done((bf16[32,2560]{1,0:T(8,128)(2,1)S(1)}, bf16[32,2560]{1,0:T(8,128)(2,1)S(1)}, u32[]{:S(2)}, u32[]{:S(2)}) %collective-permute-start.23) | collective-permute-done | bytes 163872 | tf_op jit(solution)/shard_map/ppermute | solution.py:171
  144.5 1.3 collective-permute-done.24
  145.8 0.8 fusion.10
  146.7 1.4 fusion
  148.0 0.1 bitcast_reduce_fusion
  148.2 0.1 concatenate.70
  148.3 0.1 select_reduce_fusion
  148.4 1.6 %collective-permute-start.28 = (f32[2,16]{1,0:T(2,128)S(1)}, f32[2,16]{1,0:T(2,128)S(1)}, u32[]{:S(2)}, u32[]{:S(2)}) collective-permute-start(f32[2,16]{1,0:T(2,128)S(1)} %select_reduce_fusion), channel_id=1, source_target_pairs={{0,2},{1,3},{2,0},{3,1},{4,6},{5,7},{6,4},{7,5},{8,10},{9,11},{10,... | collective-permute-start | bytes 392 | tf_op jit(solution)/shard_map/ppermute | solution.py:116
  150.0 0.3 collective-permute-start.29
  150.2 1.8 %collective-permute-done.28 = f32[2,16]{1,0:T(2,128)S(1)} collective-permute-done((f32[2,16]{1,0:T(2,128)S(1)}, f32[2,16]{1,0:T(2,128)S(1)}, u32[]{:S(2)}, u32[]{:S(2)}) %collective-permute-start.28) | collective-permute-done | bytes 160 | tf_op jit(solution)/shard_map/ppermute | solution.py:116
  152.0 0.9 collective-permute-done.29
  153.0 0.6 add_add_fusion
  (62 shorter events, 0.5 us)
Async XLA Ops:
  0.0 42.8 %copy-start.3 = (s32[16]{0:T(128)S(1)}, s32[16]{0:T(128)}, u32[]{:S(2)}) copy-start(s32[16]{0:T(128)} %owners_ref.1) | copy-start | bytes 196
  37.7 18.6 %collective-permute-start = (bf16[64,2048]{1,0:T(8,128)(2,1)}, bf16[64,2048]{1,0:T(8,128)(2,1)S(1)}, u32[]{:S(2)}, u32[]{:S(2)}) collective-permute-start(bf16[64,2048]{1,0:T(8,128)(2,1)} %get-tuple-element.12), channel_id=1, source_target_pairs={{0,8},{8,16},{16,24},{24,28},{28,20},{20,12},{12,4},{4,0},{1,9},{9... | collective-permute-start | bytes 786440 | tf_op jit(solution)/shard_map/ppermute | solution.py:171
  40.8 17.6 %collective-permute-start.1 = (bf16[64,2048]{1,0:T(8,128)(2,1)}, bf16[64,2048]{1,0:T(8,128)(2,1)S(1)}, u32[]{:S(2)}, u32[]{:S(2)}) collective-permute-start(bf16[64,2048]{1,0:T(8,128)(2,1)} %get-tuple-element.12), channel_id=1, source_target_pairs={{8,0},{16,8},{24,16},{28,24},{20,28},{12,20},{4,12},{0,4},{9,1},{1... | collective-permute-start | bytes 786440 | tf_op jit(solution)/shard_map/ppermute | solution.py:172
  40.8 31.7 %collective-permute-start.13 = (bf16[64,4608]{1,0:T(8,128)(2,1)}, bf16[64,4608]{1,0:T(8,128)(2,1)}, u32[]{:S(2)}, u32[]{:S(2)}) collective-permute-start(bf16[64,4608]{1,0:T(8,128)(2,1)} %get-tuple-element.16), channel_id=1, source_target_pairs={{0,8},{8,16},{16,24},{24,28},{28,20},{20,12},{12,4},{4,0},{1,9},{9... | collective-permute-start | bytes 1769480 | tf_op jit(solution)/shard_map/ppermute | solution.py:171
  42.8 31.3 %collective-permute-start.14 = (bf16[64,4608]{1,0:T(8,128)(2,1)}, bf16[64,4608]{1,0:T(8,128)(2,1)}, u32[]{:S(2)}, u32[]{:S(2)}) collective-permute-start(bf16[64,4608]{1,0:T(8,128)(2,1)} %get-tuple-element.16), channel_id=1, source_target_pairs={{8,0},{16,8},{24,16},{28,24},{20,28},{12,20},{4,12},{0,4},{9,1},{1... | collective-permute-start | bytes 1769480 | tf_op jit(solution)/shard_map/ppermute | solution.py:172
  52.8 3.5 %copy-start.2 = (bf16[64,2048]{1,0:T(8,128)(2,1)S(1)}, bf16[64,2048]{1,0:T(8,128)(2,1)}, u32[]{:S(2)}) copy-start(bf16[64,2048]{1,0:T(8,128)(2,1)} %get-tuple-element.12) | copy-start | bytes 786436
  52.8 14.2 %copy-start = (bf16[512,7168]{1,0:T(8,128)(2,1)S(1)}, bf16[512,7168]{1,0:T(8,128)(2,1)}, u32[]{:S(2)}) copy-start(bf16[512,7168]{1,0:T(8,128)(2,1)} %rotate.3) | copy-start | bytes 22020100
  56.4 9.1 %collective-permute-start.2 = (bf16[64,2048]{1,0:T(8,128)(2,1)S(1)}, bf16[64,2048]{1,0:T(8,128)(2,1)S(1)}, u32[]{:S(2)}, u32[]{:S(2)}) collective-permute-start(bf16[64,2048]{1,0:T(8,128)(2,1)S(1)} %collective-permute-done), channel_id=1, source_target_pairs={{0,8},{8,16},{16,24},{24,28},{28,20},{20,12},{12,4},{4,0},{1,9},{9... | collective-permute-start | bytes 786440 | tf_op jit(solution)/shard_map/ppermute | solution.py:171
  58.4 8.6 %collective-permute-start.3 = (bf16[64,2048]{1,0:T(8,128)(2,1)S(1)}, bf16[64,2048]{1,0:T(8,128)(2,1)S(1)}, u32[]{:S(2)}, u32[]{:S(2)}) collective-permute-start(bf16[64,2048]{1,0:T(8,128)(2,1)S(1)} %collective-permute-done.1), channel_id=1, source_target_pairs={{8,0},{16,8},{24,16},{28,24},{20,28},{12,20},{4,12},{0,4},{9,1},{1... | collective-permute-start | bytes 786440 | tf_op jit(solution)/shard_map/ppermute | solution.py:172
  67.1 2.5 %copy-start.4 = (bf16[64,2560]{1,0:T(8,128)(2,1)S(1)}, bf16[64,2560]{1,0:T(8,128)(2,1)}, u32[]{:S(2)}) copy-start(bf16[64,2560]{1,0:T(8,128)(2,1)} %get-tuple-element.15) | copy-start | bytes 983044
  70.4 23.7 %copy-start.1 = (bf16[512,2048]{1,0:T(8,128)(2,1)S(1)}, bf16[512,2048]{1,0:T(8,128)(2,1)}, u32[]{:S(2)}) copy-start(bf16[512,2048]{1,0:T(8,128)(2,1)} %rotate.2) | copy-start | bytes 6291460
  70.4 9.3 %collective-permute-start.4 = (bf16[64,2048]{1,0:T(8,128)(2,1)S(1)}, bf16[64,2048]{1,0:T(8,128)(2,1)S(1)}, u32[]{:S(2)}, u32[]{:S(2)}) collective-permute-start(bf16[64,2048]{1,0:T(8,128)(2,1)S(1)} %collective-permute-done.2), channel_id=1, source_target_pairs={{0,8},{8,16},{16,24},{24,28},{28,20},{20,12},{12,4},{4,0},{1,9},{9... | collective-permute-start | bytes 786440 | tf_op jit(solution)/shard_map/ppermute | solution.py:171
  72.0 9.3 %collective-permute-start.5 = (bf16[64,2048]{1,0:T(8,128)(2,1)S(1)}, bf16[64,2048]{1,0:T(8,128)(2,1)S(1)}, u32[]{:S(2)}, u32[]{:S(2)}) collective-permute-start(bf16[64,2048]{1,0:T(8,128)(2,1)S(1)} %collective-permute-done.3), channel_id=1, source_target_pairs={{8,0},{16,8},{24,16},{28,24},{20,28},{12,20},{4,12},{0,4},{9,1},{1... | collective-permute-start | bytes 786440 | tf_op jit(solution)/shard_map/ppermute | solution.py:172
  72.5 29.5 %collective-permute-start.17 = (bf16[64,4608]{1,0:T(8,128)(2,1)}, bf16[64,4608]{1,0:T(8,128)(2,1)S(1)}, u32[]{:S(2)}, u32[]{:S(2)}) collective-permute-start(bf16[64,4608]{1,0:T(8,128)(2,1)} %collective-permute-done.13), channel_id=1, source_target_pairs={{0,8},{8,16},{16,24},{24,28},{28,20},{20,12},{12,4},{4,0},{1,9},{9... | collective-permute-start | bytes 1769480 | tf_op jit(solution)/shard_map/ppermute | solution.py:171
  74.2 29.4 %collective-permute-start.18 = (bf16[64,4608]{1,0:T(8,128)(2,1)}, bf16[64,4608]{1,0:T(8,128)(2,1)S(1)}, u32[]{:S(2)}, u32[]{:S(2)}) collective-permute-start(bf16[64,4608]{1,0:T(8,128)(2,1)} %collective-permute-done.14), channel_id=1, source_target_pairs={{8,0},{16,8},{24,16},{28,24},{20,28},{12,20},{4,12},{0,4},{9,1},{1... | collective-permute-start | bytes 1769480 | tf_op jit(solution)/shard_map/ppermute | solution.py:172
  79.7 13.0 %collective-permute-start.6 = (bf16[32,2048]{1,0:T(8,128)(2,1)S(1)}, bf16[32,2048]{1,0:T(8,128)(2,1)S(1)}, u32[]{:S(2)}, u32[]{:S(2)}) collective-permute-start(bf16[32,2048]{1,0:T(8,128)(2,1)S(1)} %slice.159), channel_id=1, source_target_pairs={{0,8},{8,16},{16,24},{24,28},{28,20},{20,12},{12,4},{4,0},{1,9},{9... | collective-permute-start | bytes 393224 | tf_op jit(solution)/shard_map/ppermute | solution.py:171
  81.3 12.7 %collective-permute-start.7 = (bf16[32,2048]{1,0:T(8,128)(2,1)S(1)}, bf16[32,2048]{1,0:T(8,128)(2,1)S(1)}, u32[]{:S(2)}, u32[]{:S(2)}) collective-permute-start(bf16[32,2048]{1,0:T(8,128)(2,1)S(1)} %slice.160), channel_id=1, source_target_pairs={{8,0},{16,8},{24,16},{28,24},{20,28},{12,20},{4,12},{0,4},{9,1},{1... | collective-permute-start | bytes 393224 | tf_op jit(solution)/shard_map/ppermute | solution.py:172
  95.5 4.8 %collective-permute-start.8 = (f32[128,512]{1,0:T(8,128)S(1)}, f32[128,512]{1,0:T(8,128)S(1)}, u32[]{:S(2)}, u32[]{:S(2)}) collective-permute-start(f32[128,512]{1,0:T(8,128)S(1)} %constant_dynamic-slice_fusion), channel_id=1, source_target_pairs={{0,1},{1,0},{2,3},{3,2},{4,5},{5,4},{6,7},{7,6},{8,9},{9,8},{10,11... | collective-permute-start | bytes 786440 | tf_op jit(solution)/shard_map/ppermute | solution.py:116
  95.6 10.6 %collective-permute-start.11 = (bf16[64,2560]{1,0:T(8,128)(2,1)S(1)}, bf16[64,2560]{1,0:T(8,128)(2,1)S(1)}, u32[]{:S(2)}, u32[]{:S(2)}) collective-permute-start(bf16[64,2560]{1,0:T(8,128)(2,1)S(1)} %copy-done.4), channel_id=1, source_target_pairs={{0,8},{8,16},{16,24},{24,28},{28,20},{20,12},{12,4},{4,0},{1,9},{9... | collective-permute-start | bytes 983048 | tf_op jit(solution)/shard_map/ppermute | solution.py:171
  97.3 10.6 %collective-permute-start.12 = (bf16[64,2560]{1,0:T(8,128)(2,1)S(1)}, bf16[64,2560]{1,0:T(8,128)(2,1)S(1)}, u32[]{:S(2)}, u32[]{:S(2)}) collective-permute-start(bf16[64,2560]{1,0:T(8,128)(2,1)S(1)} %copy-done.4), channel_id=1, source_target_pairs={{8,0},{16,8},{24,16},{28,24},{20,28},{12,20},{4,12},{0,4},{9,1},{1... | collective-permute-start | bytes 983048 | tf_op jit(solution)/shard_map/ppermute | solution.py:172
  100.4 10.1 %collective-permute-start.9 = (f32[128,512]{1,0:T(8,128)S(1)}, f32[128,512]{1,0:T(8,128)S(1)}, u32[]{:S(2)}, u32[]{:S(2)}) collective-permute-start(f32[128,512]{1,0:T(8,128)S(1)} %dynamic-slice_add_fusion), channel_id=1, source_target_pairs={{0,2},{1,3},{2,0},{3,1},{4,6},{5,7},{6,4},{7,5},{8,10},{9,11},{10,... | collective-permute-start | bytes 786440 | tf_op jit(solution)/shard_map/ppermute | solution.py:116
  102.0 26.4 %collective-permute-start.21 = (bf16[64,4608]{1,0:T(8,128)(2,1)S(1)}, bf16[64,4608]{1,0:T(8,128)(2,1)S(1)}, u32[]{:S(2)}, u32[]{:S(2)}) collective-permute-start(bf16[64,4608]{1,0:T(8,128)(2,1)S(1)} %collective-permute-done.17), channel_id=1, source_target_pairs={{0,8},{8,16},{16,24},{24,28},{28,20},{20,12},{12,4},{4,0},{1,9},{9... | collective-permute-start | bytes 1769480 | tf_op jit(solution)/shard_map/ppermute | solution.py:171
  103.6 26.5 %collective-permute-start.22 = (bf16[64,4608]{1,0:T(8,128)(2,1)S(1)}, bf16[64,4608]{1,0:T(8,128)(2,1)S(1)}, u32[]{:S(2)}, u32[]{:S(2)}) collective-permute-start(bf16[64,4608]{1,0:T(8,128)(2,1)S(1)} %collective-permute-done.18), channel_id=1, source_target_pairs={{8,0},{16,8},{24,16},{28,24},{20,28},{12,20},{4,12},{0,4},{9,1},{1... | collective-permute-start | bytes 1769480 | tf_op jit(solution)/shard_map/ppermute | solution.py:172
  106.2 19.2 %collective-permute-start.15 = (bf16[64,2560]{1,0:T(8,128)(2,1)S(1)}, bf16[64,2560]{1,0:T(8,128)(2,1)S(1)}, u32[]{:S(2)}, u32[]{:S(2)}) collective-permute-start(bf16[64,2560]{1,0:T(8,128)(2,1)S(1)} %collective-permute-done.11), channel_id=1, source_target_pairs={{0,8},{8,16},{16,24},{24,28},{28,20},{20,12},{12,4},{4,0},{1,9},{9... | collective-permute-start | bytes 983048 | tf_op jit(solution)/shard_map/ppermute | solution.py:171
  107.8 19.2 %collective-permute-start.16 = (bf16[64,2560]{1,0:T(8,128)(2,1)S(1)}, bf16[64,2560]{1,0:T(8,128)(2,1)S(1)}, u32[]{:S(2)}, u32[]{:S(2)}) collective-permute-start(bf16[64,2560]{1,0:T(8,128)(2,1)S(1)} %collective-permute-done.12), channel_id=1, source_target_pairs={{8,0},{16,8},{24,16},{28,24},{20,28},{12,20},{4,12},{0,4},{9,1},{1... | collective-permute-start | bytes 983048 | tf_op jit(solution)/shard_map/ppermute | solution.py:172
  110.5 17.7 %collective-permute-start.10 = (f32[128,512]{1,0:T(8,128)S(1)}, f32[128,512]{1,0:T(8,128)S(1)}, u32[]{:S(2)}, u32[]{:S(2)}) collective-permute-start(f32[128,512]{1,0:T(8,128)S(1)} %add.175), channel_id=1, source_target_pairs={{0,1},{1,0},{2,3},{3,2},{4,5},{5,4},{6,7},{7,6},{8,9},{9,8},{10,11... | collective-permute-start | bytes 786440 | tf_op jit(solution)/shard_map/ppermute | solution.py:116
  125.4 10.6 %collective-permute-start.19 = (bf16[64,2560]{1,0:T(8,128)(2,1)S(1)}, bf16[64,2560]{1,0:T(8,128)(2,1)S(1)}, u32[]{:S(2)}, u32[]{:S(2)}) collective-permute-start(bf16[64,2560]{1,0:T(8,128)(2,1)S(1)} %collective-permute-done.15), channel_id=1, source_target_pairs={{0,8},{8,16},{16,24},{24,28},{28,20},{20,12},{12,4},{4,0},{1,9},{9... | collective-permute-start | bytes 983048 | tf_op jit(solution)/shard_map/ppermute | solution.py:171
  127.0 10.7 %collective-permute-start.20 = (bf16[64,2560]{1,0:T(8,128)(2,1)S(1)}, bf16[64,2560]{1,0:T(8,128)(2,1)S(1)}, u32[]{:S(2)}, u32[]{:S(2)}) collective-permute-start(bf16[64,2560]{1,0:T(8,128)(2,1)S(1)} %collective-permute-done.16), channel_id=1, source_target_pairs={{8,0},{16,8},{24,16},{28,24},{20,28},{12,20},{4,12},{0,4},{9,1},{1... | collective-permute-start | bytes 983048 | tf_op jit(solution)/shard_map/ppermute | solution.py:172
  128.4 18.3 %collective-permute-start.25 = (bf16[32,4608]{1,0:T(8,128)(2,1)S(1)}, bf16[32,4608]{1,0:T(8,128)(2,1)S(1)}, u32[]{:S(2)}, u32[]{:S(2)}) collective-permute-start(bf16[32,4608]{1,0:T(8,128)(2,1)S(1)} %slice.190), channel_id=1, source_target_pairs={{0,8},{8,16},{16,24},{24,28},{28,20},{20,12},{12,4},{4,0},{1,9},{9... | collective-permute-start | bytes 884744 | tf_op jit(solution)/shard_map/ppermute | solution.py:171
  130.0 16.6 %collective-permute-start.26 = (bf16[32,4608]{1,0:T(8,128)(2,1)S(1)}, bf16[32,4608]{1,0:T(8,128)(2,1)S(1)}, u32[]{:S(2)}, u32[]{:S(2)}) collective-permute-start(bf16[32,4608]{1,0:T(8,128)(2,1)S(1)} %slice.191), channel_id=1, source_target_pairs={{8,0},{16,8},{24,16},{28,24},{20,28},{12,20},{4,12},{0,4},{9,1},{1... | collective-permute-start | bytes 884744 | tf_op jit(solution)/shard_map/ppermute | solution.py:172
  136.0 8.5 %collective-permute-start.23 = (bf16[32,2560]{1,0:T(8,128)(2,1)S(1)}, bf16[32,2560]{1,0:T(8,128)(2,1)S(1)}, u32[]{:S(2)}, u32[]{:S(2)}) collective-permute-start(bf16[32,2560]{1,0:T(8,128)(2,1)S(1)} %slice.186), channel_id=1, source_target_pairs={{0,8},{8,16},{16,24},{24,28},{28,20},{20,12},{12,4},{4,0},{1,9},{9... | collective-permute-start | bytes 491528 | tf_op jit(solution)/shard_map/ppermute | solution.py:171
  137.7 8.1 %collective-permute-start.24 = (bf16[32,2560]{1,0:T(8,128)(2,1)S(1)}, bf16[32,2560]{1,0:T(8,128)(2,1)S(1)}, u32[]{:S(2)}, u32[]{:S(2)}) collective-permute-start(bf16[32,2560]{1,0:T(8,128)(2,1)S(1)} %slice.187), channel_id=1, source_target_pairs={{8,0},{16,8},{24,16},{28,24},{20,28},{12,20},{4,12},{0,4},{9,1},{1... | collective-permute-start | bytes 491528 | tf_op jit(solution)/shard_map/ppermute | solution.py:172
  148.4 1.9 %collective-permute-start.27 = (f32[2,16]{1,0:T(2,128)S(1)}, f32[2,16]{1,0:T(2,128)S(1)}, u32[]{:S(2)}, u32[]{:S(2)}) collective-permute-start(f32[2,16]{1,0:T(2,128)S(1)} %select_reduce_fusion), channel_id=1, source_target_pairs={{0,1},{1,0},{2,3},{3,2},{4,5},{5,4},{6,7},{7,6},{8,9},{9,8},{10,11... | collective-permute-start | bytes 392 | tf_op jit(solution)/shard_map/ppermute | solution.py:116
  148.4 3.6 %collective-permute-start.28 = (f32[2,16]{1,0:T(2,128)S(1)}, f32[2,16]{1,0:T(2,128)S(1)}, u32[]{:S(2)}, u32[]{:S(2)}) collective-permute-start(f32[2,16]{1,0:T(2,128)S(1)} %select_reduce_fusion), channel_id=1, source_target_pairs={{0,2},{1,3},{2,0},{3,1},{4,6},{5,7},{6,4},{7,5},{8,10},{9,11},{10,... | collective-permute-start | bytes 392 | tf_op jit(solution)/shard_map/ppermute | solution.py:116
  150.0 3.0 %collective-permute-start.29 = (f32[2,16]{1,0:T(2,128)S(1)}, f32[2,16]{1,0:T(2,128)S(1)}, u32[]{:S(2)}, u32[]{:S(2)}) collective-permute-start(f32[2,16]{1,0:T(2,128)S(1)} %select_reduce_fusion), channel_id=1, source_target_pairs={{0,3},{1,2},{2,1},{3,0},{4,7},{5,6},{6,5},{7,4},{8,11},{9,10},{10,... | collective-permute-start | bytes 392 | tf_op jit(solution)/shard_map/ppermute | solution.py:116

commit v6 on v4

--- a/solution.py
+++ b/solution.py
@@ -10,15 +10,15 @@
 LEN = 128
 
 
-def params():
-    return pltpu.CompilerParams(vmem_limit_bytes=48 * 2**20)
+def params(mebibytes):
+    return pltpu.CompilerParams(vmem_limit_bytes=mebibytes * 2**20)
 
 
 def pick_rows(groups, owners, left_store, right_store):
     per = NQ // groups
     width_left = left_store.shape[2]
     width_right = right_store.shape[2]
-    cut = max(width_right // 4 // 256 * 256, 128)
+    cut = max(width_right * 5 // 14 // 128 * 128, 128)
 
     def kernel(owners_ref, left_ref, right_ref, first_out, second_out, sems):
         group = lax.axis_index("dp")
@@ -45,14 +45,15 @@
             copy.wait()
 
     shape = lambda width: jax.ShapeDtypeStruct((per * R, width), jnp.bfloat16)
+    in_vmem = pl.BlockSpec(memory_space=pltpu.VMEM)
     in_hbm = pl.BlockSpec(memory_space=pltpu.HBM)
     return pl.pallas_call(
         kernel,
         out_shape=(shape(width_left + cut), shape(width_right - cut)),
         in_specs=[pl.BlockSpec(memory_space=pltpu.SMEM), in_hbm, in_hbm],
-        out_specs=(in_hbm, in_hbm),
+        out_specs=(in_vmem, in_vmem),
         scratch_shapes=[pltpu.SemaphoreType.DMA((per, 3))],
-        compiler_params=params(),
+        compiler_params=params(62),
         name="pick_rows",
     )(owners, left_store, right_store)
 
@@ -86,7 +87,7 @@
             ],
             out_specs=pl.BlockSpec((2 * rows, each * width), lambda k, at: (0, k)),
         ),
-        compiler_params=params(),
+        compiler_params=params(56),
         cost_estimate=pl.CostEstimate(
             flops=2 * rows * total * width,
             bytes_accessed=2 * (3 * rows * total + total * width),
@@ -116,10 +117,10 @@
     return lax.ppermute(piece, "mp", [(i, i ^ distance) for i in range(shards)])
 
 
-def small_sum(array, shards):
+def small_sum(array, shards, most):
     distance = 1
     while distance < shards:
-        reach = min(4, shards // distance)
+        reach = min(most, shards // distance)
         array = sum([swapped(array, distance * k, shards) for k in range(1, reach)], array)
         distance *= reach
     return array
@@ -163,17 +164,13 @@
     width_left = left_store.shape[2]
     cut = own[0].shape[1] - width_left
 
-    across = lax.ppermute(
-        own[0][:, :width_left], "dp", [(ring[i], ring[i - reach]) for i in range(groups)]
-    )
     steps = [[], []]
     came = []
     for hops in range(1, reach + 1):
         for piece in range(2):
             ahead, behind = steps[piece][-1] if hops > 1 else (own[piece], own[piece])
             if hops == reach:
-                base = width_left if piece == 0 else 0
-                ahead, behind = ahead[: chunk // 2, base:], behind[chunk // 2 :, base:]
+                ahead, behind = ahead[: chunk // 2], behind[chunk // 2 :]
             ahead, behind = after((ahead, behind), came[-3:-1])
             got = (lax.ppermute(ahead, "dp", forward), lax.ppermute(behind, "dp", backward))
             steps[piece].append(got)
@@ -182,18 +179,23 @@
     grads = rotate(out_grads, out_basis, shard)
     acts = rotate(hidden_acts, in_basis, 0)
 
-    steps[0][-1], steps[1][-1] = lax.optimization_barrier((steps[0][-1], steps[1][-1]))
-    first = [own[0]] + [jnp.concatenate(pair, axis=0) for pair in steps[0]]
-    second = [own[1]] + [jnp.concatenate(pair, axis=0) for pair in steps[1]]
-    left_fac = [piece[:, :width_left] for piece in first[:-1]] + [across]
-    coefficient = sum_over_shards(
-        contract_rows(grads, jnp.concatenate(left_fac, axis=0)), shards, [came[-3]]
-    )
+    steps[0][-1] = after(steps[0][-1], came[-3])
+    first_own, second_own = after(own, came[0])
+    first = [first_own] + [jnp.concatenate(pair, axis=0) for pair in steps[0]]
+    second = [second_own] + [jnp.concatenate(pair, axis=0) for pair in steps[1]]
+    left_fac = [piece[:, :width_left] for piece in first]
+    coefficient = [
+        sum_over_shards(
+            contract_rows(grads, jnp.concatenate(left_fac[:-1], axis=0)), shards, [came[-3]]
+        ),
+        small_sum(contract_rows(grads, left_fac[-1]), shards, 2),
+    ]
+    coefficient = jnp.concatenate(coefficient, axis=1)
 
     parts = []
     at = 0
     for step in range(reach + 1):
-        projected = contract_rows(acts[:, :cut], first[step][:, -cut:])
+        projected = contract_rows(acts[:, :cut], first[step][:, width_left:])
         projected += contract_rows(acts[:, cut:], second[step])
         width = projected.shape[1]
         terms = coefficient[:, at : at + width] * projected
@@ -219,7 +221,7 @@
     owner = place // per
     hit = (source[:, None] == position(owner)[None, :]) & (row[:, None] == (place % per)[None, :])
     scores = jnp.sum(jnp.where(hit[None], partial[:, :, None], 0.0), axis=1)
-    return small_sum(scores, shards)
+    return small_sum(scores, shards, 4)
 
 
 def solution(mesh):

time: 114 us -> 110 us (0.965)
  starting transfers between devices: 39.6 us -> 22.7 us
  waiting for transfers between devices: 33.8 us -> 47.5 us
  local copies, waits for them, and re-layouts: 10.3 us -> 2.52 us
  Pallas kernels: 11.9 us -> 15.9 us
  matrix products: 16 us -> 17.9 us
    ppermute x8, starting transfers between devices: 24.2 us -> 2.01 us  [on_device(): lax.ppermute(ahead, 'dp', forward)]
    ppermute x8, starting transfers between devices: 6.89 us -> 15.4 us  [on_device(): lax.ppermute(behind, 'dp', backward)]
    ppermute x8, waiting for transfers between devices: 27.2 us -> 35.4 us  [on_device(): lax.ppermute(ahead, 'dp', forward)]
    ppermute x8, waiting for transfers between devices: 0.88 us -> 8.62 us  [on_device(): lax.ppermute(behind, 'dp', backward)]
    unnamed x22 -> x14, local copies, waits for them, and re-layouts: 6.89 us -> 1.16 us
    ppermute x1 -> x0, starting transfers between devices: 4.91 us -> none  [on_device(): lax.ppermute(own[0][:, :width_left], 'dp', [(ring[i], ring[i - reach]) fo...]
    pallas_call x2, Pallas kernels: 10 us -> 12.7 us  [rotate(): pl.pallas_call(kernel, out_shape=jax.ShapeDtypeStruct((2 * rows, total),...]
    ppermute x6 -> x8, waiting for transfers between devices: 5.73 us -> 3.5 us  [swapped(): return lax.ppermute(piece, 'mp', [(i, i ^ distance) for i in range(shards)])]
  transfers between devices with their start and end apart: 23 -> 24, of which waited for: 8 -> 11; matrix products, arithmetic and copies ran while one was open for 18% -> 18% of each run, Pallas kernels for 9% -> 12%
where the time goes in v6:
time: 110 us; the launch traced here: 109 us
  waiting for transfers between devices  47.5 us (43%)
  starting transfers between devices  22.7 us (21%)
  matrix products  17.9 us (16%)
  Pallas kernels  15.9 us (14%)
  local copies, waits for them, and re-layouts  2.52 us (2%)
  other arithmetic  2.23 us (2%)
    ppermute x8, waiting for transfers between devices, on_device(): lax.ppermute(ahead, 'dp', forward)  35.4 us
    dot_general x12, matrix products, contract_rows(): lax.dot_general(both, second, (((1,), (1,)), ((), ())), preferred_element...  17.9 us
    ppermute x8, starting transfers between devices, on_device(): lax.ppermute(behind, 'dp', backward)  15.4 us
    pallas_call x2, Pallas kernels, rotate(): pl.pallas_call(kernel, out_shape=jax.ShapeDtypeStruct((2 * rows, total),...  12.7 us
    ppermute x8, waiting for transfers between devices, on_device(): lax.ppermute(behind, 'dp', backward)  8.62 us
    ppermute x8, starting transfers between devices, swapped(): return lax.ppermute(piece, 'mp', [(i, i ^ distance) for i in range(shards)])  5.25 us
    ppermute x8, waiting for transfers between devices, swapped(): return lax.ppermute(piece, 'mp', [(i, i ^ distance) for i in range(shards)])  3.5 us
    pallas_call x1, Pallas kernels, pick_rows(): pl.pallas_call(kernel, out_shape=(shape(width_left + cut), shape(width_ri...  3.21 us
  transfers between devices with their start and end apart: 24, of which 11 were waited for; matrix products, arithmetic and copies ran while one was open for 18% of the time, Pallas kernels for 12%

profile of v6, /device:TPU:0, one launch (start us, length us, event | category | flops | bytes accessed | tf_op | source)
XLA Modules:
  0.0 109.3 jit_solution(3012985837670848308)
XLA Ops:
  0.0 3.2 %pick_rows.1 = (bf16[64,4608]{1,0:T(8,128)(2,1)}, bf16[64,4608]{1,0:T(8,128)(2,1)}) custom-call(s32[16]{0:T(128)} %owners_ref.1, bf16[1,512,2048]{2,1,0:T(8,128)(2,1)} %left_ref.1, bf16[1,512,7168]{2,1,0:T(8,128)(2,1)} %right_ref.1), custom_call_target="tpu_custom_call" | custom-call | tf_op jit(solution)/shard_map/pick_rows/pallas_call | solution.py:50
  3.2 3.0 %collective-permute-start.1 = (bf16[64,4608]{1,0:T(8,128)(2,1)}, bf16[64,4608]{1,0:T(8,128)(2,1)S(1)}, u32[]{:S(2)}, u32[]{:S(2)}) collective-permute-start(bf16[64,4608]{1,0:T(8,128)(2,1)} %get-tuple-element.26), channel_id=1, source_target_pairs={{8,0},{16,8},{24,16},{28,24},{20,28},{12,20},{4,12},{0,4},{9,1},{1... | collective-permute-start | bytes 1769480 | tf_op jit(solution)/shard_map/ppermute | solution.py:175
  6.2 0.1 collective-permute-start
  6.4 1.9 %collective-permute-start.5 = (bf16[64,4608]{1,0:T(8,128)(2,1)}, bf16[64,4608]{1,0:T(8,128)(2,1)S(1)}, u32[]{:S(2)}, u32[]{:S(2)}) collective-permute-start(bf16[64,4608]{1,0:T(8,128)(2,1)} %get-tuple-element.36), channel_id=1, source_target_pairs={{8,0},{16,8},{24,16},{28,24},{20,28},{12,20},{4,12},{0,4},{9,1},{1... | collective-permute-start | bytes 1769480 | tf_op jit(solution)/shard_map/ppermute | solution.py:175
  8.2 0.1 collective-permute-start.4
  8.4 0.2 convert_reduce_fusion
  8.6 0.1 concatenate.58
  8.8 0.1 concatenate.57
  8.9 3.4 %rotate.2 = bf16[512,2048]{1,0:T(8,128)(2,1)} custom-call(s32[1]{0:T(128)} %bitcast.shard_ref, bf16[256,8192]{1,0:T(8,128)(2,1)} %matrix_ref.2, bf16[4,512,512]{2,1,0:T(8,128)(2,1)} %basis_ref.2), custom_call_target="tpu_custom_call" | custom-call | flops 536870912 | bytes 5242880 | tf_op jit(solution)/shard_map/rotate/pallas_call | solution.py:78
  12.2 9.4 %rotate.3 = bf16[512,7168]{1,0:T(8,128)(2,1)} custom-call(s32[1]{0:T(128)} %constant.123.clone.1.shard_ref, bf16[256,7168]{1,0:T(8,128)(2,1)} %matrix_ref.3, bf16[28,256,256]{2,1,0:T(8,128)(2,1)} %basis_ref.3), custom_call_target="tpu_custom_call" | custom-call | flops 939524096 | bytes 14680064 | tf_op jit(solution)/shard_map/rotate/pallas_call | solution.py:78
  21.6 0.1 compare_and_fusion
  21.7 1.0 collective-permute-done
  22.7 1.0 collective-permute-start.2
  23.7 1.0 collective-permute-start.3
  24.7 8.6 %collective-permute-done.5 = bf16[64,4608]{1,0:T(8,128)(2,1)S(1)} collective-permute-done((bf16[64,4608]{1,0:T(8,128)(2,1)}, bf16[64,4608]{1,0:T(8,128)(2,1)S(1)}, u32[]{:S(2)}, u32[]{:S(2)}) %collective-permute-start.5) | collective-permute-done | bytes 589856 | tf_op jit(solution)/shard_map/ppermute | solution.py:175
  33.3 2.1 %collective-permute-done.4 = bf16[64,4608]{1,0:T(8,128)(2,1)} collective-permute-done((bf16[64,4608]{1,0:T(8,128)(2,1)}, bf16[64,4608]{1,0:T(8,128)(2,1)}, u32[]{:S(2)}, u32[]{:S(2)}) %collective-permute-start.4) | collective-permute-done | bytes 589856 | tf_op jit(solution)/shard_map/ppermute | solution.py:175
  35.4 0.1 collective-permute-start.9
  35.5 1.9 %collective-permute-start.10 = (bf16[64,4608]{1,0:T(8,128)(2,1)S(1)}, bf16[64,4608]{1,0:T(8,128)(2,1)S(1)}, u32[]{:S(2)}, u32[]{:S(2)}) collective-permute-start(bf16[64,4608]{1,0:T(8,128)(2,1)S(1)} %collective-permute-done.5), channel_id=1, source_target_pairs={{8,0},{16,8},{24,16},{28,24},{20,28},{12,20},{4,12},{0,4},{9,1},{1... | collective-permute-start | bytes 1769480 | tf_op jit(solution)/shard_map/ppermute | solution.py:175
  37.6 2.9 %fusion.24 = f32[512,128]{0,1:T(8,128)S(1)} fusion(bf16[512,7168]{1,0:T(8,128)(2,1)} %rotate.3, bf16[128,4608]{1,0:T(8,128)(2,1)S(1)} %constant_dynamic-update-slice_fusion), kind=kOutput, calls=%fused_computation.24 | convolution fusion | flops 335544320 | bytes 3538944 | tf_op jit(solution)/shard_map/dot_general | solution.py:102
  40.5 0.9 copy-done.1
  41.5 1.5 %fusion.8 = f32[512,64]{0,1:T(8,128)S(1)} fusion(bf16[64,4608]{1,0:T(8,128)(2,1)S(1)} %copy-done.4, bf16[512,7168]{1,0:T(8,128)(2,1)S(1)} %copy-done.1), kind=kOutput, calls=%fused_computation.8 | convolution fusion | flops 301989888 | bytes 5439488 | tf_op jit(solution)/shard_map/dot_general | solution.py:102
  43.0 0.9 fusion.26
  44.0 2.8 %fusion.6 = f32[512,128]{0,1:T(8,128)S(1)} fusion(bf16[512,7168]{1,0:T(8,128)(2,1)S(1)} %copy-done.1, bf16[64,4608]{1,0:T(8,128)(2,1)S(1)} %collective-permute-done.5, bf16[64,4608]{1,0:T(8,128)(2,1)} %collective-permute-done.4), kind=kOutput, calls=%fused_computation.6 | convolution fusion | flops 606339072 | bytes 6160384 | tf_op jit(solution)/shard_map/dot_general | solution.py:102
  46.8 1.2 %collective-permute-done.2 = bf16[64,4608]{1,0:T(8,128)(2,1)S(1)} collective-permute-done((bf16[64,4608]{1,0:T(8,128)(2,1)S(1)}, bf16[64,4608]{1,0:T(8,128)(2,1)S(1)}, u32[]{:S(2)}, u32[]{:S(2)}) %collective-permute-start.2) | collective-permute-done | bytes 589856 | tf_op jit(solution)/shard_map/ppermute | solution.py:175
  48.0 0.1 collective-permute-start.6
  48.1 1.9 %collective-permute-start.7 = (bf16[64,4608]{1,0:T(8,128)(2,1)S(1)}, bf16[64,4608]{1,0:T(8,128)(2,1)S(1)}, u32[]{:S(2)}, u32[]{:S(2)}) collective-permute-start(bf16[64,4608]{1,0:T(8,128)(2,1)S(1)} %collective-permute-done.3), channel_id=1, source_target_pairs={{8,0},{16,8},{24,16},{28,24},{20,28},{12,20},{4,12},{0,4},{9,1},{1... | collective-permute-start | bytes 1769480 | tf_op jit(solution)/shard_map/ppermute | solution.py:175
  50.1 1.0 fusion.22
  51.1 9.5 %collective-permute-done.9 = bf16[64,4608]{1,0:T(8,128)(2,1)S(1)} collective-permute-done((bf16[64,4608]{1,0:T(8,128)(2,1)}, bf16[64,4608]{1,0:T(8,128)(2,1)S(1)}, u32[]{:S(2)}, u32[]{:S(2)}) %collective-permute-start.9) | collective-permute-done | bytes 589856 | tf_op jit(solution)/shard_map/ppermute | solution.py:175
  60.6 0.1 collective-permute-start.11
  60.7 1.9 %collective-permute-start.12 = (bf16[64,4608]{1,0:T(8,128)(2,1)S(1)}, bf16[64,4608]{1,0:T(8,128)(2,1)S(1)}, u32[]{:S(2)}, u32[]{:S(2)}) collective-permute-start(bf16[64,4608]{1,0:T(8,128)(2,1)S(1)} %collective-permute-done.10), channel_id=1, source_target_pairs={{8,0},{16,8},{24,16},{28,24},{20,28},{12,20},{4,12},{0,4},{9,1},{1... | collective-permute-start | bytes 1769480 | tf_op jit(solution)/shard_map/ppermute | solution.py:175
  62.6 1.7 %fusion.4 = f32[512,128]{0,1:T(8,128)S(1)} fusion(bf16[512,7168]{1,0:T(8,128)(2,1)S(1)} %copy-done.1, bf16[64,4608]{1,0:T(8,128)(2,1)S(1)} %collective-permute-done.10, bf16[64,4608]{1,0:T(8,128)(2,1)S(1)} %collective-permute-done.9), kind=kOutput, calls=%fused_computation.4 | convolution fusion | flops 606339072 | bytes 6160384 | tf_op jit(solution)/shard_map/dot_general | solution.py:102
  64.3 8.9 %collective-permute-done.6 = bf16[64,4608]{1,0:T(8,128)(2,1)S(1)} collective-permute-done((bf16[64,4608]{1,0:T(8,128)(2,1)S(1)}, bf16[64,4608]{1,0:T(8,128)(2,1)S(1)}, u32[]{:S(2)}, u32[]{:S(2)}) %collective-permute-start.6) | collective-permute-done | bytes 589856 | tf_op jit(solution)/shard_map/ppermute | solution.py:175
  73.3 0.2 collective-permute-start.15
  73.5 1.9 %collective-permute-start.16 = (bf16[32,4608]{1,0:T(8,128)(2,1)S(1)}, bf16[32,4608]{1,0:T(8,128)(2,1)S(1)}, u32[]{:S(2)}, u32[]{:S(2)}) collective-permute-start(bf16[32,4608]{1,0:T(8,128)(2,1)S(1)} %slice.226), channel_id=1, source_target_pairs={{8,0},{16,8},{24,16},{28,24},{20,28},{12,20},{4,12},{0,4},{9,1},{1... | collective-permute-start | bytes 884744 | tf_op jit(solution)/shard_map/ppermute | solution.py:175
  75.5 1.2 %fusion.10 = f32[512,448]{0,1:T(8,128)S(1)} fusion(bf16[512,2048]{1,0:T(8,128)(2,1)S(1)} %copy-done, bf16[128,2048]{1,0:T(8,128)(2,1)S(1)} %slice.197, bf16[128,2048]{1,0:T(8,128)(2,1)S(1)} %slice.196, bf16[128,2048]{1,0:T(8,128)(2,1)S(1)} %slice.195, bf16[64,2048]{1,0:T(8,128)(2,1)S(1)} %slice.151), kind=kOutput, calls=%fused_computation.10 | convolution fusion | flops 946864128 | bytes 4849664 | tf_op jit(solution)/shard_map/dot_general | solution.py:102
  76.9 9.0 %collective-permute-done.11 = bf16[64,4608]{1,0:T(8,128)(2,1)S(1)} collective-permute-done((bf16[64,4608]{1,0:T(8,128)(2,1)S(1)}, bf16[64,4608]{1,0:T(8,128)(2,1)S(1)}, u32[]{:S(2)}, u32[]{:S(2)}) %collective-permute-start.11) | collective-permute-done | bytes 589856 | tf_op jit(solution)/shard_map/ppermute | solution.py:175
  85.9 1.7 %fusion.2 = f32[512,128]{0,1:T(8,128)S(1)} fusion(bf16[512,7168]{1,0:T(8,128)(2,1)S(1)} %copy-done.1, bf16[64,4608]{1,0:T(8,128)(2,1)S(1)} %collective-permute-done.12, bf16[64,4608]{1,0:T(8,128)(2,1)S(1)} %collective-permute-done.11), kind=kOutput, calls=%fused_computation.2 | convolution fusion | flops 606339072 | bytes 6160384 | tf_op jit(solution)/shard_map/dot_general | solution.py:102
  87.6 1.0 fusion.20
  88.6 0.2 collective-permute-start.19
  88.8 1.9 %collective-permute-start.20 = (bf16[32,4608]{1,0:T(8,128)(2,1)S(1)}, bf16[32,4608]{1,0:T(8,128)(2,1)S(1)}, u32[]{:S(2)}, u32[]{:S(2)}) collective-permute-start(bf16[32,4608]{1,0:T(8,128)(2,1)S(1)} %slice.234), channel_id=1, source_target_pairs={{8,0},{16,8},{24,16},{28,24},{20,28},{12,20},{4,12},{0,4},{9,1},{1... | collective-permute-start | bytes 884744 | tf_op jit(solution)/shard_map/ppermute | solution.py:175
  90.8 1.6 %collective-permute-start.13 = (f32[128,448]{0,1:T(8,128)S(1)}, f32[128,448]{0,1:T(8,128)S(1)}, u32[]{:S(2)}, u32[]{:S(2)}) collective-permute-start(f32[128,448]{0,1:T(8,128)S(1)} %dynamic-slice_add_fusion), channel_id=1, source_target_pairs={{0,2},{1,3},{2,0},{3,1},{4,6},{5,7},{6,4},{7,5},{8,10},{9,11},{10,... | collective-permute-start | bytes 688136 | tf_op jit(solution)/shard_map/ppermute | solution.py:117
  92.4 0.8 fusion.45
  93.2 0.1 collective-permute-start.17
  93.3 3.8 %collective-permute-done.19 = bf16[32,4608]{1,0:T(8,128)(2,1)S(1)} collective-permute-done((bf16[32,4608]{1,0:T(8,128)(2,1)S(1)}, bf16[32,4608]{1,0:T(8,128)(2,1)S(1)}, u32[]{:S(2)}, u32[]{:S(2)}) %collective-permute-start.19) | collective-permute-done | bytes 294944 | tf_op jit(solution)/shard_map/ppermute | solution.py:175
  97.0 1.5 %fusion = f32[512,64]{0,1:T(8,128)S(1)} fusion(bf16[512,7168]{1,0:T(8,128)(2,1)S(1)} %copy-done.1, bf16[32,4608]{1,0:T(8,128)(2,1)S(1)} %collective-permute-done.20, bf16[32,4608]{1,0:T(8,128)(2,1)S(1)} %collective-permute-done.19), kind=kOutput, calls=%fused_computation | convolution fusion | flops 303169536 | bytes 5439488 | tf_op jit(solution)/shard_map/dot_general | solution.py:102
  98.6 1.6 %collective-permute-start.18 = (f32[256,64]{0,1:T(8,128)S(1)}, f32[256,64]{0,1:T(8,128)S(1)}, u32[]{:S(2)}, u32[]{:S(2)}) collective-permute-start(f32[256,64]{0,1:T(8,128)S(1)} %fusion.68), channel_id=1, source_target_pairs={{0,2},{1,3},{2,0},{3,1},{4,6},{5,7},{6,4},{7,5},{8,10},{9,11},{10,... | collective-permute-start | bytes 196616 | tf_op jit(solution)/shard_map/ppermute | solution.py:117
  100.2 0.9 fusion.18
  101.2 0.1 collective-permute-start.14
  101.2 1.7 %collective-permute-done.18 = f32[256,64]{0,1:T(8,128)S(1)} collective-permute-done((f32[256,64]{0,1:T(8,128)S(1)}, f32[256,64]{0,1:T(8,128)S(1)}, u32[]{:S(2)}, u32[]{:S(2)}) %collective-permute-start.18) | collective-permute-done | bytes 65568 | tf_op jit(solution)/shard_map/ppermute | solution.py:117
  103.0 0.1 reduce_sum.68
  103.4 0.1 reduce_sum.64
  103.6 0.1 fusion.48
  103.8 0.2 reduce_sum.67
  104.1 0.1 reshape.273
  104.2 0.2 reduce_sum.66
  104.5 0.1 reshape.272
  104.5 0.2 reduce_sum.65
  104.8 0.1 concatenate.70
  104.9 0.1 select_reduce_fusion
  105.1 1.6 %collective-permute-start.22 = (f32[2,16]{1,0:T(2,128)S(1)}, f32[2,16]{1,0:T(2,128)S(1)}, u32[]{:S(2)}, u32[]{:S(2)}) collective-permute-start(f32[2,16]{1,0:T(2,128)S(1)} %select_reduce_fusion), channel_id=1, source_target_pairs={{0,2},{1,3},{2,0},{3,1},{4,6},{5,7},{6,4},{7,5},{8,10},{9,11},{10,... | collective-permute-start | bytes 392 | tf_op jit(solution)/shard_map/ppermute | solution.py:117
  106.6 0.3 collective-permute-start.21
  106.9 1.1 %collective-permute-done.23 = f32[2,16]{1,0:T(2,128)S(1)} collective-permute-done((f32[2,16]{1,0:T(2,128)S(1)}, f32[2,16]{1,0:T(2,128)S(1)}, u32[]{:S(2)}, u32[]{:S(2)}) %collective-permute-start.23) | collective-permute-done | bytes 160 | tf_op jit(solution)/shard_map/ppermute | solution.py:117
  108.0 0.6 collective-permute-done.22
  108.7 0.6 add_add_fusion
  (70 shorter events, 1.5 us)
Async XLA Ops:
  0.0 8.4 %copy-start.3 = (s32[16]{0:T(128)S(1)}, s32[16]{0:T(128)}, u32[]{:S(2)}) copy-start(s32[16]{0:T(128)} %owners_ref.1) | copy-start | bytes 196
  3.2 18.5 %collective-permute-start.1 = (bf16[64,4608]{1,0:T(8,128)(2,1)}, bf16[64,4608]{1,0:T(8,128)(2,1)S(1)}, u32[]{:S(2)}, u32[]{:S(2)}) collective-permute-start(bf16[64,4608]{1,0:T(8,128)(2,1)} %get-tuple-element.26), channel_id=1, source_target_pairs={{8,0},{16,8},{24,16},{28,24},{20,28},{12,20},{4,12},{0,4},{9,1},{1... | collective-permute-start | bytes 1769480 | tf_op jit(solution)/shard_map/ppermute | solution.py:175
  6.2 16.5 %collective-permute-start = (bf16[64,4608]{1,0:T(8,128)(2,1)}, bf16[64,4608]{1,0:T(8,128)(2,1)S(1)}, u32[]{:S(2)}, u32[]{:S(2)}) collective-permute-start(bf16[64,4608]{1,0:T(8,128)(2,1)} %get-tuple-element.26), channel_id=1, source_target_pairs={{0,8},{8,16},{16,24},{24,28},{28,20},{20,12},{12,4},{4,0},{1,9},{9... | collective-permute-start | bytes 1769480 | tf_op jit(solution)/shard_map/ppermute | solution.py:175
  6.4 26.9 %collective-permute-start.5 = (bf16[64,4608]{1,0:T(8,128)(2,1)}, bf16[64,4608]{1,0:T(8,128)(2,1)S(1)}, u32[]{:S(2)}, u32[]{:S(2)}) collective-permute-start(bf16[64,4608]{1,0:T(8,128)(2,1)} %get-tuple-element.36), channel_id=1, source_target_pairs={{8,0},{16,8},{24,16},{28,24},{20,28},{12,20},{4,12},{0,4},{9,1},{1... | collective-permute-start | bytes 1769480 | tf_op jit(solution)/shard_map/ppermute | solution.py:175
  8.2 27.2 %collective-permute-start.4 = (bf16[64,4608]{1,0:T(8,128)(2,1)}, bf16[64,4608]{1,0:T(8,128)(2,1)}, u32[]{:S(2)}, u32[]{:S(2)}) collective-permute-start(bf16[64,4608]{1,0:T(8,128)(2,1)} %get-tuple-element.36), channel_id=1, source_target_pairs={{0,8},{8,16},{16,24},{24,28},{28,20},{20,12},{12,4},{4,0},{1,9},{9... | collective-permute-start | bytes 1769480 | tf_op jit(solution)/shard_map/ppermute | solution.py:175
  22.7 25.3 %collective-permute-start.2 = (bf16[64,4608]{1,0:T(8,128)(2,1)S(1)}, bf16[64,4608]{1,0:T(8,128)(2,1)S(1)}, u32[]{:S(2)}, u32[]{:S(2)}) collective-permute-start(bf16[64,4608]{1,0:T(8,128)(2,1)S(1)} %collective-permute-done), channel_id=1, source_target_pairs={{0,8},{8,16},{16,24},{24,28},{28,20},{20,12},{12,4},{4,0},{1,9},{9... | collective-permute-start | bytes 1769480 | tf_op jit(solution)/shard_map/ppermute | solution.py:175
  23.7 24.2 %collective-permute-start.3 = (bf16[64,4608]{1,0:T(8,128)(2,1)S(1)}, bf16[64,4608]{1,0:T(8,128)(2,1)S(1)}, u32[]{:S(2)}, u32[]{:S(2)}) collective-permute-start(bf16[64,4608]{1,0:T(8,128)(2,1)S(1)} %collective-permute-done.1), channel_id=1, source_target_pairs={{8,0},{16,8},{24,16},{28,24},{20,28},{12,20},{4,12},{0,4},{9,1},{1... | collective-permute-start | bytes 1769480 | tf_op jit(solution)/shard_map/ppermute | solution.py:175
  35.4 25.2 %collective-permute-start.9 = (bf16[64,4608]{1,0:T(8,128)(2,1)}, bf16[64,4608]{1,0:T(8,128)(2,1)S(1)}, u32[]{:S(2)}, u32[]{:S(2)}) collective-permute-start(bf16[64,4608]{1,0:T(8,128)(2,1)} %collective-permute-done.4), channel_id=1, source_target_pairs={{0,8},{8,16},{16,24},{24,28},{28,20},{20,12},{12,4},{4,0},{1,9},{9... | collective-permute-start | bytes 1769480 | tf_op jit(solution)/shard_map/ppermute | solution.py:175
  35.5 25.1 %collective-permute-start.10 = (bf16[64,4608]{1,0:T(8,128)(2,1)S(1)}, bf16[64,4608]{1,0:T(8,128)(2,1)S(1)}, u32[]{:S(2)}, u32[]{:S(2)}) collective-permute-start(bf16[64,4608]{1,0:T(8,128)(2,1)S(1)} %collective-permute-done.5), channel_id=1, source_target_pairs={{8,0},{16,8},{24,16},{28,24},{20,28},{12,20},{4,12},{0,4},{9,1},{1... | collective-permute-start | bytes 1769480 | tf_op jit(solution)/shard_map/ppermute | solution.py:175
  37.5 3.9 %copy-start.1 = (bf16[512,7168]{1,0:T(8,128)(2,1)S(1)}, bf16[512,7168]{1,0:T(8,128)(2,1)}, u32[]{:S(2)}) copy-start(bf16[512,7168]{1,0:T(8,128)(2,1)} %rotate.3) | copy-start | bytes 22020100
  37.6 3.9 %copy-start.4 = (bf16[64,4608]{1,0:T(8,128)(2,1)S(1)}, bf16[64,4608]{1,0:T(8,128)(2,1)}, u32[]{:S(2)}) copy-start(bf16[64,4608]{1,0:T(8,128)(2,1)} %get-tuple-element.36) | copy-start | bytes 1769476
  41.5 1.5 %copy-start.2 = (bf16[64,4608]{1,0:T(8,128)(2,1)S(1)}, bf16[64,4608]{1,0:T(8,128)(2,1)}, u32[]{:S(2)}) copy-start(bf16[64,4608]{1,0:T(8,128)(2,1)} %get-tuple-element.26) | copy-start | bytes 1769476
  48.0 25.3 %collective-permute-start.6 = (bf16[64,4608]{1,0:T(8,128)(2,1)S(1)}, bf16[64,4608]{1,0:T(8,128)(2,1)S(1)}, u32[]{:S(2)}, u32[]{:S(2)}) collective-permute-start(bf16[64,4608]{1,0:T(8,128)(2,1)S(1)} %collective-permute-done.2), channel_id=1, source_target_pairs={{0,8},{8,16},{16,24},{24,28},{28,20},{20,12},{12,4},{4,0},{1,9},{9... | collective-permute-start | bytes 1769480 | tf_op jit(solution)/shard_map/ppermute | solution.py:175
  48.1 25.2 %collective-permute-start.7 = (bf16[64,4608]{1,0:T(8,128)(2,1)S(1)}, bf16[64,4608]{1,0:T(8,128)(2,1)S(1)}, u32[]{:S(2)}, u32[]{:S(2)}) collective-permute-start(bf16[64,4608]{1,0:T(8,128)(2,1)S(1)} %collective-permute-done.3), channel_id=1, source_target_pairs={{8,0},{16,8},{24,16},{28,24},{20,28},{12,20},{4,12},{0,4},{9,1},{1... | collective-permute-start | bytes 1769480 | tf_op jit(solution)/shard_map/ppermute | solution.py:175
  60.6 25.3 %collective-permute-start.11 = (bf16[64,4608]{1,0:T(8,128)(2,1)S(1)}, bf16[64,4608]{1,0:T(8,128)(2,1)S(1)}, u32[]{:S(2)}, u32[]{:S(2)}) collective-permute-start(bf16[64,4608]{1,0:T(8,128)(2,1)S(1)} %collective-permute-done.9), channel_id=1, source_target_pairs={{0,8},{8,16},{16,24},{24,28},{28,20},{20,12},{12,4},{4,0},{1,9},{9... | collective-permute-start | bytes 1769480 | tf_op jit(solution)/shard_map/ppermute | solution.py:175
  60.7 25.2 %collective-permute-start.12 = (bf16[64,4608]{1,0:T(8,128)(2,1)S(1)}, bf16[64,4608]{1,0:T(8,128)(2,1)S(1)}, u32[]{:S(2)}, u32[]{:S(2)}) collective-permute-start(bf16[64,4608]{1,0:T(8,128)(2,1)S(1)} %collective-permute-done.10), channel_id=1, source_target_pairs={{8,0},{16,8},{24,16},{28,24},{20,28},{12,20},{4,12},{0,4},{9,1},{1... | collective-permute-start | bytes 1769480 | tf_op jit(solution)/shard_map/ppermute | solution.py:175
  64.3 11.2 %copy-start = (bf16[512,2048]{1,0:T(8,128)(2,1)S(1)}, bf16[512,2048]{1,0:T(8,128)(2,1)}, u32[]{:S(2)}) copy-start(bf16[512,2048]{1,0:T(8,128)(2,1)} %rotate.2) | copy-start | bytes 6291460
  73.3 19.1 %collective-permute-start.15 = (bf16[32,4608]{1,0:T(8,128)(2,1)S(1)}, bf16[32,4608]{1,0:T(8,128)(2,1)S(1)}, u32[]{:S(2)}, u32[]{:S(2)}) collective-permute-start(bf16[32,4608]{1,0:T(8,128)(2,1)S(1)} %slice.225), channel_id=1, source_target_pairs={{0,8},{8,16},{16,24},{24,28},{28,20},{20,12},{12,4},{4,0},{1,9},{9... | collective-permute-start | bytes 884744 | tf_op jit(solution)/shard_map/ppermute | solution.py:175
  73.5 18.9 %collective-permute-start.16 = (bf16[32,4608]{1,0:T(8,128)(2,1)S(1)}, bf16[32,4608]{1,0:T(8,128)(2,1)S(1)}, u32[]{:S(2)}, u32[]{:S(2)}) collective-permute-start(bf16[32,4608]{1,0:T(8,128)(2,1)S(1)} %slice.226), channel_id=1, source_target_pairs={{8,0},{16,8},{24,16},{28,24},{20,28},{12,20},{4,12},{0,4},{9,1},{1... | collective-permute-start | bytes 884744 | tf_op jit(solution)/shard_map/ppermute | solution.py:175
  76.8 13.9 %collective-permute-start.8 = (f32[128,448]{0,1:T(8,128)S(1)}, f32[128,448]{0,1:T(8,128)S(1)}, u32[]{:S(2)}, u32[]{:S(2)}) collective-permute-start(f32[128,448]{0,1:T(8,128)S(1)} %constant_dynamic-slice_fusion), channel_id=1, source_target_pairs={{0,1},{1,0},{2,3},{3,2},{4,5},{5,4},{6,7},{7,6},{8,9},{9,8},{10,11... | collective-permute-start | bytes 688136 | tf_op jit(solution)/shard_map/ppermute | solution.py:117
  88.6 8.4 %collective-permute-start.19 = (bf16[32,4608]{1,0:T(8,128)(2,1)S(1)}, bf16[32,4608]{1,0:T(8,128)(2,1)S(1)}, u32[]{:S(2)}, u32[]{:S(2)}) collective-permute-start(bf16[32,4608]{1,0:T(8,128)(2,1)S(1)} %slice.233), channel_id=1, source_target_pairs={{0,8},{8,16},{16,24},{24,28},{28,20},{20,12},{12,4},{4,0},{1,9},{9... | collective-permute-start | bytes 884744 | tf_op jit(solution)/shard_map/ppermute | solution.py:175
  88.8 8.2 %collective-permute-start.20 = (bf16[32,4608]{1,0:T(8,128)(2,1)S(1)}, bf16[32,4608]{1,0:T(8,128)(2,1)S(1)}, u32[]{:S(2)}, u32[]{:S(2)}) collective-permute-start(bf16[32,4608]{1,0:T(8,128)(2,1)S(1)} %slice.234), channel_id=1, source_target_pairs={{8,0},{16,8},{24,16},{28,24},{20,28},{12,20},{4,12},{0,4},{9,1},{1... | collective-permute-start | bytes 884744 | tf_op jit(solution)/shard_map/ppermute | solution.py:175
  90.8 10.4 %collective-permute-start.13 = (f32[128,448]{0,1:T(8,128)S(1)}, f32[128,448]{0,1:T(8,128)S(1)}, u32[]{:S(2)}, u32[]{:S(2)}) collective-permute-start(f32[128,448]{0,1:T(8,128)S(1)} %dynamic-slice_add_fusion), channel_id=1, source_target_pairs={{0,2},{1,3},{2,0},{3,1},{4,6},{5,7},{6,4},{7,5},{8,10},{9,11},{10,... | collective-permute-start | bytes 688136 | tf_op jit(solution)/shard_map/ppermute | solution.py:117
  93.2 5.4 %collective-permute-start.17 = (f32[256,64]{0,1:T(8,128)S(1)}, f32[256,64]{0,1:T(8,128)S(1)}, u32[]{:S(2)}, u32[]{:S(2)}) collective-permute-start(f32[256,64]{0,1:T(8,128)S(1)} %slice_add_fusion.9), channel_id=1, source_target_pairs={{0,1},{1,0},{2,3},{3,2},{4,5},{5,4},{6,7},{7,6},{8,9},{9,8},{10,11... | collective-permute-start | bytes 196616 | tf_op jit(solution)/shard_map/ppermute | solution.py:117
  98.6 4.3 %collective-permute-start.18 = (f32[256,64]{0,1:T(8,128)S(1)}, f32[256,64]{0,1:T(8,128)S(1)}, u32[]{:S(2)}, u32[]{:S(2)}) collective-permute-start(f32[256,64]{0,1:T(8,128)S(1)} %fusion.68), channel_id=1, source_target_pairs={{0,2},{1,3},{2,0},{3,1},{4,6},{5,7},{6,4},{7,5},{8,10},{9,11},{10,... | collective-permute-start | bytes 196616 | tf_op jit(solution)/shard_map/ppermute | solution.py:117
  101.2 2.1 %collective-permute-start.14 = (f32[128,448]{0,1:T(8,128)S(1)}, f32[128,448]{0,1:T(8,128)S(1)}, u32[]{:S(2)}, u32[]{:S(2)}) collective-permute-start(f32[128,448]{0,1:T(8,128)S(1)} %add.184), channel_id=1, source_target_pairs={{0,1},{1,0},{2,3},{3,2},{4,5},{5,4},{6,7},{7,6},{8,9},{9,8},{10,11... | collective-permute-start | bytes 688136 | tf_op jit(solution)/shard_map/ppermute | solution.py:117
  105.0 3.0 %collective-permute-start.23 = (f32[2,16]{1,0:T(2,128)S(1)}, f32[2,16]{1,0:T(2,128)S(1)}, u32[]{:S(2)}, u32[]{:S(2)}) collective-permute-start(f32[2,16]{1,0:T(2,128)S(1)} %select_reduce_fusion), channel_id=1, source_target_pairs={{0,3},{1,2},{2,1},{3,0},{4,7},{5,6},{6,5},{7,4},{8,11},{9,10},{10,... | collective-permute-start | bytes 392 | tf_op jit(solution)/shard_map/ppermute | solution.py:117
  105.1 3.6 %collective-permute-start.22 = (f32[2,16]{1,0:T(2,128)S(1)}, f32[2,16]{1,0:T(2,128)S(1)}, u32[]{:S(2)}, u32[]{:S(2)}) collective-permute-start(f32[2,16]{1,0:T(2,128)S(1)} %select_reduce_fusion), channel_id=1, source_target_pairs={{0,2},{1,3},{2,0},{3,1},{4,6},{5,7},{6,4},{7,5},{8,10},{9,11},{10,... | collective-permute-start | bytes 392 | tf_op jit(solution)/shard_map/ppermute | solution.py:117
  106.6 2.1 %collective-permute-start.21 = (f32[2,16]{1,0:T(2,128)S(1)}, f32[2,16]{1,0:T(2,128)S(1)}, u32[]{:S(2)}, u32[]{:S(2)}) collective-permute-start(f32[2,16]{1,0:T(2,128)S(1)} %select_reduce_fusion), channel_id=1, source_target_pairs={{0,1},{1,0},{2,3},{3,2},{4,5},{5,4},{6,7},{7,6},{8,9},{9,8},{10,11... | collective-permute-start | bytes 392 | tf_op jit(solution)/shard_map/ppermute | solution.py:117

commit v7 on v6

--- a/solution.py
+++ b/solution.py
@@ -105,6 +105,37 @@
     return out[:rows] + out[rows:]
 
 
+def score(coefficients, projected, hit):
+    sequences = coefficients[0].shape[0] // LEN
+    count = len(coefficients)
+
+    def kernel(hit_ref, *refs):
+        out = jnp.zeros((sequences, NQ), jnp.float32)
+        at = 0
+        which, base = 0, 0
+        for part_ref in refs[count:-1]:
+            width = part_ref.shape[1]
+            if base == refs[which].shape[1]:
+                which, base = which + 1, 0
+            terms = refs[which][:, base : base + width] * part_ref[...]
+            base += width
+            out += jnp.dot(
+                jnp.sum(terms.reshape(sequences, LEN, width), axis=1) * (1.0 / LEN),
+                hit_ref[at : at + width, :],
+                precision=lax.Precision.HIGHEST,
+                preferred_element_type=jnp.float32,
+            )
+            at += width
+        refs[-1][...] = out
+
+    return pl.pallas_call(
+        kernel,
+        out_shape=jax.ShapeDtypeStruct((sequences, NQ), jnp.float32),
+        compiler_params=params(32),
+        name="score",
+    )(hit, *coefficients, *projected)
+
+
 def places(owners):
     at = jnp.arange(NQ, dtype=jnp.int32)
     before = (owners[None, :] < owners[:, None]) | (
@@ -117,8 +148,7 @@
     return lax.ppermute(piece, "mp", [(i, i ^ distance) for i in range(shards)])
 
 
-def small_sum(array, shards, most):
-    distance = 1
+def small_sum(array, shards, most, distance=1):
     while distance < shards:
         reach = min(most, shards // distance)
         array = sum([swapped(array, distance * k, shards) for k in range(1, reach)], array)
@@ -127,22 +157,16 @@
 
 
 def after(value, others):
-    return lax.optimization_barrier((value, others))[0] if others else value
-
-
-def sum_over_shards(matrix, shards, others):
-    others = iter(others)
+    return lax.optimization_barrier((value, others))[0] if jax.tree.leaves(others) else value
+
+
+def sum_over_shards(matrix, shards):
     shard = lax.axis_index("mp")
     bit = shard % 2
     half = matrix.shape[0] // 2
-
     mine = lax.dynamic_slice_in_dim(matrix, bit * half, half, 0)
-    got = swapped(lax.dynamic_slice_in_dim(matrix, (1 - bit) * half, half, 0), 1, shards)
-    mine = mine + after(got, next(others, None))
-    distance = 2
-    while distance < shards:
-        mine = mine + after(swapped(mine, distance, shards), next(others, None))
-        distance *= 2
+    mine = mine + swapped(lax.dynamic_slice_in_dim(matrix, (1 - bit) * half, half, 0), 1, shards)
+    mine = small_sum(mine, shards, 2, 2)
     other = swapped(mine, 1, shards)
     return jnp.where(
         bit == 0, jnp.concatenate([mine, other], axis=0), jnp.concatenate([other, mine], axis=0)
@@ -166,61 +190,67 @@
 
     steps = [[], []]
     came = []
-    for hops in range(1, reach + 1):
-        for piece in range(2):
-            ahead, behind = steps[piece][-1] if hops > 1 else (own[piece], own[piece])
-            if hops == reach:
-                ahead, behind = ahead[: chunk // 2], behind[chunk // 2 :]
-            ahead, behind = after((ahead, behind), came[-3:-1])
-            got = (lax.ppermute(ahead, "dp", forward), lax.ppermute(behind, "dp", backward))
-            steps[piece].append(got)
-            came.append(got)
+
+    def send(piece, hops, others):
+        ahead, behind = steps[piece][-1] if hops > 1 else (own[piece], own[piece])
+        if hops == reach:
+            ahead, behind = ahead[: chunk // 2], behind[chunk // 2 :]
+        ahead, behind = after((ahead, behind), others)
+        got = (lax.ppermute(ahead, "dp", forward), lax.ppermute(behind, "dp", backward))
+        steps[piece].append(got)
+        came.append(got)
+
+    def side_by_side(step):
+        return jnp.concatenate(step, axis=0)
 
     grads = rotate(out_grads, out_basis, shard)
     acts = rotate(hidden_acts, in_basis, 0)
 
-    steps[0][-1] = after(steps[0][-1], came[-3])
-    first_own, second_own = after(own, came[0])
-    first = [first_own] + [jnp.concatenate(pair, axis=0) for pair in steps[0]]
-    second = [second_own] + [jnp.concatenate(pair, axis=0) for pair in steps[1]]
-    left_fac = [piece[:, :width_left] for piece in first]
-    coefficient = [
-        sum_over_shards(
-            contract_rows(grads, jnp.concatenate(left_fac[:-1], axis=0)), shards, [came[-3]]
-        ),
-        small_sum(contract_rows(grads, left_fac[-1]), shards, 2),
+    for hops in range(1, reach):
+        send(0, hops, came[-3:-1])
+        send(1, hops, came[-3:-1])
+    own_later = after(own, came[0])
+    first = [side_by_side(step) for step in steps[0][:-1]] + [own_later[0]]
+    second = [side_by_side(step) for step in steps[1][:-1]] + [own_later[1]]
+    left_fac = jnp.concatenate([part[:, :width_left] for part in first], axis=0)
+    coefficients = [sum_over_shards(contract_rows(grads, left_fac), shards)]
+    send(0, reach, came[-3:-1] + coefficients)
+
+    first.append(side_by_side(steps[0][reach - 2]))
+    part = contract_rows(grads, first[-1][:, :width_left])
+    coefficients.append(small_sum(part, shards, 2))
+    send(1, reach, came[-3:-1])
+
+    last = after(steps[0][-1], came[-3])
+    second.append(side_by_side(after(steps[1][reach - 2], last)))
+    first.append(side_by_side(last))
+    part = contract_rows(grads, first[-1][:, :width_left])
+    part = part + swapped(part, 1, shards)
+    second.append(side_by_side(after(steps[1][-1], part)))
+    coefficients.append(small_sum(part, shards, 2, 2))
+
+    projected = [
+        contract_rows(acts[:, :cut], one[:, width_left:]) + contract_rows(acts[:, cut:], other)
+        for one, other in zip(first, second)
     ]
-    coefficient = jnp.concatenate(coefficient, axis=1)
-
-    parts = []
-    at = 0
-    for step in range(reach + 1):
-        projected = contract_rows(acts[:, :cut], first[step][:, width_left:])
-        projected += contract_rows(acts[:, cut:], second[step])
-        width = projected.shape[1]
-        terms = coefficient[:, at : at + width] * projected
-        parts.append(jnp.sum(terms.reshape(-1, LEN, width), axis=1))
-        at += width
-    partial = jnp.concatenate(parts, axis=1) / jnp.float32(LEN)
 
     def position(index):
         return jnp.where(index % 2 == 0, index // 2, groups - 1 - index // 2)
 
     here = position(group)
     row = jnp.arange(chunk, dtype=jnp.int32) // R
-    sources = [(here + 0 * row, row)]
-    for hops in range(1, reach + 1):
-        ahead, behind = here - hops + 0 * row, here + hops + 0 * row
-        if hops < reach:
-            sources += [(ahead, row), (behind, row)]
-        else:
-            cut = chunk // 2
-            sources += [(ahead[:cut], row[:cut]), (behind[cut:], row[cut:])]
+    sources = []
+    for hops in range(1, reach):
+        if hops == reach - 1:
+            sources.append((here + 0 * row, row))
+        sources += [(here - hops + 0 * row, row), (here + hops + 0 * row, row)]
+    half = chunk // 2
+    sources += [(here - reach + 0 * row[:half], row[:half]), (here + reach + 0 * row[half:], row[half:])]
     source = jnp.concatenate([s for s, _ in sources]) % groups
     row = jnp.concatenate([r for _, r in sources])
     owner = place // per
     hit = (source[:, None] == position(owner)[None, :]) & (row[:, None] == (place % per)[None, :])
-    scores = jnp.sum(jnp.where(hit[None], partial[:, :, None], 0.0), axis=1)
+    scores = score(coefficients, projected, hit.astype(jnp.float32))
     return small_sum(scores, shards, 4)
 
 

time: 110 us -> 107 us (0.973)
  matrix products: 17.9 us -> 15.4 us
  starting transfers between devices: 22.7 us -> 24.8 us
  local copies, waits for them, and re-layouts: 2.52 us -> 0.72 us
    ppermute x8 -> x10, waiting for transfers between devices: 3.5 us -> 10.3 us  [swapped(): return lax.ppermute(piece, 'mp', [(i, i ^ distance) for i in range(shards)])]
    ppermute x16, waiting for transfers between devices: 44 us -> 37.3 us  [the longest x8 28.6 us: send(): lax.ppermute(ahead, 'dp', forward)]
    dot_general x12 -> x13, matrix products: 17.9 us -> 15.4 us  [contract_rows(): lax.dot_general(both, second, (((1,), (1,)), ((), ())), preferred_element...]
    ppermute x8 -> x10, starting transfers between devices: 5.25 us -> 7.35 us  [swapped(): return lax.ppermute(piece, 'mp', [(i, i ^ distance) for i in range(shards)])]
  transfers between devices with their start and end apart: 24 -> 26, of which waited for: 11 -> 13; matrix products, arithmetic and copies ran while one was open for 18% -> 16% of each run, Pallas kernels for 12% -> 12%
where the time goes in v7:
time: 107 us
  waiting for transfers between devices  47.6 us (44%)
  starting transfers between devices  24.8 us (23%)
  Pallas kernels  16.3 us (15%)
  matrix products  15.4 us (14%)
  other arithmetic  1.38 us (1%)
    ppermute x8, waiting for transfers between devices, send(): lax.ppermute(ahead, 'dp', forward)  28.6 us
    dot_general x13, matrix products, contract_rows(): lax.dot_general(both, second, (((1,), (1,)), ((), ())), preferred_element...  15.4 us
    ppermute x8, starting transfers between devices, send(): lax.ppermute(behind, 'dp', backward)  15.1 us
    pallas_call x2, Pallas kernels, rotate(): pl.pallas_call(kernel, out_shape=jax.ShapeDtypeStruct((2 * rows, total),...  12.8 us
    ppermute x10, waiting for transfers between devices, swapped(): return lax.ppermute(piece, 'mp', [(i, i ^ distance) for i in range(shards)])  10.3 us
    ppermute x8, waiting for transfers between devices, send(): lax.ppermute(behind, 'dp', backward)  8.62 us
    ppermute x10, starting transfers between devices, swapped(): return lax.ppermute(piece, 'mp', [(i, i ^ distance) for i in range(shards)])  7.35 us
    pallas_call x1, Pallas kernels, pick_rows(): pl.pallas_call(kernel, out_shape=(shape(width_left + cut), shape(width_ri...  3.22 us
  transfers between devices with their start and end apart: 26, of which 13 were waited for; matrix products, arithmetic and copies ran while one was open for 16% of the time, Pallas kernels for 12%

profile of v7, /device:TPU:0, one launch (start us, length us, event | category | flops | bytes accessed | tf_op | source)
XLA Modules:
  0.0 106.7 jit_solution(9582735090878712039)
XLA Ops:
  0.0 3.2 %pick_rows.1 = (bf16[64,4608]{1,0:T(8,128)(2,1)}, bf16[64,4608]{1,0:T(8,128)(2,1)}) custom-call(s32[16]{0:T(128)} %owners_ref.1, bf16[1,512,2048]{2,1,0:T(8,128)(2,1)} %left_ref.1, bf16[1,512,7168]{2,1,0:T(8,128)(2,1)} %right_ref.1), custom_call_target="tpu_custom_call" | custom-call | tf_op jit(solution)/shard_map/pick_rows/pallas_call | solution.py:50
  3.2 3.0 %collective-permute-start.1 = (bf16[64,4608]{1,0:T(8,128)(2,1)}, bf16[64,4608]{1,0:T(8,128)(2,1)S(1)}, u32[]{:S(2)}, u32[]{:S(2)}) collective-permute-start(bf16[64,4608]{1,0:T(8,128)(2,1)} %get-tuple-element.31), channel_id=1, source_target_pairs={{8,0},{16,8},{24,16},{28,24},{20,28},{12,20},{4,12},{0,4},{9,1},{1... | collective-permute-start | bytes 1769480 | tf_op jit(solution)/shard_map/ppermute | solution.py:199
  6.2 0.1 collective-permute-start
  6.4 1.9 %collective-permute-start.8 = (bf16[64,4608]{1,0:T(8,128)(2,1)}, bf16[64,4608]{1,0:T(8,128)(2,1)S(1)}, u32[]{:S(2)}, u32[]{:S(2)}) collective-permute-start(bf16[64,4608]{1,0:T(8,128)(2,1)} %get-tuple-element.42), channel_id=1, source_target_pairs={{8,0},{16,8},{24,16},{28,24},{20,28},{12,20},{4,12},{0,4},{9,1},{1... | collective-permute-start | bytes 1769480 | tf_op jit(solution)/shard_map/ppermute | solution.py:199
  8.2 0.1 collective-permute-start.7
  8.4 0.2 convert_reduce_fusion
  8.6 0.1 concatenate.51
  8.8 0.1 concatenate.50
  8.9 3.3 %rotate.2 = bf16[512,2048]{1,0:T(8,128)(2,1)} custom-call(s32[1]{0:T(128)} %bitcast.shard_ref, bf16[256,8192]{1,0:T(8,128)(2,1)} %matrix_ref.2, bf16[4,512,512]{2,1,0:T(8,128)(2,1)} %basis_ref.2), custom_call_target="tpu_custom_call" | custom-call | flops 536870912 | bytes 5242880 | tf_op jit(solution)/shard_map/rotate/pallas_call | solution.py:78
  12.2 9.4 %rotate.3 = bf16[512,7168]{1,0:T(8,128)(2,1)} custom-call(s32[1]{0:T(128)} %constant.120.clone.1.shard_ref, bf16[256,7168]{1,0:T(8,128)(2,1)} %matrix_ref.3, bf16[28,256,256]{2,1,0:T(8,128)(2,1)} %basis_ref.3), custom_call_target="tpu_custom_call" | custom-call | flops 939524096 | bytes 14680064 | tf_op jit(solution)/shard_map/rotate/pallas_call | solution.py:78
  21.6 0.2 and_convert_fusion.hit_ref
  21.9 0.8 collective-permute-done
  22.7 1.2 %collective-permute-start.2 = (bf16[64,4608]{1,0:T(8,128)(2,1)S(1)}, bf16[64,4608]{1,0:T(8,128)(2,1)S(1)}, u32[]{:S(2)}, u32[]{:S(2)}) collective-permute-start(bf16[64,4608]{1,0:T(8,128)(2,1)S(1)} %collective-permute-done), channel_id=1, source_target_pairs={{0,8},{8,16},{16,24},{24,28},{28,20},{20,12},{12,4},{4,0},{1,9},{9... | collective-permute-start | bytes 1769480 | tf_op jit(solution)/shard_map/ppermute | solution.py:199
  23.9 0.8 collective-permute-start.3
  24.7 8.6 %collective-permute-done.8 = bf16[64,4608]{1,0:T(8,128)(2,1)S(1)} collective-permute-done((bf16[64,4608]{1,0:T(8,128)(2,1)}, bf16[64,4608]{1,0:T(8,128)(2,1)S(1)}, u32[]{:S(2)}, u32[]{:S(2)}) %collective-permute-start.8) | collective-permute-done | bytes 589856 | tf_op jit(solution)/shard_map/ppermute | solution.py:199
  33.3 2.0 %collective-permute-done.7 = bf16[64,4608]{1,0:T(8,128)(2,1)S(1)} collective-permute-done((bf16[64,4608]{1,0:T(8,128)(2,1)}, bf16[64,4608]{1,0:T(8,128)(2,1)S(1)}, u32[]{:S(2)}, u32[]{:S(2)}) %collective-permute-start.7) | collective-permute-done | bytes 589856 | tf_op jit(solution)/shard_map/ppermute | solution.py:199
  35.3 0.1 collective-permute-start.13
  35.4 1.9 %collective-permute-start.14 = (bf16[64,4608]{1,0:T(8,128)(2,1)S(1)}, bf16[64,4608]{1,0:T(8,128)(2,1)S(1)}, u32[]{:S(2)}, u32[]{:S(2)}) collective-permute-start(bf16[64,4608]{1,0:T(8,128)(2,1)S(1)} %collective-permute-done.8), channel_id=1, source_target_pairs={{8,0},{16,8},{24,16},{28,24},{20,28},{12,20},{4,12},{0,4},{9,1},{1... | collective-permute-start | bytes 1769480 | tf_op jit(solution)/shard_map/ppermute | solution.py:199
  37.4 2.6 %fusion.18 = f32[512,128]{1,0:T(8,128)S(1)} fusion(bf16[512,7168]{1,0:T(8,128)(2,1)} %rotate.3, bf16[128,4608]{1,0:T(8,128)(2,1)S(1)} %constant_dynamic-update-slice_fusion), kind=kOutput, calls=%fused_computation.18 | convolution fusion | flops 335544320 | bytes 3538944 | tf_op jit(solution)/shard_map/dot_general | solution.py:102
  40.0 1.4 %fusion.4 = f32[512,64]{1,0:T(8,128)S(1)} fusion(bf16[64,4608]{1,0:T(8,128)(2,1)S(1)} %copy-done.4, bf16[512,7168]{1,0:T(8,128)(2,1)S(1)} %copy-done), kind=kOutput, calls=%fused_computation.4 | convolution fusion | flops 301989888 | bytes 5439488 | tf_op jit(solution)/shard_map/dot_general | solution.py:102
  41.4 1.4 %fusion.8 = f32[512,128]{1,0:T(8,128)S(1)} fusion(bf16[512,7168]{1,0:T(8,128)(2,1)S(1)} %copy-done, bf16[64,4608]{1,0:T(8,128)(2,1)S(1)} %collective-permute-done.8, bf16[64,4608]{1,0:T(8,128)(2,1)S(1)} %collective-permute-done.7), kind=kOutput, calls=%fused_computation.8 | convolution fusion | flops 606339072 | bytes 6160384 | tf_op jit(solution)/shard_map/dot_general | solution.py:102
  42.9 0.8 fusion.14
  43.8 4.2 %collective-permute-done.2 = bf16[64,4608]{1,0:T(8,128)(2,1)S(1)} collective-permute-done((bf16[64,4608]{1,0:T(8,128)(2,1)S(1)}, bf16[64,4608]{1,0:T(8,128)(2,1)S(1)}, u32[]{:S(2)}, u32[]{:S(2)}) %collective-permute-start.2) | collective-permute-done | bytes 589856 | tf_op jit(solution)/shard_map/ppermute | solution.py:199
  48.0 0.1 collective-permute-start.9
  48.1 1.9 %collective-permute-start.10 = (bf16[64,4608]{1,0:T(8,128)(2,1)S(1)}, bf16[64,4608]{1,0:T(8,128)(2,1)S(1)}, u32[]{:S(2)}, u32[]{:S(2)}) collective-permute-start(bf16[64,4608]{1,0:T(8,128)(2,1)S(1)} %collective-permute-done.3), channel_id=1, source_target_pairs={{8,0},{16,8},{24,16},{28,24},{20,28},{12,20},{4,12},{0,4},{9,1},{1... | collective-permute-start | bytes 1769480 | tf_op jit(solution)/shard_map/ppermute | solution.py:199
  50.0 10.6 %collective-permute-done.13 = bf16[64,4608]{1,0:T(8,128)(2,1)S(1)} collective-permute-done((bf16[64,4608]{1,0:T(8,128)(2,1)S(1)}, bf16[64,4608]{1,0:T(8,128)(2,1)S(1)}, u32[]{:S(2)}, u32[]{:S(2)}) %collective-permute-start.13) | collective-permute-done | bytes 589856 | tf_op jit(solution)/shard_map/ppermute | solution.py:199
  60.6 0.1 collective-permute-start.17
  60.7 1.9 %collective-permute-start.18 = (bf16[64,4608]{1,0:T(8,128)(2,1)S(1)}, bf16[64,4608]{1,0:T(8,128)(2,1)S(1)}, u32[]{:S(2)}, u32[]{:S(2)}) collective-permute-start(bf16[64,4608]{1,0:T(8,128)(2,1)S(1)} %collective-permute-done.14), channel_id=1, source_target_pairs={{8,0},{16,8},{24,16},{28,24},{20,28},{12,20},{4,12},{0,4},{9,1},{1... | collective-permute-start | bytes 1769480 | tf_op jit(solution)/shard_map/ppermute | solution.py:199
  62.8 1.3 %fusion.20 = f32[512,320]{1,0:T(8,128)S(1)} fusion(bf16[512,2048]{1,0:T(8,128)(2,1)S(1)} %copy-done.1, bf16[64,2048]{1,0:T(8,128)(2,1)S(1)} %slice.139, bf16[128,2048]{1,0:T(8,128)(2,1)S(1)} %slice.180, bf16[128,2048]{1,0:T(8,128)(2,1)S(1)} %slice.179), kind=kOutput, calls=%fused_computation.20 | convolution fusion | flops 675020800 | bytes 4063232 | tf_op jit(solution)/shard_map/dot_general | solution.py:102
  64.2 0.1 collective-permute-start.4
  64.2 1.4 %fusion.6 = f32[512,128]{1,0:T(8,128)S(1)} fusion(bf16[512,7168]{1,0:T(8,128)(2,1)S(1)} %copy-done, bf16[64,4608]{1,0:T(8,128)(2,1)S(1)} %collective-permute-done.14, bf16[64,4608]{1,0:T(8,128)(2,1)S(1)} %collective-permute-done.13), kind=kOutput, calls=%fused_computation.6 | convolution fusion | flops 606339072 | bytes 6160384 | tf_op jit(solution)/shard_map/dot_general | solution.py:102
  65.6 0.0 collective-permute-done.4
  65.7 1.6 %collective-permute-start.5 = (f32[128,320]{1,0:T(8,128)S(1)}, f32[128,320]{1,0:T(8,128)S(1)}, u32[]{:S(2)}, u32[]{:S(2)}) collective-permute-start(f32[128,320]{1,0:T(8,128)S(1)} %dynamic-slice_add_fusion), channel_id=1, source_target_pairs={{0,2},{1,3},{2,0},{3,1},{4,6},{5,7},{6,4},{7,5},{8,10},{9,11},{10,... | collective-permute-start | bytes 491528 | tf_op jit(solution)/shard_map/ppermute | solution.py:148
  67.3 0.8 fusion.16
  68.1 4.9 %collective-permute-done.5 = f32[128,320]{1,0:T(8,128)S(1)} collective-permute-done((f32[128,320]{1,0:T(8,128)S(1)}, f32[128,320]{1,0:T(8,128)S(1)}, u32[]{:S(2)}, u32[]{:S(2)}) %collective-permute-start.5) | collective-permute-done | bytes 163872 | tf_op jit(solution)/shard_map/ppermute | solution.py:148
  73.1 0.1 collective-permute-start.6
  73.1 0.1 collective-permute-done.9
  73.3 0.0 collective-permute-done.10
  73.3 0.7 fusion.41
  74.1 0.5 collective-permute-start.11
  74.6 0.0 collective-permute-done.6
  74.7 0.4 collective-permute-start.15
  75.1 1.7 %collective-permute-start.16 = (bf16[32,4608]{1,0:T(8,128)(2,1)S(1)}, bf16[32,4608]{1,0:T(8,128)(2,1)S(1)}, u32[]{:S(2)}, u32[]{:S(2)}) collective-permute-start(bf16[32,4608]{1,0:T(8,128)(2,1)S(1)} %slice.187), channel_id=1, source_target_pairs={{8,0},{16,8},{24,16},{28,24},{20,28},{12,20},{4,12},{0,4},{9,1},{1... | collective-permute-start | bytes 884744 | tf_op jit(solution)/shard_map/ppermute | solution.py:199
  76.8 1.6 %collective-permute-start.12 = (f32[256,128]{1,0:T(8,128)S(1)}, f32[256,128]{1,0:T(8,128)S(1)}, u32[]{:S(2)}, u32[]{:S(2)}) collective-permute-start(f32[256,128]{1,0:T(8,128)S(1)} %fusion.65), channel_id=1, source_target_pairs={{0,2},{1,3},{2,0},{3,1},{4,6},{5,7},{6,4},{7,5},{8,10},{9,11},{10,... | collective-permute-start | bytes 393224 | tf_op jit(solution)/shard_map/ppermute | solution.py:148
  78.4 0.8 fusion.12
  79.2 6.6 %collective-permute-done.17 = bf16[64,4608]{1,0:T(8,128)(2,1)S(1)} collective-permute-done((bf16[64,4608]{1,0:T(8,128)(2,1)S(1)}, bf16[64,4608]{1,0:T(8,128)(2,1)S(1)}, u32[]{:S(2)}, u32[]{:S(2)}) %collective-permute-start.17) | collective-permute-done | bytes 589856 | tf_op jit(solution)/shard_map/ppermute | solution.py:199
  85.9 0.2 collective-permute-start.21
  86.1 1.9 %collective-permute-start.22 = (bf16[32,4608]{1,0:T(8,128)(2,1)S(1)}, bf16[32,4608]{1,0:T(8,128)(2,1)S(1)}, u32[]{:S(2)}, u32[]{:S(2)}) collective-permute-start(bf16[32,4608]{1,0:T(8,128)(2,1)S(1)} %slice.216), channel_id=1, source_target_pairs={{8,0},{16,8},{24,16},{28,24},{20,28},{12,20},{4,12},{0,4},{9,1},{1... | collective-permute-start | bytes 884744 | tf_op jit(solution)/shard_map/ppermute | solution.py:199
  88.0 4.2 %collective-permute-done.15 = bf16[32,4608]{1,0:T(8,128)(2,1)S(1)} collective-permute-done((bf16[32,4608]{1,0:T(8,128)(2,1)S(1)}, bf16[32,4608]{1,0:T(8,128)(2,1)S(1)}, u32[]{:S(2)}, u32[]{:S(2)}) %collective-permute-start.15) | collective-permute-done | bytes 294944 | tf_op jit(solution)/shard_map/ppermute | solution.py:199
  92.3 0.7 fusion.45
  93.0 0.8 fusion.10
  93.8 0.1 collective-permute-start.19
  93.9 1.4 %fusion.2 = f32[512,128]{1,0:T(8,128)S(1)} fusion(bf16[512,7168]{1,0:T(8,128)(2,1)S(1)} %copy-done, bf16[64,4608]{1,0:T(8,128)(2,1)S(1)} %collective-permute-done.18, bf16[64,4608]{1,0:T(8,128)(2,1)S(1)} %collective-permute-done.17), kind=kOutput, calls=%fused_computation.2 | convolution fusion | flops 606339072 | bytes 6160384 | tf_op jit(solution)/shard_map/dot_general | solution.py:102
  95.3 1.6 %collective-permute-start.20 = (f32[256,64]{1,0:T(8,128)S(1)}, f32[256,64]{1,0:T(8,128)S(1)}, u32[]{:S(2)}, u32[]{:S(2)}) collective-permute-start(f32[256,64]{1,0:T(8,128)S(1)} %fusion.64), channel_id=1, source_target_pairs={{0,2},{1,3},{2,0},{3,1},{4,6},{5,7},{6,4},{7,5},{8,10},{9,11},{10,... | collective-permute-start | bytes 196616 | tf_op jit(solution)/shard_map/ppermute | solution.py:148
  96.9 0.1 collective-permute-done.21
  97.1 1.4 %fusion = f32[512,64]{1,0:T(8,128)S(1)} fusion(bf16[512,7168]{1,0:T(8,128)(2,1)S(1)} %copy-done, bf16[32,4608]{1,0:T(8,128)(2,1)S(1)} %collective-permute-done.22, bf16[32,4608]{1,0:T(8,128)(2,1)S(1)} %collective-permute-done.21), kind=kOutput, calls=%fused_computation | convolution fusion | flops 303169536 | bytes 5439488 | tf_op jit(solution)/shard_map/dot_general | solution.py:102
  98.5 2.8 %collective-permute-done.20 = f32[256,64]{1,0:T(8,128)S(1)} collective-permute-done((f32[256,64]{1,0:T(8,128)S(1)}, f32[256,64]{1,0:T(8,128)S(1)}, u32[]{:S(2)}, u32[]{:S(2)}) %collective-permute-start.20) | collective-permute-done | bytes 65568 | tf_op jit(solution)/shard_map/ppermute | solution.py:148
  101.3 0.3 score.1
  101.7 0.8 collective-permute-start.25
  102.5 0.7 collective-permute-start.24
  103.3 0.3 collective-permute-start.23
  103.6 1.1 %collective-permute-done.25 = f32[2,16]{1,0:T(2,128)S(1)} collective-permute-done((f32[2,16]{1,0:T(2,128)S(1)}, f32[2,16]{1,0:T(2,128)S(1)}, u32[]{:S(2)}, u32[]{:S(2)}) %collective-permute-start.25) | collective-permute-done | bytes 160 | tf_op jit(solution)/shard_map/ppermute | solution.py:148
  104.7 1.4 %collective-permute-done.24 = f32[2,16]{1,0:T(2,128)S(1)} collective-permute-done((f32[2,16]{1,0:T(2,128)S(1)}, f32[2,16]{1,0:T(2,128)S(1)}, u32[]{:S(2)}, u32[]{:S(2)}) %collective-permute-start.24) | collective-permute-done | bytes 160 | tf_op jit(solution)/shard_map/ppermute | solution.py:148
  106.1 0.6 add_add_fusion
  (63 shorter events, 1.0 us)
Async XLA Ops:
  0.0 8.4 %copy-start.3 = (s32[16]{0:T(128)S(1)}, s32[16]{0:T(128)}, u32[]{:S(2)}) copy-start(s32[16]{0:T(128)} %owners_ref.1) | copy-start | bytes 196
  3.2 18.6 %collective-permute-start.1 = (bf16[64,4608]{1,0:T(8,128)(2,1)}, bf16[64,4608]{1,0:T(8,128)(2,1)S(1)}, u32[]{:S(2)}, u32[]{:S(2)}) collective-permute-start(bf16[64,4608]{1,0:T(8,128)(2,1)} %get-tuple-element.31), channel_id=1, source_target_pairs={{8,0},{16,8},{24,16},{28,24},{20,28},{12,20},{4,12},{0,4},{9,1},{1... | collective-permute-start | bytes 1769480 | tf_op jit(solution)/shard_map/ppermute | solution.py:199
  6.2 16.5 %collective-permute-start = (bf16[64,4608]{1,0:T(8,128)(2,1)}, bf16[64,4608]{1,0:T(8,128)(2,1)S(1)}, u32[]{:S(2)}, u32[]{:S(2)}) collective-permute-start(bf16[64,4608]{1,0:T(8,128)(2,1)} %get-tuple-element.31), channel_id=1, source_target_pairs={{0,8},{8,16},{16,24},{24,28},{28,20},{20,12},{12,4},{4,0},{1,9},{9... | collective-permute-start | bytes 1769480 | tf_op jit(solution)/shard_map/ppermute | solution.py:199
  6.4 26.9 %collective-permute-start.8 = (bf16[64,4608]{1,0:T(8,128)(2,1)}, bf16[64,4608]{1,0:T(8,128)(2,1)S(1)}, u32[]{:S(2)}, u32[]{:S(2)}) collective-permute-start(bf16[64,4608]{1,0:T(8,128)(2,1)} %get-tuple-element.42), channel_id=1, source_target_pairs={{8,0},{16,8},{24,16},{28,24},{20,28},{12,20},{4,12},{0,4},{9,1},{1... | collective-permute-start | bytes 1769480 | tf_op jit(solution)/shard_map/ppermute | solution.py:199
  8.2 27.1 %collective-permute-start.7 = (bf16[64,4608]{1,0:T(8,128)(2,1)}, bf16[64,4608]{1,0:T(8,128)(2,1)S(1)}, u32[]{:S(2)}, u32[]{:S(2)}) collective-permute-start(bf16[64,4608]{1,0:T(8,128)(2,1)} %get-tuple-element.42), channel_id=1, source_target_pairs={{0,8},{8,16},{16,24},{24,28},{28,20},{20,12},{12,4},{4,0},{1,9},{9... | collective-permute-start | bytes 1769480 | tf_op jit(solution)/shard_map/ppermute | solution.py:199
  12.2 27.8 %copy-start.4 = (bf16[64,4608]{1,0:T(8,128)(2,1)S(1)}, bf16[64,4608]{1,0:T(8,128)(2,1)}, u32[]{:S(2)}) copy-start(bf16[64,4608]{1,0:T(8,128)(2,1)} %get-tuple-element.42) | copy-start | bytes 1769476
  21.6 18.4 %copy-start = (bf16[512,7168]{1,0:T(8,128)(2,1)S(1)}, bf16[512,7168]{1,0:T(8,128)(2,1)}, u32[]{:S(2)}) copy-start(bf16[512,7168]{1,0:T(8,128)(2,1)} %rotate.3) | copy-start | bytes 22020100
  22.7 25.3 %collective-permute-start.2 = (bf16[64,4608]{1,0:T(8,128)(2,1)S(1)}, bf16[64,4608]{1,0:T(8,128)(2,1)S(1)}, u32[]{:S(2)}, u32[]{:S(2)}) collective-permute-start(bf16[64,4608]{1,0:T(8,128)(2,1)S(1)} %collective-permute-done), channel_id=1, source_target_pairs={{0,8},{8,16},{16,24},{24,28},{28,20},{20,12},{12,4},{4,0},{1,9},{9... | collective-permute-start | bytes 1769480 | tf_op jit(solution)/shard_map/ppermute | solution.py:199
  23.9 24.1 %collective-permute-start.3 = (bf16[64,4608]{1,0:T(8,128)(2,1)S(1)}, bf16[64,4608]{1,0:T(8,128)(2,1)S(1)}, u32[]{:S(2)}, u32[]{:S(2)}) collective-permute-start(bf16[64,4608]{1,0:T(8,128)(2,1)S(1)} %collective-permute-done.1), channel_id=1, source_target_pairs={{8,0},{16,8},{24,16},{28,24},{20,28},{12,20},{4,12},{0,4},{9,1},{1... | collective-permute-start | bytes 1769480 | tf_op jit(solution)/shard_map/ppermute | solution.py:199
  35.3 25.3 %collective-permute-start.13 = (bf16[64,4608]{1,0:T(8,128)(2,1)S(1)}, bf16[64,4608]{1,0:T(8,128)(2,1)S(1)}, u32[]{:S(2)}, u32[]{:S(2)}) collective-permute-start(bf16[64,4608]{1,0:T(8,128)(2,1)S(1)} %collective-permute-done.7), channel_id=1, source_target_pairs={{0,8},{8,16},{16,24},{24,28},{28,20},{20,12},{12,4},{4,0},{1,9},{9... | collective-permute-start | bytes 1769480 | tf_op jit(solution)/shard_map/ppermute | solution.py:199
  35.4 25.2 %collective-permute-start.14 = (bf16[64,4608]{1,0:T(8,128)(2,1)S(1)}, bf16[64,4608]{1,0:T(8,128)(2,1)S(1)}, u32[]{:S(2)}, u32[]{:S(2)}) collective-permute-start(bf16[64,4608]{1,0:T(8,128)(2,1)S(1)} %collective-permute-done.8), channel_id=1, source_target_pairs={{8,0},{16,8},{24,16},{28,24},{20,28},{12,20},{4,12},{0,4},{9,1},{1... | collective-permute-start | bytes 1769480 | tf_op jit(solution)/shard_map/ppermute | solution.py:199
  41.4 1.5 %copy-start.2 = (bf16[64,4608]{1,0:T(8,128)(2,1)S(1)}, bf16[64,4608]{1,0:T(8,128)(2,1)}, u32[]{:S(2)}) copy-start(bf16[64,4608]{1,0:T(8,128)(2,1)} %get-tuple-element.31) | copy-start | bytes 1769476
  43.7 19.0 %copy-start.1 = (bf16[512,2048]{1,0:T(8,128)(2,1)S(1)}, bf16[512,2048]{1,0:T(8,128)(2,1)}, u32[]{:S(2)}) copy-start(bf16[512,2048]{1,0:T(8,128)(2,1)} %rotate.2) | copy-start | bytes 6291460
  48.0 25.3 %collective-permute-start.9 = (bf16[64,4608]{1,0:T(8,128)(2,1)S(1)}, bf16[64,4608]{1,0:T(8,128)(2,1)S(1)}, u32[]{:S(2)}, u32[]{:S(2)}) collective-permute-start(bf16[64,4608]{1,0:T(8,128)(2,1)S(1)} %collective-permute-done.2), channel_id=1, source_target_pairs={{0,8},{8,16},{16,24},{24,28},{28,20},{20,12},{12,4},{4,0},{1,9},{9... | collective-permute-start | bytes 1769480 | tf_op jit(solution)/shard_map/ppermute | solution.py:199
  48.1 25.2 %collective-permute-start.10 = (bf16[64,4608]{1,0:T(8,128)(2,1)S(1)}, bf16[64,4608]{1,0:T(8,128)(2,1)S(1)}, u32[]{:S(2)}, u32[]{:S(2)}) collective-permute-start(bf16[64,4608]{1,0:T(8,128)(2,1)S(1)} %collective-permute-done.3), channel_id=1, source_target_pairs={{8,0},{16,8},{24,16},{28,24},{20,28},{12,20},{4,12},{0,4},{9,1},{1... | collective-permute-start | bytes 1769480 | tf_op jit(solution)/shard_map/ppermute | solution.py:199
  60.6 25.3 %collective-permute-start.17 = (bf16[64,4608]{1,0:T(8,128)(2,1)S(1)}, bf16[64,4608]{1,0:T(8,128)(2,1)S(1)}, u32[]{:S(2)}, u32[]{:S(2)}) collective-permute-start(bf16[64,4608]{1,0:T(8,128)(2,1)S(1)} %collective-permute-done.13), channel_id=1, source_target_pairs={{0,8},{8,16},{16,24},{24,28},{28,20},{20,12},{12,4},{4,0},{1,9},{9... | collective-permute-start | bytes 1769480 | tf_op jit(solution)/shard_map/ppermute | solution.py:199
  60.7 25.2 %collective-permute-start.18 = (bf16[64,4608]{1,0:T(8,128)(2,1)S(1)}, bf16[64,4608]{1,0:T(8,128)(2,1)S(1)}, u32[]{:S(2)}, u32[]{:S(2)}) collective-permute-start(bf16[64,4608]{1,0:T(8,128)(2,1)S(1)} %collective-permute-done.14), channel_id=1, source_target_pairs={{8,0},{16,8},{24,16},{28,24},{20,28},{12,20},{4,12},{0,4},{9,1},{1... | collective-permute-start | bytes 1769480 | tf_op jit(solution)/shard_map/ppermute | solution.py:199
  64.2 1.5 %collective-permute-start.4 = (f32[128,320]{1,0:T(8,128)S(1)}, f32[128,320]{1,0:T(8,128)S(1)}, u32[]{:S(2)}, u32[]{:S(2)}) collective-permute-start(f32[128,320]{1,0:T(8,128)S(1)} %constant_dynamic-slice_fusion), channel_id=1, source_target_pairs={{0,1},{1,0},{2,3},{3,2},{4,5},{5,4},{6,7},{7,6},{8,9},{9,8},{10,11... | collective-permute-start | bytes 491528 | tf_op jit(solution)/shard_map/ppermute | solution.py:148
  65.7 7.3 %collective-permute-start.5 = (f32[128,320]{1,0:T(8,128)S(1)}, f32[128,320]{1,0:T(8,128)S(1)}, u32[]{:S(2)}, u32[]{:S(2)}) collective-permute-start(f32[128,320]{1,0:T(8,128)S(1)} %dynamic-slice_add_fusion), channel_id=1, source_target_pairs={{0,2},{1,3},{2,0},{3,1},{4,6},{5,7},{6,4},{7,5},{8,10},{9,11},{10,... | collective-permute-start | bytes 491528 | tf_op jit(solution)/shard_map/ppermute | solution.py:148
  73.1 1.5 %collective-permute-start.6 = (f32[128,320]{1,0:T(8,128)S(1)}, f32[128,320]{1,0:T(8,128)S(1)}, u32[]{:S(2)}, u32[]{:S(2)}) collective-permute-start(f32[128,320]{1,0:T(8,128)S(1)} %add.199), channel_id=1, source_target_pairs={{0,1},{1,0},{2,3},{3,2},{4,5},{5,4},{6,7},{7,6},{8,9},{9,8},{10,11... | collective-permute-start | bytes 491528 | tf_op jit(solution)/shard_map/ppermute | solution.py:148
  74.1 2.7 %collective-permute-start.11 = (f32[256,128]{1,0:T(8,128)S(1)}, f32[256,128]{1,0:T(8,128)S(1)}, u32[]{:S(2)}, u32[]{:S(2)}) collective-permute-start(f32[256,128]{1,0:T(8,128)S(1)} %slice_add_fusion.12), channel_id=1, source_target_pairs={{0,1},{1,0},{2,3},{3,2},{4,5},{5,4},{6,7},{7,6},{8,9},{9,8},{10,11... | collective-permute-start | bytes 393224 | tf_op jit(solution)/shard_map/ppermute | solution.py:148
  74.7 17.5 %collective-permute-start.15 = (bf16[32,4608]{1,0:T(8,128)(2,1)S(1)}, bf16[32,4608]{1,0:T(8,128)(2,1)S(1)}, u32[]{:S(2)}, u32[]{:S(2)}) collective-permute-start(bf16[32,4608]{1,0:T(8,128)(2,1)S(1)} %slice.186), channel_id=1, source_target_pairs={{0,8},{8,16},{16,24},{24,28},{28,20},{20,12},{12,4},{4,0},{1,9},{9... | collective-permute-start | bytes 884744 | tf_op jit(solution)/shard_map/ppermute | solution.py:199
  75.1 17.1 %collective-permute-start.16 = (bf16[32,4608]{1,0:T(8,128)(2,1)S(1)}, bf16[32,4608]{1,0:T(8,128)(2,1)S(1)}, u32[]{:S(2)}, u32[]{:S(2)}) collective-permute-start(bf16[32,4608]{1,0:T(8,128)(2,1)S(1)} %slice.187), channel_id=1, source_target_pairs={{8,0},{16,8},{24,16},{28,24},{20,28},{12,20},{4,12},{0,4},{9,1},{1... | collective-permute-start | bytes 884744 | tf_op jit(solution)/shard_map/ppermute | solution.py:199
  76.8 11.2 %collective-permute-start.12 = (f32[256,128]{1,0:T(8,128)S(1)}, f32[256,128]{1,0:T(8,128)S(1)}, u32[]{:S(2)}, u32[]{:S(2)}) collective-permute-start(f32[256,128]{1,0:T(8,128)S(1)} %fusion.65), channel_id=1, source_target_pairs={{0,2},{1,3},{2,0},{3,1},{4,6},{5,7},{6,4},{7,5},{8,10},{9,11},{10,... | collective-permute-start | bytes 393224 | tf_op jit(solution)/shard_map/ppermute | solution.py:148
  85.9 11.1 %collective-permute-start.21 = (bf16[32,4608]{1,0:T(8,128)(2,1)S(1)}, bf16[32,4608]{1,0:T(8,128)(2,1)S(1)}, u32[]{:S(2)}, u32[]{:S(2)}) collective-permute-start(bf16[32,4608]{1,0:T(8,128)(2,1)S(1)} %slice.215), channel_id=1, source_target_pairs={{0,8},{8,16},{16,24},{24,28},{28,20},{20,12},{12,4},{4,0},{1,9},{9... | collective-permute-start | bytes 884744 | tf_op jit(solution)/shard_map/ppermute | solution.py:199
  86.1 10.9 %collective-permute-start.22 = (bf16[32,4608]{1,0:T(8,128)(2,1)S(1)}, bf16[32,4608]{1,0:T(8,128)(2,1)S(1)}, u32[]{:S(2)}, u32[]{:S(2)}) collective-permute-start(bf16[32,4608]{1,0:T(8,128)(2,1)S(1)} %slice.216), channel_id=1, source_target_pairs={{8,0},{16,8},{24,16},{28,24},{20,28},{12,20},{4,12},{0,4},{9,1},{1... | collective-permute-start | bytes 884744 | tf_op jit(solution)/shard_map/ppermute | solution.py:199
  93.8 1.5 %collective-permute-start.19 = (f32[256,64]{1,0:T(8,128)S(1)}, f32[256,64]{1,0:T(8,128)S(1)}, u32[]{:S(2)}, u32[]{:S(2)}) collective-permute-start(f32[256,64]{1,0:T(8,128)S(1)} %slice_add_fusion.11), channel_id=1, source_target_pairs={{0,1},{1,0},{2,3},{3,2},{4,5},{5,4},{6,7},{7,6},{8,9},{9,8},{10,11... | collective-permute-start | bytes 196616 | tf_op jit(solution)/shard_map/ppermute | solution.py:148
  95.3 6.0 %collective-permute-start.20 = (f32[256,64]{1,0:T(8,128)S(1)}, f32[256,64]{1,0:T(8,128)S(1)}, u32[]{:S(2)}, u32[]{:S(2)}) collective-permute-start(f32[256,64]{1,0:T(8,128)S(1)} %fusion.64), channel_id=1, source_target_pairs={{0,2},{1,3},{2,0},{3,1},{4,6},{5,7},{6,4},{7,5},{8,10},{9,11},{10,... | collective-permute-start | bytes 196616 | tf_op jit(solution)/shard_map/ppermute | solution.py:148
  101.7 3.0 %collective-permute-start.25 = (f32[2,16]{1,0:T(2,128)S(1)}, f32[2,16]{1,0:T(2,128)S(1)}, u32[]{:S(2)}, u32[]{:S(2)}) collective-permute-start(f32[2,16]{1,0:T(2,128)S(1)} %score.1), channel_id=1, source_target_pairs={{0,3},{1,2},{2,1},{3,0},{4,7},{5,6},{6,5},{7,4},{8,11},{9,10},{10,... | collective-permute-start | bytes 392 | tf_op jit(solution)/shard_map/ppermute | solution.py:148
  102.5 3.6 %collective-permute-start.24 = (f32[2,16]{1,0:T(2,128)S(1)}, f32[2,16]{1,0:T(2,128)S(1)}, u32[]{:S(2)}, u32[]{:S(2)}) collective-permute-start(f32[2,16]{1,0:T(2,128)S(1)} %score.1), channel_id=1, source_target_pairs={{0,2},{1,3},{2,0},{3,1},{4,6},{5,7},{6,4},{7,5},{8,10},{9,11},{10,... | collective-permute-start | bytes 392 | tf_op jit(solution)/shard_map/ppermute | solution.py:148
  103.3 2.8 %collective-permute-start.23 = (f32[2,16]{1,0:T(2,128)S(1)}, f32[2,16]{1,0:T(2,128)S(1)}, u32[]{:S(2)}, u32[]{:S(2)}) collective-permute-start(f32[2,16]{1,0:T(2,128)S(1)} %score.1), channel_id=1, source_target_pairs={{0,1},{1,0},{2,3},{3,2},{4,5},{5,4},{6,7},{7,6},{8,9},{9,8},{10,11... | collective-permute-start | bytes 392 | tf_op jit(solution)/shard_map/ppermute | solution.py:148

commit v8 on v7

--- a/solution.py
+++ b/solution.py
@@ -14,13 +14,12 @@
     return pltpu.CompilerParams(vmem_limit_bytes=mebibytes * 2**20)
 
 
-def pick_rows(groups, owners, left_store, right_store):
+def pick_rows(groups, owners, parts):
     per = NQ // groups
-    width_left = left_store.shape[2]
-    width_right = right_store.shape[2]
-    cut = max(width_right * 5 // 14 // 128 * 128, 128)
-
-    def kernel(owners_ref, left_ref, right_ref, first_out, second_out, sems):
+    total = sum(width for _, _, width in parts)
+
+    def kernel(owners_ref, *refs):
+        stores, out_ref, sems = refs[:-2], refs[-2], refs[-1]
         group = lax.axis_index("dp")
         found = jnp.int32(0)
         queries = [jnp.int32(0)] * per
@@ -31,31 +30,31 @@
         copies = []
         for i in range(per):
             rows = pl.ds(pl.multiple_of(queries[i] * R, R), R)
-            here = pl.ds(i * R, R)
-            pairs = [
-                (left_ref.at[0, rows, :], first_out.at[here, pl.ds(0, width_left)]),
-                (right_ref.at[0, rows, pl.ds(0, cut)], first_out.at[here, pl.ds(width_left, cut)]),
-                (right_ref.at[0, rows, pl.ds(cut, width_right - cut)], second_out.at[here, :]),
-            ]
-            for j, (source, target) in enumerate(pairs):
-                copies.append(pltpu.make_async_copy(source, target, sems.at[i, j]))
+            at = 0
+            for j, (store_ref, (_, base, width)) in enumerate(zip(stores, parts)):
+                copies.append(
+                    pltpu.make_async_copy(
+                        store_ref.at[0, rows, pl.ds(base, width)],
+                        out_ref.at[pl.ds(i * R, R), pl.ds(at, width)],
+                        sems.at[i, j],
+                    )
+                )
+                at += width
         for copy in copies:
             copy.start()
         for copy in copies:
             copy.wait()
 
-    shape = lambda width: jax.ShapeDtypeStruct((per * R, width), jnp.bfloat16)
-    in_vmem = pl.BlockSpec(memory_space=pltpu.VMEM)
     in_hbm = pl.BlockSpec(memory_space=pltpu.HBM)
     return pl.pallas_call(
         kernel,
-        out_shape=(shape(width_left + cut), shape(width_right - cut)),
-        in_specs=[pl.BlockSpec(memory_space=pltpu.SMEM), in_hbm, in_hbm],
-        out_specs=(in_vmem, in_vmem),
-        scratch_shapes=[pltpu.SemaphoreType.DMA((per, 3))],
-        compiler_params=params(62),
+        out_shape=jax.ShapeDtypeStruct((per * R, total), jnp.bfloat16),
+        in_specs=[pl.BlockSpec(memory_space=pltpu.SMEM)] + [in_hbm] * len(parts),
+        out_specs=pl.BlockSpec(memory_space=pltpu.VMEM),
+        scratch_shapes=[pltpu.SemaphoreType.DMA((per, len(parts)))],
+        compiler_params=params(52),
         name="pick_rows",
-    )(owners, left_store, right_store)
+    )(owners, *[store for store, _, _ in parts])
 
 
 def rotate(matrix, basis, shard):
@@ -184,9 +183,14 @@
     backward = [(b, a) for a, b in forward]
     reach = groups // 2
 
-    own = pick_rows(groups, owners, left_store, right_store)
     width_left = left_store.shape[2]
-    cut = own[0].shape[1] - width_left
+    width_right = right_store.shape[2]
+    cut = max(width_right * 5 // 14 // 128 * 128, 128)
+    own = [pick_rows(groups, owners, [(left_store, 0, width_left), (right_store, 0, cut)])]
+    grads = rotate(out_grads, out_basis, shard)
+    own.append(
+        pick_rows(groups, after(owners, grads), [(right_store, cut, width_right - cut)])
+    )
 
     steps = [[], []]
     came = []
@@ -203,7 +207,6 @@
     def side_by_side(step):
         return jnp.concatenate(step, axis=0)
 
-    grads = rotate(out_grads, out_basis, shard)
     acts = rotate(hidden_acts, in_basis, 0)
 
     for hops in range(1, reach):
@@ -223,9 +226,10 @@
 
     last = after(steps[0][-1], came[-3])
     second.append(side_by_side(after(steps[1][reach - 2], last)))
-    first.append(side_by_side(last))
-    part = contract_rows(grads, first[-1][:, :width_left])
+    last = side_by_side(last)
+    part = contract_rows(grads, last[:, :width_left])
     part = part + swapped(part, 1, shards)
+    first.append(after(last, part))
     second.append(side_by_side(after(steps[1][-1], part)))
     coefficients.append(small_sum(part, shards, 2, 2))
 

time: 107 us -> 105 us (0.981)
  waiting for transfers between devices: 47.6 us -> 44 us
  matrix products: 15.4 us -> 16.5 us
    ppermute x10, waiting for transfers between devices: 10.3 us -> 7.05 us  [swapped(): return lax.ppermute(piece, 'mp', [(i, i ^ distance) for i in range(shards)])]
    ppermute x8, waiting for transfers between devices: 8.62 us -> 7.41 us  [send(): lax.ppermute(behind, 'dp', backward)]
    dot_general x13, matrix products: 15.4 us -> 16.5 us  [contract_rows(): lax.dot_general(both, second, (((1,), (1,)), ((), ())), preferred_element...]
    pallas_call x1 -> x2, Pallas kernels: 3.22 us -> 3.4 us  [pick_rows(): pl.pallas_call(kernel, out_shape=jax.ShapeDtypeStruct((per * R, total), j...]
  transfers between devices with their start and end apart: 26 -> 26, of which waited for: 13 -> 12; matrix products, arithmetic and copies ran while one was open for 16% -> 17% of each run, Pallas kernels for 12% -> 14%
where the time goes in v8:
time: 105 us
  waiting for transfers between devices  44 us (42%)
  starting transfers between devices  24.5 us (23%)
  Pallas kernels  16.5 us (16%)
  matrix products  16.5 us (16%)
  other arithmetic  1.39 us (1%)
  local copies, waits for them, and re-layouts  1.36 us (1%)
    ppermute x8, waiting for transfers between devices, send(): lax.ppermute(ahead, 'dp', forward)  29.5 us
    dot_general x13, matrix products, contract_rows(): lax.dot_general(both, second, (((1,), (1,)), ((), ())), preferred_element...  16.5 us
    ppermute x8, starting transfers between devices, send(): lax.ppermute(behind, 'dp', backward)  14.6 us
    pallas_call x2, Pallas kernels, rotate(): pl.pallas_call(kernel, out_shape=jax.ShapeDtypeStruct((2 * rows, total),...  12.8 us
    ppermute x8, waiting for transfers between devices, send(): lax.ppermute(behind, 'dp', backward)  7.41 us
    ppermute x10, waiting for transfers between devices, swapped(): return lax.ppermute(piece, 'mp', [(i, i ^ distance) for i in range(shards)])  7.05 us
    ppermute x10, starting transfers between devices, swapped(): return lax.ppermute(piece, 'mp', [(i, i ^ distance) for i in range(shards)])  6.95 us
    pallas_call x2, Pallas kernels, pick_rows(): pl.pallas_call(kernel, out_shape=jax.ShapeDtypeStruct((per * R, total), j...  3.4 us
  transfers between devices with their start and end apart: 26, of which 12 were waited for; matrix products, arithmetic and copies ran while one was open for 17% of the time, Pallas kernels for 14%

profile of v8, /device:TPU:0, one launch (start us, length us, event | category | flops | bytes accessed | tf_op | source)
XLA Modules:
  0.0 104.8 jit_solution(4340330549116737646)
XLA Ops:
  0.0 0.7 copy-done
  0.7 1.7 %pick_rows.2 = bf16[64,4608]{1,0:T(8,128)(2,1)S(1)} custom-call(s32[16]{0:T(128)S(1)} %copy-done, bf16[1,512,2048]{2,1,0:T(8,128)(2,1)} %refs_0_.2, bf16[1,512,7168]{2,1,0:T(8,128)(2,1)} %refs_0_.3), custom_call_target="tpu_custom_call" | custom-call | tf_op jit(solution)/shard_map/pick_rows/pallas_call | solution.py:49
  2.4 3.0 %collective-permute-start.1 = (bf16[64,4608]{1,0:T(8,128)(2,1)S(1)}, bf16[64,4608]{1,0:T(8,128)(2,1)S(1)}, u32[]{:S(2)}, u32[]{:S(2)}) collective-permute-start(bf16[64,4608]{1,0:T(8,128)(2,1)S(1)} %pick_rows.2), channel_id=1, source_target_pairs={{8,0},{16,8},{24,16},{28,24},{20,28},{12,20},{4,12},{0,4},{9,1},{1... | collective-permute-start | bytes 1769480 | tf_op jit(solution)/shard_map/ppermute | solution.py:203
  5.4 0.2 collective-permute-start
  5.6 3.4 %rotate.2 = bf16[512,2048]{1,0:T(8,128)(2,1)} custom-call(s32[1]{0:T(128)} %bitcast.shard_ref, bf16[256,8192]{1,0:T(8,128)(2,1)} %matrix_ref.2, bf16[4,512,512]{2,1,0:T(8,128)(2,1)} %basis_ref.2), custom_call_target="tpu_custom_call" | custom-call | flops 536870912 | bytes 5242880 | tf_op jit(solution)/shard_map/rotate/pallas_call | solution.py:77
  8.9 1.7 %pick_rows.3 = bf16[64,4608]{1,0:T(8,128)(2,1)S(1)} custom-call(s32[16]{0:T(128)S(1)} %copy-done.1, bf16[1,512,7168]{2,1,0:T(8,128)(2,1)} %refs_0_.3), custom_call_target="tpu_custom_call" | custom-call | tf_op jit(solution)/shard_map/pick_rows/pallas_call | solution.py:49
  10.6 1.9 %collective-permute-start.8 = (bf16[64,4608]{1,0:T(8,128)(2,1)S(1)}, bf16[64,4608]{1,0:T(8,128)(2,1)S(1)}, u32[]{:S(2)}, u32[]{:S(2)}) collective-permute-start(bf16[64,4608]{1,0:T(8,128)(2,1)S(1)} %pick_rows.3), channel_id=1, source_target_pairs={{8,0},{16,8},{24,16},{28,24},{20,28},{12,20},{4,12},{0,4},{9,1},{1... | collective-permute-start | bytes 1769480 | tf_op jit(solution)/shard_map/ppermute | solution.py:203
  12.5 0.2 collective-permute-start.7
  12.7 0.2 convert_reduce_fusion
  12.9 0.1 concatenate.51
  13.1 0.1 concatenate.50
  13.2 9.4 %rotate.3 = bf16[512,7168]{1,0:T(8,128)(2,1)} custom-call(s32[1]{0:T(128)} %constant.120.clone.1.shard_ref, bf16[256,7168]{1,0:T(8,128)(2,1)} %matrix_ref.3, bf16[28,256,256]{2,1,0:T(8,128)(2,1)} %basis_ref.3), custom_call_target="tpu_custom_call" | custom-call | flops 939524096 | bytes 14680064 | tf_op jit(solution)/shard_map/rotate/pallas_call | solution.py:77
  22.6 0.2 and_convert_fusion.hit_ref
  22.8 0.0 collective-permute-done
  22.8 2.0 %collective-permute-start.2 = (bf16[64,4608]{1,0:T(8,128)(2,1)S(1)}, bf16[64,4608]{1,0:T(8,128)(2,1)S(1)}, u32[]{:S(2)}, u32[]{:S(2)}) collective-permute-start(bf16[64,4608]{1,0:T(8,128)(2,1)S(1)} %collective-permute-done), channel_id=1, source_target_pairs={{0,8},{8,16},{16,24},{24,28},{28,20},{20,12},{12,4},{4,0},{1,9},{9... | collective-permute-start | bytes 1769480 | tf_op jit(solution)/shard_map/ppermute | solution.py:203
  24.8 0.1 collective-permute-start.3
  24.9 7.4 %collective-permute-done.8 = bf16[64,4608]{1,0:T(8,128)(2,1)S(1)} collective-permute-done((bf16[64,4608]{1,0:T(8,128)(2,1)S(1)}, bf16[64,4608]{1,0:T(8,128)(2,1)S(1)}, u32[]{:S(2)}, u32[]{:S(2)}) %collective-permute-start.8) | collective-permute-done | bytes 589856 | tf_op jit(solution)/shard_map/ppermute | solution.py:203
  32.3 2.1 %collective-permute-done.7 = bf16[64,4608]{1,0:T(8,128)(2,1)} collective-permute-done((bf16[64,4608]{1,0:T(8,128)(2,1)S(1)}, bf16[64,4608]{1,0:T(8,128)(2,1)}, u32[]{:S(2)}, u32[]{:S(2)}) %collective-permute-start.7) | collective-permute-done | bytes 589856 | tf_op jit(solution)/shard_map/ppermute | solution.py:203
  34.4 0.1 collective-permute-start.13
  34.5 1.9 %collective-permute-start.14 = (bf16[64,4608]{1,0:T(8,128)(2,1)S(1)}, bf16[64,4608]{1,0:T(8,128)(2,1)S(1)}, u32[]{:S(2)}, u32[]{:S(2)}) collective-permute-start(bf16[64,4608]{1,0:T(8,128)(2,1)S(1)} %collective-permute-done.8), channel_id=1, source_target_pairs={{8,0},{16,8},{24,16},{28,24},{20,28},{12,20},{4,12},{0,4},{9,1},{1... | collective-permute-start | bytes 1769480 | tf_op jit(solution)/shard_map/ppermute | solution.py:203
  36.5 2.6 %fusion.18 = f32[512,128]{1,0:T(8,128)S(1)} fusion(bf16[512,7168]{1,0:T(8,128)(2,1)} %rotate.3, bf16[128,4608]{1,0:T(8,128)(2,1)S(1)} %constant_dynamic-update-slice_fusion), kind=kOutput, calls=%fused_computation.18 | convolution fusion | flops 335544320 | bytes 3538944 | tf_op jit(solution)/shard_map/dot_general | solution.py:101
  39.1 1.4 %fusion.4 = f32[512,64]{1,0:T(8,128)S(1)} fusion(bf16[64,4608]{1,0:T(8,128)(2,1)S(1)} %pick_rows.3, bf16[512,7168]{1,0:T(8,128)(2,1)S(1)} %copy-done.2), kind=kOutput, calls=%fused_computation.4 | convolution fusion | flops 301989888 | bytes 5439488 | tf_op jit(solution)/shard_map/dot_general | solution.py:101
  40.5 2.4 %fusion.8 = f32[512,128]{1,0:T(8,128)S(1)} fusion(bf16[512,7168]{1,0:T(8,128)(2,1)S(1)} %copy-done.2, bf16[64,4608]{1,0:T(8,128)(2,1)S(1)} %collective-permute-done.8, bf16[64,4608]{1,0:T(8,128)(2,1)} %collective-permute-done.7), kind=kOutput, calls=%fused_computation.8 | convolution fusion | flops 606339072 | bytes 6160384 | tf_op jit(solution)/shard_map/dot_general | solution.py:101
  42.9 0.8 fusion.14
  43.9 3.0 %collective-permute-done.2 = bf16[64,4608]{1,0:T(8,128)(2,1)S(1)} collective-permute-done((bf16[64,4608]{1,0:T(8,128)(2,1)S(1)}, bf16[64,4608]{1,0:T(8,128)(2,1)S(1)}, u32[]{:S(2)}, u32[]{:S(2)}) %collective-permute-start.2) | collective-permute-done | bytes 589856 | tf_op jit(solution)/shard_map/ppermute | solution.py:203
  47.0 0.0 collective-permute-done.3
  47.1 1.3 %fusion.20 = f32[512,320]{1,0:T(8,128)S(1)} fusion(bf16[512,2048]{1,0:T(8,128)(2,1)S(1)} %copy-done.3, bf16[64,2048]{1,0:T(8,128)(2,1)S(1)} %slice.139, bf16[128,2048]{1,0:T(8,128)(2,1)S(1)} %slice.180, bf16[128,2048]{1,0:T(8,128)(2,1)S(1)} %slice.179), kind=kOutput, calls=%fused_computation.20 | convolution fusion | flops 675020800 | bytes 4063232 | tf_op jit(solution)/shard_map/dot_general | solution.py:101
  48.5 0.1 collective-permute-start.4
  48.5 0.2 collective-permute-start.9
  48.7 1.9 %collective-permute-start.10 = (bf16[64,4608]{1,0:T(8,128)(2,1)S(1)}, bf16[64,4608]{1,0:T(8,128)(2,1)S(1)}, u32[]{:S(2)}, u32[]{:S(2)}) collective-permute-start(bf16[64,4608]{1,0:T(8,128)(2,1)S(1)} %collective-permute-done.3), channel_id=1, source_target_pairs={{8,0},{16,8},{24,16},{28,24},{20,28},{12,20},{4,12},{0,4},{9,1},{1... | collective-permute-start | bytes 1769480 | tf_op jit(solution)/shard_map/ppermute | solution.py:203
  50.6 9.0 %collective-permute-done.13 = bf16[64,4608]{1,0:T(8,128)(2,1)S(1)} collective-permute-done((bf16[64,4608]{1,0:T(8,128)(2,1)}, bf16[64,4608]{1,0:T(8,128)(2,1)S(1)}, u32[]{:S(2)}, u32[]{:S(2)}) %collective-permute-start.13) | collective-permute-done | bytes 589856 | tf_op jit(solution)/shard_map/ppermute | solution.py:203
  59.6 0.1 collective-permute-start.17
  59.7 1.9 %collective-permute-start.18 = (bf16[64,4608]{1,0:T(8,128)(2,1)S(1)}, bf16[64,4608]{1,0:T(8,128)(2,1)S(1)}, u32[]{:S(2)}, u32[]{:S(2)}) collective-permute-start(bf16[64,4608]{1,0:T(8,128)(2,1)S(1)} %collective-permute-done.14), channel_id=1, source_target_pairs={{8,0},{16,8},{24,16},{28,24},{20,28},{12,20},{4,12},{0,4},{9,1},{1... | collective-permute-start | bytes 1769480 | tf_op jit(solution)/shard_map/ppermute | solution.py:203
  61.6 1.4 %fusion.6 = f32[512,128]{1,0:T(8,128)S(1)} fusion(bf16[512,7168]{1,0:T(8,128)(2,1)S(1)} %copy-done.2, bf16[64,4608]{1,0:T(8,128)(2,1)S(1)} %collective-permute-done.14, bf16[64,4608]{1,0:T(8,128)(2,1)S(1)} %collective-permute-done.13), kind=kOutput, calls=%fused_computation.6 | convolution fusion | flops 606339072 | bytes 6160384 | tf_op jit(solution)/shard_map/dot_general | solution.py:101
  63.0 1.6 %collective-permute-start.5 = (f32[128,320]{1,0:T(8,128)S(1)}, f32[128,320]{1,0:T(8,128)S(1)}, u32[]{:S(2)}, u32[]{:S(2)}) collective-permute-start(f32[128,320]{1,0:T(8,128)S(1)} %dynamic-slice_add_fusion), channel_id=1, source_target_pairs={{0,2},{1,3},{2,0},{3,1},{4,6},{5,7},{6,4},{7,5},{8,10},{9,11},{10,... | collective-permute-start | bytes 491528 | tf_op jit(solution)/shard_map/ppermute | solution.py:147
  64.6 0.8 fusion.16
  65.5 3.3 %collective-permute-done.5 = f32[128,320]{1,0:T(8,128)S(1)} collective-permute-done((f32[128,320]{1,0:T(8,128)S(1)}, f32[128,320]{1,0:T(8,128)S(1)}, u32[]{:S(2)}, u32[]{:S(2)}) %collective-permute-start.5) | collective-permute-done | bytes 163872 | tf_op jit(solution)/shard_map/ppermute | solution.py:147
  68.8 0.1 collective-permute-start.6
  68.9 3.3 %collective-permute-done.9 = bf16[64,4608]{1,0:T(8,128)(2,1)S(1)} collective-permute-done((bf16[64,4608]{1,0:T(8,128)(2,1)S(1)}, bf16[64,4608]{1,0:T(8,128)(2,1)S(1)}, u32[]{:S(2)}, u32[]{:S(2)}) %collective-permute-start.9) | collective-permute-done | bytes 589856 | tf_op jit(solution)/shard_map/ppermute | solution.py:203
  72.3 0.7 fusion.41
  73.1 0.1 collective-permute-start.11
  73.3 0.2 collective-permute-start.15
  73.5 1.9 %collective-permute-start.16 = (bf16[32,4608]{1,0:T(8,128)(2,1)S(1)}, bf16[32,4608]{1,0:T(8,128)(2,1)S(1)}, u32[]{:S(2)}, u32[]{:S(2)}) collective-permute-start(bf16[32,4608]{1,0:T(8,128)(2,1)S(1)} %slice.187), channel_id=1, source_target_pairs={{8,0},{16,8},{24,16},{28,24},{20,28},{12,20},{4,12},{0,4},{9,1},{1... | collective-permute-start | bytes 884744 | tf_op jit(solution)/shard_map/ppermute | solution.py:203
  75.4 1.6 %collective-permute-start.12 = (f32[256,128]{1,0:T(8,128)S(1)}, f32[256,128]{1,0:T(8,128)S(1)}, u32[]{:S(2)}, u32[]{:S(2)}) collective-permute-start(f32[256,128]{1,0:T(8,128)S(1)} %fusion.65), channel_id=1, source_target_pairs={{0,2},{1,3},{2,0},{3,1},{4,6},{5,7},{6,4},{7,5},{8,10},{9,11},{10,... | collective-permute-start | bytes 393224 | tf_op jit(solution)/shard_map/ppermute | solution.py:147
  77.0 0.9 fusion.12
  77.8 7.0 %collective-permute-done.17 = bf16[64,4608]{1,0:T(8,128)(2,1)S(1)} collective-permute-done((bf16[64,4608]{1,0:T(8,128)(2,1)S(1)}, bf16[64,4608]{1,0:T(8,128)(2,1)S(1)}, u32[]{:S(2)}, u32[]{:S(2)}) %collective-permute-start.17) | collective-permute-done | bytes 589856 | tf_op jit(solution)/shard_map/ppermute | solution.py:203
  84.9 0.2 collective-permute-start.21
  85.1 1.9 %collective-permute-start.22 = (bf16[32,4608]{1,0:T(8,128)(2,1)S(1)}, bf16[32,4608]{1,0:T(8,128)(2,1)S(1)}, u32[]{:S(2)}, u32[]{:S(2)}) collective-permute-start(bf16[32,4608]{1,0:T(8,128)(2,1)S(1)} %slice.215), channel_id=1, source_target_pairs={{8,0},{16,8},{24,16},{28,24},{20,28},{12,20},{4,12},{0,4},{9,1},{1... | collective-permute-start | bytes 884744 | tf_op jit(solution)/shard_map/ppermute | solution.py:203
  87.0 4.2 %collective-permute-done.15 = bf16[32,4608]{1,0:T(8,128)(2,1)S(1)} collective-permute-done((bf16[32,4608]{1,0:T(8,128)(2,1)S(1)}, bf16[32,4608]{1,0:T(8,128)(2,1)S(1)}, u32[]{:S(2)}, u32[]{:S(2)}) %collective-permute-start.15) | collective-permute-done | bytes 294944 | tf_op jit(solution)/shard_map/ppermute | solution.py:203
  91.2 0.7 fusion.45
  92.0 0.1 collective-permute-start.19
  92.0 1.4 %fusion.2 = f32[512,128]{1,0:T(8,128)S(1)} fusion(bf16[512,7168]{1,0:T(8,128)(2,1)S(1)} %copy-done.2, bf16[64,4608]{1,0:T(8,128)(2,1)S(1)} %collective-permute-done.18, bf16[64,4608]{1,0:T(8,128)(2,1)S(1)} %collective-permute-done.17), kind=kOutput, calls=%fused_computation.2 | convolution fusion | flops 606339072 | bytes 6160384 | tf_op jit(solution)/shard_map/dot_general | solution.py:101
  93.5 1.6 %collective-permute-start.20 = (f32[256,64]{1,0:T(8,128)S(1)}, f32[256,64]{1,0:T(8,128)S(1)}, u32[]{:S(2)}, u32[]{:S(2)}) collective-permute-start(f32[256,64]{1,0:T(8,128)S(1)} %fusion.64), channel_id=1, source_target_pairs={{0,2},{1,3},{2,0},{3,1},{4,6},{5,7},{6,4},{7,5},{8,10},{9,11},{10,... | collective-permute-start | bytes 196616 | tf_op jit(solution)/shard_map/ppermute | solution.py:147
  95.1 0.9 collective-permute-done.21
  96.0 0.8 fusion.10
  96.9 1.4 %fusion = f32[512,64]{1,0:T(8,128)S(1)} fusion(bf16[512,7168]{1,0:T(8,128)(2,1)S(1)} %copy-done.2, bf16[32,4608]{1,0:T(8,128)(2,1)S(1)} %collective-permute-done.22, bf16[32,4608]{1,0:T(8,128)(2,1)S(1)} %collective-permute-done.21), kind=kOutput, calls=%fused_computation | convolution fusion | flops 303169536 | bytes 5439488 | tf_op jit(solution)/shard_map/dot_general | solution.py:101
  98.3 1.2 %collective-permute-done.20 = f32[256,64]{1,0:T(8,128)S(1)} collective-permute-done((f32[256,64]{1,0:T(8,128)S(1)}, f32[256,64]{1,0:T(8,128)S(1)}, u32[]{:S(2)}, u32[]{:S(2)}) %collective-permute-start.20) | collective-permute-done | bytes 65568 | tf_op jit(solution)/shard_map/ppermute | solution.py:147
  99.5 0.3 score.1
  99.8 0.8 collective-permute-start.25
  100.7 0.7 collective-permute-start.24
  101.4 0.3 collective-permute-start.23
  101.7 1.1 %collective-permute-done.25 = f32[2,16]{1,0:T(2,128)S(1)} collective-permute-done((f32[2,16]{1,0:T(2,128)S(1)}, f32[2,16]{1,0:T(2,128)S(1)}, u32[]{:S(2)}, u32[]{:S(2)}) %collective-permute-start.25) | collective-permute-done | bytes 160 | tf_op jit(solution)/shard_map/ppermute | solution.py:147
  102.9 1.4 %collective-permute-done.24 = f32[2,16]{1,0:T(2,128)S(1)} collective-permute-done((f32[2,16]{1,0:T(2,128)S(1)}, f32[2,16]{1,0:T(2,128)S(1)}, u32[]{:S(2)}, u32[]{:S(2)}) %collective-permute-start.24) | collective-permute-done | bytes 160 | tf_op jit(solution)/shard_map/ppermute | solution.py:147
  104.2 0.6 add_add_fusion
  (62 shorter events, 1.0 us)
Async XLA Ops:
  0.0 0.7 copy-start
  2.4 20.4 %collective-permute-start.1 = (bf16[64,4608]{1,0:T(8,128)(2,1)S(1)}, bf16[64,4608]{1,0:T(8,128)(2,1)S(1)}, u32[]{:S(2)}, u32[]{:S(2)}) collective-permute-start(bf16[64,4608]{1,0:T(8,128)(2,1)S(1)} %pick_rows.2), channel_id=1, source_target_pairs={{8,0},{16,8},{24,16},{28,24},{20,28},{12,20},{4,12},{0,4},{9,1},{1... | collective-permute-start | bytes 1769480 | tf_op jit(solution)/shard_map/ppermute | solution.py:203
  5.4 17.4 %collective-permute-start = (bf16[64,4608]{1,0:T(8,128)(2,1)S(1)}, bf16[64,4608]{1,0:T(8,128)(2,1)S(1)}, u32[]{:S(2)}, u32[]{:S(2)}) collective-permute-start(bf16[64,4608]{1,0:T(8,128)(2,1)S(1)} %pick_rows.2), channel_id=1, source_target_pairs={{0,8},{8,16},{16,24},{24,28},{28,20},{20,12},{12,4},{4,0},{1,9},{9... | collective-permute-start | bytes 1769480 | tf_op jit(solution)/shard_map/ppermute | solution.py:203
  5.6 3.4 %copy-start.1 = (s32[16]{0:T(128)S(1)}, s32[16]{0:T(128)}, u32[]{:S(2)}) copy-start(s32[16]{0:T(128)} %owners_ref.2) | copy-start | bytes 196
  10.6 21.7 %collective-permute-start.8 = (bf16[64,4608]{1,0:T(8,128)(2,1)S(1)}, bf16[64,4608]{1,0:T(8,128)(2,1)S(1)}, u32[]{:S(2)}, u32[]{:S(2)}) collective-permute-start(bf16[64,4608]{1,0:T(8,128)(2,1)S(1)} %pick_rows.3), channel_id=1, source_target_pairs={{8,0},{16,8},{24,16},{28,24},{20,28},{12,20},{4,12},{0,4},{9,1},{1... | collective-permute-start | bytes 1769480 | tf_op jit(solution)/shard_map/ppermute | solution.py:203
  12.5 21.9 %collective-permute-start.7 = (bf16[64,4608]{1,0:T(8,128)(2,1)S(1)}, bf16[64,4608]{1,0:T(8,128)(2,1)}, u32[]{:S(2)}, u32[]{:S(2)}) collective-permute-start(bf16[64,4608]{1,0:T(8,128)(2,1)S(1)} %pick_rows.3), channel_id=1, source_target_pairs={{0,8},{8,16},{16,24},{24,28},{28,20},{20,12},{12,4},{4,0},{1,9},{9... | collective-permute-start | bytes 1769480 | tf_op jit(solution)/shard_map/ppermute | solution.py:203
  22.6 16.5 %copy-start.2 = (bf16[512,7168]{1,0:T(8,128)(2,1)S(1)}, bf16[512,7168]{1,0:T(8,128)(2,1)}, u32[]{:S(2)}) copy-start(bf16[512,7168]{1,0:T(8,128)(2,1)} %rotate.3) | copy-start | bytes 22020100
  22.8 24.1 %collective-permute-start.2 = (bf16[64,4608]{1,0:T(8,128)(2,1)S(1)}, bf16[64,4608]{1,0:T(8,128)(2,1)S(1)}, u32[]{:S(2)}, u32[]{:S(2)}) collective-permute-start(bf16[64,4608]{1,0:T(8,128)(2,1)S(1)} %collective-permute-done), channel_id=1, source_target_pairs={{0,8},{8,16},{16,24},{24,28},{28,20},{20,12},{12,4},{4,0},{1,9},{9... | collective-permute-start | bytes 1769480 | tf_op jit(solution)/shard_map/ppermute | solution.py:203
  24.8 22.2 %collective-permute-start.3 = (bf16[64,4608]{1,0:T(8,128)(2,1)S(1)}, bf16[64,4608]{1,0:T(8,128)(2,1)S(1)}, u32[]{:S(2)}, u32[]{:S(2)}) collective-permute-start(bf16[64,4608]{1,0:T(8,128)(2,1)S(1)} %collective-permute-done.1), channel_id=1, source_target_pairs={{8,0},{16,8},{24,16},{28,24},{20,28},{12,20},{4,12},{0,4},{9,1},{1... | collective-permute-start | bytes 1769480 | tf_op jit(solution)/shard_map/ppermute | solution.py:203
  34.4 25.2 %collective-permute-start.13 = (bf16[64,4608]{1,0:T(8,128)(2,1)}, bf16[64,4608]{1,0:T(8,128)(2,1)S(1)}, u32[]{:S(2)}, u32[]{:S(2)}) collective-permute-start(bf16[64,4608]{1,0:T(8,128)(2,1)} %collective-permute-done.7), channel_id=1, source_target_pairs={{0,8},{8,16},{16,24},{24,28},{28,20},{20,12},{12,4},{4,0},{1,9},{9... | collective-permute-start | bytes 1769480 | tf_op jit(solution)/shard_map/ppermute | solution.py:203
  34.5 25.1 %collective-permute-start.14 = (bf16[64,4608]{1,0:T(8,128)(2,1)S(1)}, bf16[64,4608]{1,0:T(8,128)(2,1)S(1)}, u32[]{:S(2)}, u32[]{:S(2)}) collective-permute-start(bf16[64,4608]{1,0:T(8,128)(2,1)S(1)} %collective-permute-done.8), channel_id=1, source_target_pairs={{8,0},{16,8},{24,16},{28,24},{20,28},{12,20},{4,12},{0,4},{9,1},{1... | collective-permute-start | bytes 1769480 | tf_op jit(solution)/shard_map/ppermute | solution.py:203
  43.8 3.3 %copy-start.3 = (bf16[512,2048]{1,0:T(8,128)(2,1)S(1)}, bf16[512,2048]{1,0:T(8,128)(2,1)}, u32[]{:S(2)}) copy-start(bf16[512,2048]{1,0:T(8,128)(2,1)} %rotate.2) | copy-start | bytes 6291460
  48.5 14.5 %collective-permute-start.4 = (f32[128,320]{1,0:T(8,128)S(1)}, f32[128,320]{1,0:T(8,128)S(1)}, u32[]{:S(2)}, u32[]{:S(2)}) collective-permute-start(f32[128,320]{1,0:T(8,128)S(1)} %constant_dynamic-slice_fusion), channel_id=1, source_target_pairs={{0,1},{1,0},{2,3},{3,2},{4,5},{5,4},{6,7},{7,6},{8,9},{9,8},{10,11... | collective-permute-start | bytes 491528 | tf_op jit(solution)/shard_map/ppermute | solution.py:147
  48.5 23.7 %collective-permute-start.9 = (bf16[64,4608]{1,0:T(8,128)(2,1)S(1)}, bf16[64,4608]{1,0:T(8,128)(2,1)S(1)}, u32[]{:S(2)}, u32[]{:S(2)}) collective-permute-start(bf16[64,4608]{1,0:T(8,128)(2,1)S(1)} %collective-permute-done.2), channel_id=1, source_target_pairs={{0,8},{8,16},{16,24},{24,28},{28,20},{20,12},{12,4},{4,0},{1,9},{9... | collective-permute-start | bytes 1769480 | tf_op jit(solution)/shard_map/ppermute | solution.py:203
  48.7 23.6 %collective-permute-start.10 = (bf16[64,4608]{1,0:T(8,128)(2,1)S(1)}, bf16[64,4608]{1,0:T(8,128)(2,1)S(1)}, u32[]{:S(2)}, u32[]{:S(2)}) collective-permute-start(bf16[64,4608]{1,0:T(8,128)(2,1)S(1)} %collective-permute-done.3), channel_id=1, source_target_pairs={{8,0},{16,8},{24,16},{28,24},{20,28},{12,20},{4,12},{0,4},{9,1},{1... | collective-permute-start | bytes 1769480 | tf_op jit(solution)/shard_map/ppermute | solution.py:203
  59.6 25.3 %collective-permute-start.17 = (bf16[64,4608]{1,0:T(8,128)(2,1)S(1)}, bf16[64,4608]{1,0:T(8,128)(2,1)S(1)}, u32[]{:S(2)}, u32[]{:S(2)}) collective-permute-start(bf16[64,4608]{1,0:T(8,128)(2,1)S(1)} %collective-permute-done.13), channel_id=1, source_target_pairs={{0,8},{8,16},{16,24},{24,28},{28,20},{20,12},{12,4},{4,0},{1,9},{9... | collective-permute-start | bytes 1769480 | tf_op jit(solution)/shard_map/ppermute | solution.py:203
  59.7 25.2 %collective-permute-start.18 = (bf16[64,4608]{1,0:T(8,128)(2,1)S(1)}, bf16[64,4608]{1,0:T(8,128)(2,1)S(1)}, u32[]{:S(2)}, u32[]{:S(2)}) collective-permute-start(bf16[64,4608]{1,0:T(8,128)(2,1)S(1)} %collective-permute-done.14), channel_id=1, source_target_pairs={{8,0},{16,8},{24,16},{28,24},{20,28},{12,20},{4,12},{0,4},{9,1},{1... | collective-permute-start | bytes 1769480 | tf_op jit(solution)/shard_map/ppermute | solution.py:203
  63.0 5.7 %collective-permute-start.5 = (f32[128,320]{1,0:T(8,128)S(1)}, f32[128,320]{1,0:T(8,128)S(1)}, u32[]{:S(2)}, u32[]{:S(2)}) collective-permute-start(f32[128,320]{1,0:T(8,128)S(1)} %dynamic-slice_add_fusion), channel_id=1, source_target_pairs={{0,2},{1,3},{2,0},{3,1},{4,6},{5,7},{6,4},{7,5},{8,10},{9,11},{10,... | collective-permute-start | bytes 491528 | tf_op jit(solution)/shard_map/ppermute | solution.py:147
  68.8 4.4 %collective-permute-start.6 = (f32[128,320]{1,0:T(8,128)S(1)}, f32[128,320]{1,0:T(8,128)S(1)}, u32[]{:S(2)}, u32[]{:S(2)}) collective-permute-start(f32[128,320]{1,0:T(8,128)S(1)} %add.199), channel_id=1, source_target_pairs={{0,1},{1,0},{2,3},{3,2},{4,5},{5,4},{6,7},{7,6},{8,9},{9,8},{10,11... | collective-permute-start | bytes 491528 | tf_op jit(solution)/shard_map/ppermute | solution.py:147
  73.1 2.3 %collective-permute-start.11 = (f32[256,128]{1,0:T(8,128)S(1)}, f32[256,128]{1,0:T(8,128)S(1)}, u32[]{:S(2)}, u32[]{:S(2)}) collective-permute-start(f32[256,128]{1,0:T(8,128)S(1)} %slice_add_fusion.12), channel_id=1, source_target_pairs={{0,1},{1,0},{2,3},{3,2},{4,5},{5,4},{6,7},{7,6},{8,9},{9,8},{10,11... | collective-permute-start | bytes 393224 | tf_op jit(solution)/shard_map/ppermute | solution.py:147
  73.3 17.9 %collective-permute-start.15 = (bf16[32,4608]{1,0:T(8,128)(2,1)S(1)}, bf16[32,4608]{1,0:T(8,128)(2,1)S(1)}, u32[]{:S(2)}, u32[]{:S(2)}) collective-permute-start(bf16[32,4608]{1,0:T(8,128)(2,1)S(1)} %slice.186), channel_id=1, source_target_pairs={{0,8},{8,16},{16,24},{24,28},{28,20},{20,12},{12,4},{4,0},{1,9},{9... | collective-permute-start | bytes 884744 | tf_op jit(solution)/shard_map/ppermute | solution.py:203
  73.5 17.7 %collective-permute-start.16 = (bf16[32,4608]{1,0:T(8,128)(2,1)S(1)}, bf16[32,4608]{1,0:T(8,128)(2,1)S(1)}, u32[]{:S(2)}, u32[]{:S(2)}) collective-permute-start(bf16[32,4608]{1,0:T(8,128)(2,1)S(1)} %slice.187), channel_id=1, source_target_pairs={{8,0},{16,8},{24,16},{28,24},{20,28},{12,20},{4,12},{0,4},{9,1},{1... | collective-permute-start | bytes 884744 | tf_op jit(solution)/shard_map/ppermute | solution.py:203
  75.4 11.6 %collective-permute-start.12 = (f32[256,128]{1,0:T(8,128)S(1)}, f32[256,128]{1,0:T(8,128)S(1)}, u32[]{:S(2)}, u32[]{:S(2)}) collective-permute-start(f32[256,128]{1,0:T(8,128)S(1)} %fusion.65), channel_id=1, source_target_pairs={{0,2},{1,3},{2,0},{3,1},{4,6},{5,7},{6,4},{7,5},{8,10},{9,11},{10,... | collective-permute-start | bytes 393224 | tf_op jit(solution)/shard_map/ppermute | solution.py:147
  84.9 11.1 %collective-permute-start.21 = (bf16[32,4608]{1,0:T(8,128)(2,1)S(1)}, bf16[32,4608]{1,0:T(8,128)(2,1)S(1)}, u32[]{:S(2)}, u32[]{:S(2)}) collective-permute-start(bf16[32,4608]{1,0:T(8,128)(2,1)S(1)} %slice.214), channel_id=1, source_target_pairs={{0,8},{8,16},{16,24},{24,28},{28,20},{20,12},{12,4},{4,0},{1,9},{9... | collective-permute-start | bytes 884744 | tf_op jit(solution)/shard_map/ppermute | solution.py:203
  85.1 10.9 %collective-permute-start.22 = (bf16[32,4608]{1,0:T(8,128)(2,1)S(1)}, bf16[32,4608]{1,0:T(8,128)(2,1)S(1)}, u32[]{:S(2)}, u32[]{:S(2)}) collective-permute-start(bf16[32,4608]{1,0:T(8,128)(2,1)S(1)} %slice.215), channel_id=1, source_target_pairs={{8,0},{16,8},{24,16},{28,24},{20,28},{12,20},{4,12},{0,4},{9,1},{1... | collective-permute-start | bytes 884744 | tf_op jit(solution)/shard_map/ppermute | solution.py:203
  92.0 1.5 %collective-permute-start.19 = (f32[256,64]{1,0:T(8,128)S(1)}, f32[256,64]{1,0:T(8,128)S(1)}, u32[]{:S(2)}, u32[]{:S(2)}) collective-permute-start(f32[256,64]{1,0:T(8,128)S(1)} %slice_add_fusion.11), channel_id=1, source_target_pairs={{0,1},{1,0},{2,3},{3,2},{4,5},{5,4},{6,7},{7,6},{8,9},{9,8},{10,11... | collective-permute-start | bytes 196616 | tf_op jit(solution)/shard_map/ppermute | solution.py:147
  93.5 6.0 %collective-permute-start.20 = (f32[256,64]{1,0:T(8,128)S(1)}, f32[256,64]{1,0:T(8,128)S(1)}, u32[]{:S(2)}, u32[]{:S(2)}) collective-permute-start(f32[256,64]{1,0:T(8,128)S(1)} %fusion.64), channel_id=1, source_target_pairs={{0,2},{1,3},{2,0},{3,1},{4,6},{5,7},{6,4},{7,5},{8,10},{9,11},{10,... | collective-permute-start | bytes 196616 | tf_op jit(solution)/shard_map/ppermute | solution.py:147
  99.8 3.0 %collective-permute-start.25 = (f32[2,16]{1,0:T(2,128)S(1)}, f32[2,16]{1,0:T(2,128)S(1)}, u32[]{:S(2)}, u32[]{:S(2)}) collective-permute-start(f32[2,16]{1,0:T(2,128)S(1)} %score.1), channel_id=1, source_target_pairs={{0,3},{1,2},{2,1},{3,0},{4,7},{5,6},{6,5},{7,4},{8,11},{9,10},{10,... | collective-permute-start | bytes 392 | tf_op jit(solution)/shard_map/ppermute | solution.py:147
  100.7 3.6 %collective-permute-start.24 = (f32[2,16]{1,0:T(2,128)S(1)}, f32[2,16]{1,0:T(2,128)S(1)}, u32[]{:S(2)}, u32[]{:S(2)}) collective-permute-start(f32[2,16]{1,0:T(2,128)S(1)} %score.1), channel_id=1, source_target_pairs={{0,2},{1,3},{2,0},{3,1},{4,6},{5,7},{6,4},{7,5},{8,10},{9,11},{10,... | collective-permute-start | bytes 392 | tf_op jit(solution)/shard_map/ppermute | solution.py:147
  101.4 2.8 %collective-permute-start.23 = (f32[2,16]{1,0:T(2,128)S(1)}, f32[2,16]{1,0:T(2,128)S(1)}, u32[]{:S(2)}, u32[]{:S(2)}) collective-permute-start(f32[2,16]{1,0:T(2,128)S(1)} %score.1), channel_id=1, source_target_pairs={{0,1},{1,0},{2,3},{3,2},{4,5},{5,4},{6,7},{7,6},{8,9},{9,8},{10,11... | collective-permute-start | bytes 392 | tf_op jit(solution)/shard_map/ppermute | solution.py:147

commit v9 on v8

--- a/solution.py
+++ b/solution.py
@@ -228,10 +228,10 @@
     second.append(side_by_side(after(steps[1][reach - 2], last)))
     last = side_by_side(last)
     part = contract_rows(grads, last[:, :width_left])
-    part = part + swapped(part, 1, shards)
+    last_sum = small_sum(part, shards, 4)
     first.append(after(last, part))
-    second.append(side_by_side(after(steps[1][-1], part)))
-    coefficients.append(small_sum(part, shards, 2, 2))
+    second.append(side_by_side(steps[1][-1]))
+    coefficients.append(last_sum)
 
     projected = [
         contract_rows(acts[:, :cut], one[:, width_left:]) + contract_rows(acts[:, cut:], other)

time: 105 us -> 106 us (level)
    ppermute x10 -> x11, waiting for transfers between devices: 7.05 us -> 8.15 us  [swapped(): return lax.ppermute(piece, 'mp', [(i, i ^ distance) for i in range(shards)])]
    ppermute x10 -> x11, starting transfers between devices: 6.95 us -> 7.2 us  [swapped(): return lax.ppermute(piece, 'mp', [(i, i ^ distance) for i in range(shards)])]
  transfers between devices with their start and end apart: 26 -> 27, of which waited for: 12 -> 12; matrix products, arithmetic and copies ran while one was open for 17% -> 17% of each run, Pallas kernels for 14% -> 14%
where the time goes in v9:
time: 106 us; the launch traced here: 105 us
  waiting for transfers between devices  44.2 us (42%)
  starting transfers between devices  24.8 us (23%)
  Pallas kernels  16.5 us (16%)
  matrix products  16.5 us (16%)
  other arithmetic  1.39 us (1%)
  local copies, waits for them, and re-layouts  1.36 us (1%)
    ppermute x8, waiting for transfers between devices, send(): lax.ppermute(ahead, 'dp', forward)  28.6 us
    dot_general x13, matrix products, contract_rows(): lax.dot_general(both, second, (((1,), (1,)), ((), ())), preferred_element...  16.5 us
    ppermute x8, starting transfers between devices, send(): lax.ppermute(behind, 'dp', backward)  14.6 us
    pallas_call x2, Pallas kernels, rotate(): pl.pallas_call(kernel, out_shape=jax.ShapeDtypeStruct((2 * rows, total),...  12.7 us
    ppermute x11, waiting for transfers between devices, swapped(): return lax.ppermute(piece, 'mp', [(i, i ^ distance) for i in range(shards)])  8.15 us
    ppermute x8, waiting for transfers between devices, send(): lax.ppermute(behind, 'dp', backward)  7.42 us
    ppermute x11, starting transfers between devices, swapped(): return lax.ppermute(piece, 'mp', [(i, i ^ distance) for i in range(shards)])  7.2 us
    pallas_call x2, Pallas kernels, pick_rows(): pl.pallas_call(kernel, out_shape=jax.ShapeDtypeStruct((per * R, total), j...  3.4 us
  transfers between devices with their start and end apart: 27, of which 12 were waited for; matrix products, arithmetic and copies ran while one was open for 17% of the time, Pallas kernels for 14%

profile of v9, /device:TPU:0, one launch (start us, length us, event | category | flops | bytes accessed | tf_op | source)
XLA Modules:
  0.0 105.2 jit_solution(11989082131776798046)
XLA Ops:
  0.0 0.7 copy-done
  0.7 1.7 %pick_rows.2 = bf16[64,4608]{1,0:T(8,128)(2,1)S(1)} custom-call(s32[16]{0:T(128)S(1)} %copy-done, bf16[1,512,2048]{2,1,0:T(8,128)(2,1)} %refs_0_.2, bf16[1,512,7168]{2,1,0:T(8,128)(2,1)} %refs_0_.3), custom_call_target="tpu_custom_call" | custom-call | tf_op jit(solution)/shard_map/pick_rows/pallas_call | solution.py:49
  2.4 3.0 %collective-permute-start.1 = (bf16[64,4608]{1,0:T(8,128)(2,1)S(1)}, bf16[64,4608]{1,0:T(8,128)(2,1)S(1)}, u32[]{:S(2)}, u32[]{:S(2)}) collective-permute-start(bf16[64,4608]{1,0:T(8,128)(2,1)S(1)} %pick_rows.2), channel_id=1, source_target_pairs={{8,0},{16,8},{24,16},{28,24},{20,28},{12,20},{4,12},{0,4},{9,1},{1... | collective-permute-start | bytes 1769480 | tf_op jit(solution)/shard_map/ppermute | solution.py:203
  5.4 0.2 collective-permute-start
  5.6 3.4 %rotate.2 = bf16[512,2048]{1,0:T(8,128)(2,1)} custom-call(s32[1]{0:T(128)} %bitcast.shard_ref, bf16[256,8192]{1,0:T(8,128)(2,1)} %matrix_ref.2, bf16[4,512,512]{2,1,0:T(8,128)(2,1)} %basis_ref.2), custom_call_target="tpu_custom_call" | custom-call | flops 536870912 | bytes 5242880 | tf_op jit(solution)/shard_map/rotate/pallas_call | solution.py:77
  8.9 1.7 %pick_rows.3 = bf16[64,4608]{1,0:T(8,128)(2,1)S(1)} custom-call(s32[16]{0:T(128)S(1)} %copy-done.1, bf16[1,512,7168]{2,1,0:T(8,128)(2,1)} %refs_0_.3), custom_call_target="tpu_custom_call" | custom-call | tf_op jit(solution)/shard_map/pick_rows/pallas_call | solution.py:49
  10.6 1.9 %collective-permute-start.8 = (bf16[64,4608]{1,0:T(8,128)(2,1)S(1)}, bf16[64,4608]{1,0:T(8,128)(2,1)S(1)}, u32[]{:S(2)}, u32[]{:S(2)}) collective-permute-start(bf16[64,4608]{1,0:T(8,128)(2,1)S(1)} %pick_rows.3), channel_id=1, source_target_pairs={{8,0},{16,8},{24,16},{28,24},{20,28},{12,20},{4,12},{0,4},{9,1},{1... | collective-permute-start | bytes 1769480 | tf_op jit(solution)/shard_map/ppermute | solution.py:203
  12.5 0.2 collective-permute-start.7
  12.7 0.2 convert_reduce_fusion
  12.9 0.1 concatenate.51
  13.1 0.1 concatenate.50
  13.2 9.4 %rotate.3 = bf16[512,7168]{1,0:T(8,128)(2,1)} custom-call(s32[1]{0:T(128)} %constant.120.clone.1.shard_ref, bf16[256,7168]{1,0:T(8,128)(2,1)} %matrix_ref.3, bf16[28,256,256]{2,1,0:T(8,128)(2,1)} %basis_ref.3), custom_call_target="tpu_custom_call" | custom-call | flops 939524096 | bytes 14680064 | tf_op jit(solution)/shard_map/rotate/pallas_call | solution.py:77
  22.6 0.2 and_convert_fusion.hit_ref
  22.8 0.0 collective-permute-done.1
  22.8 2.0 %collective-permute-start.2 = (bf16[64,4608]{1,0:T(8,128)(2,1)S(1)}, bf16[64,4608]{1,0:T(8,128)(2,1)S(1)}, u32[]{:S(2)}, u32[]{:S(2)}) collective-permute-start(bf16[64,4608]{1,0:T(8,128)(2,1)S(1)} %collective-permute-done), channel_id=1, source_target_pairs={{0,8},{8,16},{16,24},{24,28},{28,20},{20,12},{12,4},{4,0},{1,9},{9... | collective-permute-start | bytes 1769480 | tf_op jit(solution)/shard_map/ppermute | solution.py:203
  24.8 0.1 collective-permute-start.3
  24.9 7.4 %collective-permute-done.8 = bf16[64,4608]{1,0:T(8,128)(2,1)S(1)} collective-permute-done((bf16[64,4608]{1,0:T(8,128)(2,1)S(1)}, bf16[64,4608]{1,0:T(8,128)(2,1)S(1)}, u32[]{:S(2)}, u32[]{:S(2)}) %collective-permute-start.8) | collective-permute-done | bytes 589856 | tf_op jit(solution)/shard_map/ppermute | solution.py:203
  32.3 2.1 %collective-permute-done.7 = bf16[64,4608]{1,0:T(8,128)(2,1)} collective-permute-done((bf16[64,4608]{1,0:T(8,128)(2,1)S(1)}, bf16[64,4608]{1,0:T(8,128)(2,1)}, u32[]{:S(2)}, u32[]{:S(2)}) %collective-permute-start.7) | collective-permute-done | bytes 589856 | tf_op jit(solution)/shard_map/ppermute | solution.py:203
  34.4 0.1 collective-permute-start.13
  34.5 1.9 %collective-permute-start.14 = (bf16[64,4608]{1,0:T(8,128)(2,1)S(1)}, bf16[64,4608]{1,0:T(8,128)(2,1)S(1)}, u32[]{:S(2)}, u32[]{:S(2)}) collective-permute-start(bf16[64,4608]{1,0:T(8,128)(2,1)S(1)} %collective-permute-done.8), channel_id=1, source_target_pairs={{8,0},{16,8},{24,16},{28,24},{20,28},{12,20},{4,12},{0,4},{9,1},{1... | collective-permute-start | bytes 1769480 | tf_op jit(solution)/shard_map/ppermute | solution.py:203
  36.5 2.6 %fusion.18 = f32[512,128]{1,0:T(8,128)S(1)} fusion(bf16[512,7168]{1,0:T(8,128)(2,1)} %rotate.3, bf16[128,4608]{1,0:T(8,128)(2,1)S(1)} %constant_dynamic-update-slice_fusion), kind=kOutput, calls=%fused_computation.18 | convolution fusion | flops 335544320 | bytes 3538944 | tf_op jit(solution)/shard_map/dot_general | solution.py:101
  39.1 1.4 %fusion.4 = f32[512,64]{1,0:T(8,128)S(1)} fusion(bf16[64,4608]{1,0:T(8,128)(2,1)S(1)} %pick_rows.3, bf16[512,7168]{1,0:T(8,128)(2,1)S(1)} %copy-done.2), kind=kOutput, calls=%fused_computation.4 | convolution fusion | flops 301989888 | bytes 5439488 | tf_op jit(solution)/shard_map/dot_general | solution.py:101
  40.5 2.4 %fusion.8 = f32[512,128]{1,0:T(8,128)S(1)} fusion(bf16[512,7168]{1,0:T(8,128)(2,1)S(1)} %copy-done.2, bf16[64,4608]{1,0:T(8,128)(2,1)S(1)} %collective-permute-done.8, bf16[64,4608]{1,0:T(8,128)(2,1)} %collective-permute-done.7), kind=kOutput, calls=%fused_computation.8 | convolution fusion | flops 606339072 | bytes 6160384 | tf_op jit(solution)/shard_map/dot_general | solution.py:101
  42.9 0.8 fusion.14
  43.9 3.0 %collective-permute-done.2 = bf16[64,4608]{1,0:T(8,128)(2,1)S(1)} collective-permute-done((bf16[64,4608]{1,0:T(8,128)(2,1)S(1)}, bf16[64,4608]{1,0:T(8,128)(2,1)S(1)}, u32[]{:S(2)}, u32[]{:S(2)}) %collective-permute-start.2) | collective-permute-done | bytes 589856 | tf_op jit(solution)/shard_map/ppermute | solution.py:203
  47.1 1.3 %fusion.20 = f32[512,320]{1,0:T(8,128)S(1)} fusion(bf16[512,2048]{1,0:T(8,128)(2,1)S(1)} %copy-done.3, bf16[64,2048]{1,0:T(8,128)(2,1)S(1)} %slice.139, bf16[128,2048]{1,0:T(8,128)(2,1)S(1)} %slice.180, bf16[128,2048]{1,0:T(8,128)(2,1)S(1)} %slice.179), kind=kOutput, calls=%fused_computation.20 | convolution fusion | flops 675020800 | bytes 4063232 | tf_op jit(solution)/shard_map/dot_general | solution.py:101
  48.5 0.1 collective-permute-start.4
  48.5 0.2 collective-permute-start.9
  48.7 1.9 %collective-permute-start.10 = (bf16[64,4608]{1,0:T(8,128)(2,1)S(1)}, bf16[64,4608]{1,0:T(8,128)(2,1)S(1)}, u32[]{:S(2)}, u32[]{:S(2)}) collective-permute-start(bf16[64,4608]{1,0:T(8,128)(2,1)S(1)} %collective-permute-done.3), channel_id=1, source_target_pairs={{8,0},{16,8},{24,16},{28,24},{20,28},{12,20},{4,12},{0,4},{9,1},{1... | collective-permute-start | bytes 1769480 | tf_op jit(solution)/shard_map/ppermute | solution.py:203
  50.6 9.0 %collective-permute-done.13 = bf16[64,4608]{1,0:T(8,128)(2,1)S(1)} collective-permute-done((bf16[64,4608]{1,0:T(8,128)(2,1)}, bf16[64,4608]{1,0:T(8,128)(2,1)S(1)}, u32[]{:S(2)}, u32[]{:S(2)}) %collective-permute-start.13) | collective-permute-done | bytes 589856 | tf_op jit(solution)/shard_map/ppermute | solution.py:203
  59.6 0.1 collective-permute-start.17
  59.7 1.9 %collective-permute-start.18 = (bf16[64,4608]{1,0:T(8,128)(2,1)S(1)}, bf16[64,4608]{1,0:T(8,128)(2,1)S(1)}, u32[]{:S(2)}, u32[]{:S(2)}) collective-permute-start(bf16[64,4608]{1,0:T(8,128)(2,1)S(1)} %collective-permute-done.14), channel_id=1, source_target_pairs={{8,0},{16,8},{24,16},{28,24},{20,28},{12,20},{4,12},{0,4},{9,1},{1... | collective-permute-start | bytes 1769480 | tf_op jit(solution)/shard_map/ppermute | solution.py:203
  61.6 1.4 %fusion.6 = f32[512,128]{1,0:T(8,128)S(1)} fusion(bf16[512,7168]{1,0:T(8,128)(2,1)S(1)} %copy-done.2, bf16[64,4608]{1,0:T(8,128)(2,1)S(1)} %collective-permute-done.14, bf16[64,4608]{1,0:T(8,128)(2,1)S(1)} %collective-permute-done.13), kind=kOutput, calls=%fused_computation.6 | convolution fusion | flops 606339072 | bytes 6160384 | tf_op jit(solution)/shard_map/dot_general | solution.py:101
  63.0 1.6 %collective-permute-start.5 = (f32[128,320]{1,0:T(8,128)S(1)}, f32[128,320]{1,0:T(8,128)S(1)}, u32[]{:S(2)}, u32[]{:S(2)}) collective-permute-start(f32[128,320]{1,0:T(8,128)S(1)} %dynamic-slice_add_fusion), channel_id=1, source_target_pairs={{0,2},{1,3},{2,0},{3,1},{4,6},{5,7},{6,4},{7,5},{8,10},{9,11},{10,... | collective-permute-start | bytes 491528 | tf_op jit(solution)/shard_map/ppermute | solution.py:147
  64.6 0.8 fusion.16
  65.5 3.3 %collective-permute-done.5 = f32[128,320]{1,0:T(8,128)S(1)} collective-permute-done((f32[128,320]{1,0:T(8,128)S(1)}, f32[128,320]{1,0:T(8,128)S(1)}, u32[]{:S(2)}, u32[]{:S(2)}) %collective-permute-start.5) | collective-permute-done | bytes 163872 | tf_op jit(solution)/shard_map/ppermute | solution.py:147
  68.8 0.1 collective-permute-start.6
  68.9 3.3 %collective-permute-done.9 = bf16[64,4608]{1,0:T(8,128)(2,1)S(1)} collective-permute-done((bf16[64,4608]{1,0:T(8,128)(2,1)S(1)}, bf16[64,4608]{1,0:T(8,128)(2,1)S(1)}, u32[]{:S(2)}, u32[]{:S(2)}) %collective-permute-start.9) | collective-permute-done | bytes 589856 | tf_op jit(solution)/shard_map/ppermute | solution.py:203
  72.3 0.7 fusion.41
  73.1 0.1 collective-permute-start.11
  73.3 0.2 collective-permute-start.15
  73.5 1.9 %collective-permute-start.16 = (bf16[32,4608]{1,0:T(8,128)(2,1)S(1)}, bf16[32,4608]{1,0:T(8,128)(2,1)S(1)}, u32[]{:S(2)}, u32[]{:S(2)}) collective-permute-start(bf16[32,4608]{1,0:T(8,128)(2,1)S(1)} %slice.187), channel_id=1, source_target_pairs={{8,0},{16,8},{24,16},{28,24},{20,28},{12,20},{4,12},{0,4},{9,1},{1... | collective-permute-start | bytes 884744 | tf_op jit(solution)/shard_map/ppermute | solution.py:203
  75.4 1.6 %collective-permute-start.12 = (f32[256,128]{1,0:T(8,128)S(1)}, f32[256,128]{1,0:T(8,128)S(1)}, u32[]{:S(2)}, u32[]{:S(2)}) collective-permute-start(f32[256,128]{1,0:T(8,128)S(1)} %fusion.64), channel_id=1, source_target_pairs={{0,2},{1,3},{2,0},{3,1},{4,6},{5,7},{6,4},{7,5},{8,10},{9,11},{10,... | collective-permute-start | bytes 393224 | tf_op jit(solution)/shard_map/ppermute | solution.py:147
  77.0 0.9 fusion.12
  77.8 7.0 %collective-permute-done.17 = bf16[64,4608]{1,0:T(8,128)(2,1)S(1)} collective-permute-done((bf16[64,4608]{1,0:T(8,128)(2,1)S(1)}, bf16[64,4608]{1,0:T(8,128)(2,1)S(1)}, u32[]{:S(2)}, u32[]{:S(2)}) %collective-permute-start.17) | collective-permute-done | bytes 589856 | tf_op jit(solution)/shard_map/ppermute | solution.py:203
  84.9 0.2 collective-permute-start.22
  85.1 1.9 %collective-permute-start.23 = (bf16[32,4608]{1,0:T(8,128)(2,1)S(1)}, bf16[32,4608]{1,0:T(8,128)(2,1)S(1)}, u32[]{:S(2)}, u32[]{:S(2)}) collective-permute-start(bf16[32,4608]{1,0:T(8,128)(2,1)S(1)} %slice.215), channel_id=1, source_target_pairs={{8,0},{16,8},{24,16},{28,24},{20,28},{12,20},{4,12},{0,4},{9,1},{1... | collective-permute-start | bytes 884744 | tf_op jit(solution)/shard_map/ppermute | solution.py:203
  87.0 4.2 %collective-permute-done.15 = bf16[32,4608]{1,0:T(8,128)(2,1)S(1)} collective-permute-done((bf16[32,4608]{1,0:T(8,128)(2,1)S(1)}, bf16[32,4608]{1,0:T(8,128)(2,1)S(1)}, u32[]{:S(2)}, u32[]{:S(2)}) %collective-permute-start.15) | collective-permute-done | bytes 294944 | tf_op jit(solution)/shard_map/ppermute | solution.py:203
  91.2 0.7 fusion.45
  92.0 0.1 collective-permute-start.21
  92.0 1.6 %collective-permute-start.20 = (f32[256,64]{1,0:T(8,128)S(1)}, f32[256,64]{1,0:T(8,128)S(1)}, u32[]{:S(2)}, u32[]{:S(2)}) collective-permute-start(f32[256,64]{1,0:T(8,128)S(1)} %slice_add_fusion.11), channel_id=1, source_target_pairs={{0,2},{1,3},{2,0},{3,1},{4,6},{5,7},{6,4},{7,5},{8,10},{9,11},{10,... | collective-permute-start | bytes 196616 | tf_op jit(solution)/shard_map/ppermute | solution.py:147
  93.6 0.3 collective-permute-start.19
  93.9 1.4 %fusion.2 = f32[512,128]{1,0:T(8,128)S(1)} fusion(bf16[512,7168]{1,0:T(8,128)(2,1)S(1)} %copy-done.2, bf16[64,4608]{1,0:T(8,128)(2,1)S(1)} %collective-permute-done.18, bf16[64,4608]{1,0:T(8,128)(2,1)S(1)} %collective-permute-done.17), kind=kOutput, calls=%fused_computation.2 | convolution fusion | flops 606339072 | bytes 6160384 | tf_op jit(solution)/shard_map/dot_general | solution.py:101
  95.3 0.8 fusion.10
  96.1 1.4 %fusion = f32[512,64]{1,0:T(8,128)S(1)} fusion(bf16[512,7168]{1,0:T(8,128)(2,1)S(1)} %copy-done.2, bf16[32,4608]{1,0:T(8,128)(2,1)S(1)} %collective-permute-done.23, bf16[32,4608]{1,0:T(8,128)(2,1)S(1)} %collective-permute-done.22), kind=kOutput, calls=%fused_computation | convolution fusion | flops 303169536 | bytes 5439488 | tf_op jit(solution)/shard_map/dot_general | solution.py:101
  97.5 0.2 collective-permute-done.21
  97.7 2.9 %collective-permute-done.20 = f32[256,64]{1,0:T(8,128)S(1)} collective-permute-done((f32[256,64]{1,0:T(8,128)S(1)}, f32[256,64]{1,0:T(8,128)S(1)}, u32[]{:S(2)}, u32[]{:S(2)}) %collective-permute-start.20) | collective-permute-done | bytes 65568 | tf_op jit(solution)/shard_map/ppermute | solution.py:147
  100.7 0.3 score.1
  101.0 0.0 collective-permute-start.26
  101.0 1.7 %collective-permute-start.25 = (f32[2,16]{1,0:T(2,128)S(1)}, f32[2,16]{1,0:T(2,128)S(1)}, u32[]{:S(2)}, u32[]{:S(2)}) collective-permute-start(f32[2,16]{1,0:T(2,128)S(1)} %score.1), channel_id=1, source_target_pairs={{0,2},{1,3},{2,0},{3,1},{4,6},{5,7},{6,4},{7,5},{8,10},{9,11},{10,... | collective-permute-start | bytes 392 | tf_op jit(solution)/shard_map/ppermute | solution.py:147
  102.7 0.2 collective-permute-start.24
  102.9 1.1 %collective-permute-done.26 = f32[2,16]{1,0:T(2,128)S(1)} collective-permute-done((f32[2,16]{1,0:T(2,128)S(1)}, f32[2,16]{1,0:T(2,128)S(1)}, u32[]{:S(2)}, u32[]{:S(2)}) %collective-permute-start.26) | collective-permute-done | bytes 160 | tf_op jit(solution)/shard_map/ppermute | solution.py:147
  104.0 0.6 collective-permute-done.25
  104.7 0.6 add_add_fusion.1
  (63 shorter events, 1.0 us)
Async XLA Ops:
  0.0 0.7 copy-start
  2.4 20.4 %collective-permute-start.1 = (bf16[64,4608]{1,0:T(8,128)(2,1)S(1)}, bf16[64,4608]{1,0:T(8,128)(2,1)S(1)}, u32[]{:S(2)}, u32[]{:S(2)}) collective-permute-start(bf16[64,4608]{1,0:T(8,128)(2,1)S(1)} %pick_rows.2), channel_id=1, source_target_pairs={{8,0},{16,8},{24,16},{28,24},{20,28},{12,20},{4,12},{0,4},{9,1},{1... | collective-permute-start | bytes 1769480 | tf_op jit(solution)/shard_map/ppermute | solution.py:203
  5.4 17.4 %collective-permute-start = (bf16[64,4608]{1,0:T(8,128)(2,1)S(1)}, bf16[64,4608]{1,0:T(8,128)(2,1)S(1)}, u32[]{:S(2)}, u32[]{:S(2)}) collective-permute-start(bf16[64,4608]{1,0:T(8,128)(2,1)S(1)} %pick_rows.2), channel_id=1, source_target_pairs={{0,8},{8,16},{16,24},{24,28},{28,20},{20,12},{12,4},{4,0},{1,9},{9... | collective-permute-start | bytes 1769480 | tf_op jit(solution)/shard_map/ppermute | solution.py:203
  5.6 3.4 %copy-start.1 = (s32[16]{0:T(128)S(1)}, s32[16]{0:T(128)}, u32[]{:S(2)}) copy-start(s32[16]{0:T(128)} %owners_ref.2) | copy-start | bytes 196
  10.6 21.7 %collective-permute-start.8 = (bf16[64,4608]{1,0:T(8,128)(2,1)S(1)}, bf16[64,4608]{1,0:T(8,128)(2,1)S(1)}, u32[]{:S(2)}, u32[]{:S(2)}) collective-permute-start(bf16[64,4608]{1,0:T(8,128)(2,1)S(1)} %pick_rows.3), channel_id=1, source_target_pairs={{8,0},{16,8},{24,16},{28,24},{20,28},{12,20},{4,12},{0,4},{9,1},{1... | collective-permute-start | bytes 1769480 | tf_op jit(solution)/shard_map/ppermute | solution.py:203
  12.5 21.9 %collective-permute-start.7 = (bf16[64,4608]{1,0:T(8,128)(2,1)S(1)}, bf16[64,4608]{1,0:T(8,128)(2,1)}, u32[]{:S(2)}, u32[]{:S(2)}) collective-permute-start(bf16[64,4608]{1,0:T(8,128)(2,1)S(1)} %pick_rows.3), channel_id=1, source_target_pairs={{0,8},{8,16},{16,24},{24,28},{28,20},{20,12},{12,4},{4,0},{1,9},{9... | collective-permute-start | bytes 1769480 | tf_op jit(solution)/shard_map/ppermute | solution.py:203
  22.6 16.5 %copy-start.2 = (bf16[512,7168]{1,0:T(8,128)(2,1)S(1)}, bf16[512,7168]{1,0:T(8,128)(2,1)}, u32[]{:S(2)}) copy-start(bf16[512,7168]{1,0:T(8,128)(2,1)} %rotate.3) | copy-start | bytes 22020100
  22.8 24.1 %collective-permute-start.2 = (bf16[64,4608]{1,0:T(8,128)(2,1)S(1)}, bf16[64,4608]{1,0:T(8,128)(2,1)S(1)}, u32[]{:S(2)}, u32[]{:S(2)}) collective-permute-start(bf16[64,4608]{1,0:T(8,128)(2,1)S(1)} %collective-permute-done), channel_id=1, source_target_pairs={{0,8},{8,16},{16,24},{24,28},{28,20},{20,12},{12,4},{4,0},{1,9},{9... | collective-permute-start | bytes 1769480 | tf_op jit(solution)/shard_map/ppermute | solution.py:203
  24.8 22.2 %collective-permute-start.3 = (bf16[64,4608]{1,0:T(8,128)(2,1)S(1)}, bf16[64,4608]{1,0:T(8,128)(2,1)S(1)}, u32[]{:S(2)}, u32[]{:S(2)}) collective-permute-start(bf16[64,4608]{1,0:T(8,128)(2,1)S(1)} %collective-permute-done.1), channel_id=1, source_target_pairs={{8,0},{16,8},{24,16},{28,24},{20,28},{12,20},{4,12},{0,4},{9,1},{1... | collective-permute-start | bytes 1769480 | tf_op jit(solution)/shard_map/ppermute | solution.py:203
  34.4 25.2 %collective-permute-start.13 = (bf16[64,4608]{1,0:T(8,128)(2,1)}, bf16[64,4608]{1,0:T(8,128)(2,1)S(1)}, u32[]{:S(2)}, u32[]{:S(2)}) collective-permute-start(bf16[64,4608]{1,0:T(8,128)(2,1)} %collective-permute-done.7), channel_id=1, source_target_pairs={{0,8},{8,16},{16,24},{24,28},{28,20},{20,12},{12,4},{4,0},{1,9},{9... | collective-permute-start | bytes 1769480 | tf_op jit(solution)/shard_map/ppermute | solution.py:203
  34.5 25.1 %collective-permute-start.14 = (bf16[64,4608]{1,0:T(8,128)(2,1)S(1)}, bf16[64,4608]{1,0:T(8,128)(2,1)S(1)}, u32[]{:S(2)}, u32[]{:S(2)}) collective-permute-start(bf16[64,4608]{1,0:T(8,128)(2,1)S(1)} %collective-permute-done.8), channel_id=1, source_target_pairs={{8,0},{16,8},{24,16},{28,24},{20,28},{12,20},{4,12},{0,4},{9,1},{1... | collective-permute-start | bytes 1769480 | tf_op jit(solution)/shard_map/ppermute | solution.py:203
  43.8 3.3 %copy-start.3 = (bf16[512,2048]{1,0:T(8,128)(2,1)S(1)}, bf16[512,2048]{1,0:T(8,128)(2,1)}, u32[]{:S(2)}) copy-start(bf16[512,2048]{1,0:T(8,128)(2,1)} %rotate.2) | copy-start | bytes 6291460
  48.5 14.5 %collective-permute-start.4 = (f32[128,320]{1,0:T(8,128)S(1)}, f32[128,320]{1,0:T(8,128)S(1)}, u32[]{:S(2)}, u32[]{:S(2)}) collective-permute-start(f32[128,320]{1,0:T(8,128)S(1)} %constant_dynamic-slice_fusion), channel_id=1, source_target_pairs={{0,1},{1,0},{2,3},{3,2},{4,5},{5,4},{6,7},{7,6},{8,9},{9,8},{10,11... | collective-permute-start | bytes 491528 | tf_op jit(solution)/shard_map/ppermute | solution.py:147
  48.5 23.7 %collective-permute-start.9 = (bf16[64,4608]{1,0:T(8,128)(2,1)S(1)}, bf16[64,4608]{1,0:T(8,128)(2,1)S(1)}, u32[]{:S(2)}, u32[]{:S(2)}) collective-permute-start(bf16[64,4608]{1,0:T(8,128)(2,1)S(1)} %collective-permute-done.2), channel_id=1, source_target_pairs={{0,8},{8,16},{16,24},{24,28},{28,20},{20,12},{12,4},{4,0},{1,9},{9... | collective-permute-start | bytes 1769480 | tf_op jit(solution)/shard_map/ppermute | solution.py:203
  48.7 23.6 %collective-permute-start.10 = (bf16[64,4608]{1,0:T(8,128)(2,1)S(1)}, bf16[64,4608]{1,0:T(8,128)(2,1)S(1)}, u32[]{:S(2)}, u32[]{:S(2)}) collective-permute-start(bf16[64,4608]{1,0:T(8,128)(2,1)S(1)} %collective-permute-done.3), channel_id=1, source_target_pairs={{8,0},{16,8},{24,16},{28,24},{20,28},{12,20},{4,12},{0,4},{9,1},{1... | collective-permute-start | bytes 1769480 | tf_op jit(solution)/shard_map/ppermute | solution.py:203
  59.6 25.3 %collective-permute-start.17 = (bf16[64,4608]{1,0:T(8,128)(2,1)S(1)}, bf16[64,4608]{1,0:T(8,128)(2,1)S(1)}, u32[]{:S(2)}, u32[]{:S(2)}) collective-permute-start(bf16[64,4608]{1,0:T(8,128)(2,1)S(1)} %collective-permute-done.13), channel_id=1, source_target_pairs={{0,8},{8,16},{16,24},{24,28},{28,20},{20,12},{12,4},{4,0},{1,9},{9... | collective-permute-start | bytes 1769480 | tf_op jit(solution)/shard_map/ppermute | solution.py:203
  59.7 25.2 %collective-permute-start.18 = (bf16[64,4608]{1,0:T(8,128)(2,1)S(1)}, bf16[64,4608]{1,0:T(8,128)(2,1)S(1)}, u32[]{:S(2)}, u32[]{:S(2)}) collective-permute-start(bf16[64,4608]{1,0:T(8,128)(2,1)S(1)} %collective-permute-done.14), channel_id=1, source_target_pairs={{8,0},{16,8},{24,16},{28,24},{20,28},{12,20},{4,12},{0,4},{9,1},{1... | collective-permute-start | bytes 1769480 | tf_op jit(solution)/shard_map/ppermute | solution.py:203
  63.0 5.7 %collective-permute-start.5 = (f32[128,320]{1,0:T(8,128)S(1)}, f32[128,320]{1,0:T(8,128)S(1)}, u32[]{:S(2)}, u32[]{:S(2)}) collective-permute-start(f32[128,320]{1,0:T(8,128)S(1)} %dynamic-slice_add_fusion), channel_id=1, source_target_pairs={{0,2},{1,3},{2,0},{3,1},{4,6},{5,7},{6,4},{7,5},{8,10},{9,11},{10,... | collective-permute-start | bytes 491528 | tf_op jit(solution)/shard_map/ppermute | solution.py:147
  68.8 4.4 %collective-permute-start.6 = (f32[128,320]{1,0:T(8,128)S(1)}, f32[128,320]{1,0:T(8,128)S(1)}, u32[]{:S(2)}, u32[]{:S(2)}) collective-permute-start(f32[128,320]{1,0:T(8,128)S(1)} %add.202), channel_id=1, source_target_pairs={{0,1},{1,0},{2,3},{3,2},{4,5},{5,4},{6,7},{7,6},{8,9},{9,8},{10,11... | collective-permute-start | bytes 491528 | tf_op jit(solution)/shard_map/ppermute | solution.py:147
  73.1 2.3 %collective-permute-start.11 = (f32[256,128]{1,0:T(8,128)S(1)}, f32[256,128]{1,0:T(8,128)S(1)}, u32[]{:S(2)}, u32[]{:S(2)}) collective-permute-start(f32[256,128]{1,0:T(8,128)S(1)} %slice_add_fusion.12), channel_id=1, source_target_pairs={{0,1},{1,0},{2,3},{3,2},{4,5},{5,4},{6,7},{7,6},{8,9},{9,8},{10,11... | collective-permute-start | bytes 393224 | tf_op jit(solution)/shard_map/ppermute | solution.py:147
  73.3 17.9 %collective-permute-start.15 = (bf16[32,4608]{1,0:T(8,128)(2,1)S(1)}, bf16[32,4608]{1,0:T(8,128)(2,1)S(1)}, u32[]{:S(2)}, u32[]{:S(2)}) collective-permute-start(bf16[32,4608]{1,0:T(8,128)(2,1)S(1)} %slice.186), channel_id=1, source_target_pairs={{0,8},{8,16},{16,24},{24,28},{28,20},{20,12},{12,4},{4,0},{1,9},{9... | collective-permute-start | bytes 884744 | tf_op jit(solution)/shard_map/ppermute | solution.py:203
  73.5 17.7 %collective-permute-start.16 = (bf16[32,4608]{1,0:T(8,128)(2,1)S(1)}, bf16[32,4608]{1,0:T(8,128)(2,1)S(1)}, u32[]{:S(2)}, u32[]{:S(2)}) collective-permute-start(bf16[32,4608]{1,0:T(8,128)(2,1)S(1)} %slice.187), channel_id=1, source_target_pairs={{8,0},{16,8},{24,16},{28,24},{20,28},{12,20},{4,12},{0,4},{9,1},{1... | collective-permute-start | bytes 884744 | tf_op jit(solution)/shard_map/ppermute | solution.py:203
  75.4 11.6 %collective-permute-start.12 = (f32[256,128]{1,0:T(8,128)S(1)}, f32[256,128]{1,0:T(8,128)S(1)}, u32[]{:S(2)}, u32[]{:S(2)}) collective-permute-start(f32[256,128]{1,0:T(8,128)S(1)} %fusion.64), channel_id=1, source_target_pairs={{0,2},{1,3},{2,0},{3,1},{4,6},{5,7},{6,4},{7,5},{8,10},{9,11},{10,... | collective-permute-start | bytes 393224 | tf_op jit(solution)/shard_map/ppermute | solution.py:147
  84.9 11.2 %collective-permute-start.22 = (bf16[32,4608]{1,0:T(8,128)(2,1)S(1)}, bf16[32,4608]{1,0:T(8,128)(2,1)S(1)}, u32[]{:S(2)}, u32[]{:S(2)}) collective-permute-start(bf16[32,4608]{1,0:T(8,128)(2,1)S(1)} %slice.214), channel_id=1, source_target_pairs={{0,8},{8,16},{16,24},{24,28},{28,20},{20,12},{12,4},{4,0},{1,9},{9... | collective-permute-start | bytes 884744 | tf_op jit(solution)/shard_map/ppermute | solution.py:203
  85.1 11.1 %collective-permute-start.23 = (bf16[32,4608]{1,0:T(8,128)(2,1)S(1)}, bf16[32,4608]{1,0:T(8,128)(2,1)S(1)}, u32[]{:S(2)}, u32[]{:S(2)}) collective-permute-start(bf16[32,4608]{1,0:T(8,128)(2,1)S(1)} %slice.215), channel_id=1, source_target_pairs={{8,0},{16,8},{24,16},{28,24},{20,28},{12,20},{4,12},{0,4},{9,1},{1... | collective-permute-start | bytes 884744 | tf_op jit(solution)/shard_map/ppermute | solution.py:203
  92.0 5.8 %collective-permute-start.21 = (f32[256,64]{1,0:T(8,128)S(1)}, f32[256,64]{1,0:T(8,128)S(1)}, u32[]{:S(2)}, u32[]{:S(2)}) collective-permute-start(f32[256,64]{1,0:T(8,128)S(1)} %slice_add_fusion.11), channel_id=1, source_target_pairs={{0,3},{1,2},{2,1},{3,0},{4,7},{5,6},{6,5},{7,4},{8,11},{9,10},{10,... | collective-permute-start | bytes 196616 | tf_op jit(solution)/shard_map/ppermute | solution.py:147
  92.0 8.6 %collective-permute-start.20 = (f32[256,64]{1,0:T(8,128)S(1)}, f32[256,64]{1,0:T(8,128)S(1)}, u32[]{:S(2)}, u32[]{:S(2)}) collective-permute-start(f32[256,64]{1,0:T(8,128)S(1)} %slice_add_fusion.11), channel_id=1, source_target_pairs={{0,2},{1,3},{2,0},{3,1},{4,6},{5,7},{6,4},{7,5},{8,10},{9,11},{10,... | collective-permute-start | bytes 196616 | tf_op jit(solution)/shard_map/ppermute | solution.py:147
  93.6 7.0 %collective-permute-start.19 = (f32[256,64]{1,0:T(8,128)S(1)}, f32[256,64]{1,0:T(8,128)S(1)}, u32[]{:S(2)}, u32[]{:S(2)}) collective-permute-start(f32[256,64]{1,0:T(8,128)S(1)} %slice_add_fusion.11), channel_id=1, source_target_pairs={{0,1},{1,0},{2,3},{3,2},{4,5},{5,4},{6,7},{7,6},{8,9},{9,8},{10,11... | collective-permute-start | bytes 196616 | tf_op jit(solution)/shard_map/ppermute | solution.py:147
  101.0 3.0 %collective-permute-start.26 = (f32[2,16]{1,0:T(2,128)S(1)}, f32[2,16]{1,0:T(2,128)S(1)}, u32[]{:S(2)}, u32[]{:S(2)}) collective-permute-start(f32[2,16]{1,0:T(2,128)S(1)} %score.1), channel_id=1, source_target_pairs={{0,3},{1,2},{2,1},{3,0},{4,7},{5,6},{6,5},{7,4},{8,11},{9,10},{10,... | collective-permute-start | bytes 392 | tf_op jit(solution)/shard_map/ppermute | solution.py:147
  101.0 3.6 %collective-permute-start.25 = (f32[2,16]{1,0:T(2,128)S(1)}, f32[2,16]{1,0:T(2,128)S(1)}, u32[]{:S(2)}, u32[]{:S(2)}) collective-permute-start(f32[2,16]{1,0:T(2,128)S(1)} %score.1), channel_id=1, source_target_pairs={{0,2},{1,3},{2,0},{3,1},{4,6},{5,7},{6,4},{7,5},{8,10},{9,11},{10,... | collective-permute-start | bytes 392 | tf_op jit(solution)/shard_map/ppermute | solution.py:147
  102.7 1.9 %collective-permute-start.24 = (f32[2,16]{1,0:T(2,128)S(1)}, f32[2,16]{1,0:T(2,128)S(1)}, u32[]{:S(2)}, u32[]{:S(2)}) collective-permute-start(f32[2,16]{1,0:T(2,128)S(1)} %score.1), channel_id=1, source_target_pairs={{0,1},{1,0},{2,3},{3,2},{4,5},{5,4},{6,7},{7,6},{8,9},{9,8},{10,11... | collective-permute-start | bytes 392 | tf_op jit(solution)/shard_map/ppermute | solution.py:147

commit v10 on v9

--- a/solution.py
+++ b/solution.py
@@ -105,7 +105,7 @@
 
 
 def score(coefficients, projected, hit):
-    sequences = coefficients[0].shape[0] // LEN
+    sequences = projected[0].shape[0] // LEN
     count = len(coefficients)
 
     def kernel(hit_ref, *refs):
@@ -116,10 +116,18 @@
             width = part_ref.shape[1]
             if base == refs[which].shape[1]:
                 which, base = which + 1, 0
-            terms = refs[which][:, base : base + width] * part_ref[...]
-            base += width
+            if which < count - 1:
+                terms = (refs[which][:, base : base + width] * part_ref[...]).reshape(sequences, LEN, width)
+                base += width
+            else:
+                terms = jnp.stack(
+                    [
+                        refs[which][:, i * width : (i + 1) * width] * part_ref[i * LEN : (i + 1) * LEN, :]
+                        for i in range(sequences)
+                    ]
+                )
             out += jnp.dot(
-                jnp.sum(terms.reshape(sequences, LEN, width), axis=1) * (1.0 / LEN),
+                jnp.sum(terms, axis=1) * (1.0 / LEN),
                 hit_ref[at : at + width, :],
                 precision=lax.Precision.HIGHEST,
                 preferred_element_type=jnp.float32,
@@ -227,7 +235,8 @@
     last = after(steps[0][-1], came[-3])
     second.append(side_by_side(after(steps[1][reach - 2], last)))
     last = side_by_side(last)
-    part = contract_rows(grads, last[:, :width_left])
+    part = contract_rows(grads, last[:, :width_left]).reshape(-1, LEN, chunk)
+    part = jnp.concatenate([part[i] for i in range(part.shape[0])], axis=1)
     last_sum = small_sum(part, shards, 4)
     first.append(after(last, part))
     second.append(side_by_side(steps[1][-1]))

time: 106 us -> 104 us (0.981)
  waiting for transfers between devices: 44.2 us -> 42.3 us
    ppermute x11, waiting for transfers between devices: 8.15 us -> 6.19 us  [swapped(): return lax.ppermute(piece, 'mp', [(i, i ^ distance) for i in range(shards)])]
  transfers between devices with their start and end apart: 27 -> 27, of which waited for: 12 -> 11; matrix products, arithmetic and copies ran while one was open for 17% -> 17% of each run, Pallas kernels for 14% -> 14%
where the time goes in v10:
time: 104 us; the launch traced here: 103 us
  waiting for transfers between devices  42.3 us (41%)
  starting transfers between devices  24.8 us (24%)
  matrix products  16.5 us (16%)
  Pallas kernels  16.4 us (16%)
  other arithmetic  1.43 us (1%)
  local copies, waits for them, and re-layouts  1.38 us (1%)
    ppermute x8, waiting for transfers between devices, send(): lax.ppermute(ahead, 'dp', forward)  28.6 us
    dot_general x13, matrix products, contract_rows(): lax.dot_general(both, second, (((1,), (1,)), ((), ())), preferred_element...  16.5 us
    ppermute x8, starting transfers between devices, send(): lax.ppermute(behind, 'dp', backward)  14.6 us
    pallas_call x2, Pallas kernels, rotate(): pl.pallas_call(kernel, out_shape=jax.ShapeDtypeStruct((2 * rows, total),...  12.7 us
    ppermute x8, waiting for transfers between devices, send(): lax.ppermute(behind, 'dp', backward)  7.46 us
    ppermute x11, starting transfers between devices, swapped(): return lax.ppermute(piece, 'mp', [(i, i ^ distance) for i in range(shards)])  7.2 us
    ppermute x11, waiting for transfers between devices, swapped(): return lax.ppermute(piece, 'mp', [(i, i ^ distance) for i in range(shards)])  6.19 us
    pallas_call x2, Pallas kernels, pick_rows(): pl.pallas_call(kernel, out_shape=jax.ShapeDtypeStruct((per * R, total), j...  3.4 us
  transfers between devices with their start and end apart: 27, of which 11 were waited for; matrix products, arithmetic and copies ran while one was open for 17% of the time, Pallas kernels for 14%

profile of v10, /device:TPU:0, one launch (start us, length us, event | category | flops | bytes accessed | tf_op | source)
XLA Modules:
  0.0 103.4 jit_solution(2724982619849069688)
XLA Ops:
  0.0 0.7 copy-done
  0.7 1.7 %pick_rows.2 = bf16[64,4608]{1,0:T(8,128)(2,1)S(1)} custom-call(s32[16]{0:T(128)S(1)} %copy-done, bf16[1,512,2048]{2,1,0:T(8,128)(2,1)} %refs_0_.2, bf16[1,512,7168]{2,1,0:T(8,128)(2,1)} %refs_0_.3), custom_call_target="tpu_custom_call" | custom-call | tf_op jit(solution)/shard_map/pick_rows/pallas_call | solution.py:49
  2.4 3.0 %collective-permute-start.1 = (bf16[64,4608]{1,0:T(8,128)(2,1)S(1)}, bf16[64,4608]{1,0:T(8,128)(2,1)S(1)}, u32[]{:S(2)}, u32[]{:S(2)}) collective-permute-start(bf16[64,4608]{1,0:T(8,128)(2,1)S(1)} %pick_rows.2), channel_id=1, source_target_pairs={{8,0},{16,8},{24,16},{28,24},{20,28},{12,20},{4,12},{0,4},{9,1},{1... | collective-permute-start | bytes 1769480 | tf_op jit(solution)/shard_map/ppermute | solution.py:211
  5.4 0.2 collective-permute-start
  5.6 3.3 %rotate.2 = bf16[512,2048]{1,0:T(8,128)(2,1)} custom-call(s32[1]{0:T(128)} %bitcast.shard_ref, bf16[256,8192]{1,0:T(8,128)(2,1)} %matrix_ref.2, bf16[4,512,512]{2,1,0:T(8,128)(2,1)} %basis_ref.2), custom_call_target="tpu_custom_call" | custom-call | flops 536870912 | bytes 5242880 | tf_op jit(solution)/shard_map/rotate/pallas_call | solution.py:77
  8.9 1.7 %pick_rows.3 = bf16[64,4608]{1,0:T(8,128)(2,1)S(1)} custom-call(s32[16]{0:T(128)S(1)} %copy-done.1, bf16[1,512,7168]{2,1,0:T(8,128)(2,1)} %refs_0_.3), custom_call_target="tpu_custom_call" | custom-call | tf_op jit(solution)/shard_map/pick_rows/pallas_call | solution.py:49
  10.6 1.9 %collective-permute-start.8 = (bf16[64,4608]{1,0:T(8,128)(2,1)S(1)}, bf16[64,4608]{1,0:T(8,128)(2,1)S(1)}, u32[]{:S(2)}, u32[]{:S(2)}) collective-permute-start(bf16[64,4608]{1,0:T(8,128)(2,1)S(1)} %pick_rows.3), channel_id=1, source_target_pairs={{8,0},{16,8},{24,16},{28,24},{20,28},{12,20},{4,12},{0,4},{9,1},{1... | collective-permute-start | bytes 1769480 | tf_op jit(solution)/shard_map/ppermute | solution.py:211
  12.5 0.2 collective-permute-start.7
  12.7 0.2 convert_reduce_fusion
  12.9 0.1 concatenate.54
  13.1 0.1 concatenate.53
  13.2 9.4 %rotate.3 = bf16[512,7168]{1,0:T(8,128)(2,1)} custom-call(s32[1]{0:T(128)} %constant.120.clone.1.shard_ref, bf16[256,7168]{1,0:T(8,128)(2,1)} %matrix_ref.3, bf16[28,256,256]{2,1,0:T(8,128)(2,1)} %basis_ref.3), custom_call_target="tpu_custom_call" | custom-call | flops 939524096 | bytes 14680064 | tf_op jit(solution)/shard_map/rotate/pallas_call | solution.py:77
  22.5 0.2 and_convert_fusion.hit_ref
  22.7 0.0 collective-permute-done.1
  22.8 2.0 %collective-permute-start.2 = (bf16[64,4608]{1,0:T(8,128)(2,1)S(1)}, bf16[64,4608]{1,0:T(8,128)(2,1)S(1)}, u32[]{:S(2)}, u32[]{:S(2)}) collective-permute-start(bf16[64,4608]{1,0:T(8,128)(2,1)S(1)} %collective-permute-done), channel_id=1, source_target_pairs={{0,8},{8,16},{16,24},{24,28},{28,20},{20,12},{12,4},{4,0},{1,9},{9... | collective-permute-start | bytes 1769480 | tf_op jit(solution)/shard_map/ppermute | solution.py:211
  24.8 0.1 collective-permute-start.3
  24.8 7.4 %collective-permute-done.8 = bf16[64,4608]{1,0:T(8,128)(2,1)S(1)} collective-permute-done((bf16[64,4608]{1,0:T(8,128)(2,1)S(1)}, bf16[64,4608]{1,0:T(8,128)(2,1)S(1)}, u32[]{:S(2)}, u32[]{:S(2)}) %collective-permute-start.8) | collective-permute-done | bytes 589856 | tf_op jit(solution)/shard_map/ppermute | solution.py:211
  32.3 2.1 %collective-permute-done.7 = bf16[64,4608]{1,0:T(8,128)(2,1)} collective-permute-done((bf16[64,4608]{1,0:T(8,128)(2,1)S(1)}, bf16[64,4608]{1,0:T(8,128)(2,1)}, u32[]{:S(2)}, u32[]{:S(2)}) %collective-permute-start.7) | collective-permute-done | bytes 589856 | tf_op jit(solution)/shard_map/ppermute | solution.py:211
  34.4 0.1 collective-permute-start.13
  34.5 1.9 %collective-permute-start.14 = (bf16[64,4608]{1,0:T(8,128)(2,1)S(1)}, bf16[64,4608]{1,0:T(8,128)(2,1)S(1)}, u32[]{:S(2)}, u32[]{:S(2)}) collective-permute-start(bf16[64,4608]{1,0:T(8,128)(2,1)S(1)} %collective-permute-done.8), channel_id=1, source_target_pairs={{8,0},{16,8},{24,16},{28,24},{20,28},{12,20},{4,12},{0,4},{9,1},{1... | collective-permute-start | bytes 1769480 | tf_op jit(solution)/shard_map/ppermute | solution.py:211
  36.5 2.6 %fusion.18 = f32[512,128]{1,0:T(8,128)S(1)} fusion(bf16[512,7168]{1,0:T(8,128)(2,1)} %rotate.3, bf16[128,4608]{1,0:T(8,128)(2,1)S(1)} %constant_dynamic-update-slice_fusion), kind=kOutput, calls=%fused_computation.18 | convolution fusion | flops 335544320 | bytes 3538944 | tf_op jit(solution)/shard_map/dot_general | solution.py:101
  39.1 1.4 %fusion.4 = f32[512,64]{1,0:T(8,128)S(1)} fusion(bf16[64,4608]{1,0:T(8,128)(2,1)S(1)} %pick_rows.3, bf16[512,7168]{1,0:T(8,128)(2,1)S(1)} %copy-done.2), kind=kOutput, calls=%fused_computation.4 | convolution fusion | flops 301989888 | bytes 5439488 | tf_op jit(solution)/shard_map/dot_general | solution.py:101
  40.5 2.4 %fusion.8 = f32[512,128]{1,0:T(8,128)S(1)} fusion(bf16[512,7168]{1,0:T(8,128)(2,1)S(1)} %copy-done.2, bf16[64,4608]{1,0:T(8,128)(2,1)S(1)} %collective-permute-done.8, bf16[64,4608]{1,0:T(8,128)(2,1)} %collective-permute-done.7), kind=kOutput, calls=%fused_computation.8 | convolution fusion | flops 606339072 | bytes 6160384 | tf_op jit(solution)/shard_map/dot_general | solution.py:101
  42.9 0.8 fusion.14
  43.9 3.0 %collective-permute-done.2 = bf16[64,4608]{1,0:T(8,128)(2,1)S(1)} collective-permute-done((bf16[64,4608]{1,0:T(8,128)(2,1)S(1)}, bf16[64,4608]{1,0:T(8,128)(2,1)S(1)}, u32[]{:S(2)}, u32[]{:S(2)}) %collective-permute-start.2) | collective-permute-done | bytes 589856 | tf_op jit(solution)/shard_map/ppermute | solution.py:211
  47.1 1.3 %fusion.20 = f32[512,320]{1,0:T(8,128)S(1)} fusion(bf16[512,2048]{1,0:T(8,128)(2,1)S(1)} %copy-done.3, bf16[64,2048]{1,0:T(8,128)(2,1)S(1)} %slice.147, bf16[128,2048]{1,0:T(8,128)(2,1)S(1)} %slice.190, bf16[128,2048]{1,0:T(8,128)(2,1)S(1)} %slice.189), kind=kOutput, calls=%fused_computation.20 | convolution fusion | flops 675020800 | bytes 4063232 | tf_op jit(solution)/shard_map/dot_general | solution.py:101
  48.5 0.1 collective-permute-start.4
  48.5 0.2 collective-permute-start.9
  48.7 1.9 %collective-permute-start.10 = (bf16[64,4608]{1,0:T(8,128)(2,1)S(1)}, bf16[64,4608]{1,0:T(8,128)(2,1)S(1)}, u32[]{:S(2)}, u32[]{:S(2)}) collective-permute-start(bf16[64,4608]{1,0:T(8,128)(2,1)S(1)} %collective-permute-done.3), channel_id=1, source_target_pairs={{8,0},{16,8},{24,16},{28,24},{20,28},{12,20},{4,12},{0,4},{9,1},{1... | collective-permute-start | bytes 1769480 | tf_op jit(solution)/shard_map/ppermute | solution.py:211
  50.6 9.0 %collective-permute-done.13 = bf16[64,4608]{1,0:T(8,128)(2,1)S(1)} collective-permute-done((bf16[64,4608]{1,0:T(8,128)(2,1)}, bf16[64,4608]{1,0:T(8,128)(2,1)S(1)}, u32[]{:S(2)}, u32[]{:S(2)}) %collective-permute-start.13) | collective-permute-done | bytes 589856 | tf_op jit(solution)/shard_map/ppermute | solution.py:211
  59.6 0.1 collective-permute-start.17
  59.7 1.9 %collective-permute-start.18 = (bf16[64,4608]{1,0:T(8,128)(2,1)S(1)}, bf16[64,4608]{1,0:T(8,128)(2,1)S(1)}, u32[]{:S(2)}, u32[]{:S(2)}) collective-permute-start(bf16[64,4608]{1,0:T(8,128)(2,1)S(1)} %collective-permute-done.14), channel_id=1, source_target_pairs={{8,0},{16,8},{24,16},{28,24},{20,28},{12,20},{4,12},{0,4},{9,1},{1... | collective-permute-start | bytes 1769480 | tf_op jit(solution)/shard_map/ppermute | solution.py:211
  61.6 1.4 %fusion.6 = f32[512,128]{1,0:T(8,128)S(1)} fusion(bf16[512,7168]{1,0:T(8,128)(2,1)S(1)} %copy-done.2, bf16[64,4608]{1,0:T(8,128)(2,1)S(1)} %collective-permute-done.14, bf16[64,4608]{1,0:T(8,128)(2,1)S(1)} %collective-permute-done.13), kind=kOutput, calls=%fused_computation.6 | convolution fusion | flops 606339072 | bytes 6160384 | tf_op jit(solution)/shard_map/dot_general | solution.py:101
  63.0 1.6 %collective-permute-start.5 = (f32[128,320]{1,0:T(8,128)S(1)}, f32[128,320]{1,0:T(8,128)S(1)}, u32[]{:S(2)}, u32[]{:S(2)}) collective-permute-start(f32[128,320]{1,0:T(8,128)S(1)} %dynamic-slice_add_fusion), channel_id=1, source_target_pairs={{0,2},{1,3},{2,0},{3,1},{4,6},{5,7},{6,4},{7,5},{8,10},{9,11},{10,... | collective-permute-start | bytes 491528 | tf_op jit(solution)/shard_map/ppermute | solution.py:155
  64.6 0.8 fusion.16
  65.5 3.3 %collective-permute-done.5 = f32[128,320]{1,0:T(8,128)S(1)} collective-permute-done((f32[128,320]{1,0:T(8,128)S(1)}, f32[128,320]{1,0:T(8,128)S(1)}, u32[]{:S(2)}, u32[]{:S(2)}) %collective-permute-start.5) | collective-permute-done | bytes 163872 | tf_op jit(solution)/shard_map/ppermute | solution.py:155
  68.8 0.1 collective-permute-start.6
  68.9 3.3 %collective-permute-done.9 = bf16[64,4608]{1,0:T(8,128)(2,1)S(1)} collective-permute-done((bf16[64,4608]{1,0:T(8,128)(2,1)S(1)}, bf16[64,4608]{1,0:T(8,128)(2,1)S(1)}, u32[]{:S(2)}, u32[]{:S(2)}) %collective-permute-start.9) | collective-permute-done | bytes 589856 | tf_op jit(solution)/shard_map/ppermute | solution.py:211
  72.3 0.7 fusion.41
  73.1 0.1 collective-permute-start.11
  73.3 0.2 collective-permute-start.15
  73.5 1.9 %collective-permute-start.16 = (bf16[32,4608]{1,0:T(8,128)(2,1)S(1)}, bf16[32,4608]{1,0:T(8,128)(2,1)S(1)}, u32[]{:S(2)}, u32[]{:S(2)}) collective-permute-start(bf16[32,4608]{1,0:T(8,128)(2,1)S(1)} %slice.197), channel_id=1, source_target_pairs={{8,0},{16,8},{24,16},{28,24},{20,28},{12,20},{4,12},{0,4},{9,1},{1... | collective-permute-start | bytes 884744 | tf_op jit(solution)/shard_map/ppermute | solution.py:211
  75.4 1.6 %collective-permute-start.12 = (f32[256,128]{1,0:T(8,128)S(1)}, f32[256,128]{1,0:T(8,128)S(1)}, u32[]{:S(2)}, u32[]{:S(2)}) collective-permute-start(f32[256,128]{1,0:T(8,128)S(1)} %fusion.65), channel_id=1, source_target_pairs={{0,2},{1,3},{2,0},{3,1},{4,6},{5,7},{6,4},{7,5},{8,10},{9,11},{10,... | collective-permute-start | bytes 393224 | tf_op jit(solution)/shard_map/ppermute | solution.py:155
  77.0 0.8 fusion.12
  77.8 7.0 %collective-permute-done.17 = bf16[64,4608]{1,0:T(8,128)(2,1)S(1)} collective-permute-done((bf16[64,4608]{1,0:T(8,128)(2,1)S(1)}, bf16[64,4608]{1,0:T(8,128)(2,1)S(1)}, u32[]{:S(2)}, u32[]{:S(2)}) %collective-permute-start.17) | collective-permute-done | bytes 589856 | tf_op jit(solution)/shard_map/ppermute | solution.py:211
  84.9 0.2 collective-permute-start.22
  85.1 1.9 %collective-permute-start.23 = (bf16[32,4608]{1,0:T(8,128)(2,1)S(1)}, bf16[32,4608]{1,0:T(8,128)(2,1)S(1)}, u32[]{:S(2)}, u32[]{:S(2)}) collective-permute-start(bf16[32,4608]{1,0:T(8,128)(2,1)S(1)} %slice.227), channel_id=1, source_target_pairs={{8,0},{16,8},{24,16},{28,24},{20,28},{12,20},{4,12},{0,4},{9,1},{1... | collective-permute-start | bytes 884744 | tf_op jit(solution)/shard_map/ppermute | solution.py:211
  87.0 4.2 %collective-permute-done.15 = bf16[32,4608]{1,0:T(8,128)(2,1)S(1)} collective-permute-done((bf16[32,4608]{1,0:T(8,128)(2,1)S(1)}, bf16[32,4608]{1,0:T(8,128)(2,1)S(1)}, u32[]{:S(2)}, u32[]{:S(2)}) %collective-permute-start.15) | collective-permute-done | bytes 294944 | tf_op jit(solution)/shard_map/ppermute | solution.py:211
  91.2 0.7 fusion.45
  92.0 0.1 pad_maximum_fusion
  92.1 0.1 collective-permute-start.21
  92.1 1.6 %collective-permute-start.20 = (f32[128,128]{1,0:T(8,128)S(1)}, f32[128,128]{1,0:T(8,128)S(1)}, u32[]{:S(2)}, u32[]{:S(2)}) collective-permute-start(f32[128,128]{1,0:T(8,128)S(1)} %pad_maximum_fusion), channel_id=1, source_target_pairs={{0,2},{1,3},{2,0},{3,1},{4,6},{5,7},{6,4},{7,5},{8,10},{9,11},{10,... | collective-permute-start | bytes 196616 | tf_op jit(solution)/shard_map/ppermute | solution.py:155
  93.7 0.3 collective-permute-start.19
  94.0 1.4 %fusion.2 = f32[512,128]{1,0:T(8,128)S(1)} fusion(bf16[512,7168]{1,0:T(8,128)(2,1)S(1)} %copy-done.2, bf16[64,4608]{1,0:T(8,128)(2,1)S(1)} %collective-permute-done.18, bf16[64,4608]{1,0:T(8,128)(2,1)S(1)} %collective-permute-done.17), kind=kOutput, calls=%fused_computation.2 | convolution fusion | flops 606339072 | bytes 6160384 | tf_op jit(solution)/shard_map/dot_general | solution.py:101
  95.4 0.8 fusion.10
  96.3 1.4 %fusion = f32[512,64]{1,0:T(8,128)S(1)} fusion(bf16[512,7168]{1,0:T(8,128)(2,1)S(1)} %copy-done.2, bf16[32,4608]{1,0:T(8,128)(2,1)S(1)} %collective-permute-done.23, bf16[32,4608]{1,0:T(8,128)(2,1)S(1)} %collective-permute-done.22), kind=kOutput, calls=%fused_computation | convolution fusion | flops 303169536 | bytes 5439488 | tf_op jit(solution)/shard_map/dot_general | solution.py:101
  97.7 0.3 collective-permute-done.20
  97.9 0.3 score.1
  98.3 0.9 collective-permute-start.26
  99.2 0.8 collective-permute-start.25
  100.0 0.2 collective-permute-start.24
  100.2 1.1 %collective-permute-done.26 = f32[2,16]{1,0:T(2,128)S(1)} collective-permute-done((f32[2,16]{1,0:T(2,128)S(1)}, f32[2,16]{1,0:T(2,128)S(1)}, u32[]{:S(2)}, u32[]{:S(2)}) %collective-permute-start.26) | collective-permute-done | bytes 160 | tf_op jit(solution)/shard_map/ppermute | solution.py:155
  101.3 1.5 %collective-permute-done.25 = f32[2,16]{1,0:T(2,128)S(1)} collective-permute-done((f32[2,16]{1,0:T(2,128)S(1)}, f32[2,16]{1,0:T(2,128)S(1)}, u32[]{:S(2)}, u32[]{:S(2)}) %collective-permute-start.25) | collective-permute-done | bytes 160 | tf_op jit(solution)/shard_map/ppermute | solution.py:155
  102.8 0.6 add_add_fusion.1
  (65 shorter events, 1.0 us)
Async XLA Ops:
  0.0 0.7 copy-start
  2.4 20.3 %collective-permute-start.1 = (bf16[64,4608]{1,0:T(8,128)(2,1)S(1)}, bf16[64,4608]{1,0:T(8,128)(2,1)S(1)}, u32[]{:S(2)}, u32[]{:S(2)}) collective-permute-start(bf16[64,4608]{1,0:T(8,128)(2,1)S(1)} %pick_rows.2), channel_id=1, source_target_pairs={{8,0},{16,8},{24,16},{28,24},{20,28},{12,20},{4,12},{0,4},{9,1},{1... | collective-permute-start | bytes 1769480 | tf_op jit(solution)/shard_map/ppermute | solution.py:211
  5.4 17.4 %collective-permute-start = (bf16[64,4608]{1,0:T(8,128)(2,1)S(1)}, bf16[64,4608]{1,0:T(8,128)(2,1)S(1)}, u32[]{:S(2)}, u32[]{:S(2)}) collective-permute-start(bf16[64,4608]{1,0:T(8,128)(2,1)S(1)} %pick_rows.2), channel_id=1, source_target_pairs={{0,8},{8,16},{16,24},{24,28},{28,20},{20,12},{12,4},{4,0},{1,9},{9... | collective-permute-start | bytes 1769480 | tf_op jit(solution)/shard_map/ppermute | solution.py:211
  5.6 3.4 %copy-start.1 = (s32[16]{0:T(128)S(1)}, s32[16]{0:T(128)}, u32[]{:S(2)}) copy-start(s32[16]{0:T(128)} %owners_ref.2) | copy-start | bytes 196
  10.6 21.7 %collective-permute-start.8 = (bf16[64,4608]{1,0:T(8,128)(2,1)S(1)}, bf16[64,4608]{1,0:T(8,128)(2,1)S(1)}, u32[]{:S(2)}, u32[]{:S(2)}) collective-permute-start(bf16[64,4608]{1,0:T(8,128)(2,1)S(1)} %pick_rows.3), channel_id=1, source_target_pairs={{8,0},{16,8},{24,16},{28,24},{20,28},{12,20},{4,12},{0,4},{9,1},{1... | collective-permute-start | bytes 1769480 | tf_op jit(solution)/shard_map/ppermute | solution.py:211
  12.5 21.9 %collective-permute-start.7 = (bf16[64,4608]{1,0:T(8,128)(2,1)S(1)}, bf16[64,4608]{1,0:T(8,128)(2,1)}, u32[]{:S(2)}, u32[]{:S(2)}) collective-permute-start(bf16[64,4608]{1,0:T(8,128)(2,1)S(1)} %pick_rows.3), channel_id=1, source_target_pairs={{0,8},{8,16},{16,24},{24,28},{28,20},{20,12},{12,4},{4,0},{1,9},{9... | collective-permute-start | bytes 1769480 | tf_op jit(solution)/shard_map/ppermute | solution.py:211
  22.5 16.6 %copy-start.2 = (bf16[512,7168]{1,0:T(8,128)(2,1)S(1)}, bf16[512,7168]{1,0:T(8,128)(2,1)}, u32[]{:S(2)}) copy-start(bf16[512,7168]{1,0:T(8,128)(2,1)} %rotate.3) | copy-start | bytes 22020100
  22.8 24.2 %collective-permute-start.2 = (bf16[64,4608]{1,0:T(8,128)(2,1)S(1)}, bf16[64,4608]{1,0:T(8,128)(2,1)S(1)}, u32[]{:S(2)}, u32[]{:S(2)}) collective-permute-start(bf16[64,4608]{1,0:T(8,128)(2,1)S(1)} %collective-permute-done), channel_id=1, source_target_pairs={{0,8},{8,16},{16,24},{24,28},{28,20},{20,12},{12,4},{4,0},{1,9},{9... | collective-permute-start | bytes 1769480 | tf_op jit(solution)/shard_map/ppermute | solution.py:211
  24.8 22.2 %collective-permute-start.3 = (bf16[64,4608]{1,0:T(8,128)(2,1)S(1)}, bf16[64,4608]{1,0:T(8,128)(2,1)S(1)}, u32[]{:S(2)}, u32[]{:S(2)}) collective-permute-start(bf16[64,4608]{1,0:T(8,128)(2,1)S(1)} %collective-permute-done.1), channel_id=1, source_target_pairs={{8,0},{16,8},{24,16},{28,24},{20,28},{12,20},{4,12},{0,4},{9,1},{1... | collective-permute-start | bytes 1769480 | tf_op jit(solution)/shard_map/ppermute | solution.py:211
  34.4 25.2 %collective-permute-start.13 = (bf16[64,4608]{1,0:T(8,128)(2,1)}, bf16[64,4608]{1,0:T(8,128)(2,1)S(1)}, u32[]{:S(2)}, u32[]{:S(2)}) collective-permute-start(bf16[64,4608]{1,0:T(8,128)(2,1)} %collective-permute-done.7), channel_id=1, source_target_pairs={{0,8},{8,16},{16,24},{24,28},{28,20},{20,12},{12,4},{4,0},{1,9},{9... | collective-permute-start | bytes 1769480 | tf_op jit(solution)/shard_map/ppermute | solution.py:211
  34.5 25.1 %collective-permute-start.14 = (bf16[64,4608]{1,0:T(8,128)(2,1)S(1)}, bf16[64,4608]{1,0:T(8,128)(2,1)S(1)}, u32[]{:S(2)}, u32[]{:S(2)}) collective-permute-start(bf16[64,4608]{1,0:T(8,128)(2,1)S(1)} %collective-permute-done.8), channel_id=1, source_target_pairs={{8,0},{16,8},{24,16},{28,24},{20,28},{12,20},{4,12},{0,4},{9,1},{1... | collective-permute-start | bytes 1769480 | tf_op jit(solution)/shard_map/ppermute | solution.py:211
  43.8 3.3 %copy-start.3 = (bf16[512,2048]{1,0:T(8,128)(2,1)S(1)}, bf16[512,2048]{1,0:T(8,128)(2,1)}, u32[]{:S(2)}) copy-start(bf16[512,2048]{1,0:T(8,128)(2,1)} %rotate.2) | copy-start | bytes 6291460
  48.5 14.5 %collective-permute-start.4 = (f32[128,320]{1,0:T(8,128)S(1)}, f32[128,320]{1,0:T(8,128)S(1)}, u32[]{:S(2)}, u32[]{:S(2)}) collective-permute-start(f32[128,320]{1,0:T(8,128)S(1)} %constant_dynamic-slice_fusion), channel_id=1, source_target_pairs={{0,1},{1,0},{2,3},{3,2},{4,5},{5,4},{6,7},{7,6},{8,9},{9,8},{10,11... | collective-permute-start | bytes 491528 | tf_op jit(solution)/shard_map/ppermute | solution.py:155
  48.5 23.7 %collective-permute-start.9 = (bf16[64,4608]{1,0:T(8,128)(2,1)S(1)}, bf16[64,4608]{1,0:T(8,128)(2,1)S(1)}, u32[]{:S(2)}, u32[]{:S(2)}) collective-permute-start(bf16[64,4608]{1,0:T(8,128)(2,1)S(1)} %collective-permute-done.2), channel_id=1, source_target_pairs={{0,8},{8,16},{16,24},{24,28},{28,20},{20,12},{12,4},{4,0},{1,9},{9... | collective-permute-start | bytes 1769480 | tf_op jit(solution)/shard_map/ppermute | solution.py:211
  48.7 23.6 %collective-permute-start.10 = (bf16[64,4608]{1,0:T(8,128)(2,1)S(1)}, bf16[64,4608]{1,0:T(8,128)(2,1)S(1)}, u32[]{:S(2)}, u32[]{:S(2)}) collective-permute-start(bf16[64,4608]{1,0:T(8,128)(2,1)S(1)} %collective-permute-done.3), channel_id=1, source_target_pairs={{8,0},{16,8},{24,16},{28,24},{20,28},{12,20},{4,12},{0,4},{9,1},{1... | collective-permute-start | bytes 1769480 | tf_op jit(solution)/shard_map/ppermute | solution.py:211
  59.6 25.3 %collective-permute-start.17 = (bf16[64,4608]{1,0:T(8,128)(2,1)S(1)}, bf16[64,4608]{1,0:T(8,128)(2,1)S(1)}, u32[]{:S(2)}, u32[]{:S(2)}) collective-permute-start(bf16[64,4608]{1,0:T(8,128)(2,1)S(1)} %collective-permute-done.13), channel_id=1, source_target_pairs={{0,8},{8,16},{16,24},{24,28},{28,20},{20,12},{12,4},{4,0},{1,9},{9... | collective-permute-start | bytes 1769480 | tf_op jit(solution)/shard_map/ppermute | solution.py:211
  59.7 25.2 %collective-permute-start.18 = (bf16[64,4608]{1,0:T(8,128)(2,1)S(1)}, bf16[64,4608]{1,0:T(8,128)(2,1)S(1)}, u32[]{:S(2)}, u32[]{:S(2)}) collective-permute-start(bf16[64,4608]{1,0:T(8,128)(2,1)S(1)} %collective-permute-done.14), channel_id=1, source_target_pairs={{8,0},{16,8},{24,16},{28,24},{20,28},{12,20},{4,12},{0,4},{9,1},{1... | collective-permute-start | bytes 1769480 | tf_op jit(solution)/shard_map/ppermute | solution.py:211
  63.0 5.7 %collective-permute-start.5 = (f32[128,320]{1,0:T(8,128)S(1)}, f32[128,320]{1,0:T(8,128)S(1)}, u32[]{:S(2)}, u32[]{:S(2)}) collective-permute-start(f32[128,320]{1,0:T(8,128)S(1)} %dynamic-slice_add_fusion), channel_id=1, source_target_pairs={{0,2},{1,3},{2,0},{3,1},{4,6},{5,7},{6,4},{7,5},{8,10},{9,11},{10,... | collective-permute-start | bytes 491528 | tf_op jit(solution)/shard_map/ppermute | solution.py:155
  68.8 4.4 %collective-permute-start.6 = (f32[128,320]{1,0:T(8,128)S(1)}, f32[128,320]{1,0:T(8,128)S(1)}, u32[]{:S(2)}, u32[]{:S(2)}) collective-permute-start(f32[128,320]{1,0:T(8,128)S(1)} %add.202), channel_id=1, source_target_pairs={{0,1},{1,0},{2,3},{3,2},{4,5},{5,4},{6,7},{7,6},{8,9},{9,8},{10,11... | collective-permute-start | bytes 491528 | tf_op jit(solution)/shard_map/ppermute | solution.py:155
  73.1 2.3 %collective-permute-start.11 = (f32[256,128]{1,0:T(8,128)S(1)}, f32[256,128]{1,0:T(8,128)S(1)}, u32[]{:S(2)}, u32[]{:S(2)}) collective-permute-start(f32[256,128]{1,0:T(8,128)S(1)} %slice_add_fusion.12), channel_id=1, source_target_pairs={{0,1},{1,0},{2,3},{3,2},{4,5},{5,4},{6,7},{7,6},{8,9},{9,8},{10,11... | collective-permute-start | bytes 393224 | tf_op jit(solution)/shard_map/ppermute | solution.py:155
  73.3 17.9 %collective-permute-start.15 = (bf16[32,4608]{1,0:T(8,128)(2,1)S(1)}, bf16[32,4608]{1,0:T(8,128)(2,1)S(1)}, u32[]{:S(2)}, u32[]{:S(2)}) collective-permute-start(bf16[32,4608]{1,0:T(8,128)(2,1)S(1)} %slice.196), channel_id=1, source_target_pairs={{0,8},{8,16},{16,24},{24,28},{28,20},{20,12},{12,4},{4,0},{1,9},{9... | collective-permute-start | bytes 884744 | tf_op jit(solution)/shard_map/ppermute | solution.py:211
  73.5 17.7 %collective-permute-start.16 = (bf16[32,4608]{1,0:T(8,128)(2,1)S(1)}, bf16[32,4608]{1,0:T(8,128)(2,1)S(1)}, u32[]{:S(2)}, u32[]{:S(2)}) collective-permute-start(bf16[32,4608]{1,0:T(8,128)(2,1)S(1)} %slice.197), channel_id=1, source_target_pairs={{8,0},{16,8},{24,16},{28,24},{20,28},{12,20},{4,12},{0,4},{9,1},{1... | collective-permute-start | bytes 884744 | tf_op jit(solution)/shard_map/ppermute | solution.py:211
  75.4 11.6 %collective-permute-start.12 = (f32[256,128]{1,0:T(8,128)S(1)}, f32[256,128]{1,0:T(8,128)S(1)}, u32[]{:S(2)}, u32[]{:S(2)}) collective-permute-start(f32[256,128]{1,0:T(8,128)S(1)} %fusion.65), channel_id=1, source_target_pairs={{0,2},{1,3},{2,0},{3,1},{4,6},{5,7},{6,4},{7,5},{8,10},{9,11},{10,... | collective-permute-start | bytes 393224 | tf_op jit(solution)/shard_map/ppermute | solution.py:155
  84.9 11.3 %collective-permute-start.22 = (bf16[32,4608]{1,0:T(8,128)(2,1)S(1)}, bf16[32,4608]{1,0:T(8,128)(2,1)S(1)}, u32[]{:S(2)}, u32[]{:S(2)}) collective-permute-start(bf16[32,4608]{1,0:T(8,128)(2,1)S(1)} %slice.226), channel_id=1, source_target_pairs={{0,8},{8,16},{16,24},{24,28},{28,20},{20,12},{12,4},{4,0},{1,9},{9... | collective-permute-start | bytes 884744 | tf_op jit(solution)/shard_map/ppermute | solution.py:211
  85.1 11.2 %collective-permute-start.23 = (bf16[32,4608]{1,0:T(8,128)(2,1)S(1)}, bf16[32,4608]{1,0:T(8,128)(2,1)S(1)}, u32[]{:S(2)}, u32[]{:S(2)}) collective-permute-start(bf16[32,4608]{1,0:T(8,128)(2,1)S(1)} %slice.227), channel_id=1, source_target_pairs={{8,0},{16,8},{24,16},{28,24},{20,28},{12,20},{4,12},{0,4},{9,1},{1... | collective-permute-start | bytes 884744 | tf_op jit(solution)/shard_map/ppermute | solution.py:211
  92.1 5.6 %collective-permute-start.21 = (f32[128,128]{1,0:T(8,128)S(1)}, f32[128,128]{1,0:T(8,128)S(1)}, u32[]{:S(2)}, u32[]{:S(2)}) collective-permute-start(f32[128,128]{1,0:T(8,128)S(1)} %pad_maximum_fusion), channel_id=1, source_target_pairs={{0,3},{1,2},{2,1},{3,0},{4,7},{5,6},{6,5},{7,4},{8,11},{9,10},{10,... | collective-permute-start | bytes 196616 | tf_op jit(solution)/shard_map/ppermute | solution.py:155
  92.1 5.8 %collective-permute-start.20 = (f32[128,128]{1,0:T(8,128)S(1)}, f32[128,128]{1,0:T(8,128)S(1)}, u32[]{:S(2)}, u32[]{:S(2)}) collective-permute-start(f32[128,128]{1,0:T(8,128)S(1)} %pad_maximum_fusion), channel_id=1, source_target_pairs={{0,2},{1,3},{2,0},{3,1},{4,6},{5,7},{6,4},{7,5},{8,10},{9,11},{10,... | collective-permute-start | bytes 196616 | tf_op jit(solution)/shard_map/ppermute | solution.py:155
  93.7 4.2 %collective-permute-start.19 = (f32[128,128]{1,0:T(8,128)S(1)}, f32[128,128]{1,0:T(8,128)S(1)}, u32[]{:S(2)}, u32[]{:S(2)}) collective-permute-start(f32[128,128]{1,0:T(8,128)S(1)} %pad_maximum_fusion), channel_id=1, source_target_pairs={{0,1},{1,0},{2,3},{3,2},{4,5},{5,4},{6,7},{7,6},{8,9},{9,8},{10,11... | collective-permute-start | bytes 196616 | tf_op jit(solution)/shard_map/ppermute | solution.py:155
  98.3 3.0 %collective-permute-start.26 = (f32[2,16]{1,0:T(2,128)S(1)}, f32[2,16]{1,0:T(2,128)S(1)}, u32[]{:S(2)}, u32[]{:S(2)}) collective-permute-start(f32[2,16]{1,0:T(2,128)S(1)} %score.1), channel_id=1, source_target_pairs={{0,3},{1,2},{2,1},{3,0},{4,7},{5,6},{6,5},{7,4},{8,11},{9,10},{10,... | collective-permute-start | bytes 392 | tf_op jit(solution)/shard_map/ppermute | solution.py:155
  99.2 3.6 %collective-permute-start.25 = (f32[2,16]{1,0:T(2,128)S(1)}, f32[2,16]{1,0:T(2,128)S(1)}, u32[]{:S(2)}, u32[]{:S(2)}) collective-permute-start(f32[2,16]{1,0:T(2,128)S(1)} %score.1), channel_id=1, source_target_pairs={{0,2},{1,3},{2,0},{3,1},{4,6},{5,7},{6,4},{7,5},{8,10},{9,11},{10,... | collective-permute-start | bytes 392 | tf_op jit(solution)/shard_map/ppermute | solution.py:155
  100.0 2.8 %collective-permute-start.24 = (f32[2,16]{1,0:T(2,128)S(1)}, f32[2,16]{1,0:T(2,128)S(1)}, u32[]{:S(2)}, u32[]{:S(2)}) collective-permute-start(f32[2,16]{1,0:T(2,128)S(1)} %score.1), channel_id=1, source_target_pairs={{0,1},{1,0},{2,3},{3,2},{4,5},{5,4},{6,7},{7,6},{8,9},{9,8},{10,11... | collective-permute-start | bytes 392 | tf_op jit(solution)/shard_map/ppermute | solution.py:155

commit v11 on v10

--- a/solution.py
+++ b/solution.py
@@ -233,7 +233,7 @@
     send(1, reach, came[-3:-1])
 
     last = after(steps[0][-1], came[-3])
-    second.append(side_by_side(after(steps[1][reach - 2], last)))
+    second.append(side_by_side(after(steps[1][reach - 2], coefficients[1:2])))
     last = side_by_side(last)
     part = contract_rows(grads, last[:, :width_left]).reshape(-1, LEN, chunk)
     part = jnp.concatenate([part[i] for i in range(part.shape[0])], axis=1)

time: 104 us -> 103 us (level)
    ppermute x8, waiting for transfers between devices: 28.6 us -> 27.2 us  [send(): lax.ppermute(ahead, 'dp', forward)]
  transfers between devices with their start and end apart: 27 -> 27, of which waited for: 11 -> 13; matrix products, arithmetic and copies ran while one was open for 17% -> 18% of each run, Pallas kernels for 14% -> 14%
where the time goes in v11:
time: 103 us
  waiting for transfers between devices  41.8 us (41%)
  starting transfers between devices  24.8 us (24%)
  matrix products  16.5 us (16%)
  Pallas kernels  16.4 us (16%)
  other arithmetic  1.43 us (1%)
  local copies, waits for them, and re-layouts  1.38 us (1%)
    ppermute x8, waiting for transfers between devices, send(): lax.ppermute(ahead, 'dp', forward)  27.2 us
    dot_general x13, matrix products, contract_rows(): lax.dot_general(both, second, (((1,), (1,)), ((), ())), preferred_element...  16.5 us
    ppermute x8, starting transfers between devices, send(): lax.ppermute(behind, 'dp', backward)  14.1 us
    pallas_call x2, Pallas kernels, rotate(): pl.pallas_call(kernel, out_shape=jax.ShapeDtypeStruct((2 * rows, total),...  12.7 us
    ppermute x8, waiting for transfers between devices, send(): lax.ppermute(behind, 'dp', backward)  7.46 us
    ppermute x11, waiting for transfers between devices, swapped(): return lax.ppermute(piece, 'mp', [(i, i ^ distance) for i in range(shards)])  7.2 us
    ppermute x11, starting transfers between devices, swapped(): return lax.ppermute(piece, 'mp', [(i, i ^ distance) for i in range(shards)])  7.2 us
    ppermute x8, starting transfers between devices, send(): lax.ppermute(ahead, 'dp', forward)  3.44 us
  transfers between devices with their start and end apart: 27, of which 13 were waited for; matrix products, arithmetic and copies ran while one was open for 18% of the time, Pallas kernels for 14%

profile of v11, /device:TPU:0, one launch (start us, length us, event | category | flops | bytes accessed | tf_op | source)
XLA Modules:
  0.0 102.9 jit_solution(8968135864561166010)
XLA Ops:
  0.0 0.7 copy-done
  0.7 1.7 %pick_rows.2 = bf16[64,4608]{1,0:T(8,128)(2,1)S(1)} custom-call(s32[16]{0:T(128)S(1)} %copy-done, bf16[1,512,2048]{2,1,0:T(8,128)(2,1)} %refs_0_.2, bf16[1,512,7168]{2,1,0:T(8,128)(2,1)} %refs_0_.3), custom_call_target="tpu_custom_call" | custom-call | tf_op jit(solution)/shard_map/pick_rows/pallas_call | solution.py:49
  2.4 3.0 %collective-permute-start.1 = (bf16[64,4608]{1,0:T(8,128)(2,1)S(1)}, bf16[64,4608]{1,0:T(8,128)(2,1)S(1)}, u32[]{:S(2)}, u32[]{:S(2)}) collective-permute-start(bf16[64,4608]{1,0:T(8,128)(2,1)S(1)} %pick_rows.2), channel_id=1, source_target_pairs={{8,0},{16,8},{24,16},{28,24},{20,28},{12,20},{4,12},{0,4},{9,1},{1... | collective-permute-start | bytes 1769480 | tf_op jit(solution)/shard_map/ppermute | solution.py:211
  5.4 0.2 collective-permute-start
  5.6 3.3 %rotate.2 = bf16[512,2048]{1,0:T(8,128)(2,1)} custom-call(s32[1]{0:T(128)} %bitcast.shard_ref, bf16[256,8192]{1,0:T(8,128)(2,1)} %matrix_ref.2, bf16[4,512,512]{2,1,0:T(8,128)(2,1)} %basis_ref.2), custom_call_target="tpu_custom_call" | custom-call | flops 536870912 | bytes 5242880 | tf_op jit(solution)/shard_map/rotate/pallas_call | solution.py:77
  8.9 1.7 %pick_rows.3 = bf16[64,4608]{1,0:T(8,128)(2,1)S(1)} custom-call(s32[16]{0:T(128)S(1)} %copy-done.1, bf16[1,512,7168]{2,1,0:T(8,128)(2,1)} %refs_0_.3), custom_call_target="tpu_custom_call" | custom-call | tf_op jit(solution)/shard_map/pick_rows/pallas_call | solution.py:49
  10.6 1.9 %collective-permute-start.8 = (bf16[64,4608]{1,0:T(8,128)(2,1)S(1)}, bf16[64,4608]{1,0:T(8,128)(2,1)S(1)}, u32[]{:S(2)}, u32[]{:S(2)}) collective-permute-start(bf16[64,4608]{1,0:T(8,128)(2,1)S(1)} %pick_rows.3), channel_id=1, source_target_pairs={{8,0},{16,8},{24,16},{28,24},{20,28},{12,20},{4,12},{0,4},{9,1},{1... | collective-permute-start | bytes 1769480 | tf_op jit(solution)/shard_map/ppermute | solution.py:211
  12.5 0.2 collective-permute-start.7
  12.7 0.2 convert_reduce_fusion
  12.9 0.1 concatenate.54
  13.1 0.1 concatenate.53
  13.2 9.4 %rotate.3 = bf16[512,7168]{1,0:T(8,128)(2,1)} custom-call(s32[1]{0:T(128)} %constant.120.clone.1.shard_ref, bf16[256,7168]{1,0:T(8,128)(2,1)} %matrix_ref.3, bf16[28,256,256]{2,1,0:T(8,128)(2,1)} %basis_ref.3), custom_call_target="tpu_custom_call" | custom-call | flops 939524096 | bytes 14680064 | tf_op jit(solution)/shard_map/rotate/pallas_call | solution.py:77
  22.5 0.2 and_convert_fusion.hit_ref
  22.8 2.0 %collective-permute-start.2 = (bf16[64,4608]{1,0:T(8,128)(2,1)S(1)}, bf16[64,4608]{1,0:T(8,128)(2,1)S(1)}, u32[]{:S(2)}, u32[]{:S(2)}) collective-permute-start(bf16[64,4608]{1,0:T(8,128)(2,1)S(1)} %collective-permute-done), channel_id=1, source_target_pairs={{0,8},{8,16},{16,24},{24,28},{28,20},{20,12},{12,4},{4,0},{1,9},{9... | collective-permute-start | bytes 1769480 | tf_op jit(solution)/shard_map/ppermute | solution.py:211
  24.8 7.4 %collective-permute-done.8 = bf16[64,4608]{1,0:T(8,128)(2,1)S(1)} collective-permute-done((bf16[64,4608]{1,0:T(8,128)(2,1)S(1)}, bf16[64,4608]{1,0:T(8,128)(2,1)S(1)}, u32[]{:S(2)}, u32[]{:S(2)}) %collective-permute-start.8) | collective-permute-done | bytes 589856 | tf_op jit(solution)/shard_map/ppermute | solution.py:211
  32.3 2.1 %collective-permute-done.7 = bf16[64,4608]{1,0:T(8,128)(2,1)} collective-permute-done((bf16[64,4608]{1,0:T(8,128)(2,1)S(1)}, bf16[64,4608]{1,0:T(8,128)(2,1)}, u32[]{:S(2)}, u32[]{:S(2)}) %collective-permute-start.7) | collective-permute-done | bytes 589856 | tf_op jit(solution)/shard_map/ppermute | solution.py:211
  34.4 0.1 collective-permute-start.13
  34.5 1.9 %collective-permute-start.14 = (bf16[64,4608]{1,0:T(8,128)(2,1)S(1)}, bf16[64,4608]{1,0:T(8,128)(2,1)S(1)}, u32[]{:S(2)}, u32[]{:S(2)}) collective-permute-start(bf16[64,4608]{1,0:T(8,128)(2,1)S(1)} %collective-permute-done.8), channel_id=1, source_target_pairs={{8,0},{16,8},{24,16},{28,24},{20,28},{12,20},{4,12},{0,4},{9,1},{1... | collective-permute-start | bytes 1769480 | tf_op jit(solution)/shard_map/ppermute | solution.py:211
  36.5 2.6 %fusion.18 = f32[512,128]{1,0:T(8,128)S(1)} fusion(bf16[512,7168]{1,0:T(8,128)(2,1)} %rotate.3, bf16[128,4608]{1,0:T(8,128)(2,1)S(1)} %constant_dynamic-update-slice_fusion), kind=kOutput, calls=%fused_computation.18 | convolution fusion | flops 335544320 | bytes 3538944 | tf_op jit(solution)/shard_map/dot_general | solution.py:101
  39.1 1.4 %fusion.4 = f32[512,64]{1,0:T(8,128)S(1)} fusion(bf16[64,4608]{1,0:T(8,128)(2,1)S(1)} %pick_rows.3, bf16[512,7168]{1,0:T(8,128)(2,1)S(1)} %copy-done.2), kind=kOutput, calls=%fused_computation.4 | convolution fusion | flops 301989888 | bytes 5439488 | tf_op jit(solution)/shard_map/dot_general | solution.py:101
  40.5 2.4 %fusion.8 = f32[512,128]{1,0:T(8,128)S(1)} fusion(bf16[512,7168]{1,0:T(8,128)(2,1)S(1)} %copy-done.2, bf16[64,4608]{1,0:T(8,128)(2,1)S(1)} %collective-permute-done.8, bf16[64,4608]{1,0:T(8,128)(2,1)} %collective-permute-done.7), kind=kOutput, calls=%fused_computation.8 | convolution fusion | flops 606339072 | bytes 6160384 | tf_op jit(solution)/shard_map/dot_general | solution.py:101
  42.9 0.8 fusion.14
  43.9 3.0 %collective-permute-done.2 = bf16[64,4608]{1,0:T(8,128)(2,1)S(1)} collective-permute-done((bf16[64,4608]{1,0:T(8,128)(2,1)S(1)}, bf16[64,4608]{1,0:T(8,128)(2,1)S(1)}, u32[]{:S(2)}, u32[]{:S(2)}) %collective-permute-start.2) | collective-permute-done | bytes 589856 | tf_op jit(solution)/shard_map/ppermute | solution.py:211
  47.1 1.3 %fusion.20 = f32[512,320]{1,0:T(8,128)S(1)} fusion(bf16[512,2048]{1,0:T(8,128)(2,1)S(1)} %copy-done.3, bf16[64,2048]{1,0:T(8,128)(2,1)S(1)} %slice.147, bf16[128,2048]{1,0:T(8,128)(2,1)S(1)} %slice.190, bf16[128,2048]{1,0:T(8,128)(2,1)S(1)} %slice.189), kind=kOutput, calls=%fused_computation.20 | convolution fusion | flops 675020800 | bytes 4063232 | tf_op jit(solution)/shard_map/dot_general | solution.py:101
  48.5 0.1 collective-permute-start.4
  48.5 0.2 collective-permute-start.9
  48.7 1.9 %collective-permute-start.10 = (bf16[64,4608]{1,0:T(8,128)(2,1)S(1)}, bf16[64,4608]{1,0:T(8,128)(2,1)S(1)}, u32[]{:S(2)}, u32[]{:S(2)}) collective-permute-start(bf16[64,4608]{1,0:T(8,128)(2,1)S(1)} %collective-permute-done.3), channel_id=1, source_target_pairs={{8,0},{16,8},{24,16},{28,24},{20,28},{12,20},{4,12},{0,4},{9,1},{1... | collective-permute-start | bytes 1769480 | tf_op jit(solution)/shard_map/ppermute | solution.py:211
  50.6 9.0 %collective-permute-done.13 = bf16[64,4608]{1,0:T(8,128)(2,1)S(1)} collective-permute-done((bf16[64,4608]{1,0:T(8,128)(2,1)}, bf16[64,4608]{1,0:T(8,128)(2,1)S(1)}, u32[]{:S(2)}, u32[]{:S(2)}) %collective-permute-start.13) | collective-permute-done | bytes 589856 | tf_op jit(solution)/shard_map/ppermute | solution.py:211
  59.6 0.1 collective-permute-start.17
  59.7 1.9 %collective-permute-start.18 = (bf16[64,4608]{1,0:T(8,128)(2,1)S(1)}, bf16[64,4608]{1,0:T(8,128)(2,1)S(1)}, u32[]{:S(2)}, u32[]{:S(2)}) collective-permute-start(bf16[64,4608]{1,0:T(8,128)(2,1)S(1)} %collective-permute-done.14), channel_id=1, source_target_pairs={{8,0},{16,8},{24,16},{28,24},{20,28},{12,20},{4,12},{0,4},{9,1},{1... | collective-permute-start | bytes 1769480 | tf_op jit(solution)/shard_map/ppermute | solution.py:211
  61.6 1.4 %fusion.6 = f32[512,128]{1,0:T(8,128)S(1)} fusion(bf16[512,7168]{1,0:T(8,128)(2,1)S(1)} %copy-done.2, bf16[64,4608]{1,0:T(8,128)(2,1)S(1)} %collective-permute-done.14, bf16[64,4608]{1,0:T(8,128)(2,1)S(1)} %collective-permute-done.13), kind=kOutput, calls=%fused_computation.6 | convolution fusion | flops 606339072 | bytes 6160384 | tf_op jit(solution)/shard_map/dot_general | solution.py:101
  63.0 1.6 %collective-permute-start.5 = (f32[128,320]{1,0:T(8,128)S(1)}, f32[128,320]{1,0:T(8,128)S(1)}, u32[]{:S(2)}, u32[]{:S(2)}) collective-permute-start(f32[128,320]{1,0:T(8,128)S(1)} %dynamic-slice_add_fusion), channel_id=1, source_target_pairs={{0,2},{1,3},{2,0},{3,1},{4,6},{5,7},{6,4},{7,5},{8,10},{9,11},{10,... | collective-permute-start | bytes 491528 | tf_op jit(solution)/shard_map/ppermute | solution.py:155
  64.6 0.8 fusion.16
  65.5 3.3 %collective-permute-done.5 = f32[128,320]{1,0:T(8,128)S(1)} collective-permute-done((f32[128,320]{1,0:T(8,128)S(1)}, f32[128,320]{1,0:T(8,128)S(1)}, u32[]{:S(2)}, u32[]{:S(2)}) %collective-permute-start.5) | collective-permute-done | bytes 163872 | tf_op jit(solution)/shard_map/ppermute | solution.py:155
  68.8 0.1 collective-permute-start.6
  68.9 3.3 %collective-permute-done.9 = bf16[64,4608]{1,0:T(8,128)(2,1)S(1)} collective-permute-done((bf16[64,4608]{1,0:T(8,128)(2,1)S(1)}, bf16[64,4608]{1,0:T(8,128)(2,1)S(1)}, u32[]{:S(2)}, u32[]{:S(2)}) %collective-permute-start.9) | collective-permute-done | bytes 589856 | tf_op jit(solution)/shard_map/ppermute | solution.py:211
  72.3 0.7 fusion.41
  73.1 0.1 collective-permute-start.11
  73.2 1.2 %collective-permute-done.11 = f32[256,128]{1,0:T(8,128)S(1)} collective-permute-done((f32[256,128]{1,0:T(8,128)S(1)}, f32[256,128]{1,0:T(8,128)S(1)}, u32[]{:S(2)}, u32[]{:S(2)}) %collective-permute-start.11) | collective-permute-done | bytes 131104 | tf_op jit(solution)/shard_map/ppermute | solution.py:155
  74.5 1.6 %collective-permute-start.12 = (f32[256,128]{1,0:T(8,128)S(1)}, f32[256,128]{1,0:T(8,128)S(1)}, u32[]{:S(2)}, u32[]{:S(2)}) collective-permute-start(f32[256,128]{1,0:T(8,128)S(1)} %fusion.65), channel_id=1, source_target_pairs={{0,2},{1,3},{2,0},{3,1},{4,6},{5,7},{6,4},{7,5},{8,10},{9,11},{10,... | collective-permute-start | bytes 393224 | tf_op jit(solution)/shard_map/ppermute | solution.py:155
  76.1 0.9 fusion.12
  77.0 0.6 collective-permute-start.15
  77.6 1.5 %collective-permute-start.16 = (bf16[32,4608]{1,0:T(8,128)(2,1)S(1)}, bf16[32,4608]{1,0:T(8,128)(2,1)S(1)}, u32[]{:S(2)}, u32[]{:S(2)}) collective-permute-start(bf16[32,4608]{1,0:T(8,128)(2,1)S(1)} %slice.197), channel_id=1, source_target_pairs={{8,0},{16,8},{24,16},{28,24},{20,28},{12,20},{4,12},{0,4},{9,1},{1... | collective-permute-start | bytes 884744 | tf_op jit(solution)/shard_map/ppermute | solution.py:211
  79.1 5.8 %collective-permute-done.17 = bf16[64,4608]{1,0:T(8,128)(2,1)S(1)} collective-permute-done((bf16[64,4608]{1,0:T(8,128)(2,1)S(1)}, bf16[64,4608]{1,0:T(8,128)(2,1)S(1)}, u32[]{:S(2)}, u32[]{:S(2)}) %collective-permute-start.17) | collective-permute-done | bytes 589856 | tf_op jit(solution)/shard_map/ppermute | solution.py:211
  84.9 0.2 collective-permute-start.22
  85.1 1.9 %collective-permute-start.23 = (bf16[32,4608]{1,0:T(8,128)(2,1)S(1)}, bf16[32,4608]{1,0:T(8,128)(2,1)S(1)}, u32[]{:S(2)}, u32[]{:S(2)}) collective-permute-start(bf16[32,4608]{1,0:T(8,128)(2,1)S(1)} %slice.227), channel_id=1, source_target_pairs={{8,0},{16,8},{24,16},{28,24},{20,28},{12,20},{4,12},{0,4},{9,1},{1... | collective-permute-start | bytes 884744 | tf_op jit(solution)/shard_map/ppermute | solution.py:211
  87.0 1.4 %fusion.2 = f32[512,128]{1,0:T(8,128)S(1)} fusion(bf16[512,7168]{1,0:T(8,128)(2,1)S(1)} %copy-done.2, bf16[64,4608]{1,0:T(8,128)(2,1)S(1)} %collective-permute-done.18, bf16[64,4608]{1,0:T(8,128)(2,1)S(1)} %collective-permute-done.17), kind=kOutput, calls=%fused_computation.2 | convolution fusion | flops 606339072 | bytes 6160384 | tf_op jit(solution)/shard_map/dot_general | solution.py:101
  88.4 2.7 %collective-permute-done.15 = bf16[32,4608]{1,0:T(8,128)(2,1)S(1)} collective-permute-done((bf16[32,4608]{1,0:T(8,128)(2,1)S(1)}, bf16[32,4608]{1,0:T(8,128)(2,1)S(1)}, u32[]{:S(2)}, u32[]{:S(2)}) %collective-permute-start.15) | collective-permute-done | bytes 294944 | tf_op jit(solution)/shard_map/ppermute | solution.py:211
  91.2 0.7 fusion.45
  92.0 0.1 pad_maximum_fusion
  92.1 0.1 collective-permute-start.21
  92.1 1.6 %collective-permute-start.20 = (f32[128,128]{1,0:T(8,128)S(1)}, f32[128,128]{1,0:T(8,128)S(1)}, u32[]{:S(2)}, u32[]{:S(2)}) collective-permute-start(f32[128,128]{1,0:T(8,128)S(1)} %pad_maximum_fusion), channel_id=1, source_target_pairs={{0,2},{1,3},{2,0},{3,1},{4,6},{5,7},{6,4},{7,5},{8,10},{9,11},{10,... | collective-permute-start | bytes 196616 | tf_op jit(solution)/shard_map/ppermute | solution.py:155
  93.7 0.3 collective-permute-start.19
  94.0 0.8 fusion.10
  94.8 1.2 %collective-permute-done.22 = bf16[32,4608]{1,0:T(8,128)(2,1)S(1)} collective-permute-done((bf16[32,4608]{1,0:T(8,128)(2,1)S(1)}, bf16[32,4608]{1,0:T(8,128)(2,1)S(1)}, u32[]{:S(2)}, u32[]{:S(2)}) %collective-permute-start.22) | collective-permute-done | bytes 294944 | tf_op jit(solution)/shard_map/ppermute | solution.py:211
  96.0 1.4 %fusion = f32[512,64]{1,0:T(8,128)S(1)} fusion(bf16[512,7168]{1,0:T(8,128)(2,1)S(1)} %copy-done.2, bf16[32,4608]{1,0:T(8,128)(2,1)S(1)} %collective-permute-done.23, bf16[32,4608]{1,0:T(8,128)(2,1)S(1)} %collective-permute-done.22), kind=kOutput, calls=%fused_computation | convolution fusion | flops 303169536 | bytes 5439488 | tf_op jit(solution)/shard_map/dot_general | solution.py:101
  97.4 0.5 collective-permute-done.20
  97.9 0.3 score.1
  98.3 0.5 collective-permute-start.26
  98.8 1.2 %collective-permute-start.25 = (f32[2,16]{1,0:T(2,128)S(1)}, f32[2,16]{1,0:T(2,128)S(1)}, u32[]{:S(2)}, u32[]{:S(2)}) collective-permute-start(f32[2,16]{1,0:T(2,128)S(1)} %score.1), channel_id=1, source_target_pairs={{0,2},{1,3},{2,0},{3,1},{4,6},{5,7},{6,4},{7,5},{8,10},{9,11},{10,... | collective-permute-start | bytes 392 | tf_op jit(solution)/shard_map/ppermute | solution.py:155
  100.0 0.2 collective-permute-start.24
  100.2 1.1 %collective-permute-done.26 = f32[2,16]{1,0:T(2,128)S(1)} collective-permute-done((f32[2,16]{1,0:T(2,128)S(1)}, f32[2,16]{1,0:T(2,128)S(1)}, u32[]{:S(2)}, u32[]{:S(2)}) %collective-permute-start.26) | collective-permute-done | bytes 160 | tf_op jit(solution)/shard_map/ppermute | solution.py:155
  101.3 1.0 collective-permute-done.25
  102.3 0.6 add_add_fusion.1
  (65 shorter events, 1.1 us)
Async XLA Ops:
  0.0 0.7 copy-start
  2.4 20.3 %collective-permute-start.1 = (bf16[64,4608]{1,0:T(8,128)(2,1)S(1)}, bf16[64,4608]{1,0:T(8,128)(2,1)S(1)}, u32[]{:S(2)}, u32[]{:S(2)}) collective-permute-start(bf16[64,4608]{1,0:T(8,128)(2,1)S(1)} %pick_rows.2), channel_id=1, source_target_pairs={{8,0},{16,8},{24,16},{28,24},{20,28},{12,20},{4,12},{0,4},{9,1},{1... | collective-permute-start | bytes 1769480 | tf_op jit(solution)/shard_map/ppermute | solution.py:211
  5.4 17.4 %collective-permute-start = (bf16[64,4608]{1,0:T(8,128)(2,1)S(1)}, bf16[64,4608]{1,0:T(8,128)(2,1)S(1)}, u32[]{:S(2)}, u32[]{:S(2)}) collective-permute-start(bf16[64,4608]{1,0:T(8,128)(2,1)S(1)} %pick_rows.2), channel_id=1, source_target_pairs={{0,8},{8,16},{16,24},{24,28},{28,20},{20,12},{12,4},{4,0},{1,9},{9... | collective-permute-start | bytes 1769480 | tf_op jit(solution)/shard_map/ppermute | solution.py:211
  5.6 3.4 %copy-start.1 = (s32[16]{0:T(128)S(1)}, s32[16]{0:T(128)}, u32[]{:S(2)}) copy-start(s32[16]{0:T(128)} %owners_ref.2) | copy-start | bytes 196
  10.6 21.7 %collective-permute-start.8 = (bf16[64,4608]{1,0:T(8,128)(2,1)S(1)}, bf16[64,4608]{1,0:T(8,128)(2,1)S(1)}, u32[]{:S(2)}, u32[]{:S(2)}) collective-permute-start(bf16[64,4608]{1,0:T(8,128)(2,1)S(1)} %pick_rows.3), channel_id=1, source_target_pairs={{8,0},{16,8},{24,16},{28,24},{20,28},{12,20},{4,12},{0,4},{9,1},{1... | collective-permute-start | bytes 1769480 | tf_op jit(solution)/shard_map/ppermute | solution.py:211
  12.5 21.9 %collective-permute-start.7 = (bf16[64,4608]{1,0:T(8,128)(2,1)S(1)}, bf16[64,4608]{1,0:T(8,128)(2,1)}, u32[]{:S(2)}, u32[]{:S(2)}) collective-permute-start(bf16[64,4608]{1,0:T(8,128)(2,1)S(1)} %pick_rows.3), channel_id=1, source_target_pairs={{0,8},{8,16},{16,24},{24,28},{28,20},{20,12},{12,4},{4,0},{1,9},{9... | collective-permute-start | bytes 1769480 | tf_op jit(solution)/shard_map/ppermute | solution.py:211
  22.5 16.6 %copy-start.2 = (bf16[512,7168]{1,0:T(8,128)(2,1)S(1)}, bf16[512,7168]{1,0:T(8,128)(2,1)}, u32[]{:S(2)}) copy-start(bf16[512,7168]{1,0:T(8,128)(2,1)} %rotate.3) | copy-start | bytes 22020100
  22.8 24.2 %collective-permute-start.2 = (bf16[64,4608]{1,0:T(8,128)(2,1)S(1)}, bf16[64,4608]{1,0:T(8,128)(2,1)S(1)}, u32[]{:S(2)}, u32[]{:S(2)}) collective-permute-start(bf16[64,4608]{1,0:T(8,128)(2,1)S(1)} %collective-permute-done), channel_id=1, source_target_pairs={{0,8},{8,16},{16,24},{24,28},{28,20},{20,12},{12,4},{4,0},{1,9},{9... | collective-permute-start | bytes 1769480 | tf_op jit(solution)/shard_map/ppermute | solution.py:211
  24.8 22.2 %collective-permute-start.3 = (bf16[64,4608]{1,0:T(8,128)(2,1)S(1)}, bf16[64,4608]{1,0:T(8,128)(2,1)S(1)}, u32[]{:S(2)}, u32[]{:S(2)}) collective-permute-start(bf16[64,4608]{1,0:T(8,128)(2,1)S(1)} %collective-permute-done.1), channel_id=1, source_target_pairs={{8,0},{16,8},{24,16},{28,24},{20,28},{12,20},{4,12},{0,4},{9,1},{1... | collective-permute-start | bytes 1769480 | tf_op jit(solution)/shard_map/ppermute | solution.py:211
  34.4 25.2 %collective-permute-start.13 = (bf16[64,4608]{1,0:T(8,128)(2,1)}, bf16[64,4608]{1,0:T(8,128)(2,1)S(1)}, u32[]{:S(2)}, u32[]{:S(2)}) collective-permute-start(bf16[64,4608]{1,0:T(8,128)(2,1)} %collective-permute-done.7), channel_id=1, source_target_pairs={{0,8},{8,16},{16,24},{24,28},{28,20},{20,12},{12,4},{4,0},{1,9},{9... | collective-permute-start | bytes 1769480 | tf_op jit(solution)/shard_map/ppermute | solution.py:211
  34.5 25.1 %collective-permute-start.14 = (bf16[64,4608]{1,0:T(8,128)(2,1)S(1)}, bf16[64,4608]{1,0:T(8,128)(2,1)S(1)}, u32[]{:S(2)}, u32[]{:S(2)}) collective-permute-start(bf16[64,4608]{1,0:T(8,128)(2,1)S(1)} %collective-permute-done.8), channel_id=1, source_target_pairs={{8,0},{16,8},{24,16},{28,24},{20,28},{12,20},{4,12},{0,4},{9,1},{1... | collective-permute-start | bytes 1769480 | tf_op jit(solution)/shard_map/ppermute | solution.py:211
  43.8 3.3 %copy-start.3 = (bf16[512,2048]{1,0:T(8,128)(2,1)S(1)}, bf16[512,2048]{1,0:T(8,128)(2,1)}, u32[]{:S(2)}) copy-start(bf16[512,2048]{1,0:T(8,128)(2,1)} %rotate.2) | copy-start | bytes 6291460
  48.5 14.5 %collective-permute-start.4 = (f32[128,320]{1,0:T(8,128)S(1)}, f32[128,320]{1,0:T(8,128)S(1)}, u32[]{:S(2)}, u32[]{:S(2)}) collective-permute-start(f32[128,320]{1,0:T(8,128)S(1)} %constant_dynamic-slice_fusion), channel_id=1, source_target_pairs={{0,1},{1,0},{2,3},{3,2},{4,5},{5,4},{6,7},{7,6},{8,9},{9,8},{10,11... | collective-permute-start | bytes 491528 | tf_op jit(solution)/shard_map/ppermute | solution.py:155
  48.5 23.7 %collective-permute-start.9 = (bf16[64,4608]{1,0:T(8,128)(2,1)S(1)}, bf16[64,4608]{1,0:T(8,128)(2,1)S(1)}, u32[]{:S(2)}, u32[]{:S(2)}) collective-permute-start(bf16[64,4608]{1,0:T(8,128)(2,1)S(1)} %collective-permute-done.2), channel_id=1, source_target_pairs={{0,8},{8,16},{16,24},{24,28},{28,20},{20,12},{12,4},{4,0},{1,9},{9... | collective-permute-start | bytes 1769480 | tf_op jit(solution)/shard_map/ppermute | solution.py:211
  48.7 23.6 %collective-permute-start.10 = (bf16[64,4608]{1,0:T(8,128)(2,1)S(1)}, bf16[64,4608]{1,0:T(8,128)(2,1)S(1)}, u32[]{:S(2)}, u32[]{:S(2)}) collective-permute-start(bf16[64,4608]{1,0:T(8,128)(2,1)S(1)} %collective-permute-done.3), channel_id=1, source_target_pairs={{8,0},{16,8},{24,16},{28,24},{20,28},{12,20},{4,12},{0,4},{9,1},{1... | collective-permute-start | bytes 1769480 | tf_op jit(solution)/shard_map/ppermute | solution.py:211
  59.6 25.3 %collective-permute-start.17 = (bf16[64,4608]{1,0:T(8,128)(2,1)S(1)}, bf16[64,4608]{1,0:T(8,128)(2,1)S(1)}, u32[]{:S(2)}, u32[]{:S(2)}) collective-permute-start(bf16[64,4608]{1,0:T(8,128)(2,1)S(1)} %collective-permute-done.13), channel_id=1, source_target_pairs={{0,8},{8,16},{16,24},{24,28},{28,20},{20,12},{12,4},{4,0},{1,9},{9... | collective-permute-start | bytes 1769480 | tf_op jit(solution)/shard_map/ppermute | solution.py:211
  59.7 25.2 %collective-permute-start.18 = (bf16[64,4608]{1,0:T(8,128)(2,1)S(1)}, bf16[64,4608]{1,0:T(8,128)(2,1)S(1)}, u32[]{:S(2)}, u32[]{:S(2)}) collective-permute-start(bf16[64,4608]{1,0:T(8,128)(2,1)S(1)} %collective-permute-done.14), channel_id=1, source_target_pairs={{8,0},{16,8},{24,16},{28,24},{20,28},{12,20},{4,12},{0,4},{9,1},{1... | collective-permute-start | bytes 1769480 | tf_op jit(solution)/shard_map/ppermute | solution.py:211
  63.0 5.7 %collective-permute-start.5 = (f32[128,320]{1,0:T(8,128)S(1)}, f32[128,320]{1,0:T(8,128)S(1)}, u32[]{:S(2)}, u32[]{:S(2)}) collective-permute-start(f32[128,320]{1,0:T(8,128)S(1)} %dynamic-slice_add_fusion), channel_id=1, source_target_pairs={{0,2},{1,3},{2,0},{3,1},{4,6},{5,7},{6,4},{7,5},{8,10},{9,11},{10,... | collective-permute-start | bytes 491528 | tf_op jit(solution)/shard_map/ppermute | solution.py:155
  68.8 4.4 %collective-permute-start.6 = (f32[128,320]{1,0:T(8,128)S(1)}, f32[128,320]{1,0:T(8,128)S(1)}, u32[]{:S(2)}, u32[]{:S(2)}) collective-permute-start(f32[128,320]{1,0:T(8,128)S(1)} %add.202), channel_id=1, source_target_pairs={{0,1},{1,0},{2,3},{3,2},{4,5},{5,4},{6,7},{7,6},{8,9},{9,8},{10,11... | collective-permute-start | bytes 491528 | tf_op jit(solution)/shard_map/ppermute | solution.py:155
  73.1 1.4 %collective-permute-start.11 = (f32[256,128]{1,0:T(8,128)S(1)}, f32[256,128]{1,0:T(8,128)S(1)}, u32[]{:S(2)}, u32[]{:S(2)}) collective-permute-start(f32[256,128]{1,0:T(8,128)S(1)} %slice_add_fusion.12), channel_id=1, source_target_pairs={{0,1},{1,0},{2,3},{3,2},{4,5},{5,4},{6,7},{7,6},{8,9},{9,8},{10,11... | collective-permute-start | bytes 393224 | tf_op jit(solution)/shard_map/ppermute | solution.py:155
  74.5 12.5 %collective-permute-start.12 = (f32[256,128]{1,0:T(8,128)S(1)}, f32[256,128]{1,0:T(8,128)S(1)}, u32[]{:S(2)}, u32[]{:S(2)}) collective-permute-start(f32[256,128]{1,0:T(8,128)S(1)} %fusion.65), channel_id=1, source_target_pairs={{0,2},{1,3},{2,0},{3,1},{4,6},{5,7},{6,4},{7,5},{8,10},{9,11},{10,... | collective-permute-start | bytes 393224 | tf_op jit(solution)/shard_map/ppermute | solution.py:155
  77.0 14.2 %collective-permute-start.15 = (bf16[32,4608]{1,0:T(8,128)(2,1)S(1)}, bf16[32,4608]{1,0:T(8,128)(2,1)S(1)}, u32[]{:S(2)}, u32[]{:S(2)}) collective-permute-start(bf16[32,4608]{1,0:T(8,128)(2,1)S(1)} %slice.196), channel_id=1, source_target_pairs={{0,8},{8,16},{16,24},{24,28},{28,20},{20,12},{12,4},{4,0},{1,9},{9... | collective-permute-start | bytes 884744 | tf_op jit(solution)/shard_map/ppermute | solution.py:211
  77.6 13.6 %collective-permute-start.16 = (bf16[32,4608]{1,0:T(8,128)(2,1)S(1)}, bf16[32,4608]{1,0:T(8,128)(2,1)S(1)}, u32[]{:S(2)}, u32[]{:S(2)}) collective-permute-start(bf16[32,4608]{1,0:T(8,128)(2,1)S(1)} %slice.197), channel_id=1, source_target_pairs={{8,0},{16,8},{24,16},{28,24},{20,28},{12,20},{4,12},{0,4},{9,1},{1... | collective-permute-start | bytes 884744 | tf_op jit(solution)/shard_map/ppermute | solution.py:211
  84.9 11.1 %collective-permute-start.22 = (bf16[32,4608]{1,0:T(8,128)(2,1)S(1)}, bf16[32,4608]{1,0:T(8,128)(2,1)S(1)}, u32[]{:S(2)}, u32[]{:S(2)}) collective-permute-start(bf16[32,4608]{1,0:T(8,128)(2,1)S(1)} %slice.226), channel_id=1, source_target_pairs={{0,8},{8,16},{16,24},{24,28},{28,20},{20,12},{12,4},{4,0},{1,9},{9... | collective-permute-start | bytes 884744 | tf_op jit(solution)/shard_map/ppermute | solution.py:211
  85.1 10.9 %collective-permute-start.23 = (bf16[32,4608]{1,0:T(8,128)(2,1)S(1)}, bf16[32,4608]{1,0:T(8,128)(2,1)S(1)}, u32[]{:S(2)}, u32[]{:S(2)}) collective-permute-start(bf16[32,4608]{1,0:T(8,128)(2,1)S(1)} %slice.227), channel_id=1, source_target_pairs={{8,0},{16,8},{24,16},{28,24},{20,28},{12,20},{4,12},{0,4},{9,1},{1... | collective-permute-start | bytes 884744 | tf_op jit(solution)/shard_map/ppermute | solution.py:211
  92.1 5.4 %collective-permute-start.21 = (f32[128,128]{1,0:T(8,128)S(1)}, f32[128,128]{1,0:T(8,128)S(1)}, u32[]{:S(2)}, u32[]{:S(2)}) collective-permute-start(f32[128,128]{1,0:T(8,128)S(1)} %pad_maximum_fusion), channel_id=1, source_target_pairs={{0,3},{1,2},{2,1},{3,0},{4,7},{5,6},{6,5},{7,4},{8,11},{9,10},{10,... | collective-permute-start | bytes 196616 | tf_op jit(solution)/shard_map/ppermute | solution.py:155
  92.1 5.8 %collective-permute-start.20 = (f32[128,128]{1,0:T(8,128)S(1)}, f32[128,128]{1,0:T(8,128)S(1)}, u32[]{:S(2)}, u32[]{:S(2)}) collective-permute-start(f32[128,128]{1,0:T(8,128)S(1)} %pad_maximum_fusion), channel_id=1, source_target_pairs={{0,2},{1,3},{2,0},{3,1},{4,6},{5,7},{6,4},{7,5},{8,10},{9,11},{10,... | collective-permute-start | bytes 196616 | tf_op jit(solution)/shard_map/ppermute | solution.py:155
  93.7 4.2 %collective-permute-start.19 = (f32[128,128]{1,0:T(8,128)S(1)}, f32[128,128]{1,0:T(8,128)S(1)}, u32[]{:S(2)}, u32[]{:S(2)}) collective-permute-start(f32[128,128]{1,0:T(8,128)S(1)} %pad_maximum_fusion), channel_id=1, source_target_pairs={{0,1},{1,0},{2,3},{3,2},{4,5},{5,4},{6,7},{7,6},{8,9},{9,8},{10,11... | collective-permute-start | bytes 196616 | tf_op jit(solution)/shard_map/ppermute | solution.py:155
  98.3 3.0 %collective-permute-start.26 = (f32[2,16]{1,0:T(2,128)S(1)}, f32[2,16]{1,0:T(2,128)S(1)}, u32[]{:S(2)}, u32[]{:S(2)}) collective-permute-start(f32[2,16]{1,0:T(2,128)S(1)} %score.1), channel_id=1, source_target_pairs={{0,3},{1,2},{2,1},{3,0},{4,7},{5,6},{6,5},{7,4},{8,11},{9,10},{10,... | collective-permute-start | bytes 392 | tf_op jit(solution)/shard_map/ppermute | solution.py:155
  98.8 3.6 %collective-permute-start.25 = (f32[2,16]{1,0:T(2,128)S(1)}, f32[2,16]{1,0:T(2,128)S(1)}, u32[]{:S(2)}, u32[]{:S(2)}) collective-permute-start(f32[2,16]{1,0:T(2,128)S(1)} %score.1), channel_id=1, source_target_pairs={{0,2},{1,3},{2,0},{3,1},{4,6},{5,7},{6,4},{7,5},{8,10},{9,11},{10,... | collective-permute-start | bytes 392 | tf_op jit(solution)/shard_map/ppermute | solution.py:155
  100.0 2.3 %collective-permute-start.24 = (f32[2,16]{1,0:T(2,128)S(1)}, f32[2,16]{1,0:T(2,128)S(1)}, u32[]{:S(2)}, u32[]{:S(2)}) collective-permute-start(f32[2,16]{1,0:T(2,128)S(1)} %score.1), channel_id=1, source_target_pairs={{0,1},{1,0},{2,3},{3,2},{4,5},{5,4},{6,7},{7,6},{8,9},{9,8},{10,11... | collective-permute-start | bytes 392 | tf_op jit(solution)/shard_map/ppermute | solution.py:155

commit v12 on v11

--- a/solution.py
+++ b/solution.py
@@ -264,7 +264,7 @@
     owner = place // per
     hit = (source[:, None] == position(owner)[None, :]) & (row[:, None] == (place % per)[None, :])
     scores = score(coefficients, projected, hit.astype(jnp.float32))
-    return small_sum(scores, shards, 4)
+    return small_sum(scores, shards, 2)
 
 
 def solution(mesh):

time: 103 us -> 104 us (level)
  waiting for transfers between devices: 41.8 us -> 43.3 us
    ppermute x11 -> x10, waiting for transfers between devices: 7.2 us -> 8.66 us  [swapped(): return lax.ppermute(piece, 'mp', [(i, i ^ distance) for i in range(shards)])]
    ppermute x11 -> x10, starting transfers between devices: 7.2 us -> 6.44 us  [swapped(): return lax.ppermute(piece, 'mp', [(i, i ^ distance) for i in range(shards)])]
  transfers between devices with their start and end apart: 27 -> 26, of which waited for: 13 -> 13; matrix products, arithmetic and copies ran while one was open for 18% -> 17% of each run, Pallas kernels for 14% -> 14%
where the time goes in v12:
time: 104 us
  waiting for transfers between devices  43.3 us (42%)
  starting transfers between devices  24 us (23%)
  Pallas kernels  16.5 us (16%)
  matrix products  16.5 us (16%)
  other arithmetic  1.43 us (1%)
  local copies, waits for them, and re-layouts  1.38 us (1%)
    ppermute x8, waiting for transfers between devices, send(): lax.ppermute(ahead, 'dp', forward)  27.2 us
    dot_general x13, matrix products, contract_rows(): lax.dot_general(both, second, (((1,), (1,)), ((), ())), preferred_element...  16.5 us
    ppermute x8, starting transfers between devices, send(): lax.ppermute(behind, 'dp', backward)  14.1 us
    pallas_call x2, Pallas kernels, rotate(): pl.pallas_call(kernel, out_shape=jax.ShapeDtypeStruct((2 * rows, total),...  12.7 us
    ppermute x10, waiting for transfers between devices, swapped(): return lax.ppermute(piece, 'mp', [(i, i ^ distance) for i in range(shards)])  8.66 us
    ppermute x8, waiting for transfers between devices, send(): lax.ppermute(behind, 'dp', backward)  7.42 us
    ppermute x10, starting transfers between devices, swapped(): return lax.ppermute(piece, 'mp', [(i, i ^ distance) for i in range(shards)])  6.44 us
    ppermute x8, starting transfers between devices, send(): lax.ppermute(ahead, 'dp', forward)  3.44 us
  transfers between devices with their start and end apart: 26, of which 13 were waited for; matrix products, arithmetic and copies ran while one was open for 17% of the time, Pallas kernels for 14%

profile of v12, /device:TPU:0, one launch (start us, length us, event | category | flops | bytes accessed | tf_op | source)
XLA Modules:
  0.0 103.6 jit_solution(10747137133279365801)
XLA Ops:
  0.0 0.7 copy-done
  0.7 1.7 %pick_rows.2 = bf16[64,4608]{1,0:T(8,128)(2,1)S(1)} custom-call(s32[16]{0:T(128)S(1)} %copy-done, bf16[1,512,2048]{2,1,0:T(8,128)(2,1)} %refs_0_.2, bf16[1,512,7168]{2,1,0:T(8,128)(2,1)} %refs_0_.3), custom_call_target="tpu_custom_call" | custom-call | tf_op jit(solution)/shard_map/pick_rows/pallas_call | solution.py:49
  2.4 3.0 %collective-permute-start.1 = (bf16[64,4608]{1,0:T(8,128)(2,1)S(1)}, bf16[64,4608]{1,0:T(8,128)(2,1)S(1)}, u32[]{:S(2)}, u32[]{:S(2)}) collective-permute-start(bf16[64,4608]{1,0:T(8,128)(2,1)S(1)} %pick_rows.2), channel_id=1, source_target_pairs={{8,0},{16,8},{24,16},{28,24},{20,28},{12,20},{4,12},{0,4},{9,1},{1... | collective-permute-start | bytes 1769480 | tf_op jit(solution)/shard_map/ppermute | solution.py:211
  5.4 0.2 collective-permute-start
  5.6 3.4 %rotate.2 = bf16[512,2048]{1,0:T(8,128)(2,1)} custom-call(s32[1]{0:T(128)} %bitcast.shard_ref, bf16[256,8192]{1,0:T(8,128)(2,1)} %matrix_ref.2, bf16[4,512,512]{2,1,0:T(8,128)(2,1)} %basis_ref.2), custom_call_target="tpu_custom_call" | custom-call | flops 536870912 | bytes 5242880 | tf_op jit(solution)/shard_map/rotate/pallas_call | solution.py:77
  8.9 1.7 %pick_rows.3 = bf16[64,4608]{1,0:T(8,128)(2,1)S(1)} custom-call(s32[16]{0:T(128)S(1)} %copy-done.1, bf16[1,512,7168]{2,1,0:T(8,128)(2,1)} %refs_0_.3), custom_call_target="tpu_custom_call" | custom-call | tf_op jit(solution)/shard_map/pick_rows/pallas_call | solution.py:49
  10.6 1.9 %collective-permute-start.8 = (bf16[64,4608]{1,0:T(8,128)(2,1)S(1)}, bf16[64,4608]{1,0:T(8,128)(2,1)S(1)}, u32[]{:S(2)}, u32[]{:S(2)}) collective-permute-start(bf16[64,4608]{1,0:T(8,128)(2,1)S(1)} %pick_rows.3), channel_id=1, source_target_pairs={{8,0},{16,8},{24,16},{28,24},{20,28},{12,20},{4,12},{0,4},{9,1},{1... | collective-permute-start | bytes 1769480 | tf_op jit(solution)/shard_map/ppermute | solution.py:211
  12.5 0.2 collective-permute-start.7
  12.7 0.2 convert_reduce_fusion
  12.9 0.1 concatenate.54
  13.1 0.1 concatenate.53
  13.2 9.4 %rotate.3 = bf16[512,7168]{1,0:T(8,128)(2,1)} custom-call(s32[1]{0:T(128)} %constant.120.clone.1.shard_ref, bf16[256,7168]{1,0:T(8,128)(2,1)} %matrix_ref.3, bf16[28,256,256]{2,1,0:T(8,128)(2,1)} %basis_ref.3), custom_call_target="tpu_custom_call" | custom-call | flops 939524096 | bytes 14680064 | tf_op jit(solution)/shard_map/rotate/pallas_call | solution.py:77
  22.6 0.2 and_convert_fusion.hit_ref
  22.8 2.0 %collective-permute-start.2 = (bf16[64,4608]{1,0:T(8,128)(2,1)S(1)}, bf16[64,4608]{1,0:T(8,128)(2,1)S(1)}, u32[]{:S(2)}, u32[]{:S(2)}) collective-permute-start(bf16[64,4608]{1,0:T(8,128)(2,1)S(1)} %collective-permute-done), channel_id=1, source_target_pairs={{0,8},{8,16},{16,24},{24,28},{28,20},{20,12},{12,4},{4,0},{1,9},{9... | collective-permute-start | bytes 1769480 | tf_op jit(solution)/shard_map/ppermute | solution.py:211
  24.8 0.1 collective-permute-start.3
  24.9 7.4 %collective-permute-done.8 = bf16[64,4608]{1,0:T(8,128)(2,1)S(1)} collective-permute-done((bf16[64,4608]{1,0:T(8,128)(2,1)S(1)}, bf16[64,4608]{1,0:T(8,128)(2,1)S(1)}, u32[]{:S(2)}, u32[]{:S(2)}) %collective-permute-start.8) | collective-permute-done | bytes 589856 | tf_op jit(solution)/shard_map/ppermute | solution.py:211
  32.3 2.1 %collective-permute-done.7 = bf16[64,4608]{1,0:T(8,128)(2,1)} collective-permute-done((bf16[64,4608]{1,0:T(8,128)(2,1)S(1)}, bf16[64,4608]{1,0:T(8,128)(2,1)}, u32[]{:S(2)}, u32[]{:S(2)}) %collective-permute-start.7) | collective-permute-done | bytes 589856 | tf_op jit(solution)/shard_map/ppermute | solution.py:211
  34.4 0.1 collective-permute-start.13
  34.5 1.9 %collective-permute-start.14 = (bf16[64,4608]{1,0:T(8,128)(2,1)S(1)}, bf16[64,4608]{1,0:T(8,128)(2,1)S(1)}, u32[]{:S(2)}, u32[]{:S(2)}) collective-permute-start(bf16[64,4608]{1,0:T(8,128)(2,1)S(1)} %collective-permute-done.8), channel_id=1, source_target_pairs={{8,0},{16,8},{24,16},{28,24},{20,28},{12,20},{4,12},{0,4},{9,1},{1... | collective-permute-start | bytes 1769480 | tf_op jit(solution)/shard_map/ppermute | solution.py:211
  36.5 2.6 %fusion.18 = f32[512,128]{1,0:T(8,128)S(1)} fusion(bf16[512,7168]{1,0:T(8,128)(2,1)} %rotate.3, bf16[128,4608]{1,0:T(8,128)(2,1)S(1)} %constant_dynamic-update-slice_fusion), kind=kOutput, calls=%fused_computation.18 | convolution fusion | flops 335544320 | bytes 3538944 | tf_op jit(solution)/shard_map/dot_general | solution.py:101
  39.1 1.4 %fusion.4 = f32[512,64]{1,0:T(8,128)S(1)} fusion(bf16[64,4608]{1,0:T(8,128)(2,1)S(1)} %pick_rows.3, bf16[512,7168]{1,0:T(8,128)(2,1)S(1)} %copy-done.2), kind=kOutput, calls=%fused_computation.4 | convolution fusion | flops 301989888 | bytes 5439488 | tf_op jit(solution)/shard_map/dot_general | solution.py:101
  40.5 2.4 %fusion.8 = f32[512,128]{1,0:T(8,128)S(1)} fusion(bf16[512,7168]{1,0:T(8,128)(2,1)S(1)} %copy-done.2, bf16[64,4608]{1,0:T(8,128)(2,1)S(1)} %collective-permute-done.8, bf16[64,4608]{1,0:T(8,128)(2,1)} %collective-permute-done.7), kind=kOutput, calls=%fused_computation.8 | convolution fusion | flops 606339072 | bytes 6160384 | tf_op jit(solution)/shard_map/dot_general | solution.py:101
  42.9 0.8 fusion.14
  43.9 3.0 %collective-permute-done.2 = bf16[64,4608]{1,0:T(8,128)(2,1)S(1)} collective-permute-done((bf16[64,4608]{1,0:T(8,128)(2,1)S(1)}, bf16[64,4608]{1,0:T(8,128)(2,1)S(1)}, u32[]{:S(2)}, u32[]{:S(2)}) %collective-permute-start.2) | collective-permute-done | bytes 589856 | tf_op jit(solution)/shard_map/ppermute | solution.py:211
  47.1 1.3 %fusion.20 = f32[512,320]{1,0:T(8,128)S(1)} fusion(bf16[512,2048]{1,0:T(8,128)(2,1)S(1)} %copy-done.3, bf16[64,2048]{1,0:T(8,128)(2,1)S(1)} %slice.147, bf16[128,2048]{1,0:T(8,128)(2,1)S(1)} %slice.190, bf16[128,2048]{1,0:T(8,128)(2,1)S(1)} %slice.189), kind=kOutput, calls=%fused_computation.20 | convolution fusion | flops 675020800 | bytes 4063232 | tf_op jit(solution)/shard_map/dot_general | solution.py:101
  48.5 0.1 collective-permute-start.4
  48.5 0.2 collective-permute-start.9
  48.7 1.9 %collective-permute-start.10 = (bf16[64,4608]{1,0:T(8,128)(2,1)S(1)}, bf16[64,4608]{1,0:T(8,128)(2,1)S(1)}, u32[]{:S(2)}, u32[]{:S(2)}) collective-permute-start(bf16[64,4608]{1,0:T(8,128)(2,1)S(1)} %collective-permute-done.3), channel_id=1, source_target_pairs={{8,0},{16,8},{24,16},{28,24},{20,28},{12,20},{4,12},{0,4},{9,1},{1... | collective-permute-start | bytes 1769480 | tf_op jit(solution)/shard_map/ppermute | solution.py:211
  50.6 9.0 %collective-permute-done.13 = bf16[64,4608]{1,0:T(8,128)(2,1)S(1)} collective-permute-done((bf16[64,4608]{1,0:T(8,128)(2,1)}, bf16[64,4608]{1,0:T(8,128)(2,1)S(1)}, u32[]{:S(2)}, u32[]{:S(2)}) %collective-permute-start.13) | collective-permute-done | bytes 589856 | tf_op jit(solution)/shard_map/ppermute | solution.py:211
  59.6 0.1 collective-permute-start.17
  59.7 1.9 %collective-permute-start.18 = (bf16[64,4608]{1,0:T(8,128)(2,1)S(1)}, bf16[64,4608]{1,0:T(8,128)(2,1)S(1)}, u32[]{:S(2)}, u32[]{:S(2)}) collective-permute-start(bf16[64,4608]{1,0:T(8,128)(2,1)S(1)} %collective-permute-done.14), channel_id=1, source_target_pairs={{8,0},{16,8},{24,16},{28,24},{20,28},{12,20},{4,12},{0,4},{9,1},{1... | collective-permute-start | bytes 1769480 | tf_op jit(solution)/shard_map/ppermute | solution.py:211
  61.6 1.4 %fusion.6 = f32[512,128]{1,0:T(8,128)S(1)} fusion(bf16[512,7168]{1,0:T(8,128)(2,1)S(1)} %copy-done.2, bf16[64,4608]{1,0:T(8,128)(2,1)S(1)} %collective-permute-done.14, bf16[64,4608]{1,0:T(8,128)(2,1)S(1)} %collective-permute-done.13), kind=kOutput, calls=%fused_computation.6 | convolution fusion | flops 606339072 | bytes 6160384 | tf_op jit(solution)/shard_map/dot_general | solution.py:101
  63.0 1.6 %collective-permute-start.5 = (f32[128,320]{1,0:T(8,128)S(1)}, f32[128,320]{1,0:T(8,128)S(1)}, u32[]{:S(2)}, u32[]{:S(2)}) collective-permute-start(f32[128,320]{1,0:T(8,128)S(1)} %dynamic-slice_add_fusion), channel_id=1, source_target_pairs={{0,2},{1,3},{2,0},{3,1},{4,6},{5,7},{6,4},{7,5},{8,10},{9,11},{10,... | collective-permute-start | bytes 491528 | tf_op jit(solution)/shard_map/ppermute | solution.py:155
  64.6 0.8 fusion.16
  65.5 3.3 %collective-permute-done.5 = f32[128,320]{1,0:T(8,128)S(1)} collective-permute-done((f32[128,320]{1,0:T(8,128)S(1)}, f32[128,320]{1,0:T(8,128)S(1)}, u32[]{:S(2)}, u32[]{:S(2)}) %collective-permute-start.5) | collective-permute-done | bytes 163872 | tf_op jit(solution)/shard_map/ppermute | solution.py:155
  68.8 0.1 collective-permute-start.6
  68.9 3.3 %collective-permute-done.9 = bf16[64,4608]{1,0:T(8,128)(2,1)S(1)} collective-permute-done((bf16[64,4608]{1,0:T(8,128)(2,1)S(1)}, bf16[64,4608]{1,0:T(8,128)(2,1)S(1)}, u32[]{:S(2)}, u32[]{:S(2)}) %collective-permute-start.9) | collective-permute-done | bytes 589856 | tf_op jit(solution)/shard_map/ppermute | solution.py:211
  72.3 0.7 fusion.41
  73.1 0.1 collective-permute-start.11
  73.2 1.2 %collective-permute-done.11 = f32[256,128]{1,0:T(8,128)S(1)} collective-permute-done((f32[256,128]{1,0:T(8,128)S(1)}, f32[256,128]{1,0:T(8,128)S(1)}, u32[]{:S(2)}, u32[]{:S(2)}) %collective-permute-start.11) | collective-permute-done | bytes 131104 | tf_op jit(solution)/shard_map/ppermute | solution.py:155
  74.5 1.6 %collective-permute-start.12 = (f32[256,128]{1,0:T(8,128)S(1)}, f32[256,128]{1,0:T(8,128)S(1)}, u32[]{:S(2)}, u32[]{:S(2)}) collective-permute-start(f32[256,128]{1,0:T(8,128)S(1)} %fusion.65), channel_id=1, source_target_pairs={{0,2},{1,3},{2,0},{3,1},{4,6},{5,7},{6,4},{7,5},{8,10},{9,11},{10,... | collective-permute-start | bytes 393224 | tf_op jit(solution)/shard_map/ppermute | solution.py:155
  76.1 0.9 fusion.12
  77.0 0.6 collective-permute-start.15
  77.6 1.5 %collective-permute-start.16 = (bf16[32,4608]{1,0:T(8,128)(2,1)S(1)}, bf16[32,4608]{1,0:T(8,128)(2,1)S(1)}, u32[]{:S(2)}, u32[]{:S(2)}) collective-permute-start(bf16[32,4608]{1,0:T(8,128)(2,1)S(1)} %slice.197), channel_id=1, source_target_pairs={{8,0},{16,8},{24,16},{28,24},{20,28},{12,20},{4,12},{0,4},{9,1},{1... | collective-permute-start | bytes 884744 | tf_op jit(solution)/shard_map/ppermute | solution.py:211
  79.1 5.8 %collective-permute-done.17 = bf16[64,4608]{1,0:T(8,128)(2,1)S(1)} collective-permute-done((bf16[64,4608]{1,0:T(8,128)(2,1)S(1)}, bf16[64,4608]{1,0:T(8,128)(2,1)S(1)}, u32[]{:S(2)}, u32[]{:S(2)}) %collective-permute-start.17) | collective-permute-done | bytes 589856 | tf_op jit(solution)/shard_map/ppermute | solution.py:211
  84.9 0.2 collective-permute-start.22
  85.1 1.9 %collective-permute-start.23 = (bf16[32,4608]{1,0:T(8,128)(2,1)S(1)}, bf16[32,4608]{1,0:T(8,128)(2,1)S(1)}, u32[]{:S(2)}, u32[]{:S(2)}) collective-permute-start(bf16[32,4608]{1,0:T(8,128)(2,1)S(1)} %slice.227), channel_id=1, source_target_pairs={{8,0},{16,8},{24,16},{28,24},{20,28},{12,20},{4,12},{0,4},{9,1},{1... | collective-permute-start | bytes 884744 | tf_op jit(solution)/shard_map/ppermute | solution.py:211
  87.0 1.4 %fusion.2 = f32[512,128]{1,0:T(8,128)S(1)} fusion(bf16[512,7168]{1,0:T(8,128)(2,1)S(1)} %copy-done.2, bf16[64,4608]{1,0:T(8,128)(2,1)S(1)} %collective-permute-done.18, bf16[64,4608]{1,0:T(8,128)(2,1)S(1)} %collective-permute-done.17), kind=kOutput, calls=%fused_computation.2 | convolution fusion | flops 606339072 | bytes 6160384 | tf_op jit(solution)/shard_map/dot_general | solution.py:101
  88.4 2.7 %collective-permute-done.15 = bf16[32,4608]{1,0:T(8,128)(2,1)S(1)} collective-permute-done((bf16[32,4608]{1,0:T(8,128)(2,1)S(1)}, bf16[32,4608]{1,0:T(8,128)(2,1)S(1)}, u32[]{:S(2)}, u32[]{:S(2)}) %collective-permute-start.15) | collective-permute-done | bytes 294944 | tf_op jit(solution)/shard_map/ppermute | solution.py:211
  91.2 0.7 fusion.45
  92.0 0.1 pad_maximum_fusion
  92.1 0.1 collective-permute-start.21
  92.1 1.6 %collective-permute-start.20 = (f32[128,128]{1,0:T(8,128)S(1)}, f32[128,128]{1,0:T(8,128)S(1)}, u32[]{:S(2)}, u32[]{:S(2)}) collective-permute-start(f32[128,128]{1,0:T(8,128)S(1)} %pad_maximum_fusion), channel_id=1, source_target_pairs={{0,2},{1,3},{2,0},{3,1},{4,6},{5,7},{6,4},{7,5},{8,10},{9,11},{10,... | collective-permute-start | bytes 196616 | tf_op jit(solution)/shard_map/ppermute | solution.py:155
  93.7 0.3 collective-permute-start.19
  94.0 0.8 fusion.10
  94.8 1.2 %collective-permute-done.22 = bf16[32,4608]{1,0:T(8,128)(2,1)S(1)} collective-permute-done((bf16[32,4608]{1,0:T(8,128)(2,1)S(1)}, bf16[32,4608]{1,0:T(8,128)(2,1)S(1)}, u32[]{:S(2)}, u32[]{:S(2)}) %collective-permute-start.22) | collective-permute-done | bytes 294944 | tf_op jit(solution)/shard_map/ppermute | solution.py:211
  96.0 1.4 %fusion = f32[512,64]{1,0:T(8,128)S(1)} fusion(bf16[512,7168]{1,0:T(8,128)(2,1)S(1)} %copy-done.2, bf16[32,4608]{1,0:T(8,128)(2,1)S(1)} %collective-permute-done.23, bf16[32,4608]{1,0:T(8,128)(2,1)S(1)} %collective-permute-done.22), kind=kOutput, calls=%fused_computation | convolution fusion | flops 303169536 | bytes 5439488 | tf_op jit(solution)/shard_map/dot_general | solution.py:101
  97.4 0.5 collective-permute-done.20
  97.9 0.3 score.1
  98.3 0.1 collective-permute-start.24
  98.4 1.1 %collective-permute-done.24 = f32[2,16]{1,0:T(2,128)S(1)} collective-permute-done((f32[2,16]{1,0:T(2,128)S(1)}, f32[2,16]{1,0:T(2,128)S(1)}, u32[]{:S(2)}, u32[]{:S(2)}) %collective-permute-start.24) | collective-permute-done | bytes 160 | tf_op jit(solution)/shard_map/ppermute | solution.py:155
  99.5 1.1 %collective-permute-start.25 = (f32[2,16]{1,0:T(2,128)S(1)}, f32[2,16]{1,0:T(2,128)S(1)}, u32[]{:S(2)}, u32[]{:S(2)}) collective-permute-start(f32[2,16]{1,0:T(2,128)S(1)} %add.222), channel_id=1, source_target_pairs={{0,2},{1,3},{2,0},{3,1},{4,6},{5,7},{6,4},{7,5},{8,10},{9,11},{10,... | collective-permute-start | bytes 392 | tf_op jit(solution)/shard_map/ppermute | solution.py:155
  100.5 2.5 %collective-permute-done.25 = f32[2,16]{1,0:T(2,128)S(1)} collective-permute-done((f32[2,16]{1,0:T(2,128)S(1)}, f32[2,16]{1,0:T(2,128)S(1)}, u32[]{:S(2)}, u32[]{:S(2)}) %collective-permute-start.25) | collective-permute-done | bytes 160 | tf_op jit(solution)/shard_map/ppermute | solution.py:155
  103.0 0.6 add.223
  (64 shorter events, 1.0 us)
Async XLA Ops:
  0.0 0.7 copy-start
  2.4 20.4 %collective-permute-start.1 = (bf16[64,4608]{1,0:T(8,128)(2,1)S(1)}, bf16[64,4608]{1,0:T(8,128)(2,1)S(1)}, u32[]{:S(2)}, u32[]{:S(2)}) collective-permute-start(bf16[64,4608]{1,0:T(8,128)(2,1)S(1)} %pick_rows.2), channel_id=1, source_target_pairs={{8,0},{16,8},{24,16},{28,24},{20,28},{12,20},{4,12},{0,4},{9,1},{1... | collective-permute-start | bytes 1769480 | tf_op jit(solution)/shard_map/ppermute | solution.py:211
  5.4 17.4 %collective-permute-start = (bf16[64,4608]{1,0:T(8,128)(2,1)S(1)}, bf16[64,4608]{1,0:T(8,128)(2,1)S(1)}, u32[]{:S(2)}, u32[]{:S(2)}) collective-permute-start(bf16[64,4608]{1,0:T(8,128)(2,1)S(1)} %pick_rows.2), channel_id=1, source_target_pairs={{0,8},{8,16},{16,24},{24,28},{28,20},{20,12},{12,4},{4,0},{1,9},{9... | collective-permute-start | bytes 1769480 | tf_op jit(solution)/shard_map/ppermute | solution.py:211
  5.6 3.4 %copy-start.1 = (s32[16]{0:T(128)S(1)}, s32[16]{0:T(128)}, u32[]{:S(2)}) copy-start(s32[16]{0:T(128)} %owners_ref.2) | copy-start | bytes 196
  10.6 21.7 %collective-permute-start.8 = (bf16[64,4608]{1,0:T(8,128)(2,1)S(1)}, bf16[64,4608]{1,0:T(8,128)(2,1)S(1)}, u32[]{:S(2)}, u32[]{:S(2)}) collective-permute-start(bf16[64,4608]{1,0:T(8,128)(2,1)S(1)} %pick_rows.3), channel_id=1, source_target_pairs={{8,0},{16,8},{24,16},{28,24},{20,28},{12,20},{4,12},{0,4},{9,1},{1... | collective-permute-start | bytes 1769480 | tf_op jit(solution)/shard_map/ppermute | solution.py:211
  12.5 21.9 %collective-permute-start.7 = (bf16[64,4608]{1,0:T(8,128)(2,1)S(1)}, bf16[64,4608]{1,0:T(8,128)(2,1)}, u32[]{:S(2)}, u32[]{:S(2)}) collective-permute-start(bf16[64,4608]{1,0:T(8,128)(2,1)S(1)} %pick_rows.3), channel_id=1, source_target_pairs={{0,8},{8,16},{16,24},{24,28},{28,20},{20,12},{12,4},{4,0},{1,9},{9... | collective-permute-start | bytes 1769480 | tf_op jit(solution)/shard_map/ppermute | solution.py:211
  22.6 16.5 %copy-start.2 = (bf16[512,7168]{1,0:T(8,128)(2,1)S(1)}, bf16[512,7168]{1,0:T(8,128)(2,1)}, u32[]{:S(2)}) copy-start(bf16[512,7168]{1,0:T(8,128)(2,1)} %rotate.3) | copy-start | bytes 22020100
  22.8 24.1 %collective-permute-start.2 = (bf16[64,4608]{1,0:T(8,128)(2,1)S(1)}, bf16[64,4608]{1,0:T(8,128)(2,1)S(1)}, u32[]{:S(2)}, u32[]{:S(2)}) collective-permute-start(bf16[64,4608]{1,0:T(8,128)(2,1)S(1)} %collective-permute-done), channel_id=1, source_target_pairs={{0,8},{8,16},{16,24},{24,28},{28,20},{20,12},{12,4},{4,0},{1,9},{9... | collective-permute-start | bytes 1769480 | tf_op jit(solution)/shard_map/ppermute | solution.py:211
  24.8 22.2 %collective-permute-start.3 = (bf16[64,4608]{1,0:T(8,128)(2,1)S(1)}, bf16[64,4608]{1,0:T(8,128)(2,1)S(1)}, u32[]{:S(2)}, u32[]{:S(2)}) collective-permute-start(bf16[64,4608]{1,0:T(8,128)(2,1)S(1)} %collective-permute-done.1), channel_id=1, source_target_pairs={{8,0},{16,8},{24,16},{28,24},{20,28},{12,20},{4,12},{0,4},{9,1},{1... | collective-permute-start | bytes 1769480 | tf_op jit(solution)/shard_map/ppermute | solution.py:211
  34.4 25.2 %collective-permute-start.13 = (bf16[64,4608]{1,0:T(8,128)(2,1)}, bf16[64,4608]{1,0:T(8,128)(2,1)S(1)}, u32[]{:S(2)}, u32[]{:S(2)}) collective-permute-start(bf16[64,4608]{1,0:T(8,128)(2,1)} %collective-permute-done.7), channel_id=1, source_target_pairs={{0,8},{8,16},{16,24},{24,28},{28,20},{20,12},{12,4},{4,0},{1,9},{9... | collective-permute-start | bytes 1769480 | tf_op jit(solution)/shard_map/ppermute | solution.py:211
  34.5 25.1 %collective-permute-start.14 = (bf16[64,4608]{1,0:T(8,128)(2,1)S(1)}, bf16[64,4608]{1,0:T(8,128)(2,1)S(1)}, u32[]{:S(2)}, u32[]{:S(2)}) collective-permute-start(bf16[64,4608]{1,0:T(8,128)(2,1)S(1)} %collective-permute-done.8), channel_id=1, source_target_pairs={{8,0},{16,8},{24,16},{28,24},{20,28},{12,20},{4,12},{0,4},{9,1},{1... | collective-permute-start | bytes 1769480 | tf_op jit(solution)/shard_map/ppermute | solution.py:211
  43.8 3.3 %copy-start.3 = (bf16[512,2048]{1,0:T(8,128)(2,1)S(1)}, bf16[512,2048]{1,0:T(8,128)(2,1)}, u32[]{:S(2)}) copy-start(bf16[512,2048]{1,0:T(8,128)(2,1)} %rotate.2) | copy-start | bytes 6291460
  48.5 14.5 %collective-permute-start.4 = (f32[128,320]{1,0:T(8,128)S(1)}, f32[128,320]{1,0:T(8,128)S(1)}, u32[]{:S(2)}, u32[]{:S(2)}) collective-permute-start(f32[128,320]{1,0:T(8,128)S(1)} %constant_dynamic-slice_fusion), channel_id=1, source_target_pairs={{0,1},{1,0},{2,3},{3,2},{4,5},{5,4},{6,7},{7,6},{8,9},{9,8},{10,11... | collective-permute-start | bytes 491528 | tf_op jit(solution)/shard_map/ppermute | solution.py:155
  48.5 23.7 %collective-permute-start.9 = (bf16[64,4608]{1,0:T(8,128)(2,1)S(1)}, bf16[64,4608]{1,0:T(8,128)(2,1)S(1)}, u32[]{:S(2)}, u32[]{:S(2)}) collective-permute-start(bf16[64,4608]{1,0:T(8,128)(2,1)S(1)} %collective-permute-done.2), channel_id=1, source_target_pairs={{0,8},{8,16},{16,24},{24,28},{28,20},{20,12},{12,4},{4,0},{1,9},{9... | collective-permute-start | bytes 1769480 | tf_op jit(solution)/shard_map/ppermute | solution.py:211
  48.7 23.6 %collective-permute-start.10 = (bf16[64,4608]{1,0:T(8,128)(2,1)S(1)}, bf16[64,4608]{1,0:T(8,128)(2,1)S(1)}, u32[]{:S(2)}, u32[]{:S(2)}) collective-permute-start(bf16[64,4608]{1,0:T(8,128)(2,1)S(1)} %collective-permute-done.3), channel_id=1, source_target_pairs={{8,0},{16,8},{24,16},{28,24},{20,28},{12,20},{4,12},{0,4},{9,1},{1... | collective-permute-start | bytes 1769480 | tf_op jit(solution)/shard_map/ppermute | solution.py:211
  59.6 25.3 %collective-permute-start.17 = (bf16[64,4608]{1,0:T(8,128)(2,1)S(1)}, bf16[64,4608]{1,0:T(8,128)(2,1)S(1)}, u32[]{:S(2)}, u32[]{:S(2)}) collective-permute-start(bf16[64,4608]{1,0:T(8,128)(2,1)S(1)} %collective-permute-done.13), channel_id=1, source_target_pairs={{0,8},{8,16},{16,24},{24,28},{28,20},{20,12},{12,4},{4,0},{1,9},{9... | collective-permute-start | bytes 1769480 | tf_op jit(solution)/shard_map/ppermute | solution.py:211
  59.7 25.2 %collective-permute-start.18 = (bf16[64,4608]{1,0:T(8,128)(2,1)S(1)}, bf16[64,4608]{1,0:T(8,128)(2,1)S(1)}, u32[]{:S(2)}, u32[]{:S(2)}) collective-permute-start(bf16[64,4608]{1,0:T(8,128)(2,1)S(1)} %collective-permute-done.14), channel_id=1, source_target_pairs={{8,0},{16,8},{24,16},{28,24},{20,28},{12,20},{4,12},{0,4},{9,1},{1... | collective-permute-start | bytes 1769480 | tf_op jit(solution)/shard_map/ppermute | solution.py:211
  63.0 5.7 %collective-permute-start.5 = (f32[128,320]{1,0:T(8,128)S(1)}, f32[128,320]{1,0:T(8,128)S(1)}, u32[]{:S(2)}, u32[]{:S(2)}) collective-permute-start(f32[128,320]{1,0:T(8,128)S(1)} %dynamic-slice_add_fusion), channel_id=1, source_target_pairs={{0,2},{1,3},{2,0},{3,1},{4,6},{5,7},{6,4},{7,5},{8,10},{9,11},{10,... | collective-permute-start | bytes 491528 | tf_op jit(solution)/shard_map/ppermute | solution.py:155
  68.8 4.4 %collective-permute-start.6 = (f32[128,320]{1,0:T(8,128)S(1)}, f32[128,320]{1,0:T(8,128)S(1)}, u32[]{:S(2)}, u32[]{:S(2)}) collective-permute-start(f32[128,320]{1,0:T(8,128)S(1)} %add.199), channel_id=1, source_target_pairs={{0,1},{1,0},{2,3},{3,2},{4,5},{5,4},{6,7},{7,6},{8,9},{9,8},{10,11... | collective-permute-start | bytes 491528 | tf_op jit(solution)/shard_map/ppermute | solution.py:155
  73.1 1.4 %collective-permute-start.11 = (f32[256,128]{1,0:T(8,128)S(1)}, f32[256,128]{1,0:T(8,128)S(1)}, u32[]{:S(2)}, u32[]{:S(2)}) collective-permute-start(f32[256,128]{1,0:T(8,128)S(1)} %slice_add_fusion.12), channel_id=1, source_target_pairs={{0,1},{1,0},{2,3},{3,2},{4,5},{5,4},{6,7},{7,6},{8,9},{9,8},{10,11... | collective-permute-start | bytes 393224 | tf_op jit(solution)/shard_map/ppermute | solution.py:155
  74.5 12.5 %collective-permute-start.12 = (f32[256,128]{1,0:T(8,128)S(1)}, f32[256,128]{1,0:T(8,128)S(1)}, u32[]{:S(2)}, u32[]{:S(2)}) collective-permute-start(f32[256,128]{1,0:T(8,128)S(1)} %fusion.65), channel_id=1, source_target_pairs={{0,2},{1,3},{2,0},{3,1},{4,6},{5,7},{6,4},{7,5},{8,10},{9,11},{10,... | collective-permute-start | bytes 393224 | tf_op jit(solution)/shard_map/ppermute | solution.py:155
  77.0 14.2 %collective-permute-start.15 = (bf16[32,4608]{1,0:T(8,128)(2,1)S(1)}, bf16[32,4608]{1,0:T(8,128)(2,1)S(1)}, u32[]{:S(2)}, u32[]{:S(2)}) collective-permute-start(bf16[32,4608]{1,0:T(8,128)(2,1)S(1)} %slice.196), channel_id=1, source_target_pairs={{0,8},{8,16},{16,24},{24,28},{28,20},{20,12},{12,4},{4,0},{1,9},{9... | collective-permute-start | bytes 884744 | tf_op jit(solution)/shard_map/ppermute | solution.py:211
  77.6 13.6 %collective-permute-start.16 = (bf16[32,4608]{1,0:T(8,128)(2,1)S(1)}, bf16[32,4608]{1,0:T(8,128)(2,1)S(1)}, u32[]{:S(2)}, u32[]{:S(2)}) collective-permute-start(bf16[32,4608]{1,0:T(8,128)(2,1)S(1)} %slice.197), channel_id=1, source_target_pairs={{8,0},{16,8},{24,16},{28,24},{20,28},{12,20},{4,12},{0,4},{9,1},{1... | collective-permute-start | bytes 884744 | tf_op jit(solution)/shard_map/ppermute | solution.py:211
  84.9 11.1 %collective-permute-start.22 = (bf16[32,4608]{1,0:T(8,128)(2,1)S(1)}, bf16[32,4608]{1,0:T(8,128)(2,1)S(1)}, u32[]{:S(2)}, u32[]{:S(2)}) collective-permute-start(bf16[32,4608]{1,0:T(8,128)(2,1)S(1)} %slice.226), channel_id=1, source_target_pairs={{0,8},{8,16},{16,24},{24,28},{28,20},{20,12},{12,4},{4,0},{1,9},{9... | collective-permute-start | bytes 884744 | tf_op jit(solution)/shard_map/ppermute | solution.py:211
  85.1 10.9 %collective-permute-start.23 = (bf16[32,4608]{1,0:T(8,128)(2,1)S(1)}, bf16[32,4608]{1,0:T(8,128)(2,1)S(1)}, u32[]{:S(2)}, u32[]{:S(2)}) collective-permute-start(bf16[32,4608]{1,0:T(8,128)(2,1)S(1)} %slice.227), channel_id=1, source_target_pairs={{8,0},{16,8},{24,16},{28,24},{20,28},{12,20},{4,12},{0,4},{9,1},{1... | collective-permute-start | bytes 884744 | tf_op jit(solution)/shard_map/ppermute | solution.py:211
  92.1 5.4 %collective-permute-start.21 = (f32[128,128]{1,0:T(8,128)S(1)}, f32[128,128]{1,0:T(8,128)S(1)}, u32[]{:S(2)}, u32[]{:S(2)}) collective-permute-start(f32[128,128]{1,0:T(8,128)S(1)} %pad_maximum_fusion), channel_id=1, source_target_pairs={{0,3},{1,2},{2,1},{3,0},{4,7},{5,6},{6,5},{7,4},{8,11},{9,10},{10,... | collective-permute-start | bytes 196616 | tf_op jit(solution)/shard_map/ppermute | solution.py:155
  92.1 5.8 %collective-permute-start.20 = (f32[128,128]{1,0:T(8,128)S(1)}, f32[128,128]{1,0:T(8,128)S(1)}, u32[]{:S(2)}, u32[]{:S(2)}) collective-permute-start(f32[128,128]{1,0:T(8,128)S(1)} %pad_maximum_fusion), channel_id=1, source_target_pairs={{0,2},{1,3},{2,0},{3,1},{4,6},{5,7},{6,4},{7,5},{8,10},{9,11},{10,... | collective-permute-start | bytes 196616 | tf_op jit(solution)/shard_map/ppermute | solution.py:155
  93.7 4.2 %collective-permute-start.19 = (f32[128,128]{1,0:T(8,128)S(1)}, f32[128,128]{1,0:T(8,128)S(1)}, u32[]{:S(2)}, u32[]{:S(2)}) collective-permute-start(f32[128,128]{1,0:T(8,128)S(1)} %pad_maximum_fusion), channel_id=1, source_target_pairs={{0,1},{1,0},{2,3},{3,2},{4,5},{5,4},{6,7},{7,6},{8,9},{9,8},{10,11... | collective-permute-start | bytes 196616 | tf_op jit(solution)/shard_map/ppermute | solution.py:155
  98.3 1.2 %collective-permute-start.24 = (f32[2,16]{1,0:T(2,128)S(1)}, f32[2,16]{1,0:T(2,128)S(1)}, u32[]{:S(2)}, u32[]{:S(2)}) collective-permute-start(f32[2,16]{1,0:T(2,128)S(1)} %score.1), channel_id=1, source_target_pairs={{0,1},{1,0},{2,3},{3,2},{4,5},{5,4},{6,7},{7,6},{8,9},{9,8},{10,11... | collective-permute-start | bytes 392 | tf_op jit(solution)/shard_map/ppermute | solution.py:155
  99.5 3.6 %collective-permute-start.25 = (f32[2,16]{1,0:T(2,128)S(1)}, f32[2,16]{1,0:T(2,128)S(1)}, u32[]{:S(2)}, u32[]{:S(2)}) collective-permute-start(f32[2,16]{1,0:T(2,128)S(1)} %add.222), channel_id=1, source_target_pairs={{0,2},{1,3},{2,0},{3,1},{4,6},{5,7},{6,4},{7,5},{8,10},{9,11},{10,... | collective-permute-start | bytes 392 | tf_op jit(solution)/shard_map/ppermute | solution.py:155

commit v13 on v11

--- a/solution.py
+++ b/solution.py
@@ -50,7 +50,7 @@
         kernel,
         out_shape=jax.ShapeDtypeStruct((per * R, total), jnp.bfloat16),
         in_specs=[pl.BlockSpec(memory_space=pltpu.SMEM)] + [in_hbm] * len(parts),
-        out_specs=pl.BlockSpec(memory_space=pltpu.VMEM),
+        out_specs=in_hbm,
         scratch_shapes=[pltpu.SemaphoreType.DMA((per, len(parts)))],
         compiler_params=params(52),
         name="pick_rows",

time: 103 us -> 103 us (level)
  no operation moved by 1% of the time
where the time goes in v13:
time: 103 us
  waiting for transfers between devices  41.8 us (41%)
  starting transfers between devices  24.8 us (24%)
  matrix products  16.5 us (16%)
  Pallas kernels  16.4 us (16%)
  other arithmetic  1.43 us (1%)
  local copies, waits for them, and re-layouts  1.38 us (1%)
    ppermute x8, waiting for transfers between devices, send(): lax.ppermute(ahead, 'dp', forward)  27.2 us
    dot_general x13, matrix products, contract_rows(): lax.dot_general(both, second, (((1,), (1,)), ((), ())), preferred_element...  16.5 us
    ppermute x8, starting transfers between devices, send(): lax.ppermute(behind, 'dp', backward)  14.1 us
    pallas_call x2, Pallas kernels, rotate(): pl.pallas_call(kernel, out_shape=jax.ShapeDtypeStruct((2 * rows, total),...  12.7 us
    ppermute x8, waiting for transfers between devices, send(): lax.ppermute(behind, 'dp', backward)  7.46 us
    ppermute x11, waiting for transfers between devices, swapped(): return lax.ppermute(piece, 'mp', [(i, i ^ distance) for i in range(shards)])  7.2 us
    ppermute x11, starting transfers between devices, swapped(): return lax.ppermute(piece, 'mp', [(i, i ^ distance) for i in range(shards)])  7.2 us
    ppermute x8, starting transfers between devices, send(): lax.ppermute(ahead, 'dp', forward)  3.44 us
  transfers between devices with their start and end apart: 27, of which 13 were waited for; matrix products, arithmetic and copies ran while one was open for 18% of the time, Pallas kernels for 14%

profile of v13, /device:TPU:0, one launch (start us, length us, event | category | flops | bytes accessed | tf_op | source)
XLA Modules:
  0.0 102.9 jit_solution(8968135864561166010)
XLA Ops:
  0.0 0.7 copy-done
  0.7 1.7 %pick_rows.2 = bf16[64,4608]{1,0:T(8,128)(2,1)S(1)} custom-call(s32[16]{0:T(128)S(1)} %copy-done, bf16[1,512,2048]{2,1,0:T(8,128)(2,1)} %refs_0_.2, bf16[1,512,7168]{2,1,0:T(8,128)(2,1)} %refs_0_.3), custom_call_target="tpu_custom_call" | custom-call | tf_op jit(solution)/shard_map/pick_rows/pallas_call | solution.py:49
  2.4 3.0 %collective-permute-start.1 = (bf16[64,4608]{1,0:T(8,128)(2,1)S(1)}, bf16[64,4608]{1,0:T(8,128)(2,1)S(1)}, u32[]{:S(2)}, u32[]{:S(2)}) collective-permute-start(bf16[64,4608]{1,0:T(8,128)(2,1)S(1)} %pick_rows.2), channel_id=1, source_target_pairs={{8,0},{16,8},{24,16},{28,24},{20,28},{12,20},{4,12},{0,4},{9,1},{1... | collective-permute-start | bytes 1769480 | tf_op jit(solution)/shard_map/ppermute | solution.py:211
  5.4 0.2 collective-permute-start
  5.6 3.3 %rotate.2 = bf16[512,2048]{1,0:T(8,128)(2,1)} custom-call(s32[1]{0:T(128)} %bitcast.shard_ref, bf16[256,8192]{1,0:T(8,128)(2,1)} %matrix_ref.2, bf16[4,512,512]{2,1,0:T(8,128)(2,1)} %basis_ref.2), custom_call_target="tpu_custom_call" | custom-call | flops 536870912 | bytes 5242880 | tf_op jit(solution)/shard_map/rotate/pallas_call | solution.py:77
  8.9 1.7 %pick_rows.3 = bf16[64,4608]{1,0:T(8,128)(2,1)S(1)} custom-call(s32[16]{0:T(128)S(1)} %copy-done.1, bf16[1,512,7168]{2,1,0:T(8,128)(2,1)} %refs_0_.3), custom_call_target="tpu_custom_call" | custom-call | tf_op jit(solution)/shard_map/pick_rows/pallas_call | solution.py:49
  10.6 1.9 %collective-permute-start.8 = (bf16[64,4608]{1,0:T(8,128)(2,1)S(1)}, bf16[64,4608]{1,0:T(8,128)(2,1)S(1)}, u32[]{:S(2)}, u32[]{:S(2)}) collective-permute-start(bf16[64,4608]{1,0:T(8,128)(2,1)S(1)} %pick_rows.3), channel_id=1, source_target_pairs={{8,0},{16,8},{24,16},{28,24},{20,28},{12,20},{4,12},{0,4},{9,1},{1... | collective-permute-start | bytes 1769480 | tf_op jit(solution)/shard_map/ppermute | solution.py:211
  12.5 0.2 collective-permute-start.7
  12.7 0.2 convert_reduce_fusion
  12.9 0.1 concatenate.54
  13.1 0.1 concatenate.53
  13.2 9.4 %rotate.3 = bf16[512,7168]{1,0:T(8,128)(2,1)} custom-call(s32[1]{0:T(128)} %constant.120.clone.1.shard_ref, bf16[256,7168]{1,0:T(8,128)(2,1)} %matrix_ref.3, bf16[28,256,256]{2,1,0:T(8,128)(2,1)} %basis_ref.3), custom_call_target="tpu_custom_call" | custom-call | flops 939524096 | bytes 14680064 | tf_op jit(solution)/shard_map/rotate/pallas_call | solution.py:77
  22.5 0.2 and_convert_fusion.hit_ref
  22.8 2.0 %collective-permute-start.2 = (bf16[64,4608]{1,0:T(8,128)(2,1)S(1)}, bf16[64,4608]{1,0:T(8,128)(2,1)S(1)}, u32[]{:S(2)}, u32[]{:S(2)}) collective-permute-start(bf16[64,4608]{1,0:T(8,128)(2,1)S(1)} %collective-permute-done), channel_id=1, source_target_pairs={{0,8},{8,16},{16,24},{24,28},{28,20},{20,12},{12,4},{4,0},{1,9},{9... | collective-permute-start | bytes 1769480 | tf_op jit(solution)/shard_map/ppermute | solution.py:211
  24.8 7.4 %collective-permute-done.8 = bf16[64,4608]{1,0:T(8,128)(2,1)S(1)} collective-permute-done((bf16[64,4608]{1,0:T(8,128)(2,1)S(1)}, bf16[64,4608]{1,0:T(8,128)(2,1)S(1)}, u32[]{:S(2)}, u32[]{:S(2)}) %collective-permute-start.8) | collective-permute-done | bytes 589856 | tf_op jit(solution)/shard_map/ppermute | solution.py:211
  32.3 2.1 %collective-permute-done.7 = bf16[64,4608]{1,0:T(8,128)(2,1)} collective-permute-done((bf16[64,4608]{1,0:T(8,128)(2,1)S(1)}, bf16[64,4608]{1,0:T(8,128)(2,1)}, u32[]{:S(2)}, u32[]{:S(2)}) %collective-permute-start.7) | collective-permute-done | bytes 589856 | tf_op jit(solution)/shard_map/ppermute | solution.py:211
  34.4 0.1 collective-permute-start.13
  34.5 1.9 %collective-permute-start.14 = (bf16[64,4608]{1,0:T(8,128)(2,1)S(1)}, bf16[64,4608]{1,0:T(8,128)(2,1)S(1)}, u32[]{:S(2)}, u32[]{:S(2)}) collective-permute-start(bf16[64,4608]{1,0:T(8,128)(2,1)S(1)} %collective-permute-done.8), channel_id=1, source_target_pairs={{8,0},{16,8},{24,16},{28,24},{20,28},{12,20},{4,12},{0,4},{9,1},{1... | collective-permute-start | bytes 1769480 | tf_op jit(solution)/shard_map/ppermute | solution.py:211
  36.5 2.6 %fusion.18 = f32[512,128]{1,0:T(8,128)S(1)} fusion(bf16[512,7168]{1,0:T(8,128)(2,1)} %rotate.3, bf16[128,4608]{1,0:T(8,128)(2,1)S(1)} %constant_dynamic-update-slice_fusion), kind=kOutput, calls=%fused_computation.18 | convolution fusion | flops 335544320 | bytes 3538944 | tf_op jit(solution)/shard_map/dot_general | solution.py:101
  39.1 1.4 %fusion.4 = f32[512,64]{1,0:T(8,128)S(1)} fusion(bf16[64,4608]{1,0:T(8,128)(2,1)S(1)} %pick_rows.3, bf16[512,7168]{1,0:T(8,128)(2,1)S(1)} %copy-done.2), kind=kOutput, calls=%fused_computation.4 | convolution fusion | flops 301989888 | bytes 5439488 | tf_op jit(solution)/shard_map/dot_general | solution.py:101
  40.5 2.4 %fusion.8 = f32[512,128]{1,0:T(8,128)S(1)} fusion(bf16[512,7168]{1,0:T(8,128)(2,1)S(1)} %copy-done.2, bf16[64,4608]{1,0:T(8,128)(2,1)S(1)} %collective-permute-done.8, bf16[64,4608]{1,0:T(8,128)(2,1)} %collective-permute-done.7), kind=kOutput, calls=%fused_computation.8 | convolution fusion | flops 606339072 | bytes 6160384 | tf_op jit(solution)/shard_map/dot_general | solution.py:101
  42.9 0.8 fusion.14
  43.9 3.0 %collective-permute-done.2 = bf16[64,4608]{1,0:T(8,128)(2,1)S(1)} collective-permute-done((bf16[64,4608]{1,0:T(8,128)(2,1)S(1)}, bf16[64,4608]{1,0:T(8,128)(2,1)S(1)}, u32[]{:S(2)}, u32[]{:S(2)}) %collective-permute-start.2) | collective-permute-done | bytes 589856 | tf_op jit(solution)/shard_map/ppermute | solution.py:211
  47.1 1.3 %fusion.20 = f32[512,320]{1,0:T(8,128)S(1)} fusion(bf16[512,2048]{1,0:T(8,128)(2,1)S(1)} %copy-done.3, bf16[64,2048]{1,0:T(8,128)(2,1)S(1)} %slice.147, bf16[128,2048]{1,0:T(8,128)(2,1)S(1)} %slice.190, bf16[128,2048]{1,0:T(8,128)(2,1)S(1)} %slice.189), kind=kOutput, calls=%fused_computation.20 | convolution fusion | flops 675020800 | bytes 4063232 | tf_op jit(solution)/shard_map/dot_general | solution.py:101
  48.5 0.1 collective-permute-start.4
  48.5 0.2 collective-permute-start.9
  48.7 1.9 %collective-permute-start.10 = (bf16[64,4608]{1,0:T(8,128)(2,1)S(1)}, bf16[64,4608]{1,0:T(8,128)(2,1)S(1)}, u32[]{:S(2)}, u32[]{:S(2)}) collective-permute-start(bf16[64,4608]{1,0:T(8,128)(2,1)S(1)} %collective-permute-done.3), channel_id=1, source_target_pairs={{8,0},{16,8},{24,16},{28,24},{20,28},{12,20},{4,12},{0,4},{9,1},{1... | collective-permute-start | bytes 1769480 | tf_op jit(solution)/shard_map/ppermute | solution.py:211
  50.6 9.0 %collective-permute-done.13 = bf16[64,4608]{1,0:T(8,128)(2,1)S(1)} collective-permute-done((bf16[64,4608]{1,0:T(8,128)(2,1)}, bf16[64,4608]{1,0:T(8,128)(2,1)S(1)}, u32[]{:S(2)}, u32[]{:S(2)}) %collective-permute-start.13) | collective-permute-done | bytes 589856 | tf_op jit(solution)/shard_map/ppermute | solution.py:211
  59.6 0.1 collective-permute-start.17
  59.7 1.9 %collective-permute-start.18 = (bf16[64,4608]{1,0:T(8,128)(2,1)S(1)}, bf16[64,4608]{1,0:T(8,128)(2,1)S(1)}, u32[]{:S(2)}, u32[]{:S(2)}) collective-permute-start(bf16[64,4608]{1,0:T(8,128)(2,1)S(1)} %collective-permute-done.14), channel_id=1, source_target_pairs={{8,0},{16,8},{24,16},{28,24},{20,28},{12,20},{4,12},{0,4},{9,1},{1... | collective-permute-start | bytes 1769480 | tf_op jit(solution)/shard_map/ppermute | solution.py:211
  61.6 1.4 %fusion.6 = f32[512,128]{1,0:T(8,128)S(1)} fusion(bf16[512,7168]{1,0:T(8,128)(2,1)S(1)} %copy-done.2, bf16[64,4608]{1,0:T(8,128)(2,1)S(1)} %collective-permute-done.14, bf16[64,4608]{1,0:T(8,128)(2,1)S(1)} %collective-permute-done.13), kind=kOutput, calls=%fused_computation.6 | convolution fusion | flops 606339072 | bytes 6160384 | tf_op jit(solution)/shard_map/dot_general | solution.py:101
  63.0 1.6 %collective-permute-start.5 = (f32[128,320]{1,0:T(8,128)S(1)}, f32[128,320]{1,0:T(8,128)S(1)}, u32[]{:S(2)}, u32[]{:S(2)}) collective-permute-start(f32[128,320]{1,0:T(8,128)S(1)} %dynamic-slice_add_fusion), channel_id=1, source_target_pairs={{0,2},{1,3},{2,0},{3,1},{4,6},{5,7},{6,4},{7,5},{8,10},{9,11},{10,... | collective-permute-start | bytes 491528 | tf_op jit(solution)/shard_map/ppermute | solution.py:155
  64.6 0.8 fusion.16
  65.5 3.3 %collective-permute-done.5 = f32[128,320]{1,0:T(8,128)S(1)} collective-permute-done((f32[128,320]{1,0:T(8,128)S(1)}, f32[128,320]{1,0:T(8,128)S(1)}, u32[]{:S(2)}, u32[]{:S(2)}) %collective-permute-start.5) | collective-permute-done | bytes 163872 | tf_op jit(solution)/shard_map/ppermute | solution.py:155
  68.8 0.1 collective-permute-start.6
  68.9 3.3 %collective-permute-done.9 = bf16[64,4608]{1,0:T(8,128)(2,1)S(1)} collective-permute-done((bf16[64,4608]{1,0:T(8,128)(2,1)S(1)}, bf16[64,4608]{1,0:T(8,128)(2,1)S(1)}, u32[]{:S(2)}, u32[]{:S(2)}) %collective-permute-start.9) | collective-permute-done | bytes 589856 | tf_op jit(solution)/shard_map/ppermute | solution.py:211
  72.3 0.7 fusion.41
  73.1 0.1 collective-permute-start.11
  73.2 1.2 %collective-permute-done.11 = f32[256,128]{1,0:T(8,128)S(1)} collective-permute-done((f32[256,128]{1,0:T(8,128)S(1)}, f32[256,128]{1,0:T(8,128)S(1)}, u32[]{:S(2)}, u32[]{:S(2)}) %collective-permute-start.11) | collective-permute-done | bytes 131104 | tf_op jit(solution)/shard_map/ppermute | solution.py:155
  74.5 1.6 %collective-permute-start.12 = (f32[256,128]{1,0:T(8,128)S(1)}, f32[256,128]{1,0:T(8,128)S(1)}, u32[]{:S(2)}, u32[]{:S(2)}) collective-permute-start(f32[256,128]{1,0:T(8,128)S(1)} %fusion.65), channel_id=1, source_target_pairs={{0,2},{1,3},{2,0},{3,1},{4,6},{5,7},{6,4},{7,5},{8,10},{9,11},{10,... | collective-permute-start | bytes 393224 | tf_op jit(solution)/shard_map/ppermute | solution.py:155
  76.1 0.9 fusion.12
  77.0 0.6 collective-permute-start.15
  77.6 1.5 %collective-permute-start.16 = (bf16[32,4608]{1,0:T(8,128)(2,1)S(1)}, bf16[32,4608]{1,0:T(8,128)(2,1)S(1)}, u32[]{:S(2)}, u32[]{:S(2)}) collective-permute-start(bf16[32,4608]{1,0:T(8,128)(2,1)S(1)} %slice.197), channel_id=1, source_target_pairs={{8,0},{16,8},{24,16},{28,24},{20,28},{12,20},{4,12},{0,4},{9,1},{1... | collective-permute-start | bytes 884744 | tf_op jit(solution)/shard_map/ppermute | solution.py:211
  79.1 5.8 %collective-permute-done.17 = bf16[64,4608]{1,0:T(8,128)(2,1)S(1)} collective-permute-done((bf16[64,4608]{1,0:T(8,128)(2,1)S(1)}, bf16[64,4608]{1,0:T(8,128)(2,1)S(1)}, u32[]{:S(2)}, u32[]{:S(2)}) %collective-permute-start.17) | collective-permute-done | bytes 589856 | tf_op jit(solution)/shard_map/ppermute | solution.py:211
  84.9 0.2 collective-permute-start.22
  85.1 1.9 %collective-permute-start.23 = (bf16[32,4608]{1,0:T(8,128)(2,1)S(1)}, bf16[32,4608]{1,0:T(8,128)(2,1)S(1)}, u32[]{:S(2)}, u32[]{:S(2)}) collective-permute-start(bf16[32,4608]{1,0:T(8,128)(2,1)S(1)} %slice.227), channel_id=1, source_target_pairs={{8,0},{16,8},{24,16},{28,24},{20,28},{12,20},{4,12},{0,4},{9,1},{1... | collective-permute-start | bytes 884744 | tf_op jit(solution)/shard_map/ppermute | solution.py:211
  87.0 1.4 %fusion.2 = f32[512,128]{1,0:T(8,128)S(1)} fusion(bf16[512,7168]{1,0:T(8,128)(2,1)S(1)} %copy-done.2, bf16[64,4608]{1,0:T(8,128)(2,1)S(1)} %collective-permute-done.18, bf16[64,4608]{1,0:T(8,128)(2,1)S(1)} %collective-permute-done.17), kind=kOutput, calls=%fused_computation.2 | convolution fusion | flops 606339072 | bytes 6160384 | tf_op jit(solution)/shard_map/dot_general | solution.py:101
  88.4 2.7 %collective-permute-done.15 = bf16[32,4608]{1,0:T(8,128)(2,1)S(1)} collective-permute-done((bf16[32,4608]{1,0:T(8,128)(2,1)S(1)}, bf16[32,4608]{1,0:T(8,128)(2,1)S(1)}, u32[]{:S(2)}, u32[]{:S(2)}) %collective-permute-start.15) | collective-permute-done | bytes 294944 | tf_op jit(solution)/shard_map/ppermute | solution.py:211
  91.2 0.7 fusion.45
  92.0 0.1 pad_maximum_fusion
  92.1 0.1 collective-permute-start.21
  92.1 1.6 %collective-permute-start.20 = (f32[128,128]{1,0:T(8,128)S(1)}, f32[128,128]{1,0:T(8,128)S(1)}, u32[]{:S(2)}, u32[]{:S(2)}) collective-permute-start(f32[128,128]{1,0:T(8,128)S(1)} %pad_maximum_fusion), channel_id=1, source_target_pairs={{0,2},{1,3},{2,0},{3,1},{4,6},{5,7},{6,4},{7,5},{8,10},{9,11},{10,... | collective-permute-start | bytes 196616 | tf_op jit(solution)/shard_map/ppermute | solution.py:155
  93.7 0.3 collective-permute-start.19
  94.0 0.8 fusion.10
  94.8 1.2 %collective-permute-done.22 = bf16[32,4608]{1,0:T(8,128)(2,1)S(1)} collective-permute-done((bf16[32,4608]{1,0:T(8,128)(2,1)S(1)}, bf16[32,4608]{1,0:T(8,128)(2,1)S(1)}, u32[]{:S(2)}, u32[]{:S(2)}) %collective-permute-start.22) | collective-permute-done | bytes 294944 | tf_op jit(solution)/shard_map/ppermute | solution.py:211
  96.0 1.4 %fusion = f32[512,64]{1,0:T(8,128)S(1)} fusion(bf16[512,7168]{1,0:T(8,128)(2,1)S(1)} %copy-done.2, bf16[32,4608]{1,0:T(8,128)(2,1)S(1)} %collective-permute-done.23, bf16[32,4608]{1,0:T(8,128)(2,1)S(1)} %collective-permute-done.22), kind=kOutput, calls=%fused_computation | convolution fusion | flops 303169536 | bytes 5439488 | tf_op jit(solution)/shard_map/dot_general | solution.py:101
  97.4 0.5 collective-permute-done.20
  97.9 0.3 score.1
  98.3 0.5 collective-permute-start.26
  98.8 1.2 %collective-permute-start.25 = (f32[2,16]{1,0:T(2,128)S(1)}, f32[2,16]{1,0:T(2,128)S(1)}, u32[]{:S(2)}, u32[]{:S(2)}) collective-permute-start(f32[2,16]{1,0:T(2,128)S(1)} %score.1), channel_id=1, source_target_pairs={{0,2},{1,3},{2,0},{3,1},{4,6},{5,7},{6,4},{7,5},{8,10},{9,11},{10,... | collective-permute-start | bytes 392 | tf_op jit(solution)/shard_map/ppermute | solution.py:155
  100.0 0.2 collective-permute-start.24
  100.2 1.1 %collective-permute-done.26 = f32[2,16]{1,0:T(2,128)S(1)} collective-permute-done((f32[2,16]{1,0:T(2,128)S(1)}, f32[2,16]{1,0:T(2,128)S(1)}, u32[]{:S(2)}, u32[]{:S(2)}) %collective-permute-start.26) | collective-permute-done | bytes 160 | tf_op jit(solution)/shard_map/ppermute | solution.py:155
  101.3 1.0 collective-permute-done.25
  102.3 0.6 add_add_fusion.1
  (65 shorter events, 1.1 us)
Async XLA Ops:
  0.0 0.7 copy-start
  2.4 20.3 %collective-permute-start.1 = (bf16[64,4608]{1,0:T(8,128)(2,1)S(1)}, bf16[64,4608]{1,0:T(8,128)(2,1)S(1)}, u32[]{:S(2)}, u32[]{:S(2)}) collective-permute-start(bf16[64,4608]{1,0:T(8,128)(2,1)S(1)} %pick_rows.2), channel_id=1, source_target_pairs={{8,0},{16,8},{24,16},{28,24},{20,28},{12,20},{4,12},{0,4},{9,1},{1... | collective-permute-start | bytes 1769480 | tf_op jit(solution)/shard_map/ppermute | solution.py:211
  5.4 17.4 %collective-permute-start = (bf16[64,4608]{1,0:T(8,128)(2,1)S(1)}, bf16[64,4608]{1,0:T(8,128)(2,1)S(1)}, u32[]{:S(2)}, u32[]{:S(2)}) collective-permute-start(bf16[64,4608]{1,0:T(8,128)(2,1)S(1)} %pick_rows.2), channel_id=1, source_target_pairs={{0,8},{8,16},{16,24},{24,28},{28,20},{20,12},{12,4},{4,0},{1,9},{9... | collective-permute-start | bytes 1769480 | tf_op jit(solution)/shard_map/ppermute | solution.py:211
  5.6 3.4 %copy-start.1 = (s32[16]{0:T(128)S(1)}, s32[16]{0:T(128)}, u32[]{:S(2)}) copy-start(s32[16]{0:T(128)} %owners_ref.2) | copy-start | bytes 196
  10.6 21.7 %collective-permute-start.8 = (bf16[64,4608]{1,0:T(8,128)(2,1)S(1)}, bf16[64,4608]{1,0:T(8,128)(2,1)S(1)}, u32[]{:S(2)}, u32[]{:S(2)}) collective-permute-start(bf16[64,4608]{1,0:T(8,128)(2,1)S(1)} %pick_rows.3), channel_id=1, source_target_pairs={{8,0},{16,8},{24,16},{28,24},{20,28},{12,20},{4,12},{0,4},{9,1},{1... | collective-permute-start | bytes 1769480 | tf_op jit(solution)/shard_map/ppermute | solution.py:211
  12.5 21.9 %collective-permute-start.7 = (bf16[64,4608]{1,0:T(8,128)(2,1)S(1)}, bf16[64,4608]{1,0:T(8,128)(2,1)}, u32[]{:S(2)}, u32[]{:S(2)}) collective-permute-start(bf16[64,4608]{1,0:T(8,128)(2,1)S(1)} %pick_rows.3), channel_id=1, source_target_pairs={{0,8},{8,16},{16,24},{24,28},{28,20},{20,12},{12,4},{4,0},{1,9},{9... | collective-permute-start | bytes 1769480 | tf_op jit(solution)/shard_map/ppermute | solution.py:211
  22.5 16.6 %copy-start.2 = (bf16[512,7168]{1,0:T(8,128)(2,1)S(1)}, bf16[512,7168]{1,0:T(8,128)(2,1)}, u32[]{:S(2)}) copy-start(bf16[512,7168]{1,0:T(8,128)(2,1)} %rotate.3) | copy-start | bytes 22020100
  22.8 24.2 %collective-permute-start.2 = (bf16[64,4608]{1,0:T(8,128)(2,1)S(1)}, bf16[64,4608]{1,0:T(8,128)(2,1)S(1)}, u32[]{:S(2)}, u32[]{:S(2)}) collective-permute-start(bf16[64,4608]{1,0:T(8,128)(2,1)S(1)} %collective-permute-done), channel_id=1, source_target_pairs={{0,8},{8,16},{16,24},{24,28},{28,20},{20,12},{12,4},{4,0},{1,9},{9... | collective-permute-start | bytes 1769480 | tf_op jit(solution)/shard_map/ppermute | solution.py:211
  24.8 22.2 %collective-permute-start.3 = (bf16[64,4608]{1,0:T(8,128)(2,1)S(1)}, bf16[64,4608]{1,0:T(8,128)(2,1)S(1)}, u32[]{:S(2)}, u32[]{:S(2)}) collective-permute-start(bf16[64,4608]{1,0:T(8,128)(2,1)S(1)} %collective-permute-done.1), channel_id=1, source_target_pairs={{8,0},{16,8},{24,16},{28,24},{20,28},{12,20},{4,12},{0,4},{9,1},{1... | collective-permute-start | bytes 1769480 | tf_op jit(solution)/shard_map/ppermute | solution.py:211
  34.4 25.2 %collective-permute-start.13 = (bf16[64,4608]{1,0:T(8,128)(2,1)}, bf16[64,4608]{1,0:T(8,128)(2,1)S(1)}, u32[]{:S(2)}, u32[]{:S(2)}) collective-permute-start(bf16[64,4608]{1,0:T(8,128)(2,1)} %collective-permute-done.7), channel_id=1, source_target_pairs={{0,8},{8,16},{16,24},{24,28},{28,20},{20,12},{12,4},{4,0},{1,9},{9... | collective-permute-start | bytes 1769480 | tf_op jit(solution)/shard_map/ppermute | solution.py:211
  34.5 25.1 %collective-permute-start.14 = (bf16[64,4608]{1,0:T(8,128)(2,1)S(1)}, bf16[64,4608]{1,0:T(8,128)(2,1)S(1)}, u32[]{:S(2)}, u32[]{:S(2)}) collective-permute-start(bf16[64,4608]{1,0:T(8,128)(2,1)S(1)} %collective-permute-done.8), channel_id=1, source_target_pairs={{8,0},{16,8},{24,16},{28,24},{20,28},{12,20},{4,12},{0,4},{9,1},{1... | collective-permute-start | bytes 1769480 | tf_op jit(solution)/shard_map/ppermute | solution.py:211
  43.8 3.3 %copy-start.3 = (bf16[512,2048]{1,0:T(8,128)(2,1)S(1)}, bf16[512,2048]{1,0:T(8,128)(2,1)}, u32[]{:S(2)}) copy-start(bf16[512,2048]{1,0:T(8,128)(2,1)} %rotate.2) | copy-start | bytes 6291460
  48.5 14.5 %collective-permute-start.4 = (f32[128,320]{1,0:T(8,128)S(1)}, f32[128,320]{1,0:T(8,128)S(1)}, u32[]{:S(2)}, u32[]{:S(2)}) collective-permute-start(f32[128,320]{1,0:T(8,128)S(1)} %constant_dynamic-slice_fusion), channel_id=1, source_target_pairs={{0,1},{1,0},{2,3},{3,2},{4,5},{5,4},{6,7},{7,6},{8,9},{9,8},{10,11... | collective-permute-start | bytes 491528 | tf_op jit(solution)/shard_map/ppermute | solution.py:155
  48.5 23.7 %collective-permute-start.9 = (bf16[64,4608]{1,0:T(8,128)(2,1)S(1)}, bf16[64,4608]{1,0:T(8,128)(2,1)S(1)}, u32[]{:S(2)}, u32[]{:S(2)}) collective-permute-start(bf16[64,4608]{1,0:T(8,128)(2,1)S(1)} %collective-permute-done.2), channel_id=1, source_target_pairs={{0,8},{8,16},{16,24},{24,28},{28,20},{20,12},{12,4},{4,0},{1,9},{9... | collective-permute-start | bytes 1769480 | tf_op jit(solution)/shard_map/ppermute | solution.py:211
  48.7 23.6 %collective-permute-start.10 = (bf16[64,4608]{1,0:T(8,128)(2,1)S(1)}, bf16[64,4608]{1,0:T(8,128)(2,1)S(1)}, u32[]{:S(2)}, u32[]{:S(2)}) collective-permute-start(bf16[64,4608]{1,0:T(8,128)(2,1)S(1)} %collective-permute-done.3), channel_id=1, source_target_pairs={{8,0},{16,8},{24,16},{28,24},{20,28},{12,20},{4,12},{0,4},{9,1},{1... | collective-permute-start | bytes 1769480 | tf_op jit(solution)/shard_map/ppermute | solution.py:211
  59.6 25.3 %collective-permute-start.17 = (bf16[64,4608]{1,0:T(8,128)(2,1)S(1)}, bf16[64,4608]{1,0:T(8,128)(2,1)S(1)}, u32[]{:S(2)}, u32[]{:S(2)}) collective-permute-start(bf16[64,4608]{1,0:T(8,128)(2,1)S(1)} %collective-permute-done.13), channel_id=1, source_target_pairs={{0,8},{8,16},{16,24},{24,28},{28,20},{20,12},{12,4},{4,0},{1,9},{9... | collective-permute-start | bytes 1769480 | tf_op jit(solution)/shard_map/ppermute | solution.py:211
  59.7 25.2 %collective-permute-start.18 = (bf16[64,4608]{1,0:T(8,128)(2,1)S(1)}, bf16[64,4608]{1,0:T(8,128)(2,1)S(1)}, u32[]{:S(2)}, u32[]{:S(2)}) collective-permute-start(bf16[64,4608]{1,0:T(8,128)(2,1)S(1)} %collective-permute-done.14), channel_id=1, source_target_pairs={{8,0},{16,8},{24,16},{28,24},{20,28},{12,20},{4,12},{0,4},{9,1},{1... | collective-permute-start | bytes 1769480 | tf_op jit(solution)/shard_map/ppermute | solution.py:211
  63.0 5.7 %collective-permute-start.5 = (f32[128,320]{1,0:T(8,128)S(1)}, f32[128,320]{1,0:T(8,128)S(1)}, u32[]{:S(2)}, u32[]{:S(2)}) collective-permute-start(f32[128,320]{1,0:T(8,128)S(1)} %dynamic-slice_add_fusion), channel_id=1, source_target_pairs={{0,2},{1,3},{2,0},{3,1},{4,6},{5,7},{6,4},{7,5},{8,10},{9,11},{10,... | collective-permute-start | bytes 491528 | tf_op jit(solution)/shard_map/ppermute | solution.py:155
  68.8 4.4 %collective-permute-start.6 = (f32[128,320]{1,0:T(8,128)S(1)}, f32[128,320]{1,0:T(8,128)S(1)}, u32[]{:S(2)}, u32[]{:S(2)}) collective-permute-start(f32[128,320]{1,0:T(8,128)S(1)} %add.202), channel_id=1, source_target_pairs={{0,1},{1,0},{2,3},{3,2},{4,5},{5,4},{6,7},{7,6},{8,9},{9,8},{10,11... | collective-permute-start | bytes 491528 | tf_op jit(solution)/shard_map/ppermute | solution.py:155
  73.1 1.4 %collective-permute-start.11 = (f32[256,128]{1,0:T(8,128)S(1)}, f32[256,128]{1,0:T(8,128)S(1)}, u32[]{:S(2)}, u32[]{:S(2)}) collective-permute-start(f32[256,128]{1,0:T(8,128)S(1)} %slice_add_fusion.12), channel_id=1, source_target_pairs={{0,1},{1,0},{2,3},{3,2},{4,5},{5,4},{6,7},{7,6},{8,9},{9,8},{10,11... | collective-permute-start | bytes 393224 | tf_op jit(solution)/shard_map/ppermute | solution.py:155
  74.5 12.5 %collective-permute-start.12 = (f32[256,128]{1,0:T(8,128)S(1)}, f32[256,128]{1,0:T(8,128)S(1)}, u32[]{:S(2)}, u32[]{:S(2)}) collective-permute-start(f32[256,128]{1,0:T(8,128)S(1)} %fusion.65), channel_id=1, source_target_pairs={{0,2},{1,3},{2,0},{3,1},{4,6},{5,7},{6,4},{7,5},{8,10},{9,11},{10,... | collective-permute-start | bytes 393224 | tf_op jit(solution)/shard_map/ppermute | solution.py:155
  77.0 14.2 %collective-permute-start.15 = (bf16[32,4608]{1,0:T(8,128)(2,1)S(1)}, bf16[32,4608]{1,0:T(8,128)(2,1)S(1)}, u32[]{:S(2)}, u32[]{:S(2)}) collective-permute-start(bf16[32,4608]{1,0:T(8,128)(2,1)S(1)} %slice.196), channel_id=1, source_target_pairs={{0,8},{8,16},{16,24},{24,28},{28,20},{20,12},{12,4},{4,0},{1,9},{9... | collective-permute-start | bytes 884744 | tf_op jit(solution)/shard_map/ppermute | solution.py:211
  77.6 13.6 %collective-permute-start.16 = (bf16[32,4608]{1,0:T(8,128)(2,1)S(1)}, bf16[32,4608]{1,0:T(8,128)(2,1)S(1)}, u32[]{:S(2)}, u32[]{:S(2)}) collective-permute-start(bf16[32,4608]{1,0:T(8,128)(2,1)S(1)} %slice.197), channel_id=1, source_target_pairs={{8,0},{16,8},{24,16},{28,24},{20,28},{12,20},{4,12},{0,4},{9,1},{1... | collective-permute-start | bytes 884744 | tf_op jit(solution)/shard_map/ppermute | solution.py:211
  84.9 11.1 %collective-permute-start.22 = (bf16[32,4608]{1,0:T(8,128)(2,1)S(1)}, bf16[32,4608]{1,0:T(8,128)(2,1)S(1)}, u32[]{:S(2)}, u32[]{:S(2)}) collective-permute-start(bf16[32,4608]{1,0:T(8,128)(2,1)S(1)} %slice.226), channel_id=1, source_target_pairs={{0,8},{8,16},{16,24},{24,28},{28,20},{20,12},{12,4},{4,0},{1,9},{9... | collective-permute-start | bytes 884744 | tf_op jit(solution)/shard_map/ppermute | solution.py:211
  85.1 10.9 %collective-permute-start.23 = (bf16[32,4608]{1,0:T(8,128)(2,1)S(1)}, bf16[32,4608]{1,0:T(8,128)(2,1)S(1)}, u32[]{:S(2)}, u32[]{:S(2)}) collective-permute-start(bf16[32,4608]{1,0:T(8,128)(2,1)S(1)} %slice.227), channel_id=1, source_target_pairs={{8,0},{16,8},{24,16},{28,24},{20,28},{12,20},{4,12},{0,4},{9,1},{1... | collective-permute-start | bytes 884744 | tf_op jit(solution)/shard_map/ppermute | solution.py:211
  92.1 5.4 %collective-permute-start.21 = (f32[128,128]{1,0:T(8,128)S(1)}, f32[128,128]{1,0:T(8,128)S(1)}, u32[]{:S(2)}, u32[]{:S(2)}) collective-permute-start(f32[128,128]{1,0:T(8,128)S(1)} %pad_maximum_fusion), channel_id=1, source_target_pairs={{0,3},{1,2},{2,1},{3,0},{4,7},{5,6},{6,5},{7,4},{8,11},{9,10},{10,... | collective-permute-start | bytes 196616 | tf_op jit(solution)/shard_map/ppermute | solution.py:155
  92.1 5.8 %collective-permute-start.20 = (f32[128,128]{1,0:T(8,128)S(1)}, f32[128,128]{1,0:T(8,128)S(1)}, u32[]{:S(2)}, u32[]{:S(2)}) collective-permute-start(f32[128,128]{1,0:T(8,128)S(1)} %pad_maximum_fusion), channel_id=1, source_target_pairs={{0,2},{1,3},{2,0},{3,1},{4,6},{5,7},{6,4},{7,5},{8,10},{9,11},{10,... | collective-permute-start | bytes 196616 | tf_op jit(solution)/shard_map/ppermute | solution.py:155
  93.7 4.2 %collective-permute-start.19 = (f32[128,128]{1,0:T(8,128)S(1)}, f32[128,128]{1,0:T(8,128)S(1)}, u32[]{:S(2)}, u32[]{:S(2)}) collective-permute-start(f32[128,128]{1,0:T(8,128)S(1)} %pad_maximum_fusion), channel_id=1, source_target_pairs={{0,1},{1,0},{2,3},{3,2},{4,5},{5,4},{6,7},{7,6},{8,9},{9,8},{10,11... | collective-permute-start | bytes 196616 | tf_op jit(solution)/shard_map/ppermute | solution.py:155
  98.3 3.0 %collective-permute-start.26 = (f32[2,16]{1,0:T(2,128)S(1)}, f32[2,16]{1,0:T(2,128)S(1)}, u32[]{:S(2)}, u32[]{:S(2)}) collective-permute-start(f32[2,16]{1,0:T(2,128)S(1)} %score.1), channel_id=1, source_target_pairs={{0,3},{1,2},{2,1},{3,0},{4,7},{5,6},{6,5},{7,4},{8,11},{9,10},{10,... | collective-permute-start | bytes 392 | tf_op jit(solution)/shard_map/ppermute | solution.py:155
  98.8 3.6 %collective-permute-start.25 = (f32[2,16]{1,0:T(2,128)S(1)}, f32[2,16]{1,0:T(2,128)S(1)}, u32[]{:S(2)}, u32[]{:S(2)}) collective-permute-start(f32[2,16]{1,0:T(2,128)S(1)} %score.1), channel_id=1, source_target_pairs={{0,2},{1,3},{2,0},{3,1},{4,6},{5,7},{6,4},{7,5},{8,10},{9,11},{10,... | collective-permute-start | bytes 392 | tf_op jit(solution)/shard_map/ppermute | solution.py:155
  100.0 2.3 %collective-permute-start.24 = (f32[2,16]{1,0:T(2,128)S(1)}, f32[2,16]{1,0:T(2,128)S(1)}, u32[]{:S(2)}, u32[]{:S(2)}) collective-permute-start(f32[2,16]{1,0:T(2,128)S(1)} %score.1), channel_id=1, source_target_pairs={{0,1},{1,0},{2,3},{3,2},{4,5},{5,4},{6,7},{7,6},{8,9},{9,8},{10,11... | collective-permute-start | bytes 392 | tf_op jit(solution)/shard_map/ppermute | solution.py:155

commit v14 on v11

--- a/solution.py
+++ b/solution.py
@@ -155,11 +155,12 @@
     return lax.ppermute(piece, "mp", [(i, i ^ distance) for i in range(shards)])
 
 
-def small_sum(array, shards, most, distance=1):
+def small_sum(array, shards, most, distance=1, others=None):
     while distance < shards:
         reach = min(most, shards // distance)
-        array = sum([swapped(array, distance * k, shards) for k in range(1, reach)], array)
+        copies = [swapped(array, distance * k, shards) for k in range(1, reach)]
         distance *= reach
+        array = sum(copies if distance < shards else after(copies, others), array)
     return array
 
 
@@ -193,7 +194,7 @@
 
     width_left = left_store.shape[2]
     width_right = right_store.shape[2]
-    cut = max(width_right * 5 // 14 // 128 * 128, 128)
+    cut = max(width_right * 9 // 28 // 128 * 128, 128)
     own = [pick_rows(groups, owners, [(left_store, 0, width_left), (right_store, 0, cut)])]
     grads = rotate(out_grads, out_basis, shard)
     own.append(
@@ -237,15 +238,15 @@
     last = side_by_side(last)
     part = contract_rows(grads, last[:, :width_left]).reshape(-1, LEN, chunk)
     part = jnp.concatenate([part[i] for i in range(part.shape[0])], axis=1)
-    last_sum = small_sum(part, shards, 4)
     first.append(after(last, part))
     second.append(side_by_side(steps[1][-1]))
-    coefficients.append(last_sum)
 
     projected = [
         contract_rows(acts[:, :cut], one[:, width_left:]) + contract_rows(acts[:, cut:], other)
         for one, other in zip(first, second)
     ]
+
+    coefficients.append(small_sum(part, shards, 4, others=projected[-1]))
 
     def position(index):
         return jnp.where(index % 2 == 0, index // 2, groups - 1 - index // 2)

time: 103 us -> 103 us (level)
  waiting for transfers between devices: 41.8 us -> 38.8 us
  matrix products: 16.5 us -> 19.1 us
    ppermute x8, waiting for transfers between devices: 7.46 us -> 0.02 us  [send(): lax.ppermute(behind, 'dp', backward)]
    ppermute x8, waiting for transfers between devices: 27.2 us -> 32.6 us  [send(): lax.ppermute(ahead, 'dp', forward)]
    dot_general x13, matrix products: 16.5 us -> 19.1 us  [contract_rows(): lax.dot_general(both, second, (((1,), (1,)), ((), ())), preferred_element...]
    ppermute x11, waiting for transfers between devices: 7.2 us -> 6.15 us  [swapped(): return lax.ppermute(piece, 'mp', [(i, i ^ distance) for i in range(shards)])]
  transfers between devices with their start and end apart: 27 -> 27, of which waited for: 13 -> 11; matrix products, arithmetic and copies ran while one was open for 18% -> 20% of each run, Pallas kernels for 14% -> 14%
where the time goes in v14:
time: 103 us
  waiting for transfers between devices  38.8 us (38%)
  starting transfers between devices  24.8 us (24%)
  matrix products  19.1 us (19%)
  Pallas kernels  16.5 us (16%)
  other arithmetic  1.44 us (1%)
  local copies, waits for them, and re-layouts  1.37 us (1%)
    ppermute x8, waiting for transfers between devices, send(): lax.ppermute(ahead, 'dp', forward)  32.6 us
    dot_general x13, matrix products, contract_rows(): lax.dot_general(both, second, (((1,), (1,)), ((), ())), preferred_element...  19.1 us
    ppermute x8, starting transfers between devices, send(): lax.ppermute(behind, 'dp', backward)  14.1 us
    pallas_call x2, Pallas kernels, rotate(): pl.pallas_call(kernel, out_shape=jax.ShapeDtypeStruct((2 * rows, total),...  12.8 us
    ppermute x11, starting transfers between devices, swapped(): return lax.ppermute(piece, 'mp', [(i, i ^ distance) for i in range(shards)])  7.2 us
    ppermute x11, waiting for transfers between devices, swapped(): return lax.ppermute(piece, 'mp', [(i, i ^ distance) for i in range(shards)])  6.15 us
    ppermute x8, starting transfers between devices, send(): lax.ppermute(ahead, 'dp', forward)  3.47 us
    pallas_call x2, Pallas kernels, pick_rows(): pl.pallas_call(kernel, out_shape=jax.ShapeDtypeStruct((per * R, total), j...  3.4 us
  transfers between devices with their start and end apart: 27, of which 11 were waited for; matrix products, arithmetic and copies ran while one was open for 20% of the time, Pallas kernels for 14%

profile of v14, /device:TPU:0, one launch (start us, length us, event | category | flops | bytes accessed | tf_op | source)
XLA Modules:
  0.0 102.5 jit_solution(15868851606867676745)
XLA Ops:
  0.0 0.7 copy-done
  0.7 1.7 %pick_rows.2 = bf16[64,4352]{1,0:T(8,128)(2,1)S(1)} custom-call(s32[16]{0:T(128)S(1)} %copy-done, bf16[1,512,2048]{2,1,0:T(8,128)(2,1)} %refs_0_.2, bf16[1,512,7168]{2,1,0:T(8,128)(2,1)} %refs_0_.3), custom_call_target="tpu_custom_call" | custom-call | tf_op jit(solution)/shard_map/pick_rows/pallas_call | solution.py:49
  2.4 3.0 %collective-permute-start.1 = (bf16[64,4352]{1,0:T(8,128)(2,1)S(1)}, bf16[64,4352]{1,0:T(8,128)(2,1)S(1)}, u32[]{:S(2)}, u32[]{:S(2)}) collective-permute-start(bf16[64,4352]{1,0:T(8,128)(2,1)S(1)} %pick_rows.2), channel_id=1, source_target_pairs={{8,0},{16,8},{24,16},{28,24},{20,28},{12,20},{4,12},{0,4},{9,1},{1... | collective-permute-start | bytes 1671176 | tf_op jit(solution)/shard_map/ppermute | solution.py:212
  5.4 0.2 collective-permute-start
  5.5 3.4 %rotate.2 = bf16[512,2048]{1,0:T(8,128)(2,1)} custom-call(s32[1]{0:T(128)} %bitcast.shard_ref, bf16[256,8192]{1,0:T(8,128)(2,1)} %matrix_ref.2, bf16[4,512,512]{2,1,0:T(8,128)(2,1)} %basis_ref.2), custom_call_target="tpu_custom_call" | custom-call | flops 536870912 | bytes 5242880 | tf_op jit(solution)/shard_map/rotate/pallas_call | solution.py:77
  8.9 1.7 %pick_rows.3 = bf16[64,4864]{1,0:T(8,128)(2,1)S(1)} custom-call(s32[16]{0:T(128)S(1)} %copy-done.1, bf16[1,512,7168]{2,1,0:T(8,128)(2,1)} %refs_0_.3), custom_call_target="tpu_custom_call" | custom-call | tf_op jit(solution)/shard_map/pick_rows/pallas_call | solution.py:49
  10.6 1.9 %collective-permute-start.8 = (bf16[64,4864]{1,0:T(8,128)(2,1)S(1)}, bf16[64,4864]{1,0:T(8,128)(2,1)S(1)}, u32[]{:S(2)}, u32[]{:S(2)}) collective-permute-start(bf16[64,4864]{1,0:T(8,128)(2,1)S(1)} %pick_rows.3), channel_id=1, source_target_pairs={{8,0},{16,8},{24,16},{28,24},{20,28},{12,20},{4,12},{0,4},{9,1},{1... | collective-permute-start | bytes 1867784 | tf_op jit(solution)/shard_map/ppermute | solution.py:212
  12.5 0.2 collective-permute-start.7
  12.7 0.2 convert_reduce_fusion
  12.9 0.1 concatenate.54
  13.1 0.1 concatenate.53
  13.2 9.4 %rotate.3 = bf16[512,7168]{1,0:T(8,128)(2,1)} custom-call(s32[1]{0:T(128)} %constant.120.clone.1.shard_ref, bf16[256,7168]{1,0:T(8,128)(2,1)} %matrix_ref.3, bf16[28,256,256]{2,1,0:T(8,128)(2,1)} %basis_ref.3), custom_call_target="tpu_custom_call" | custom-call | flops 939524096 | bytes 14680064 | tf_op jit(solution)/shard_map/rotate/pallas_call | solution.py:77
  22.6 0.2 and_convert_fusion.hit_ref
  22.8 2.0 %collective-permute-start.2 = (bf16[64,4352]{1,0:T(8,128)(2,1)S(1)}, bf16[64,4352]{1,0:T(8,128)(2,1)S(1)}, u32[]{:S(2)}, u32[]{:S(2)}) collective-permute-start(bf16[64,4352]{1,0:T(8,128)(2,1)S(1)} %collective-permute-done), channel_id=1, source_target_pairs={{0,8},{8,16},{16,24},{24,28},{28,20},{20,12},{12,4},{4,0},{1,9},{9... | collective-permute-start | bytes 1671176 | tf_op jit(solution)/shard_map/ppermute | solution.py:212
  24.8 0.1 collective-permute-start.3
  24.9 2.6 %fusion.27 = f32[512,64]{1,0:T(8,128)S(1)} fusion(bf16[512,7168]{1,0:T(8,128)(2,1)} %rotate.3, bf16[64,4352]{1,0:T(8,128)(2,1)S(1)} %pick_rows.2), kind=kOutput, calls=%fused_computation.27 | convolution fusion | flops 150994944 | bytes 2785280 | tf_op jit(solution)/shard_map/dot_general | solution.py:101
  27.6 4.0 %fusion.2 = f32[512,64]{1,0:T(8,128)S(1)} fusion(bf16[64,4864]{1,0:T(8,128)(2,1)S(1)} %pick_rows.3, bf16[512,7168]{1,0:T(8,128)(2,1)} %rotate.3), kind=kOutput, calls=%fused_computation.2 | convolution fusion | flops 318767104 | bytes 5734400 | tf_op jit(solution)/shard_map/dot_general | solution.py:101
  31.7 0.8 fusion.31
  32.5 1.9 %collective-permute-done.7 = bf16[64,4864]{1,0:T(8,128)(2,1)} collective-permute-done((bf16[64,4864]{1,0:T(8,128)(2,1)S(1)}, bf16[64,4864]{1,0:T(8,128)(2,1)}, u32[]{:S(2)}, u32[]{:S(2)}) %collective-permute-start.7) | collective-permute-done | bytes 622624 | tf_op jit(solution)/shard_map/ppermute | solution.py:212
  34.4 0.1 collective-permute-start.13
  34.5 1.9 %collective-permute-start.14 = (bf16[64,4864]{1,0:T(8,128)(2,1)S(1)}, bf16[64,4864]{1,0:T(8,128)(2,1)S(1)}, u32[]{:S(2)}, u32[]{:S(2)}) collective-permute-start(bf16[64,4864]{1,0:T(8,128)(2,1)S(1)} %collective-permute-done.8), channel_id=1, source_target_pairs={{8,0},{16,8},{24,16},{28,24},{20,28},{12,20},{4,12},{0,4},{9,1},{1... | collective-permute-start | bytes 1867784 | tf_op jit(solution)/shard_map/ppermute | solution.py:212
  36.4 2.5 %fusion.6 = f32[512,128]{1,0:T(8,128)S(1)} fusion(bf16[512,7168]{1,0:T(8,128)(2,1)S(1)} %bitcast.6, bf16[64,4864]{1,0:T(8,128)(2,1)S(1)} %collective-permute-done.8, bf16[64,4864]{1,0:T(8,128)(2,1)} %collective-permute-done.7), kind=kOutput, calls=%fused_computation.6 | convolution fusion | flops 640024576 | bytes 6488064 | tf_op jit(solution)/shard_map/dot_general | solution.py:101
  39.0 7.2 %collective-permute-done.2 = bf16[64,4352]{1,0:T(8,128)(2,1)S(1)} collective-permute-done((bf16[64,4352]{1,0:T(8,128)(2,1)S(1)}, bf16[64,4352]{1,0:T(8,128)(2,1)S(1)}, u32[]{:S(2)}, u32[]{:S(2)}) %collective-permute-start.2) | collective-permute-done | bytes 557088 | tf_op jit(solution)/shard_map/ppermute | solution.py:212
  46.4 1.3 %fusion.10 = f32[512,320]{1,0:T(8,128)S(1)} fusion(bf16[512,2048]{1,0:T(8,128)(2,1)S(1)} %copy-done.2, bf16[64,2048]{1,0:T(8,128)(2,1)S(1)} %slice.147, bf16[128,2048]{1,0:T(8,128)(2,1)S(1)} %slice.190, bf16[128,2048]{1,0:T(8,128)(2,1)S(1)} %slice.189), kind=kOutput, calls=%fused_computation.10 | convolution fusion | flops 675020800 | bytes 4063232 | tf_op jit(solution)/shard_map/dot_general | solution.py:101
  47.7 0.1 collective-permute-start.4
  47.8 0.2 collective-permute-start.9
  48.0 1.9 %collective-permute-start.10 = (bf16[64,4352]{1,0:T(8,128)(2,1)S(1)}, bf16[64,4352]{1,0:T(8,128)(2,1)S(1)}, u32[]{:S(2)}, u32[]{:S(2)}) collective-permute-start(bf16[64,4352]{1,0:T(8,128)(2,1)S(1)} %collective-permute-done.3), channel_id=1, source_target_pairs={{8,0},{16,8},{24,16},{28,24},{20,28},{12,20},{4,12},{0,4},{9,1},{1... | collective-permute-start | bytes 1671176 | tf_op jit(solution)/shard_map/ppermute | solution.py:212
  49.9 0.8 fusion.29
  50.7 8.9 %collective-permute-done.13 = bf16[64,4864]{1,0:T(8,128)(2,1)S(1)} collective-permute-done((bf16[64,4864]{1,0:T(8,128)(2,1)}, bf16[64,4864]{1,0:T(8,128)(2,1)S(1)}, u32[]{:S(2)}, u32[]{:S(2)}) %collective-permute-start.13) | collective-permute-done | bytes 622624 | tf_op jit(solution)/shard_map/ppermute | solution.py:212
  59.6 0.1 collective-permute-start.17
  59.7 1.9 %collective-permute-start.18 = (bf16[64,4864]{1,0:T(8,128)(2,1)S(1)}, bf16[64,4864]{1,0:T(8,128)(2,1)S(1)}, u32[]{:S(2)}, u32[]{:S(2)}) collective-permute-start(bf16[64,4864]{1,0:T(8,128)(2,1)S(1)} %collective-permute-done.14), channel_id=1, source_target_pairs={{8,0},{16,8},{24,16},{28,24},{20,28},{12,20},{4,12},{0,4},{9,1},{1... | collective-permute-start | bytes 1867784 | tf_op jit(solution)/shard_map/ppermute | solution.py:212
  61.6 1.6 %collective-permute-start.5 = (f32[128,320]{1,0:T(8,128)S(1)}, f32[128,320]{1,0:T(8,128)S(1)}, u32[]{:S(2)}, u32[]{:S(2)}) collective-permute-start(f32[128,320]{1,0:T(8,128)S(1)} %dynamic-slice_add_fusion), channel_id=1, source_target_pairs={{0,2},{1,3},{2,0},{3,1},{4,6},{5,7},{6,4},{7,5},{8,10},{9,11},{10,... | collective-permute-start | bytes 491528 | tf_op jit(solution)/shard_map/ppermute | solution.py:155
  63.2 1.4 %fusion.4 = f32[512,128]{1,0:T(8,128)S(1)} fusion(bf16[512,7168]{1,0:T(8,128)(2,1)S(1)} %bitcast.6, bf16[64,4864]{1,0:T(8,128)(2,1)S(1)} %collective-permute-done.14, bf16[64,4864]{1,0:T(8,128)(2,1)S(1)} %collective-permute-done.13), kind=kOutput, calls=%fused_computation.4 | convolution fusion | flops 640024576 | bytes 6488064 | tf_op jit(solution)/shard_map/dot_general | solution.py:101
  64.7 2.7 %collective-permute-done.5 = f32[128,320]{1,0:T(8,128)S(1)} collective-permute-done((f32[128,320]{1,0:T(8,128)S(1)}, f32[128,320]{1,0:T(8,128)S(1)}, u32[]{:S(2)}, u32[]{:S(2)}) %collective-permute-start.5) | collective-permute-done | bytes 163872 | tf_op jit(solution)/shard_map/ppermute | solution.py:155
  67.4 0.1 collective-permute-start.6
  67.5 4.0 %collective-permute-done.9 = bf16[64,4352]{1,0:T(8,128)(2,1)S(1)} collective-permute-done((bf16[64,4352]{1,0:T(8,128)(2,1)S(1)}, bf16[64,4352]{1,0:T(8,128)(2,1)S(1)}, u32[]{:S(2)}, u32[]{:S(2)}) %collective-permute-start.9) | collective-permute-done | bytes 557088 | tf_op jit(solution)/shard_map/ppermute | solution.py:212
  71.6 0.7 fusion.41
  72.3 0.1 collective-permute-start.11
  72.5 1.2 %collective-permute-done.11 = f32[256,128]{1,0:T(8,128)S(1)} collective-permute-done((f32[256,128]{1,0:T(8,128)S(1)}, f32[256,128]{1,0:T(8,128)S(1)}, u32[]{:S(2)}, u32[]{:S(2)}) %collective-permute-start.11) | collective-permute-done | bytes 131104 | tf_op jit(solution)/shard_map/ppermute | solution.py:155
  73.8 1.6 %collective-permute-start.12 = (f32[256,128]{1,0:T(8,128)S(1)}, f32[256,128]{1,0:T(8,128)S(1)}, u32[]{:S(2)}, u32[]{:S(2)}) collective-permute-start(f32[256,128]{1,0:T(8,128)S(1)} %fusion.65), channel_id=1, source_target_pairs={{0,2},{1,3},{2,0},{3,1},{4,6},{5,7},{6,4},{7,5},{8,10},{9,11},{10,... | collective-permute-start | bytes 393224 | tf_op jit(solution)/shard_map/ppermute | solution.py:155
  75.4 0.8 fusion.25
  76.2 0.6 collective-permute-start.15
  76.8 1.5 %collective-permute-start.16 = (bf16[32,4352]{1,0:T(8,128)(2,1)S(1)}, bf16[32,4352]{1,0:T(8,128)(2,1)S(1)}, u32[]{:S(2)}, u32[]{:S(2)}) collective-permute-start(bf16[32,4352]{1,0:T(8,128)(2,1)S(1)} %slice.197), channel_id=1, source_target_pairs={{8,0},{16,8},{24,16},{28,24},{20,28},{12,20},{4,12},{0,4},{9,1},{1... | collective-permute-start | bytes 835592 | tf_op jit(solution)/shard_map/ppermute | solution.py:212
  78.3 6.6 %collective-permute-done.17 = bf16[64,4864]{1,0:T(8,128)(2,1)S(1)} collective-permute-done((bf16[64,4864]{1,0:T(8,128)(2,1)S(1)}, bf16[64,4864]{1,0:T(8,128)(2,1)S(1)}, u32[]{:S(2)}, u32[]{:S(2)}) %collective-permute-start.17) | collective-permute-done | bytes 622624 | tf_op jit(solution)/shard_map/ppermute | solution.py:212
  84.9 0.2 collective-permute-start.22
  85.1 1.9 %collective-permute-start.23 = (bf16[32,4864]{1,0:T(8,128)(2,1)S(1)}, bf16[32,4864]{1,0:T(8,128)(2,1)S(1)}, u32[]{:S(2)}, u32[]{:S(2)}) collective-permute-start(bf16[32,4864]{1,0:T(8,128)(2,1)S(1)} %slice.208), channel_id=1, source_target_pairs={{8,0},{16,8},{24,16},{28,24},{20,28},{12,20},{4,12},{0,4},{9,1},{1... | collective-permute-start | bytes 933896 | tf_op jit(solution)/shard_map/ppermute | solution.py:212
  87.0 1.4 %fusion = f32[512,128]{1,0:T(8,128)S(1)} fusion(bf16[512,7168]{1,0:T(8,128)(2,1)S(1)} %bitcast.6, bf16[64,4864]{1,0:T(8,128)(2,1)S(1)} %collective-permute-done.18, bf16[64,4864]{1,0:T(8,128)(2,1)S(1)} %collective-permute-done.17), kind=kOutput, calls=%fused_computation | convolution fusion | flops 640024576 | bytes 6488064 | tf_op jit(solution)/shard_map/dot_general | solution.py:101
  88.5 2.3 %collective-permute-done.15 = bf16[32,4352]{1,0:T(8,128)(2,1)S(1)} collective-permute-done((bf16[32,4352]{1,0:T(8,128)(2,1)S(1)}, bf16[32,4352]{1,0:T(8,128)(2,1)S(1)}, u32[]{:S(2)}, u32[]{:S(2)}) %collective-permute-start.15) | collective-permute-done | bytes 278560 | tf_op jit(solution)/shard_map/ppermute | solution.py:212
  90.9 0.7 fusion.45
  91.6 0.1 pad_maximum_fusion
  91.7 0.1 collective-permute-start.21
  91.8 1.6 %collective-permute-start.20 = (f32[128,128]{1,0:T(8,128)S(1)}, f32[128,128]{1,0:T(8,128)S(1)}, u32[]{:S(2)}, u32[]{:S(2)}) collective-permute-start(f32[128,128]{1,0:T(8,128)S(1)} %pad_maximum_fusion), channel_id=1, source_target_pairs={{0,2},{1,3},{2,0},{3,1},{4,6},{5,7},{6,4},{7,5},{8,10},{9,11},{10,... | collective-permute-start | bytes 196616 | tf_op jit(solution)/shard_map/ppermute | solution.py:155
  93.4 0.3 collective-permute-start.19
  93.6 0.8 fusion.33
  94.4 1.6 %collective-permute-done.22 = bf16[32,4864]{1,0:T(8,128)(2,1)S(1)} collective-permute-done((bf16[32,4864]{1,0:T(8,128)(2,1)S(1)}, bf16[32,4864]{1,0:T(8,128)(2,1)S(1)}, u32[]{:S(2)}, u32[]{:S(2)}) %collective-permute-start.22) | collective-permute-done | bytes 311328 | tf_op jit(solution)/shard_map/ppermute | solution.py:212
  96.0 1.4 %fusion.8 = f32[512,64]{1,0:T(8,128)S(1)} fusion(bf16[512,7168]{1,0:T(8,128)(2,1)S(1)} %bitcast.6, bf16[32,4864]{1,0:T(8,128)(2,1)S(1)} %collective-permute-done.23, bf16[32,4864]{1,0:T(8,128)(2,1)S(1)} %collective-permute-done.22), kind=kOutput, calls=%fused_computation.8 | convolution fusion | flops 320012288 | bytes 5734400 | tf_op jit(solution)/shard_map/dot_general | solution.py:101
  97.5 0.1 collective-permute-done.20
  97.6 0.3 score.1
  97.9 0.5 collective-permute-start.26
  98.4 1.2 %collective-permute-start.25 = (f32[2,16]{1,0:T(2,128)S(1)}, f32[2,16]{1,0:T(2,128)S(1)}, u32[]{:S(2)}, u32[]{:S(2)}) collective-permute-start(f32[2,16]{1,0:T(2,128)S(1)} %score.1), channel_id=1, source_target_pairs={{0,2},{1,3},{2,0},{3,1},{4,6},{5,7},{6,4},{7,5},{8,10},{9,11},{10,... | collective-permute-start | bytes 392 | tf_op jit(solution)/shard_map/ppermute | solution.py:155
  99.6 0.2 collective-permute-start.24
  99.8 1.1 %collective-permute-done.26 = f32[2,16]{1,0:T(2,128)S(1)} collective-permute-done((f32[2,16]{1,0:T(2,128)S(1)}, f32[2,16]{1,0:T(2,128)S(1)}, u32[]{:S(2)}, u32[]{:S(2)}) %collective-permute-start.26) | collective-permute-done | bytes 160 | tf_op jit(solution)/shard_map/ppermute | solution.py:155
  101.0 1.0 collective-permute-done.25
  102.0 0.6 add_add_fusion.1
  (68 shorter events, 1.0 us)
Async XLA Ops:
  0.0 0.7 copy-start
  2.4 20.4 %collective-permute-start.1 = (bf16[64,4352]{1,0:T(8,128)(2,1)S(1)}, bf16[64,4352]{1,0:T(8,128)(2,1)S(1)}, u32[]{:S(2)}, u32[]{:S(2)}) collective-permute-start(bf16[64,4352]{1,0:T(8,128)(2,1)S(1)} %pick_rows.2), channel_id=1, source_target_pairs={{8,0},{16,8},{24,16},{28,24},{20,28},{12,20},{4,12},{0,4},{9,1},{1... | collective-permute-start | bytes 1671176 | tf_op jit(solution)/shard_map/ppermute | solution.py:212
  5.4 17.4 %collective-permute-start = (bf16[64,4352]{1,0:T(8,128)(2,1)S(1)}, bf16[64,4352]{1,0:T(8,128)(2,1)S(1)}, u32[]{:S(2)}, u32[]{:S(2)}) collective-permute-start(bf16[64,4352]{1,0:T(8,128)(2,1)S(1)} %pick_rows.2), channel_id=1, source_target_pairs={{0,8},{8,16},{16,24},{24,28},{28,20},{20,12},{12,4},{4,0},{1,9},{9... | collective-permute-start | bytes 1671176 | tf_op jit(solution)/shard_map/ppermute | solution.py:212
  5.5 3.4 %copy-start.1 = (s32[16]{0:T(128)S(1)}, s32[16]{0:T(128)}, u32[]{:S(2)}) copy-start(s32[16]{0:T(128)} %owners_ref.2) | copy-start | bytes 196
  10.6 21.9 %collective-permute-start.8 = (bf16[64,4864]{1,0:T(8,128)(2,1)S(1)}, bf16[64,4864]{1,0:T(8,128)(2,1)S(1)}, u32[]{:S(2)}, u32[]{:S(2)}) collective-permute-start(bf16[64,4864]{1,0:T(8,128)(2,1)S(1)} %pick_rows.3), channel_id=1, source_target_pairs={{8,0},{16,8},{24,16},{28,24},{20,28},{12,20},{4,12},{0,4},{9,1},{1... | collective-permute-start | bytes 1867784 | tf_op jit(solution)/shard_map/ppermute | solution.py:212
  12.5 21.9 %collective-permute-start.7 = (bf16[64,4864]{1,0:T(8,128)(2,1)S(1)}, bf16[64,4864]{1,0:T(8,128)(2,1)}, u32[]{:S(2)}, u32[]{:S(2)}) collective-permute-start(bf16[64,4864]{1,0:T(8,128)(2,1)S(1)} %pick_rows.3), channel_id=1, source_target_pairs={{0,8},{8,16},{16,24},{24,28},{28,20},{20,12},{12,4},{4,0},{1,9},{9... | collective-permute-start | bytes 1867784 | tf_op jit(solution)/shard_map/ppermute | solution.py:212
  22.8 23.4 %collective-permute-start.2 = (bf16[64,4352]{1,0:T(8,128)(2,1)S(1)}, bf16[64,4352]{1,0:T(8,128)(2,1)S(1)}, u32[]{:S(2)}, u32[]{:S(2)}) collective-permute-start(bf16[64,4352]{1,0:T(8,128)(2,1)S(1)} %collective-permute-done), channel_id=1, source_target_pairs={{0,8},{8,16},{16,24},{24,28},{28,20},{20,12},{12,4},{4,0},{1,9},{9... | collective-permute-start | bytes 1671176 | tf_op jit(solution)/shard_map/ppermute | solution.py:212
  24.8 21.4 %collective-permute-start.3 = (bf16[64,4352]{1,0:T(8,128)(2,1)S(1)}, bf16[64,4352]{1,0:T(8,128)(2,1)S(1)}, u32[]{:S(2)}, u32[]{:S(2)}) collective-permute-start(bf16[64,4352]{1,0:T(8,128)(2,1)S(1)} %collective-permute-done.1), channel_id=1, source_target_pairs={{8,0},{16,8},{24,16},{28,24},{20,28},{12,20},{4,12},{0,4},{9,1},{1... | collective-permute-start | bytes 1671176 | tf_op jit(solution)/shard_map/ppermute | solution.py:212
  24.9 6.8 %slice-start = ((s8[7340032]{0:T(1024)(128)(4,1)}), s8[4194304]{0:T(1024)(128)(4,1)S(1)}, s32[]{:S(2)}) async-start(s8[7340032]{0:T(1024)(128)(4,1)} %bitcast.5), calls=%async_computation | async-start | bytes 8388608
  27.6 4.1 %slice-start.1 = ((s8[7340032]{0:T(1024)(128)(4,1)}), s8[3145728]{0:T(1024)(128)(4,1)S(1)}, s32[]{:S(2)}) async-start(s8[7340032]{0:T(1024)(128)(4,1)} %bitcast.5), calls=%async_computation.1 | async-start | bytes 6291456
  34.4 25.2 %collective-permute-start.13 = (bf16[64,4864]{1,0:T(8,128)(2,1)}, bf16[64,4864]{1,0:T(8,128)(2,1)S(1)}, u32[]{:S(2)}, u32[]{:S(2)}) collective-permute-start(bf16[64,4864]{1,0:T(8,128)(2,1)} %collective-permute-done.7), channel_id=1, source_target_pairs={{0,8},{8,16},{16,24},{24,28},{28,20},{20,12},{12,4},{4,0},{1,9},{9... | collective-permute-start | bytes 1867784 | tf_op jit(solution)/shard_map/ppermute | solution.py:212
  34.5 25.1 %collective-permute-start.14 = (bf16[64,4864]{1,0:T(8,128)(2,1)S(1)}, bf16[64,4864]{1,0:T(8,128)(2,1)S(1)}, u32[]{:S(2)}, u32[]{:S(2)}) collective-permute-start(bf16[64,4864]{1,0:T(8,128)(2,1)S(1)} %collective-permute-done.8), channel_id=1, source_target_pairs={{8,0},{16,8},{24,16},{28,24},{20,28},{12,20},{4,12},{0,4},{9,1},{1... | collective-permute-start | bytes 1867784 | tf_op jit(solution)/shard_map/ppermute | solution.py:212
  38.9 7.4 %copy-start.2 = (bf16[512,2048]{1,0:T(8,128)(2,1)S(1)}, bf16[512,2048]{1,0:T(8,128)(2,1)}, u32[]{:S(2)}) copy-start(bf16[512,2048]{1,0:T(8,128)(2,1)} %rotate.2) | copy-start | bytes 6291460
  47.7 13.9 %collective-permute-start.4 = (f32[128,320]{1,0:T(8,128)S(1)}, f32[128,320]{1,0:T(8,128)S(1)}, u32[]{:S(2)}, u32[]{:S(2)}) collective-permute-start(f32[128,320]{1,0:T(8,128)S(1)} %constant_dynamic-slice_fusion), channel_id=1, source_target_pairs={{0,1},{1,0},{2,3},{3,2},{4,5},{5,4},{6,7},{7,6},{8,9},{9,8},{10,11... | collective-permute-start | bytes 491528 | tf_op jit(solution)/shard_map/ppermute | solution.py:155
  47.8 23.7 %collective-permute-start.9 = (bf16[64,4352]{1,0:T(8,128)(2,1)S(1)}, bf16[64,4352]{1,0:T(8,128)(2,1)S(1)}, u32[]{:S(2)}, u32[]{:S(2)}) collective-permute-start(bf16[64,4352]{1,0:T(8,128)(2,1)S(1)} %collective-permute-done.2), channel_id=1, source_target_pairs={{0,8},{8,16},{16,24},{24,28},{28,20},{20,12},{12,4},{4,0},{1,9},{9... | collective-permute-start | bytes 1671176 | tf_op jit(solution)/shard_map/ppermute | solution.py:212
  48.0 23.6 %collective-permute-start.10 = (bf16[64,4352]{1,0:T(8,128)(2,1)S(1)}, bf16[64,4352]{1,0:T(8,128)(2,1)S(1)}, u32[]{:S(2)}, u32[]{:S(2)}) collective-permute-start(bf16[64,4352]{1,0:T(8,128)(2,1)S(1)} %collective-permute-done.3), channel_id=1, source_target_pairs={{8,0},{16,8},{24,16},{28,24},{20,28},{12,20},{4,12},{0,4},{9,1},{1... | collective-permute-start | bytes 1671176 | tf_op jit(solution)/shard_map/ppermute | solution.py:212
  59.6 25.3 %collective-permute-start.17 = (bf16[64,4864]{1,0:T(8,128)(2,1)S(1)}, bf16[64,4864]{1,0:T(8,128)(2,1)S(1)}, u32[]{:S(2)}, u32[]{:S(2)}) collective-permute-start(bf16[64,4864]{1,0:T(8,128)(2,1)S(1)} %collective-permute-done.13), channel_id=1, source_target_pairs={{0,8},{8,16},{16,24},{24,28},{28,20},{20,12},{12,4},{4,0},{1,9},{9... | collective-permute-start | bytes 1867784 | tf_op jit(solution)/shard_map/ppermute | solution.py:212
  59.7 25.2 %collective-permute-start.18 = (bf16[64,4864]{1,0:T(8,128)(2,1)S(1)}, bf16[64,4864]{1,0:T(8,128)(2,1)S(1)}, u32[]{:S(2)}, u32[]{:S(2)}) collective-permute-start(bf16[64,4864]{1,0:T(8,128)(2,1)S(1)} %collective-permute-done.14), channel_id=1, source_target_pairs={{8,0},{16,8},{24,16},{28,24},{20,28},{12,20},{4,12},{0,4},{9,1},{1... | collective-permute-start | bytes 1867784 | tf_op jit(solution)/shard_map/ppermute | solution.py:212
  61.6 5.7 %collective-permute-start.5 = (f32[128,320]{1,0:T(8,128)S(1)}, f32[128,320]{1,0:T(8,128)S(1)}, u32[]{:S(2)}, u32[]{:S(2)}) collective-permute-start(f32[128,320]{1,0:T(8,128)S(1)} %dynamic-slice_add_fusion), channel_id=1, source_target_pairs={{0,2},{1,3},{2,0},{3,1},{4,6},{5,7},{6,4},{7,5},{8,10},{9,11},{10,... | collective-permute-start | bytes 491528 | tf_op jit(solution)/shard_map/ppermute | solution.py:155
  67.4 5.1 %collective-permute-start.6 = (f32[128,320]{1,0:T(8,128)S(1)}, f32[128,320]{1,0:T(8,128)S(1)}, u32[]{:S(2)}, u32[]{:S(2)}) collective-permute-start(f32[128,320]{1,0:T(8,128)S(1)} %add.202), channel_id=1, source_target_pairs={{0,1},{1,0},{2,3},{3,2},{4,5},{5,4},{6,7},{7,6},{8,9},{9,8},{10,11... | collective-permute-start | bytes 491528 | tf_op jit(solution)/shard_map/ppermute | solution.py:155
  72.3 1.4 %collective-permute-start.11 = (f32[256,128]{1,0:T(8,128)S(1)}, f32[256,128]{1,0:T(8,128)S(1)}, u32[]{:S(2)}, u32[]{:S(2)}) collective-permute-start(f32[256,128]{1,0:T(8,128)S(1)} %slice_add_fusion.12), channel_id=1, source_target_pairs={{0,1},{1,0},{2,3},{3,2},{4,5},{5,4},{6,7},{7,6},{8,9},{9,8},{10,11... | collective-permute-start | bytes 393224 | tf_op jit(solution)/shard_map/ppermute | solution.py:155
  73.8 13.2 %collective-permute-start.12 = (f32[256,128]{1,0:T(8,128)S(1)}, f32[256,128]{1,0:T(8,128)S(1)}, u32[]{:S(2)}, u32[]{:S(2)}) collective-permute-start(f32[256,128]{1,0:T(8,128)S(1)} %fusion.65), channel_id=1, source_target_pairs={{0,2},{1,3},{2,0},{3,1},{4,6},{5,7},{6,4},{7,5},{8,10},{9,11},{10,... | collective-permute-start | bytes 393224 | tf_op jit(solution)/shard_map/ppermute | solution.py:155
  76.2 14.6 %collective-permute-start.15 = (bf16[32,4352]{1,0:T(8,128)(2,1)S(1)}, bf16[32,4352]{1,0:T(8,128)(2,1)S(1)}, u32[]{:S(2)}, u32[]{:S(2)}) collective-permute-start(bf16[32,4352]{1,0:T(8,128)(2,1)S(1)} %slice.196), channel_id=1, source_target_pairs={{0,8},{8,16},{16,24},{24,28},{28,20},{20,12},{12,4},{4,0},{1,9},{9... | collective-permute-start | bytes 835592 | tf_op jit(solution)/shard_map/ppermute | solution.py:212
  76.8 14.0 %collective-permute-start.16 = (bf16[32,4352]{1,0:T(8,128)(2,1)S(1)}, bf16[32,4352]{1,0:T(8,128)(2,1)S(1)}, u32[]{:S(2)}, u32[]{:S(2)}) collective-permute-start(bf16[32,4352]{1,0:T(8,128)(2,1)S(1)} %slice.197), channel_id=1, source_target_pairs={{8,0},{16,8},{24,16},{28,24},{20,28},{12,20},{4,12},{0,4},{9,1},{1... | collective-permute-start | bytes 835592 | tf_op jit(solution)/shard_map/ppermute | solution.py:212
  84.9 11.1 %collective-permute-start.22 = (bf16[32,4864]{1,0:T(8,128)(2,1)S(1)}, bf16[32,4864]{1,0:T(8,128)(2,1)S(1)}, u32[]{:S(2)}, u32[]{:S(2)}) collective-permute-start(bf16[32,4864]{1,0:T(8,128)(2,1)S(1)} %slice.207), channel_id=1, source_target_pairs={{0,8},{8,16},{16,24},{24,28},{28,20},{20,12},{12,4},{4,0},{1,9},{9... | collective-permute-start | bytes 933896 | tf_op jit(solution)/shard_map/ppermute | solution.py:212
  85.1 10.9 %collective-permute-start.23 = (bf16[32,4864]{1,0:T(8,128)(2,1)S(1)}, bf16[32,4864]{1,0:T(8,128)(2,1)S(1)}, u32[]{:S(2)}, u32[]{:S(2)}) collective-permute-start(bf16[32,4864]{1,0:T(8,128)(2,1)S(1)} %slice.208), channel_id=1, source_target_pairs={{8,0},{16,8},{24,16},{28,24},{20,28},{12,20},{4,12},{0,4},{9,1},{1... | collective-permute-start | bytes 933896 | tf_op jit(solution)/shard_map/ppermute | solution.py:212
  91.7 5.8 %collective-permute-start.21 = (f32[128,128]{1,0:T(8,128)S(1)}, f32[128,128]{1,0:T(8,128)S(1)}, u32[]{:S(2)}, u32[]{:S(2)}) collective-permute-start(f32[128,128]{1,0:T(8,128)S(1)} %pad_maximum_fusion), channel_id=1, source_target_pairs={{0,3},{1,2},{2,1},{3,0},{4,7},{5,6},{6,5},{7,4},{8,11},{9,10},{10,... | collective-permute-start | bytes 196616 | tf_op jit(solution)/shard_map/ppermute | solution.py:155
  91.8 5.8 %collective-permute-start.20 = (f32[128,128]{1,0:T(8,128)S(1)}, f32[128,128]{1,0:T(8,128)S(1)}, u32[]{:S(2)}, u32[]{:S(2)}) collective-permute-start(f32[128,128]{1,0:T(8,128)S(1)} %pad_maximum_fusion), channel_id=1, source_target_pairs={{0,2},{1,3},{2,0},{3,1},{4,6},{5,7},{6,4},{7,5},{8,10},{9,11},{10,... | collective-permute-start | bytes 196616 | tf_op jit(solution)/shard_map/ppermute | solution.py:155
  93.4 4.2 %collective-permute-start.19 = (f32[128,128]{1,0:T(8,128)S(1)}, f32[128,128]{1,0:T(8,128)S(1)}, u32[]{:S(2)}, u32[]{:S(2)}) collective-permute-start(f32[128,128]{1,0:T(8,128)S(1)} %pad_maximum_fusion), channel_id=1, source_target_pairs={{0,1},{1,0},{2,3},{3,2},{4,5},{5,4},{6,7},{7,6},{8,9},{9,8},{10,11... | collective-permute-start | bytes 196616 | tf_op jit(solution)/shard_map/ppermute | solution.py:155
  97.9 3.0 %collective-permute-start.26 = (f32[2,16]{1,0:T(2,128)S(1)}, f32[2,16]{1,0:T(2,128)S(1)}, u32[]{:S(2)}, u32[]{:S(2)}) collective-permute-start(f32[2,16]{1,0:T(2,128)S(1)} %score.1), channel_id=1, source_target_pairs={{0,3},{1,2},{2,1},{3,0},{4,7},{5,6},{6,5},{7,4},{8,11},{9,10},{10,... | collective-permute-start | bytes 392 | tf_op jit(solution)/shard_map/ppermute | solution.py:155
  98.4 3.6 %collective-permute-start.25 = (f32[2,16]{1,0:T(2,128)S(1)}, f32[2,16]{1,0:T(2,128)S(1)}, u32[]{:S(2)}, u32[]{:S(2)}) collective-permute-start(f32[2,16]{1,0:T(2,128)S(1)} %score.1), channel_id=1, source_target_pairs={{0,2},{1,3},{2,0},{3,1},{4,6},{5,7},{6,4},{7,5},{8,10},{9,11},{10,... | collective-permute-start | bytes 392 | tf_op jit(solution)/shard_map/ppermute | solution.py:155
  99.6 2.3 %collective-permute-start.24 = (f32[2,16]{1,0:T(2,128)S(1)}, f32[2,16]{1,0:T(2,128)S(1)}, u32[]{:S(2)}, u32[]{:S(2)}) collective-permute-start(f32[2,16]{1,0:T(2,128)S(1)} %score.1), channel_id=1, source_target_pairs={{0,1},{1,0},{2,3},{3,2},{4,5},{5,4},{6,7},{7,6},{8,9},{9,8},{10,11... | collective-permute-start | bytes 392 | tf_op jit(solution)/shard_map/ppermute | solution.py:155

commit v15 on v14

--- a/solution.py
+++ b/solution.py
@@ -52,7 +52,7 @@
         in_specs=[pl.BlockSpec(memory_space=pltpu.SMEM)] + [in_hbm] * len(parts),
         out_specs=pl.BlockSpec(memory_space=pltpu.VMEM),
         scratch_shapes=[pltpu.SemaphoreType.DMA((per, len(parts)))],
-        compiler_params=params(52),
+        compiler_params=pltpu.CompilerParams(vmem_limit_bytes=54 * 2**20),
         name="pick_rows",
     )(owners, *[store for store, _, _ in parts])
 

time: 103 us -> 103 us (level)
  Pallas kernels: 16.5 us -> 18.5 us
    pallas_call x2, Pallas kernels: 3.4 us -> 5.42 us  [pick_rows(): pl.pallas_call(kernel, out_shape=jax.ShapeDtypeStruct((per * R, total), j...]
    dot_general x13, matrix products: 19.1 us -> 18.1 us  [contract_rows(): lax.dot_general(both, second, (((1,), (1,)), ((), ())), preferred_element...]
  transfers between devices with their start and end apart: 27 -> 27, of which waited for: 11 -> 11; matrix products, arithmetic and copies ran while one was open for 20% -> 19% of each run, Pallas kernels for 14% -> 15%
where the time goes in v15:
time: 103 us
  waiting for transfers between devices  38.9 us (38%)
  starting transfers between devices  24.8 us (24%)
  Pallas kernels  18.5 us (18%)
  matrix products  18.1 us (18%)
  other arithmetic  1.45 us (1%)
    ppermute x8, waiting for transfers between devices, send(): lax.ppermute(ahead, 'dp', forward)  32.8 us
    dot_general x13, matrix products, contract_rows(): lax.dot_general(both, second, (((1,), (1,)), ((), ())), preferred_element...  18.1 us
    ppermute x8, starting transfers between devices, send(): lax.ppermute(behind, 'dp', backward)  13.1 us
    pallas_call x2, Pallas kernels, rotate(): pl.pallas_call(kernel, out_shape=jax.ShapeDtypeStruct((2 * rows, total),...  12.8 us
    ppermute x11, starting transfers between devices, swapped(): return lax.ppermute(piece, 'mp', [(i, i ^ distance) for i in range(shards)])  7.2 us
    ppermute x11, waiting for transfers between devices, swapped(): return lax.ppermute(piece, 'mp', [(i, i ^ distance) for i in range(shards)])  6.15 us
    pallas_call x2, Pallas kernels, pick_rows(): pl.pallas_call(kernel, out_shape=jax.ShapeDtypeStruct((per * R, total), j...  5.42 us
    ppermute x8, starting transfers between devices, send(): lax.ppermute(ahead, 'dp', forward)  4.45 us
  transfers between devices with their start and end apart: 27, of which 11 were waited for; matrix products, arithmetic and copies ran while one was open for 19% of the time, Pallas kernels for 15%

profile of v15, /device:TPU:0, one launch (start us, length us, event | category | flops | bytes accessed | tf_op | source)
XLA Modules:
  0.0 103.0 jit_solution(3358279165266709083)
XLA Ops:
  0.0 2.7 %pick_rows.2 = bf16[64,4352]{1,0:T(8,128)(2,1)} custom-call(s32[16]{0:T(128)} %owners_ref.2, bf16[1,512,2048]{2,1,0:T(8,128)(2,1)} %refs_0_.2, bf16[1,512,7168]{2,1,0:T(8,128)(2,1)} %refs_0_.3), custom_call_target="tpu_custom_call" | custom-call | tf_op jit(solution)/shard_map/pick_rows/pallas_call | solution.py:49
  2.7 3.0 %collective-permute-start.1 = (bf16[64,4352]{1,0:T(8,128)(2,1)}, bf16[64,4352]{1,0:T(8,128)(2,1)S(1)}, u32[]{:S(2)}, u32[]{:S(2)}) collective-permute-start(bf16[64,4352]{1,0:T(8,128)(2,1)} %pick_rows.2), channel_id=1, source_target_pairs={{8,0},{16,8},{24,16},{28,24},{20,28},{12,20},{4,12},{0,4},{9,1},{1... | collective-permute-start | bytes 1671176 | tf_op jit(solution)/shard_map/ppermute | solution.py:212
  5.7 0.1 collective-permute-start
  5.8 3.3 %rotate.2 = bf16[512,2048]{1,0:T(8,128)(2,1)} custom-call(s32[1]{0:T(128)} %bitcast.shard_ref, bf16[256,8192]{1,0:T(8,128)(2,1)} %matrix_ref.2, bf16[4,512,512]{2,1,0:T(8,128)(2,1)} %basis_ref.2), custom_call_target="tpu_custom_call" | custom-call | flops 536870912 | bytes 5242880 | tf_op jit(solution)/shard_map/rotate/pallas_call | solution.py:77
  9.2 2.7 %pick_rows.3 = bf16[64,4864]{1,0:T(8,128)(2,1)} custom-call(s32[16]{0:T(128)} %owners_ref.2, bf16[1,512,7168]{2,1,0:T(8,128)(2,1)} %refs_0_.3), custom_call_target="tpu_custom_call" | custom-call | tf_op jit(solution)/shard_map/pick_rows/pallas_call | solution.py:49
  11.9 1.9 %collective-permute-start.8 = (bf16[64,4864]{1,0:T(8,128)(2,1)}, bf16[64,4864]{1,0:T(8,128)(2,1)S(1)}, u32[]{:S(2)}, u32[]{:S(2)}) collective-permute-start(bf16[64,4864]{1,0:T(8,128)(2,1)} %pick_rows.3), channel_id=1, source_target_pairs={{8,0},{16,8},{24,16},{28,24},{20,28},{12,20},{4,12},{0,4},{9,1},{1... | collective-permute-start | bytes 1867784 | tf_op jit(solution)/shard_map/ppermute | solution.py:212
  13.8 0.2 collective-permute-start.7
  14.0 0.2 convert_reduce_fusion
  14.3 0.1 concatenate.54
  14.4 0.1 concatenate.53
  14.5 9.4 %rotate.3 = bf16[512,7168]{1,0:T(8,128)(2,1)} custom-call(s32[1]{0:T(128)} %constant.120.clone.1.shard_ref, bf16[256,7168]{1,0:T(8,128)(2,1)} %matrix_ref.3, bf16[28,256,256]{2,1,0:T(8,128)(2,1)} %basis_ref.3), custom_call_target="tpu_custom_call" | custom-call | flops 939524096 | bytes 14680064 | tf_op jit(solution)/shard_map/rotate/pallas_call | solution.py:77
  23.9 0.2 and_convert_fusion.hit_ref
  24.1 0.0 collective-permute-done
  24.2 2.0 %collective-permute-start.2 = (bf16[64,4352]{1,0:T(8,128)(2,1)S(1)}, bf16[64,4352]{1,0:T(8,128)(2,1)S(1)}, u32[]{:S(2)}, u32[]{:S(2)}) collective-permute-start(bf16[64,4352]{1,0:T(8,128)(2,1)S(1)} %collective-permute-done), channel_id=1, source_target_pairs={{0,8},{8,16},{16,24},{24,28},{28,20},{20,12},{12,4},{4,0},{1,9},{9... | collective-permute-start | bytes 1671176 | tf_op jit(solution)/shard_map/ppermute | solution.py:212
  26.2 0.1 collective-permute-start.3
  26.3 2.6 %fusion.27 = f32[512,64]{1,0:T(8,128)S(1)} fusion(bf16[512,7168]{1,0:T(8,128)(2,1)} %rotate.3, bf16[64,4352]{1,0:T(8,128)(2,1)S(1)} %copy-done.1), kind=kOutput, calls=%fused_computation.27 | convolution fusion | flops 150994944 | bytes 2785280 | tf_op jit(solution)/shard_map/dot_general | solution.py:101
  29.0 4.0 %fusion.2 = f32[512,64]{1,0:T(8,128)S(1)} fusion(bf16[64,4864]{1,0:T(8,128)(2,1)S(1)} %copy-done.2, bf16[512,7168]{1,0:T(8,128)(2,1)} %rotate.3), kind=kOutput, calls=%fused_computation.2 | convolution fusion | flops 318767104 | bytes 5734400 | tf_op jit(solution)/shard_map/dot_general | solution.py:101
  33.1 0.8 fusion.31
  33.9 0.9 collective-permute-done.7
  34.8 1.1 %collective-permute-start.13 = (bf16[64,4864]{1,0:T(8,128)(2,1)S(1)}, bf16[64,4864]{1,0:T(8,128)(2,1)S(1)}, u32[]{:S(2)}, u32[]{:S(2)}) collective-permute-start(bf16[64,4864]{1,0:T(8,128)(2,1)S(1)} %collective-permute-done.7), channel_id=1, source_target_pairs={{0,8},{8,16},{16,24},{24,28},{28,20},{20,12},{12,4},{4,0},{1,9},{9... | collective-permute-start | bytes 1867784 | tf_op jit(solution)/shard_map/ppermute | solution.py:212
  35.9 0.9 collective-permute-start.14
  36.8 1.4 %fusion.6 = f32[512,128]{1,0:T(8,128)S(1)} fusion(bf16[512,7168]{1,0:T(8,128)(2,1)S(1)} %bitcast.6, bf16[64,4864]{1,0:T(8,128)(2,1)S(1)} %collective-permute-done.8, bf16[64,4864]{1,0:T(8,128)(2,1)S(1)} %collective-permute-done.7), kind=kOutput, calls=%fused_computation.6 | convolution fusion | flops 640024576 | bytes 6488064 | tf_op jit(solution)/shard_map/dot_general | solution.py:101
  38.3 8.4 %collective-permute-done.2 = bf16[64,4352]{1,0:T(8,128)(2,1)S(1)} collective-permute-done((bf16[64,4352]{1,0:T(8,128)(2,1)S(1)}, bf16[64,4352]{1,0:T(8,128)(2,1)S(1)}, u32[]{:S(2)}, u32[]{:S(2)}) %collective-permute-start.2) | collective-permute-done | bytes 557088 | tf_op jit(solution)/shard_map/ppermute | solution.py:212
  46.9 1.3 %fusion.10 = f32[512,320]{1,0:T(8,128)S(1)} fusion(bf16[512,2048]{1,0:T(8,128)(2,1)S(1)} %copy-done, bf16[64,2048]{1,0:T(8,128)(2,1)S(1)} %slice.147, bf16[128,2048]{1,0:T(8,128)(2,1)S(1)} %slice.190, bf16[128,2048]{1,0:T(8,128)(2,1)S(1)} %slice.189), kind=kOutput, calls=%fused_computation.10 | convolution fusion | flops 675020800 | bytes 4063232 | tf_op jit(solution)/shard_map/dot_general | solution.py:101
  48.2 0.1 collective-permute-start.4
  48.3 0.2 collective-permute-start.9
  48.5 1.9 %collective-permute-start.10 = (bf16[64,4352]{1,0:T(8,128)(2,1)S(1)}, bf16[64,4352]{1,0:T(8,128)(2,1)S(1)}, u32[]{:S(2)}, u32[]{:S(2)}) collective-permute-start(bf16[64,4352]{1,0:T(8,128)(2,1)S(1)} %collective-permute-done.3), channel_id=1, source_target_pairs={{8,0},{16,8},{24,16},{28,24},{20,28},{12,20},{4,12},{0,4},{9,1},{1... | collective-permute-start | bytes 1671176 | tf_op jit(solution)/shard_map/ppermute | solution.py:212
  50.4 0.8 fusion.29
  51.2 8.9 %collective-permute-done.13 = bf16[64,4864]{1,0:T(8,128)(2,1)S(1)} collective-permute-done((bf16[64,4864]{1,0:T(8,128)(2,1)S(1)}, bf16[64,4864]{1,0:T(8,128)(2,1)S(1)}, u32[]{:S(2)}, u32[]{:S(2)}) %collective-permute-start.13) | collective-permute-done | bytes 622624 | tf_op jit(solution)/shard_map/ppermute | solution.py:212
  60.1 0.1 collective-permute-start.17
  60.2 1.9 %collective-permute-start.18 = (bf16[64,4864]{1,0:T(8,128)(2,1)S(1)}, bf16[64,4864]{1,0:T(8,128)(2,1)S(1)}, u32[]{:S(2)}, u32[]{:S(2)}) collective-permute-start(bf16[64,4864]{1,0:T(8,128)(2,1)S(1)} %collective-permute-done.14), channel_id=1, source_target_pairs={{8,0},{16,8},{24,16},{28,24},{20,28},{12,20},{4,12},{0,4},{9,1},{1... | collective-permute-start | bytes 1867784 | tf_op jit(solution)/shard_map/ppermute | solution.py:212
  62.1 1.6 %collective-permute-start.5 = (f32[128,320]{1,0:T(8,128)S(1)}, f32[128,320]{1,0:T(8,128)S(1)}, u32[]{:S(2)}, u32[]{:S(2)}) collective-permute-start(f32[128,320]{1,0:T(8,128)S(1)} %dynamic-slice_add_fusion), channel_id=1, source_target_pairs={{0,2},{1,3},{2,0},{3,1},{4,6},{5,7},{6,4},{7,5},{8,10},{9,11},{10,... | collective-permute-start | bytes 491528 | tf_op jit(solution)/shard_map/ppermute | solution.py:155
  63.7 1.4 %fusion.4 = f32[512,128]{1,0:T(8,128)S(1)} fusion(bf16[512,7168]{1,0:T(8,128)(2,1)S(1)} %bitcast.6, bf16[64,4864]{1,0:T(8,128)(2,1)S(1)} %collective-permute-done.14, bf16[64,4864]{1,0:T(8,128)(2,1)S(1)} %collective-permute-done.13), kind=kOutput, calls=%fused_computation.4 | convolution fusion | flops 640024576 | bytes 6488064 | tf_op jit(solution)/shard_map/dot_general | solution.py:101
  65.2 2.7 %collective-permute-done.5 = f32[128,320]{1,0:T(8,128)S(1)} collective-permute-done((f32[128,320]{1,0:T(8,128)S(1)}, f32[128,320]{1,0:T(8,128)S(1)}, u32[]{:S(2)}, u32[]{:S(2)}) %collective-permute-start.5) | collective-permute-done | bytes 163872 | tf_op jit(solution)/shard_map/ppermute | solution.py:155
  67.9 0.1 collective-permute-start.6
  68.0 4.0 %collective-permute-done.9 = bf16[64,4352]{1,0:T(8,128)(2,1)S(1)} collective-permute-done((bf16[64,4352]{1,0:T(8,128)(2,1)S(1)}, bf16[64,4352]{1,0:T(8,128)(2,1)S(1)}, u32[]{:S(2)}, u32[]{:S(2)}) %collective-permute-start.9) | collective-permute-done | bytes 557088 | tf_op jit(solution)/shard_map/ppermute | solution.py:212
  72.1 0.7 fusion.41
  72.8 0.1 collective-permute-start.11
  73.0 1.2 %collective-permute-done.11 = f32[256,128]{1,0:T(8,128)S(1)} collective-permute-done((f32[256,128]{1,0:T(8,128)S(1)}, f32[256,128]{1,0:T(8,128)S(1)}, u32[]{:S(2)}, u32[]{:S(2)}) %collective-permute-start.11) | collective-permute-done | bytes 131104 | tf_op jit(solution)/shard_map/ppermute | solution.py:155
  74.3 1.6 %collective-permute-start.12 = (f32[256,128]{1,0:T(8,128)S(1)}, f32[256,128]{1,0:T(8,128)S(1)}, u32[]{:S(2)}, u32[]{:S(2)}) collective-permute-start(f32[256,128]{1,0:T(8,128)S(1)} %fusion.65), channel_id=1, source_target_pairs={{0,2},{1,3},{2,0},{3,1},{4,6},{5,7},{6,4},{7,5},{8,10},{9,11},{10,... | collective-permute-start | bytes 393224 | tf_op jit(solution)/shard_map/ppermute | solution.py:155
  75.9 0.8 fusion.25
  76.7 0.6 collective-permute-start.15
  77.3 1.5 %collective-permute-start.16 = (bf16[32,4352]{1,0:T(8,128)(2,1)S(1)}, bf16[32,4352]{1,0:T(8,128)(2,1)S(1)}, u32[]{:S(2)}, u32[]{:S(2)}) collective-permute-start(bf16[32,4352]{1,0:T(8,128)(2,1)S(1)} %slice.197), channel_id=1, source_target_pairs={{8,0},{16,8},{24,16},{28,24},{20,28},{12,20},{4,12},{0,4},{9,1},{1... | collective-permute-start | bytes 835592 | tf_op jit(solution)/shard_map/ppermute | solution.py:212
  78.8 6.6 %collective-permute-done.17 = bf16[64,4864]{1,0:T(8,128)(2,1)S(1)} collective-permute-done((bf16[64,4864]{1,0:T(8,128)(2,1)S(1)}, bf16[64,4864]{1,0:T(8,128)(2,1)S(1)}, u32[]{:S(2)}, u32[]{:S(2)}) %collective-permute-start.17) | collective-permute-done | bytes 622624 | tf_op jit(solution)/shard_map/ppermute | solution.py:212
  85.4 0.2 collective-permute-start.22
  85.6 1.9 %collective-permute-start.23 = (bf16[32,4864]{1,0:T(8,128)(2,1)S(1)}, bf16[32,4864]{1,0:T(8,128)(2,1)S(1)}, u32[]{:S(2)}, u32[]{:S(2)}) collective-permute-start(bf16[32,4864]{1,0:T(8,128)(2,1)S(1)} %slice.208), channel_id=1, source_target_pairs={{8,0},{16,8},{24,16},{28,24},{20,28},{12,20},{4,12},{0,4},{9,1},{1... | collective-permute-start | bytes 933896 | tf_op jit(solution)/shard_map/ppermute | solution.py:212
  87.5 1.4 %fusion = f32[512,128]{1,0:T(8,128)S(1)} fusion(bf16[512,7168]{1,0:T(8,128)(2,1)S(1)} %bitcast.6, bf16[64,4864]{1,0:T(8,128)(2,1)S(1)} %collective-permute-done.18, bf16[64,4864]{1,0:T(8,128)(2,1)S(1)} %collective-permute-done.17), kind=kOutput, calls=%fused_computation | convolution fusion | flops 640024576 | bytes 6488064 | tf_op jit(solution)/shard_map/dot_general | solution.py:101
  89.0 2.3 %collective-permute-done.15 = bf16[32,4352]{1,0:T(8,128)(2,1)S(1)} collective-permute-done((bf16[32,4352]{1,0:T(8,128)(2,1)S(1)}, bf16[32,4352]{1,0:T(8,128)(2,1)S(1)}, u32[]{:S(2)}, u32[]{:S(2)}) %collective-permute-start.15) | collective-permute-done | bytes 278560 | tf_op jit(solution)/shard_map/ppermute | solution.py:212
  91.4 0.7 fusion.45
  92.1 0.1 pad_maximum_fusion
  92.2 0.1 collective-permute-start.21
  92.3 1.6 %collective-permute-start.20 = (f32[128,128]{1,0:T(8,128)S(1)}, f32[128,128]{1,0:T(8,128)S(1)}, u32[]{:S(2)}, u32[]{:S(2)}) collective-permute-start(f32[128,128]{1,0:T(8,128)S(1)} %pad_maximum_fusion), channel_id=1, source_target_pairs={{0,2},{1,3},{2,0},{3,1},{4,6},{5,7},{6,4},{7,5},{8,10},{9,11},{10,... | collective-permute-start | bytes 196616 | tf_op jit(solution)/shard_map/ppermute | solution.py:155
  93.9 0.3 collective-permute-start.19
  94.1 0.8 fusion.33
  94.9 1.6 %collective-permute-done.22 = bf16[32,4864]{1,0:T(8,128)(2,1)S(1)} collective-permute-done((bf16[32,4864]{1,0:T(8,128)(2,1)S(1)}, bf16[32,4864]{1,0:T(8,128)(2,1)S(1)}, u32[]{:S(2)}, u32[]{:S(2)}) %collective-permute-start.22) | collective-permute-done | bytes 311328 | tf_op jit(solution)/shard_map/ppermute | solution.py:212
  96.5 1.4 %fusion.8 = f32[512,64]{1,0:T(8,128)S(1)} fusion(bf16[512,7168]{1,0:T(8,128)(2,1)S(1)} %bitcast.6, bf16[32,4864]{1,0:T(8,128)(2,1)S(1)} %collective-permute-done.23, bf16[32,4864]{1,0:T(8,128)(2,1)S(1)} %collective-permute-done.22), kind=kOutput, calls=%fused_computation.8 | convolution fusion | flops 320012288 | bytes 5734400 | tf_op jit(solution)/shard_map/dot_general | solution.py:101
  98.0 0.0 collective-permute-done.20
  98.1 0.3 score.1
  98.4 0.5 collective-permute-start.26
  98.9 1.2 %collective-permute-start.25 = (f32[2,16]{1,0:T(2,128)S(1)}, f32[2,16]{1,0:T(2,128)S(1)}, u32[]{:S(2)}, u32[]{:S(2)}) collective-permute-start(f32[2,16]{1,0:T(2,128)S(1)} %score.1), channel_id=1, source_target_pairs={{0,2},{1,3},{2,0},{3,1},{4,6},{5,7},{6,4},{7,5},{8,10},{9,11},{10,... | collective-permute-start | bytes 392 | tf_op jit(solution)/shard_map/ppermute | solution.py:155
  100.1 0.2 collective-permute-start.24
  100.3 1.1 %collective-permute-done.26 = f32[2,16]{1,0:T(2,128)S(1)} collective-permute-done((f32[2,16]{1,0:T(2,128)S(1)}, f32[2,16]{1,0:T(2,128)S(1)}, u32[]{:S(2)}, u32[]{:S(2)}) %collective-permute-start.26) | collective-permute-done | bytes 160 | tf_op jit(solution)/shard_map/ppermute | solution.py:155
  101.4 1.0 collective-permute-done.25
  102.5 0.6 add_add_fusion.1
  (70 shorter events, 1.0 us)
Async XLA Ops:
  2.7 21.5 %collective-permute-start.1 = (bf16[64,4352]{1,0:T(8,128)(2,1)}, bf16[64,4352]{1,0:T(8,128)(2,1)S(1)}, u32[]{:S(2)}, u32[]{:S(2)}) collective-permute-start(bf16[64,4352]{1,0:T(8,128)(2,1)} %pick_rows.2), channel_id=1, source_target_pairs={{8,0},{16,8},{24,16},{28,24},{20,28},{12,20},{4,12},{0,4},{9,1},{1... | collective-permute-start | bytes 1671176 | tf_op jit(solution)/shard_map/ppermute | solution.py:212
  5.7 18.5 %collective-permute-start = (bf16[64,4352]{1,0:T(8,128)(2,1)}, bf16[64,4352]{1,0:T(8,128)(2,1)S(1)}, u32[]{:S(2)}, u32[]{:S(2)}) collective-permute-start(bf16[64,4352]{1,0:T(8,128)(2,1)} %pick_rows.2), channel_id=1, source_target_pairs={{0,8},{8,16},{16,24},{24,28},{28,20},{20,12},{12,4},{4,0},{1,9},{9... | collective-permute-start | bytes 1671176 | tf_op jit(solution)/shard_map/ppermute | solution.py:212
  9.2 4.8 %copy-start.3 = (s32[16]{0:T(128)S(1)}, s32[16]{0:T(128)}, u32[]{:S(2)}) copy-start(s32[16]{0:T(128)} %owners_ref.2) | copy-start | bytes 196
  11.9 22.0 %collective-permute-start.8 = (bf16[64,4864]{1,0:T(8,128)(2,1)}, bf16[64,4864]{1,0:T(8,128)(2,1)S(1)}, u32[]{:S(2)}, u32[]{:S(2)}) collective-permute-start(bf16[64,4864]{1,0:T(8,128)(2,1)} %pick_rows.3), channel_id=1, source_target_pairs={{8,0},{16,8},{24,16},{28,24},{20,28},{12,20},{4,12},{0,4},{9,1},{1... | collective-permute-start | bytes 1867784 | tf_op jit(solution)/shard_map/ppermute | solution.py:212
  13.8 20.9 %collective-permute-start.7 = (bf16[64,4864]{1,0:T(8,128)(2,1)}, bf16[64,4864]{1,0:T(8,128)(2,1)S(1)}, u32[]{:S(2)}, u32[]{:S(2)}) collective-permute-start(bf16[64,4864]{1,0:T(8,128)(2,1)} %pick_rows.3), channel_id=1, source_target_pairs={{0,8},{8,16},{16,24},{24,28},{28,20},{20,12},{12,4},{4,0},{1,9},{9... | collective-permute-start | bytes 1867784 | tf_op jit(solution)/shard_map/ppermute | solution.py:212
  14.5 11.7 %copy-start.1 = (bf16[64,4352]{1,0:T(8,128)(2,1)S(1)}, bf16[64,4352]{1,0:T(8,128)(2,1)}, u32[]{:S(2)}) copy-start(bf16[64,4352]{1,0:T(8,128)(2,1)} %pick_rows.2) | copy-start | bytes 1671172
  24.2 22.6 %collective-permute-start.2 = (bf16[64,4352]{1,0:T(8,128)(2,1)S(1)}, bf16[64,4352]{1,0:T(8,128)(2,1)S(1)}, u32[]{:S(2)}, u32[]{:S(2)}) collective-permute-start(bf16[64,4352]{1,0:T(8,128)(2,1)S(1)} %collective-permute-done), channel_id=1, source_target_pairs={{0,8},{8,16},{16,24},{24,28},{28,20},{20,12},{12,4},{4,0},{1,9},{9... | collective-permute-start | bytes 1671176 | tf_op jit(solution)/shard_map/ppermute | solution.py:212
  26.2 20.6 %collective-permute-start.3 = (bf16[64,4352]{1,0:T(8,128)(2,1)S(1)}, bf16[64,4352]{1,0:T(8,128)(2,1)S(1)}, u32[]{:S(2)}, u32[]{:S(2)}) collective-permute-start(bf16[64,4352]{1,0:T(8,128)(2,1)S(1)} %collective-permute-done.1), channel_id=1, source_target_pairs={{8,0},{16,8},{24,16},{28,24},{20,28},{12,20},{4,12},{0,4},{9,1},{1... | collective-permute-start | bytes 1671176 | tf_op jit(solution)/shard_map/ppermute | solution.py:212
  26.3 2.7 %copy-start.2 = (bf16[64,4864]{1,0:T(8,128)(2,1)S(1)}, bf16[64,4864]{1,0:T(8,128)(2,1)}, u32[]{:S(2)}) copy-start(bf16[64,4864]{1,0:T(8,128)(2,1)} %pick_rows.3) | copy-start | bytes 1867780
  26.3 6.8 %slice-start = ((s8[7340032]{0:T(1024)(128)(4,1)}), s8[4194304]{0:T(1024)(128)(4,1)S(1)}, s32[]{:S(2)}) async-start(s8[7340032]{0:T(1024)(128)(4,1)} %bitcast.5), calls=%async_computation | async-start | bytes 8388608
  29.0 4.1 %slice-start.1 = ((s8[7340032]{0:T(1024)(128)(4,1)}), s8[3145728]{0:T(1024)(128)(4,1)S(1)}, s32[]{:S(2)}) async-start(s8[7340032]{0:T(1024)(128)(4,1)} %bitcast.5), calls=%async_computation.1 | async-start | bytes 6291456
  34.8 25.3 %collective-permute-start.13 = (bf16[64,4864]{1,0:T(8,128)(2,1)S(1)}, bf16[64,4864]{1,0:T(8,128)(2,1)S(1)}, u32[]{:S(2)}, u32[]{:S(2)}) collective-permute-start(bf16[64,4864]{1,0:T(8,128)(2,1)S(1)} %collective-permute-done.7), channel_id=1, source_target_pairs={{0,8},{8,16},{16,24},{24,28},{28,20},{20,12},{12,4},{4,0},{1,9},{9... | collective-permute-start | bytes 1867784 | tf_op jit(solution)/shard_map/ppermute | solution.py:212
  35.9 24.2 %collective-permute-start.14 = (bf16[64,4864]{1,0:T(8,128)(2,1)S(1)}, bf16[64,4864]{1,0:T(8,128)(2,1)S(1)}, u32[]{:S(2)}, u32[]{:S(2)}) collective-permute-start(bf16[64,4864]{1,0:T(8,128)(2,1)S(1)} %collective-permute-done.8), channel_id=1, source_target_pairs={{8,0},{16,8},{24,16},{28,24},{20,28},{12,20},{4,12},{0,4},{9,1},{1... | collective-permute-start | bytes 1867784 | tf_op jit(solution)/shard_map/ppermute | solution.py:212
  38.3 8.6 %copy-start = (bf16[512,2048]{1,0:T(8,128)(2,1)S(1)}, bf16[512,2048]{1,0:T(8,128)(2,1)}, u32[]{:S(2)}) copy-start(bf16[512,2048]{1,0:T(8,128)(2,1)} %rotate.2) | copy-start | bytes 6291460
  48.2 13.9 %collective-permute-start.4 = (f32[128,320]{1,0:T(8,128)S(1)}, f32[128,320]{1,0:T(8,128)S(1)}, u32[]{:S(2)}, u32[]{:S(2)}) collective-permute-start(f32[128,320]{1,0:T(8,128)S(1)} %constant_dynamic-slice_fusion), channel_id=1, source_target_pairs={{0,1},{1,0},{2,3},{3,2},{4,5},{5,4},{6,7},{7,6},{8,9},{9,8},{10,11... | collective-permute-start | bytes 491528 | tf_op jit(solution)/shard_map/ppermute | solution.py:155
  48.3 23.7 %collective-permute-start.9 = (bf16[64,4352]{1,0:T(8,128)(2,1)S(1)}, bf16[64,4352]{1,0:T(8,128)(2,1)S(1)}, u32[]{:S(2)}, u32[]{:S(2)}) collective-permute-start(bf16[64,4352]{1,0:T(8,128)(2,1)S(1)} %collective-permute-done.2), channel_id=1, source_target_pairs={{0,8},{8,16},{16,24},{24,28},{28,20},{20,12},{12,4},{4,0},{1,9},{9... | collective-permute-start | bytes 1671176 | tf_op jit(solution)/shard_map/ppermute | solution.py:212
  48.5 23.6 %collective-permute-start.10 = (bf16[64,4352]{1,0:T(8,128)(2,1)S(1)}, bf16[64,4352]{1,0:T(8,128)(2,1)S(1)}, u32[]{:S(2)}, u32[]{:S(2)}) collective-permute-start(bf16[64,4352]{1,0:T(8,128)(2,1)S(1)} %collective-permute-done.3), channel_id=1, source_target_pairs={{8,0},{16,8},{24,16},{28,24},{20,28},{12,20},{4,12},{0,4},{9,1},{1... | collective-permute-start | bytes 1671176 | tf_op jit(solution)/shard_map/ppermute | solution.py:212
  60.1 25.3 %collective-permute-start.17 = (bf16[64,4864]{1,0:T(8,128)(2,1)S(1)}, bf16[64,4864]{1,0:T(8,128)(2,1)S(1)}, u32[]{:S(2)}, u32[]{:S(2)}) collective-permute-start(bf16[64,4864]{1,0:T(8,128)(2,1)S(1)} %collective-permute-done.13), channel_id=1, source_target_pairs={{0,8},{8,16},{16,24},{24,28},{28,20},{20,12},{12,4},{4,0},{1,9},{9... | collective-permute-start | bytes 1867784 | tf_op jit(solution)/shard_map/ppermute | solution.py:212
  60.2 25.2 %collective-permute-start.18 = (bf16[64,4864]{1,0:T(8,128)(2,1)S(1)}, bf16[64,4864]{1,0:T(8,128)(2,1)S(1)}, u32[]{:S(2)}, u32[]{:S(2)}) collective-permute-start(bf16[64,4864]{1,0:T(8,128)(2,1)S(1)} %collective-permute-done.14), channel_id=1, source_target_pairs={{8,0},{16,8},{24,16},{28,24},{20,28},{12,20},{4,12},{0,4},{9,1},{1... | collective-permute-start | bytes 1867784 | tf_op jit(solution)/shard_map/ppermute | solution.py:212
  62.1 5.7 %collective-permute-start.5 = (f32[128,320]{1,0:T(8,128)S(1)}, f32[128,320]{1,0:T(8,128)S(1)}, u32[]{:S(2)}, u32[]{:S(2)}) collective-permute-start(f32[128,320]{1,0:T(8,128)S(1)} %dynamic-slice_add_fusion), channel_id=1, source_target_pairs={{0,2},{1,3},{2,0},{3,1},{4,6},{5,7},{6,4},{7,5},{8,10},{9,11},{10,... | collective-permute-start | bytes 491528 | tf_op jit(solution)/shard_map/ppermute | solution.py:155
  67.9 5.1 %collective-permute-start.6 = (f32[128,320]{1,0:T(8,128)S(1)}, f32[128,320]{1,0:T(8,128)S(1)}, u32[]{:S(2)}, u32[]{:S(2)}) collective-permute-start(f32[128,320]{1,0:T(8,128)S(1)} %add.202), channel_id=1, source_target_pairs={{0,1},{1,0},{2,3},{3,2},{4,5},{5,4},{6,7},{7,6},{8,9},{9,8},{10,11... | collective-permute-start | bytes 491528 | tf_op jit(solution)/shard_map/ppermute | solution.py:155
  72.8 1.4 %collective-permute-start.11 = (f32[256,128]{1,0:T(8,128)S(1)}, f32[256,128]{1,0:T(8,128)S(1)}, u32[]{:S(2)}, u32[]{:S(2)}) collective-permute-start(f32[256,128]{1,0:T(8,128)S(1)} %slice_add_fusion.12), channel_id=1, source_target_pairs={{0,1},{1,0},{2,3},{3,2},{4,5},{5,4},{6,7},{7,6},{8,9},{9,8},{10,11... | collective-permute-start | bytes 393224 | tf_op jit(solution)/shard_map/ppermute | solution.py:155
  74.3 13.2 %collective-permute-start.12 = (f32[256,128]{1,0:T(8,128)S(1)}, f32[256,128]{1,0:T(8,128)S(1)}, u32[]{:S(2)}, u32[]{:S(2)}) collective-permute-start(f32[256,128]{1,0:T(8,128)S(1)} %fusion.65), channel_id=1, source_target_pairs={{0,2},{1,3},{2,0},{3,1},{4,6},{5,7},{6,4},{7,5},{8,10},{9,11},{10,... | collective-permute-start | bytes 393224 | tf_op jit(solution)/shard_map/ppermute | solution.py:155
  76.7 14.6 %collective-permute-start.15 = (bf16[32,4352]{1,0:T(8,128)(2,1)S(1)}, bf16[32,4352]{1,0:T(8,128)(2,1)S(1)}, u32[]{:S(2)}, u32[]{:S(2)}) collective-permute-start(bf16[32,4352]{1,0:T(8,128)(2,1)S(1)} %slice.196), channel_id=1, source_target_pairs={{0,8},{8,16},{16,24},{24,28},{28,20},{20,12},{12,4},{4,0},{1,9},{9... | collective-permute-start | bytes 835592 | tf_op jit(solution)/shard_map/ppermute | solution.py:212
  77.3 14.0 %collective-permute-start.16 = (bf16[32,4352]{1,0:T(8,128)(2,1)S(1)}, bf16[32,4352]{1,0:T(8,128)(2,1)S(1)}, u32[]{:S(2)}, u32[]{:S(2)}) collective-permute-start(bf16[32,4352]{1,0:T(8,128)(2,1)S(1)} %slice.197), channel_id=1, source_target_pairs={{8,0},{16,8},{24,16},{28,24},{20,28},{12,20},{4,12},{0,4},{9,1},{1... | collective-permute-start | bytes 835592 | tf_op jit(solution)/shard_map/ppermute | solution.py:212
  85.4 11.1 %collective-permute-start.22 = (bf16[32,4864]{1,0:T(8,128)(2,1)S(1)}, bf16[32,4864]{1,0:T(8,128)(2,1)S(1)}, u32[]{:S(2)}, u32[]{:S(2)}) collective-permute-start(bf16[32,4864]{1,0:T(8,128)(2,1)S(1)} %slice.207), channel_id=1, source_target_pairs={{0,8},{8,16},{16,24},{24,28},{28,20},{20,12},{12,4},{4,0},{1,9},{9... | collective-permute-start | bytes 933896 | tf_op jit(solution)/shard_map/ppermute | solution.py:212
  85.6 10.9 %collective-permute-start.23 = (bf16[32,4864]{1,0:T(8,128)(2,1)S(1)}, bf16[32,4864]{1,0:T(8,128)(2,1)S(1)}, u32[]{:S(2)}, u32[]{:S(2)}) collective-permute-start(bf16[32,4864]{1,0:T(8,128)(2,1)S(1)} %slice.208), channel_id=1, source_target_pairs={{8,0},{16,8},{24,16},{28,24},{20,28},{12,20},{4,12},{0,4},{9,1},{1... | collective-permute-start | bytes 933896 | tf_op jit(solution)/shard_map/ppermute | solution.py:212
  92.2 5.8 %collective-permute-start.21 = (f32[128,128]{1,0:T(8,128)S(1)}, f32[128,128]{1,0:T(8,128)S(1)}, u32[]{:S(2)}, u32[]{:S(2)}) collective-permute-start(f32[128,128]{1,0:T(8,128)S(1)} %pad_maximum_fusion), channel_id=1, source_target_pairs={{0,3},{1,2},{2,1},{3,0},{4,7},{5,6},{6,5},{7,4},{8,11},{9,10},{10,... | collective-permute-start | bytes 196616 | tf_op jit(solution)/shard_map/ppermute | solution.py:155
  92.3 5.8 %collective-permute-start.20 = (f32[128,128]{1,0:T(8,128)S(1)}, f32[128,128]{1,0:T(8,128)S(1)}, u32[]{:S(2)}, u32[]{:S(2)}) collective-permute-start(f32[128,128]{1,0:T(8,128)S(1)} %pad_maximum_fusion), channel_id=1, source_target_pairs={{0,2},{1,3},{2,0},{3,1},{4,6},{5,7},{6,4},{7,5},{8,10},{9,11},{10,... | collective-permute-start | bytes 196616 | tf_op jit(solution)/shard_map/ppermute | solution.py:155
  93.9 4.2 %collective-permute-start.19 = (f32[128,128]{1,0:T(8,128)S(1)}, f32[128,128]{1,0:T(8,128)S(1)}, u32[]{:S(2)}, u32[]{:S(2)}) collective-permute-start(f32[128,128]{1,0:T(8,128)S(1)} %pad_maximum_fusion), channel_id=1, source_target_pairs={{0,1},{1,0},{2,3},{3,2},{4,5},{5,4},{6,7},{7,6},{8,9},{9,8},{10,11... | collective-permute-start | bytes 196616 | tf_op jit(solution)/shard_map/ppermute | solution.py:155
  98.4 3.0 %collective-permute-start.26 = (f32[2,16]{1,0:T(2,128)S(1)}, f32[2,16]{1,0:T(2,128)S(1)}, u32[]{:S(2)}, u32[]{:S(2)}) collective-permute-start(f32[2,16]{1,0:T(2,128)S(1)} %score.1), channel_id=1, source_target_pairs={{0,3},{1,2},{2,1},{3,0},{4,7},{5,6},{6,5},{7,4},{8,11},{9,10},{10,... | collective-permute-start | bytes 392 | tf_op jit(solution)/shard_map/ppermute | solution.py:155
  98.9 3.6 %collective-permute-start.25 = (f32[2,16]{1,0:T(2,128)S(1)}, f32[2,16]{1,0:T(2,128)S(1)}, u32[]{:S(2)}, u32[]{:S(2)}) collective-permute-start(f32[2,16]{1,0:T(2,128)S(1)} %score.1), channel_id=1, source_target_pairs={{0,2},{1,3},{2,0},{3,1},{4,6},{5,7},{6,4},{7,5},{8,10},{9,11},{10,... | collective-permute-start | bytes 392 | tf_op jit(solution)/shard_map/ppermute | solution.py:155
  100.1 2.3 %collective-permute-start.24 = (f32[2,16]{1,0:T(2,128)S(1)}, f32[2,16]{1,0:T(2,128)S(1)}, u32[]{:S(2)}, u32[]{:S(2)}) collective-permute-start(f32[2,16]{1,0:T(2,128)S(1)} %score.1), channel_id=1, source_target_pairs={{0,1},{1,0},{2,3},{3,2},{4,5},{5,4},{6,7},{7,6},{8,9},{9,8},{10,11... | collective-permute-start | bytes 392 | tf_op jit(solution)/shard_map/ppermute | solution.py:155

commit v16 on v14

--- a/solution.py
+++ b/solution.py
@@ -194,7 +194,7 @@
 
     width_left = left_store.shape[2]
     width_right = right_store.shape[2]
-    cut = max(width_right * 9 // 28 // 128 * 128, 128)
+    cut = max(width_right * 19 // 56 // 128 * 128, 128)
     own = [pick_rows(groups, owners, [(left_store, 0, width_left), (right_store, 0, cut)])]
     grads = rotate(out_grads, out_basis, shard)
     own.append(

time: 103 us -> 103 us (level)
  waiting for transfers between devices: 38.8 us -> 41.5 us
  matrix products: 19.1 us -> 16.6 us
    dot_general x13, matrix products: 19.1 us -> 16.6 us  [contract_rows(): lax.dot_general(both, second, (((1,), (1,)), ((), ())), preferred_element...]
    ppermute x8, waiting for transfers between devices: 0.02 us -> 2.5 us  [send(): lax.ppermute(behind, 'dp', backward)]
  transfers between devices with their start and end apart: 27 -> 27, of which waited for: 11 -> 13; matrix products, arithmetic and copies ran while one was open for 20% -> 18% of each run, Pallas kernels for 14% -> 14%
where the time goes in v16:
time: 103 us
  waiting for transfers between devices  41.5 us (40%)
  starting transfers between devices  24.8 us (24%)
  matrix products  16.6 us (16%)
  Pallas kernels  16.4 us (16%)
  other arithmetic  1.44 us (1%)
  local copies, waits for them, and re-layouts  1.43 us (1%)
    ppermute x8, waiting for transfers between devices, send(): lax.ppermute(ahead, 'dp', forward)  32.6 us
    dot_general x13, matrix products, contract_rows(): lax.dot_general(both, second, (((1,), (1,)), ((), ())), preferred_element...  16.6 us
    ppermute x8, starting transfers between devices, send(): lax.ppermute(behind, 'dp', backward)  14.1 us
    pallas_call x2, Pallas kernels, rotate(): pl.pallas_call(kernel, out_shape=jax.ShapeDtypeStruct((2 * rows, total),...  12.7 us
    ppermute x11, starting transfers between devices, swapped(): return lax.ppermute(piece, 'mp', [(i, i ^ distance) for i in range(shards)])  7.19 us
    ppermute x11, waiting for transfers between devices, swapped(): return lax.ppermute(piece, 'mp', [(i, i ^ distance) for i in range(shards)])  6.39 us
    ppermute x8, starting transfers between devices, send(): lax.ppermute(ahead, 'dp', forward)  3.46 us
    pallas_call x2, Pallas kernels, pick_rows(): pl.pallas_call(kernel, out_shape=jax.ShapeDtypeStruct((per * R, total), j...  3.4 us
  transfers between devices with their start and end apart: 27, of which 13 were waited for; matrix products, arithmetic and copies ran while one was open for 18% of the time, Pallas kernels for 14%

profile of v16, /device:TPU:0, one launch (start us, length us, event | category | flops | bytes accessed | tf_op | source)
XLA Modules:
  0.0 102.7 jit_solution(10637713757124818395)
XLA Ops:
  0.0 0.7 copy-done
  0.7 1.7 %pick_rows.2 = bf16[64,4480]{1,0:T(8,128)(2,1)S(1)} custom-call(s32[16]{0:T(128)S(1)} %copy-done, bf16[1,512,2048]{2,1,0:T(8,128)(2,1)} %refs_0_.2, bf16[1,512,7168]{2,1,0:T(8,128)(2,1)} %refs_0_.3), custom_call_target="tpu_custom_call" | custom-call | tf_op jit(solution)/shard_map/pick_rows/pallas_call | solution.py:49
  2.4 3.0 %collective-permute-start.1 = (bf16[64,4480]{1,0:T(8,128)(2,1)S(1)}, bf16[64,4480]{1,0:T(8,128)(2,1)S(1)}, u32[]{:S(2)}, u32[]{:S(2)}) collective-permute-start(bf16[64,4480]{1,0:T(8,128)(2,1)S(1)} %pick_rows.2), channel_id=1, source_target_pairs={{8,0},{16,8},{24,16},{28,24},{20,28},{12,20},{4,12},{0,4},{9,1},{1... | collective-permute-start | bytes 1720328 | tf_op jit(solution)/shard_map/ppermute | solution.py:212
  5.4 0.2 collective-permute-start
  5.5 3.3 %rotate.2 = bf16[512,2048]{1,0:T(8,128)(2,1)} custom-call(s32[1]{0:T(128)} %bitcast.shard_ref, bf16[256,8192]{1,0:T(8,128)(2,1)} %matrix_ref.2, bf16[4,512,512]{2,1,0:T(8,128)(2,1)} %basis_ref.2), custom_call_target="tpu_custom_call" | custom-call | flops 536870912 | bytes 5242880 | tf_op jit(solution)/shard_map/rotate/pallas_call | solution.py:77
  8.9 1.7 %pick_rows.3 = bf16[64,4736]{1,0:T(8,128)(2,1)S(1)} custom-call(s32[16]{0:T(128)S(1)} %copy-done.1, bf16[1,512,7168]{2,1,0:T(8,128)(2,1)} %refs_0_.3), custom_call_target="tpu_custom_call" | custom-call | tf_op jit(solution)/shard_map/pick_rows/pallas_call | solution.py:49
  10.6 1.9 %collective-permute-start.8 = (bf16[64,4736]{1,0:T(8,128)(2,1)S(1)}, bf16[64,4736]{1,0:T(8,128)(2,1)S(1)}, u32[]{:S(2)}, u32[]{:S(2)}) collective-permute-start(bf16[64,4736]{1,0:T(8,128)(2,1)S(1)} %pick_rows.3), channel_id=1, source_target_pairs={{8,0},{16,8},{24,16},{28,24},{20,28},{12,20},{4,12},{0,4},{9,1},{1... | collective-permute-start | bytes 1818632 | tf_op jit(solution)/shard_map/ppermute | solution.py:212
  12.5 0.2 collective-permute-start.7
  12.7 0.2 convert_reduce_fusion
  12.9 0.1 concatenate.54
  13.1 0.1 concatenate.53
  13.2 9.4 %rotate.3 = bf16[512,7168]{1,0:T(8,128)(2,1)} custom-call(s32[1]{0:T(128)} %constant.120.clone.1.shard_ref, bf16[256,7168]{1,0:T(8,128)(2,1)} %matrix_ref.3, bf16[28,256,256]{2,1,0:T(8,128)(2,1)} %basis_ref.3), custom_call_target="tpu_custom_call" | custom-call | flops 939524096 | bytes 14680064 | tf_op jit(solution)/shard_map/rotate/pallas_call | solution.py:77
  22.5 0.2 and_convert_fusion.hit_ref
  22.8 2.0 %collective-permute-start.2 = (bf16[64,4480]{1,0:T(8,128)(2,1)S(1)}, bf16[64,4480]{1,0:T(8,128)(2,1)S(1)}, u32[]{:S(2)}, u32[]{:S(2)}) collective-permute-start(bf16[64,4480]{1,0:T(8,128)(2,1)S(1)} %collective-permute-done), channel_id=1, source_target_pairs={{0,8},{8,16},{16,24},{24,28},{28,20},{20,12},{12,4},{4,0},{1,9},{9... | collective-permute-start | bytes 1720328 | tf_op jit(solution)/shard_map/ppermute | solution.py:212
  24.9 2.5 %fusion.12 = f32[512,64]{1,0:T(8,128)S(1)} fusion(bf16[512,7168]{1,0:T(8,128)(2,1)} %rotate.3, bf16[64,4480]{1,0:T(8,128)(2,1)S(1)} %pick_rows.2), kind=kOutput, calls=%fused_computation.12 | convolution fusion | flops 159383552 | bytes 2932736 | tf_op jit(solution)/shard_map/dot_general | solution.py:101
  27.5 1.4 %fusion.2 = f32[512,64]{1,0:T(8,128)S(1)} fusion(bf16[64,4736]{1,0:T(8,128)(2,1)S(1)} %pick_rows.3, bf16[512,7168]{1,0:T(8,128)(2,1)S(1)} %copy-done.2), kind=kOutput, calls=%fused_computation.2 | convolution fusion | flops 310378496 | bytes 5586944 | tf_op jit(solution)/shard_map/dot_general | solution.py:101
  29.0 0.8 fusion.16
  29.8 2.5 %collective-permute-done.8 = bf16[64,4736]{1,0:T(8,128)(2,1)S(1)} collective-permute-done((bf16[64,4736]{1,0:T(8,128)(2,1)S(1)}, bf16[64,4736]{1,0:T(8,128)(2,1)S(1)}, u32[]{:S(2)}, u32[]{:S(2)}) %collective-permute-start.8) | collective-permute-done | bytes 606240 | tf_op jit(solution)/shard_map/ppermute | solution.py:212
  32.3 2.1 %collective-permute-done.7 = bf16[64,4736]{1,0:T(8,128)(2,1)} collective-permute-done((bf16[64,4736]{1,0:T(8,128)(2,1)S(1)}, bf16[64,4736]{1,0:T(8,128)(2,1)}, u32[]{:S(2)}, u32[]{:S(2)}) %collective-permute-start.7) | collective-permute-done | bytes 606240 | tf_op jit(solution)/shard_map/ppermute | solution.py:212
  34.4 0.1 collective-permute-start.13
  34.5 1.9 %collective-permute-start.14 = (bf16[64,4736]{1,0:T(8,128)(2,1)S(1)}, bf16[64,4736]{1,0:T(8,128)(2,1)S(1)}, u32[]{:S(2)}, u32[]{:S(2)}) collective-permute-start(bf16[64,4736]{1,0:T(8,128)(2,1)S(1)} %collective-permute-done.8), channel_id=1, source_target_pairs={{8,0},{16,8},{24,16},{28,24},{20,28},{12,20},{4,12},{0,4},{9,1},{1... | collective-permute-start | bytes 1818632 | tf_op jit(solution)/shard_map/ppermute | solution.py:212
  36.4 2.5 %fusion.6 = f32[512,128]{1,0:T(8,128)S(1)} fusion(bf16[512,7168]{1,0:T(8,128)(2,1)S(1)} %copy-done.2, bf16[64,4736]{1,0:T(8,128)(2,1)S(1)} %collective-permute-done.8, bf16[64,4736]{1,0:T(8,128)(2,1)} %collective-permute-done.7), kind=kOutput, calls=%fused_computation.6 | convolution fusion | flops 623181824 | bytes 6324224 | tf_op jit(solution)/shard_map/dot_general | solution.py:101
  39.0 7.6 %collective-permute-done.2 = bf16[64,4480]{1,0:T(8,128)(2,1)S(1)} collective-permute-done((bf16[64,4480]{1,0:T(8,128)(2,1)S(1)}, bf16[64,4480]{1,0:T(8,128)(2,1)S(1)}, u32[]{:S(2)}, u32[]{:S(2)}) %collective-permute-start.2) | collective-permute-done | bytes 573472 | tf_op jit(solution)/shard_map/ppermute | solution.py:212
  46.8 1.3 %fusion.20 = f32[512,320]{1,0:T(8,128)S(1)} fusion(bf16[512,2048]{1,0:T(8,128)(2,1)S(1)} %copy-done.3, bf16[64,2048]{1,0:T(8,128)(2,1)S(1)} %slice.147, bf16[128,2048]{1,0:T(8,128)(2,1)S(1)} %slice.190, bf16[128,2048]{1,0:T(8,128)(2,1)S(1)} %slice.189), kind=kOutput, calls=%fused_computation.20 | convolution fusion | flops 675020800 | bytes 4063232 | tf_op jit(solution)/shard_map/dot_general | solution.py:101
  48.1 0.1 collective-permute-start.4
  48.2 0.2 collective-permute-start.9
  48.4 1.9 %collective-permute-start.10 = (bf16[64,4480]{1,0:T(8,128)(2,1)S(1)}, bf16[64,4480]{1,0:T(8,128)(2,1)S(1)}, u32[]{:S(2)}, u32[]{:S(2)}) collective-permute-start(bf16[64,4480]{1,0:T(8,128)(2,1)S(1)} %collective-permute-done.3), channel_id=1, source_target_pairs={{8,0},{16,8},{24,16},{28,24},{20,28},{12,20},{4,12},{0,4},{9,1},{1... | collective-permute-start | bytes 1720328 | tf_op jit(solution)/shard_map/ppermute | solution.py:212
  50.3 0.8 fusion.14
  51.1 8.5 %collective-permute-done.13 = bf16[64,4736]{1,0:T(8,128)(2,1)S(1)} collective-permute-done((bf16[64,4736]{1,0:T(8,128)(2,1)}, bf16[64,4736]{1,0:T(8,128)(2,1)S(1)}, u32[]{:S(2)}, u32[]{:S(2)}) %collective-permute-start.13) | collective-permute-done | bytes 606240 | tf_op jit(solution)/shard_map/ppermute | solution.py:212
  59.6 0.1 collective-permute-start.17
  59.7 1.9 %collective-permute-start.18 = (bf16[64,4736]{1,0:T(8,128)(2,1)S(1)}, bf16[64,4736]{1,0:T(8,128)(2,1)S(1)}, u32[]{:S(2)}, u32[]{:S(2)}) collective-permute-start(bf16[64,4736]{1,0:T(8,128)(2,1)S(1)} %collective-permute-done.14), channel_id=1, source_target_pairs={{8,0},{16,8},{24,16},{28,24},{20,28},{12,20},{4,12},{0,4},{9,1},{1... | collective-permute-start | bytes 1818632 | tf_op jit(solution)/shard_map/ppermute | solution.py:212
  61.6 1.6 %collective-permute-start.5 = (f32[128,320]{1,0:T(8,128)S(1)}, f32[128,320]{1,0:T(8,128)S(1)}, u32[]{:S(2)}, u32[]{:S(2)}) collective-permute-start(f32[128,320]{1,0:T(8,128)S(1)} %dynamic-slice_add_fusion), channel_id=1, source_target_pairs={{0,2},{1,3},{2,0},{3,1},{4,6},{5,7},{6,4},{7,5},{8,10},{9,11},{10,... | collective-permute-start | bytes 491528 | tf_op jit(solution)/shard_map/ppermute | solution.py:155
  63.2 1.4 %fusion.4 = f32[512,128]{1,0:T(8,128)S(1)} fusion(bf16[512,7168]{1,0:T(8,128)(2,1)S(1)} %copy-done.2, bf16[64,4736]{1,0:T(8,128)(2,1)S(1)} %collective-permute-done.14, bf16[64,4736]{1,0:T(8,128)(2,1)S(1)} %collective-permute-done.13), kind=kOutput, calls=%fused_computation.4 | convolution fusion | flops 623181824 | bytes 6324224 | tf_op jit(solution)/shard_map/dot_general | solution.py:101
  64.6 2.7 %collective-permute-done.5 = f32[128,320]{1,0:T(8,128)S(1)} collective-permute-done((f32[128,320]{1,0:T(8,128)S(1)}, f32[128,320]{1,0:T(8,128)S(1)}, u32[]{:S(2)}, u32[]{:S(2)}) %collective-permute-start.5) | collective-permute-done | bytes 163872 | tf_op jit(solution)/shard_map/ppermute | solution.py:155
  67.4 0.1 collective-permute-start.6
  67.5 4.4 %collective-permute-done.9 = bf16[64,4480]{1,0:T(8,128)(2,1)S(1)} collective-permute-done((bf16[64,4480]{1,0:T(8,128)(2,1)S(1)}, bf16[64,4480]{1,0:T(8,128)(2,1)S(1)}, u32[]{:S(2)}, u32[]{:S(2)}) %collective-permute-start.9) | collective-permute-done | bytes 573472 | tf_op jit(solution)/shard_map/ppermute | solution.py:212
  72.0 0.7 fusion.41
  72.7 0.1 collective-permute-start.11
  72.9 1.2 %collective-permute-done.11 = f32[256,128]{1,0:T(8,128)S(1)} collective-permute-done((f32[256,128]{1,0:T(8,128)S(1)}, f32[256,128]{1,0:T(8,128)S(1)}, u32[]{:S(2)}, u32[]{:S(2)}) %collective-permute-start.11) | collective-permute-done | bytes 131104 | tf_op jit(solution)/shard_map/ppermute | solution.py:155
  74.2 1.6 %collective-permute-start.12 = (f32[256,128]{1,0:T(8,128)S(1)}, f32[256,128]{1,0:T(8,128)S(1)}, u32[]{:S(2)}, u32[]{:S(2)}) collective-permute-start(f32[256,128]{1,0:T(8,128)S(1)} %fusion.65), channel_id=1, source_target_pairs={{0,2},{1,3},{2,0},{3,1},{4,6},{5,7},{6,4},{7,5},{8,10},{9,11},{10,... | collective-permute-start | bytes 393224 | tf_op jit(solution)/shard_map/ppermute | solution.py:155
  75.7 0.8 fusion.10
  76.6 0.6 collective-permute-start.15
  77.2 1.5 %collective-permute-start.16 = (bf16[32,4480]{1,0:T(8,128)(2,1)S(1)}, bf16[32,4480]{1,0:T(8,128)(2,1)S(1)}, u32[]{:S(2)}, u32[]{:S(2)}) collective-permute-start(bf16[32,4480]{1,0:T(8,128)(2,1)S(1)} %slice.197), channel_id=1, source_target_pairs={{8,0},{16,8},{24,16},{28,24},{20,28},{12,20},{4,12},{0,4},{9,1},{1... | collective-permute-start | bytes 860168 | tf_op jit(solution)/shard_map/ppermute | solution.py:212
  78.7 6.1 %collective-permute-done.17 = bf16[64,4736]{1,0:T(8,128)(2,1)S(1)} collective-permute-done((bf16[64,4736]{1,0:T(8,128)(2,1)S(1)}, bf16[64,4736]{1,0:T(8,128)(2,1)S(1)}, u32[]{:S(2)}, u32[]{:S(2)}) %collective-permute-start.17) | collective-permute-done | bytes 606240 | tf_op jit(solution)/shard_map/ppermute | solution.py:212
  84.9 0.2 collective-permute-start.22
  85.1 1.9 %collective-permute-start.23 = (bf16[32,4736]{1,0:T(8,128)(2,1)S(1)}, bf16[32,4736]{1,0:T(8,128)(2,1)S(1)}, u32[]{:S(2)}, u32[]{:S(2)}) collective-permute-start(bf16[32,4736]{1,0:T(8,128)(2,1)S(1)} %slice.208), channel_id=1, source_target_pairs={{8,0},{16,8},{24,16},{28,24},{20,28},{12,20},{4,12},{0,4},{9,1},{1... | collective-permute-start | bytes 909320 | tf_op jit(solution)/shard_map/ppermute | solution.py:212
  87.0 1.4 %fusion = f32[512,128]{1,0:T(8,128)S(1)} fusion(bf16[512,7168]{1,0:T(8,128)(2,1)S(1)} %copy-done.2, bf16[64,4736]{1,0:T(8,128)(2,1)S(1)} %collective-permute-done.18, bf16[64,4736]{1,0:T(8,128)(2,1)S(1)} %collective-permute-done.17), kind=kOutput, calls=%fused_computation | convolution fusion | flops 623181824 | bytes 6324224 | tf_op jit(solution)/shard_map/dot_general | solution.py:101
  88.5 2.5 %collective-permute-done.15 = bf16[32,4480]{1,0:T(8,128)(2,1)S(1)} collective-permute-done((bf16[32,4480]{1,0:T(8,128)(2,1)S(1)}, bf16[32,4480]{1,0:T(8,128)(2,1)S(1)}, u32[]{:S(2)}, u32[]{:S(2)}) %collective-permute-start.15) | collective-permute-done | bytes 286752 | tf_op jit(solution)/shard_map/ppermute | solution.py:212
  91.0 0.7 fusion.45
  91.8 0.1 pad_maximum_fusion
  91.9 0.1 collective-permute-start.21
  92.0 1.6 %collective-permute-start.20 = (f32[128,128]{1,0:T(8,128)S(1)}, f32[128,128]{1,0:T(8,128)S(1)}, u32[]{:S(2)}, u32[]{:S(2)}) collective-permute-start(f32[128,128]{1,0:T(8,128)S(1)} %pad_maximum_fusion), channel_id=1, source_target_pairs={{0,2},{1,3},{2,0},{3,1},{4,6},{5,7},{6,4},{7,5},{8,10},{9,11},{10,... | collective-permute-start | bytes 196616 | tf_op jit(solution)/shard_map/ppermute | solution.py:155
  93.5 0.3 collective-permute-start.19
  93.8 0.8 fusion.18
  94.6 1.4 %collective-permute-done.22 = bf16[32,4736]{1,0:T(8,128)(2,1)S(1)} collective-permute-done((bf16[32,4736]{1,0:T(8,128)(2,1)S(1)}, bf16[32,4736]{1,0:T(8,128)(2,1)S(1)}, u32[]{:S(2)}, u32[]{:S(2)}) %collective-permute-start.22) | collective-permute-done | bytes 303136 | tf_op jit(solution)/shard_map/ppermute | solution.py:212
  96.0 1.4 %fusion.8 = f32[512,64]{1,0:T(8,128)S(1)} fusion(bf16[512,7168]{1,0:T(8,128)(2,1)S(1)} %copy-done.2, bf16[32,4736]{1,0:T(8,128)(2,1)S(1)} %collective-permute-done.23, bf16[32,4736]{1,0:T(8,128)(2,1)S(1)} %collective-permute-done.22), kind=kOutput, calls=%fused_computation.8 | convolution fusion | flops 311590912 | bytes 5586944 | tf_op jit(solution)/shard_map/dot_general | solution.py:101
  97.5 0.3 collective-permute-done.20
  97.8 0.3 score.1
  98.1 0.5 collective-permute-start.26
  98.6 1.2 %collective-permute-start.25 = (f32[2,16]{1,0:T(2,128)S(1)}, f32[2,16]{1,0:T(2,128)S(1)}, u32[]{:S(2)}, u32[]{:S(2)}) collective-permute-start(f32[2,16]{1,0:T(2,128)S(1)} %score.1), channel_id=1, source_target_pairs={{0,2},{1,3},{2,0},{3,1},{4,6},{5,7},{6,4},{7,5},{8,10},{9,11},{10,... | collective-permute-start | bytes 392 | tf_op jit(solution)/shard_map/ppermute | solution.py:155
  99.8 0.2 collective-permute-start.24
  100.0 1.1 %collective-permute-done.26 = f32[2,16]{1,0:T(2,128)S(1)} collective-permute-done((f32[2,16]{1,0:T(2,128)S(1)}, f32[2,16]{1,0:T(2,128)S(1)}, u32[]{:S(2)}, u32[]{:S(2)}) %collective-permute-start.26) | collective-permute-done | bytes 160 | tf_op jit(solution)/shard_map/ppermute | solution.py:155
  101.1 1.0 collective-permute-done.25
  102.2 0.6 add_add_fusion.1
  (65 shorter events, 1.1 us)
Async XLA Ops:
  0.0 0.7 copy-start
  2.4 20.3 %collective-permute-start.1 = (bf16[64,4480]{1,0:T(8,128)(2,1)S(1)}, bf16[64,4480]{1,0:T(8,128)(2,1)S(1)}, u32[]{:S(2)}, u32[]{:S(2)}) collective-permute-start(bf16[64,4480]{1,0:T(8,128)(2,1)S(1)} %pick_rows.2), channel_id=1, source_target_pairs={{8,0},{16,8},{24,16},{28,24},{20,28},{12,20},{4,12},{0,4},{9,1},{1... | collective-permute-start | bytes 1720328 | tf_op jit(solution)/shard_map/ppermute | solution.py:212
  5.4 17.4 %collective-permute-start = (bf16[64,4480]{1,0:T(8,128)(2,1)S(1)}, bf16[64,4480]{1,0:T(8,128)(2,1)S(1)}, u32[]{:S(2)}, u32[]{:S(2)}) collective-permute-start(bf16[64,4480]{1,0:T(8,128)(2,1)S(1)} %pick_rows.2), channel_id=1, source_target_pairs={{0,8},{8,16},{16,24},{24,28},{28,20},{20,12},{12,4},{4,0},{1,9},{9... | collective-permute-start | bytes 1720328 | tf_op jit(solution)/shard_map/ppermute | solution.py:212
  5.5 3.4 %copy-start.1 = (s32[16]{0:T(128)S(1)}, s32[16]{0:T(128)}, u32[]{:S(2)}) copy-start(s32[16]{0:T(128)} %owners_ref.2) | copy-start | bytes 196
  10.6 21.7 %collective-permute-start.8 = (bf16[64,4736]{1,0:T(8,128)(2,1)S(1)}, bf16[64,4736]{1,0:T(8,128)(2,1)S(1)}, u32[]{:S(2)}, u32[]{:S(2)}) collective-permute-start(bf16[64,4736]{1,0:T(8,128)(2,1)S(1)} %pick_rows.3), channel_id=1, source_target_pairs={{8,0},{16,8},{24,16},{28,24},{20,28},{12,20},{4,12},{0,4},{9,1},{1... | collective-permute-start | bytes 1818632 | tf_op jit(solution)/shard_map/ppermute | solution.py:212
  12.5 21.9 %collective-permute-start.7 = (bf16[64,4736]{1,0:T(8,128)(2,1)S(1)}, bf16[64,4736]{1,0:T(8,128)(2,1)}, u32[]{:S(2)}, u32[]{:S(2)}) collective-permute-start(bf16[64,4736]{1,0:T(8,128)(2,1)S(1)} %pick_rows.3), channel_id=1, source_target_pairs={{0,8},{8,16},{16,24},{24,28},{28,20},{20,12},{12,4},{4,0},{1,9},{9... | collective-permute-start | bytes 1818632 | tf_op jit(solution)/shard_map/ppermute | solution.py:212
  22.5 4.9 %copy-start.2 = (bf16[512,7168]{1,0:T(8,128)(2,1)S(1)}, bf16[512,7168]{1,0:T(8,128)(2,1)}, u32[]{:S(2)}) copy-start(bf16[512,7168]{1,0:T(8,128)(2,1)} %rotate.3) | copy-start | bytes 22020100
  22.8 23.8 %collective-permute-start.2 = (bf16[64,4480]{1,0:T(8,128)(2,1)S(1)}, bf16[64,4480]{1,0:T(8,128)(2,1)S(1)}, u32[]{:S(2)}, u32[]{:S(2)}) collective-permute-start(bf16[64,4480]{1,0:T(8,128)(2,1)S(1)} %collective-permute-done), channel_id=1, source_target_pairs={{0,8},{8,16},{16,24},{24,28},{28,20},{20,12},{12,4},{4,0},{1,9},{9... | collective-permute-start | bytes 1720328 | tf_op jit(solution)/shard_map/ppermute | solution.py:212
  24.8 21.9 %collective-permute-start.3 = (bf16[64,4480]{1,0:T(8,128)(2,1)S(1)}, bf16[64,4480]{1,0:T(8,128)(2,1)S(1)}, u32[]{:S(2)}, u32[]{:S(2)}) collective-permute-start(bf16[64,4480]{1,0:T(8,128)(2,1)S(1)} %collective-permute-done.1), channel_id=1, source_target_pairs={{8,0},{16,8},{24,16},{28,24},{20,28},{12,20},{4,12},{0,4},{9,1},{1... | collective-permute-start | bytes 1720328 | tf_op jit(solution)/shard_map/ppermute | solution.py:212
  34.4 25.2 %collective-permute-start.13 = (bf16[64,4736]{1,0:T(8,128)(2,1)}, bf16[64,4736]{1,0:T(8,128)(2,1)S(1)}, u32[]{:S(2)}, u32[]{:S(2)}) collective-permute-start(bf16[64,4736]{1,0:T(8,128)(2,1)} %collective-permute-done.7), channel_id=1, source_target_pairs={{0,8},{8,16},{16,24},{24,28},{28,20},{20,12},{12,4},{4,0},{1,9},{9... | collective-permute-start | bytes 1818632 | tf_op jit(solution)/shard_map/ppermute | solution.py:212
  34.5 25.1 %collective-permute-start.14 = (bf16[64,4736]{1,0:T(8,128)(2,1)S(1)}, bf16[64,4736]{1,0:T(8,128)(2,1)S(1)}, u32[]{:S(2)}, u32[]{:S(2)}) collective-permute-start(bf16[64,4736]{1,0:T(8,128)(2,1)S(1)} %collective-permute-done.8), channel_id=1, source_target_pairs={{8,0},{16,8},{24,16},{28,24},{20,28},{12,20},{4,12},{0,4},{9,1},{1... | collective-permute-start | bytes 1818632 | tf_op jit(solution)/shard_map/ppermute | solution.py:212
  38.9 7.8 %copy-start.3 = (bf16[512,2048]{1,0:T(8,128)(2,1)S(1)}, bf16[512,2048]{1,0:T(8,128)(2,1)}, u32[]{:S(2)}) copy-start(bf16[512,2048]{1,0:T(8,128)(2,1)} %rotate.2) | copy-start | bytes 6291460
  48.1 13.5 %collective-permute-start.4 = (f32[128,320]{1,0:T(8,128)S(1)}, f32[128,320]{1,0:T(8,128)S(1)}, u32[]{:S(2)}, u32[]{:S(2)}) collective-permute-start(f32[128,320]{1,0:T(8,128)S(1)} %constant_dynamic-slice_fusion), channel_id=1, source_target_pairs={{0,1},{1,0},{2,3},{3,2},{4,5},{5,4},{6,7},{7,6},{8,9},{9,8},{10,11... | collective-permute-start | bytes 491528 | tf_op jit(solution)/shard_map/ppermute | solution.py:155
  48.2 23.7 %collective-permute-start.9 = (bf16[64,4480]{1,0:T(8,128)(2,1)S(1)}, bf16[64,4480]{1,0:T(8,128)(2,1)S(1)}, u32[]{:S(2)}, u32[]{:S(2)}) collective-permute-start(bf16[64,4480]{1,0:T(8,128)(2,1)S(1)} %collective-permute-done.2), channel_id=1, source_target_pairs={{0,8},{8,16},{16,24},{24,28},{28,20},{20,12},{12,4},{4,0},{1,9},{9... | collective-permute-start | bytes 1720328 | tf_op jit(solution)/shard_map/ppermute | solution.py:212
  48.4 23.5 %collective-permute-start.10 = (bf16[64,4480]{1,0:T(8,128)(2,1)S(1)}, bf16[64,4480]{1,0:T(8,128)(2,1)S(1)}, u32[]{:S(2)}, u32[]{:S(2)}) collective-permute-start(bf16[64,4480]{1,0:T(8,128)(2,1)S(1)} %collective-permute-done.3), channel_id=1, source_target_pairs={{8,0},{16,8},{24,16},{28,24},{20,28},{12,20},{4,12},{0,4},{9,1},{1... | collective-permute-start | bytes 1720328 | tf_op jit(solution)/shard_map/ppermute | solution.py:212
  59.6 25.3 %collective-permute-start.17 = (bf16[64,4736]{1,0:T(8,128)(2,1)S(1)}, bf16[64,4736]{1,0:T(8,128)(2,1)S(1)}, u32[]{:S(2)}, u32[]{:S(2)}) collective-permute-start(bf16[64,4736]{1,0:T(8,128)(2,1)S(1)} %collective-permute-done.13), channel_id=1, source_target_pairs={{0,8},{8,16},{16,24},{24,28},{28,20},{20,12},{12,4},{4,0},{1,9},{9... | collective-permute-start | bytes 1818632 | tf_op jit(solution)/shard_map/ppermute | solution.py:212
  59.7 25.2 %collective-permute-start.18 = (bf16[64,4736]{1,0:T(8,128)(2,1)S(1)}, bf16[64,4736]{1,0:T(8,128)(2,1)S(1)}, u32[]{:S(2)}, u32[]{:S(2)}) collective-permute-start(bf16[64,4736]{1,0:T(8,128)(2,1)S(1)} %collective-permute-done.14), channel_id=1, source_target_pairs={{8,0},{16,8},{24,16},{28,24},{20,28},{12,20},{4,12},{0,4},{9,1},{1... | collective-permute-start | bytes 1818632 | tf_op jit(solution)/shard_map/ppermute | solution.py:212
  61.6 5.7 %collective-permute-start.5 = (f32[128,320]{1,0:T(8,128)S(1)}, f32[128,320]{1,0:T(8,128)S(1)}, u32[]{:S(2)}, u32[]{:S(2)}) collective-permute-start(f32[128,320]{1,0:T(8,128)S(1)} %dynamic-slice_add_fusion), channel_id=1, source_target_pairs={{0,2},{1,3},{2,0},{3,1},{4,6},{5,7},{6,4},{7,5},{8,10},{9,11},{10,... | collective-permute-start | bytes 491528 | tf_op jit(solution)/shard_map/ppermute | solution.py:155
  67.4 5.5 %collective-permute-start.6 = (f32[128,320]{1,0:T(8,128)S(1)}, f32[128,320]{1,0:T(8,128)S(1)}, u32[]{:S(2)}, u32[]{:S(2)}) collective-permute-start(f32[128,320]{1,0:T(8,128)S(1)} %add.202), channel_id=1, source_target_pairs={{0,1},{1,0},{2,3},{3,2},{4,5},{5,4},{6,7},{7,6},{8,9},{9,8},{10,11... | collective-permute-start | bytes 491528 | tf_op jit(solution)/shard_map/ppermute | solution.py:155
  72.7 1.4 %collective-permute-start.11 = (f32[256,128]{1,0:T(8,128)S(1)}, f32[256,128]{1,0:T(8,128)S(1)}, u32[]{:S(2)}, u32[]{:S(2)}) collective-permute-start(f32[256,128]{1,0:T(8,128)S(1)} %slice_add_fusion.12), channel_id=1, source_target_pairs={{0,1},{1,0},{2,3},{3,2},{4,5},{5,4},{6,7},{7,6},{8,9},{9,8},{10,11... | collective-permute-start | bytes 393224 | tf_op jit(solution)/shard_map/ppermute | solution.py:155
  74.2 12.8 %collective-permute-start.12 = (f32[256,128]{1,0:T(8,128)S(1)}, f32[256,128]{1,0:T(8,128)S(1)}, u32[]{:S(2)}, u32[]{:S(2)}) collective-permute-start(f32[256,128]{1,0:T(8,128)S(1)} %fusion.65), channel_id=1, source_target_pairs={{0,2},{1,3},{2,0},{3,1},{4,6},{5,7},{6,4},{7,5},{8,10},{9,11},{10,... | collective-permute-start | bytes 393224 | tf_op jit(solution)/shard_map/ppermute | solution.py:155
  76.6 14.4 %collective-permute-start.15 = (bf16[32,4480]{1,0:T(8,128)(2,1)S(1)}, bf16[32,4480]{1,0:T(8,128)(2,1)S(1)}, u32[]{:S(2)}, u32[]{:S(2)}) collective-permute-start(bf16[32,4480]{1,0:T(8,128)(2,1)S(1)} %slice.196), channel_id=1, source_target_pairs={{0,8},{8,16},{16,24},{24,28},{28,20},{20,12},{12,4},{4,0},{1,9},{9... | collective-permute-start | bytes 860168 | tf_op jit(solution)/shard_map/ppermute | solution.py:212
  77.2 13.8 %collective-permute-start.16 = (bf16[32,4480]{1,0:T(8,128)(2,1)S(1)}, bf16[32,4480]{1,0:T(8,128)(2,1)S(1)}, u32[]{:S(2)}, u32[]{:S(2)}) collective-permute-start(bf16[32,4480]{1,0:T(8,128)(2,1)S(1)} %slice.197), channel_id=1, source_target_pairs={{8,0},{16,8},{24,16},{28,24},{20,28},{12,20},{4,12},{0,4},{9,1},{1... | collective-permute-start | bytes 860168 | tf_op jit(solution)/shard_map/ppermute | solution.py:212
  84.9 11.1 %collective-permute-start.22 = (bf16[32,4736]{1,0:T(8,128)(2,1)S(1)}, bf16[32,4736]{1,0:T(8,128)(2,1)S(1)}, u32[]{:S(2)}, u32[]{:S(2)}) collective-permute-start(bf16[32,4736]{1,0:T(8,128)(2,1)S(1)} %slice.207), channel_id=1, source_target_pairs={{0,8},{8,16},{16,24},{24,28},{28,20},{20,12},{12,4},{4,0},{1,9},{9... | collective-permute-start | bytes 909320 | tf_op jit(solution)/shard_map/ppermute | solution.py:212
  85.1 10.9 %collective-permute-start.23 = (bf16[32,4736]{1,0:T(8,128)(2,1)S(1)}, bf16[32,4736]{1,0:T(8,128)(2,1)S(1)}, u32[]{:S(2)}, u32[]{:S(2)}) collective-permute-start(bf16[32,4736]{1,0:T(8,128)(2,1)S(1)} %slice.208), channel_id=1, source_target_pairs={{8,0},{16,8},{24,16},{28,24},{20,28},{12,20},{4,12},{0,4},{9,1},{1... | collective-permute-start | bytes 909320 | tf_op jit(solution)/shard_map/ppermute | solution.py:212
  91.9 5.6 %collective-permute-start.21 = (f32[128,128]{1,0:T(8,128)S(1)}, f32[128,128]{1,0:T(8,128)S(1)}, u32[]{:S(2)}, u32[]{:S(2)}) collective-permute-start(f32[128,128]{1,0:T(8,128)S(1)} %pad_maximum_fusion), channel_id=1, source_target_pairs={{0,3},{1,2},{2,1},{3,0},{4,7},{5,6},{6,5},{7,4},{8,11},{9,10},{10,... | collective-permute-start | bytes 196616 | tf_op jit(solution)/shard_map/ppermute | solution.py:155
  92.0 5.8 %collective-permute-start.20 = (f32[128,128]{1,0:T(8,128)S(1)}, f32[128,128]{1,0:T(8,128)S(1)}, u32[]{:S(2)}, u32[]{:S(2)}) collective-permute-start(f32[128,128]{1,0:T(8,128)S(1)} %pad_maximum_fusion), channel_id=1, source_target_pairs={{0,2},{1,3},{2,0},{3,1},{4,6},{5,7},{6,4},{7,5},{8,10},{9,11},{10,... | collective-permute-start | bytes 196616 | tf_op jit(solution)/shard_map/ppermute | solution.py:155
  93.5 4.2 %collective-permute-start.19 = (f32[128,128]{1,0:T(8,128)S(1)}, f32[128,128]{1,0:T(8,128)S(1)}, u32[]{:S(2)}, u32[]{:S(2)}) collective-permute-start(f32[128,128]{1,0:T(8,128)S(1)} %pad_maximum_fusion), channel_id=1, source_target_pairs={{0,1},{1,0},{2,3},{3,2},{4,5},{5,4},{6,7},{7,6},{8,9},{9,8},{10,11... | collective-permute-start | bytes 196616 | tf_op jit(solution)/shard_map/ppermute | solution.py:155
  98.1 3.0 %collective-permute-start.26 = (f32[2,16]{1,0:T(2,128)S(1)}, f32[2,16]{1,0:T(2,128)S(1)}, u32[]{:S(2)}, u32[]{:S(2)}) collective-permute-start(f32[2,16]{1,0:T(2,128)S(1)} %score.1), channel_id=1, source_target_pairs={{0,3},{1,2},{2,1},{3,0},{4,7},{5,6},{6,5},{7,4},{8,11},{9,10},{10,... | collective-permute-start | bytes 392 | tf_op jit(solution)/shard_map/ppermute | solution.py:155
  98.6 3.6 %collective-permute-start.25 = (f32[2,16]{1,0:T(2,128)S(1)}, f32[2,16]{1,0:T(2,128)S(1)}, u32[]{:S(2)}, u32[]{:S(2)}) collective-permute-start(f32[2,16]{1,0:T(2,128)S(1)} %score.1), channel_id=1, source_target_pairs={{0,2},{1,3},{2,0},{3,1},{4,6},{5,7},{6,4},{7,5},{8,10},{9,11},{10,... | collective-permute-start | bytes 392 | tf_op jit(solution)/shard_map/ppermute | solution.py:155
  99.8 2.3 %collective-permute-start.24 = (f32[2,16]{1,0:T(2,128)S(1)}, f32[2,16]{1,0:T(2,128)S(1)}, u32[]{:S(2)}, u32[]{:S(2)}) collective-permute-start(f32[2,16]{1,0:T(2,128)S(1)} %score.1), channel_id=1, source_target_pairs={{0,1},{1,0},{2,3},{3,2},{4,5},{5,4},{6,7},{7,6},{8,9},{9,8},{10,11... | collective-permute-start | bytes 392 | tf_op jit(solution)/shard_map/ppermute | solution.py:155
